TPU v7x, 256 devices: a whole 4x4x8 slice. The times are simulated.
256 devices in a mesh: tm: 32 (over x, z), head: 8 (over y, core).
Axes of the slice: x: 4, y: 4, z: 8, core: 2. Of those that a mesh axis runs over, the one named last changes fastest.
Arguments:
- query_rows: bfloat16 [8192, 5120], P('tm', 'head'), may hold values from -6 to 6
- key_rows: bfloat16 [8192, 5120], P('tm', 'head'), may hold values from -6 to 6
- value_rows: bfloat16 [8192, 5120], P('tm', 'head'), may hold values from -6 to 6
- residual_in: bfloat16 [8192, 5120], P('tm', 'head'), may hold values from -6 to 6
- out_weight: bfloat16 [5120, 5120], P('head'), may hold values from -0.078125 to 0.078125
- time_proj: bfloat16 [256, 5120], P(None, 'head'), may hold values from -0.375 to 0.375
- levels: int32 [32], P('tm'), may hold values from 0 to 49
- timestep_table: int32 [50], replicated, may hold values from 0 to 999
- window_offset: int32 [1], replicated, may hold values from 0 to 31
Outputs:
- advanced: bfloat16 [8192, 5120], P('tm', 'head')
All inputs are finite; a program needn't handle non-finite values.
Results may differ from a plain program's by a relative error of at most 0.0075.
Values may be sent and summed in bfloat16 or wider, within the bound.
No kernel may reach another device: no remote copies, remote signals or barrier semaphores. Data moves between devices by JAX's collectives and lax.ppermute only.
A program may use at most 128 MiB of HBM per device.

v0:
```python
import math

import jax
import jax.numpy as jnp
from jax import lax
from jax.sharding import PartitionSpec as P

HEAD_DIM = 128


NEGATIVE = -1e30


def passed_along(shard, axis, by):
    size = lax.axis_size(axis)
    return lax.ppermute(shard, axis, [(i, (i + by) % size) for i in range(size)])


def attend(running, query_heads, query_place, key_heads, value_heads, key_place):
    scores = jnp.einsum(
        "qhd,khd->hqk", query_heads, key_heads, preferred_element_type=jnp.float32
    ) * (1.0 / math.sqrt(HEAD_DIM))
    allowed = key_place[None, :] <= query_place[:, None]
    masked = jnp.where(allowed[None], scores, NEGATIVE)
    maximum_old, total_old, accum_old = running
    maximum_new = jnp.maximum(maximum_old, jnp.max(masked, axis=2))
    weights = jnp.exp(masked - maximum_new[:, :, None]) * allowed[None].astype(jnp.float32)
    factor = jnp.exp(maximum_old - maximum_new)
    total_new = total_old * factor + jnp.sum(weights, axis=2)
    accum_new = accum_old * factor[:, :, None] + jnp.einsum(
        "hqk,khd->hqd",
        weights.astype(jnp.bfloat16),
        value_heads,
        preferred_element_type=jnp.float32,
    )
    return (maximum_new, total_new, accum_new)


def guarded(running, query_heads, query_place, key_heads, value_heads, key_place, needed):

    def compute(carried):
        return attend(carried, query_heads, query_place, key_heads, value_heads, key_place)

    def keep(carried):
        return carried

    return lax.cond(needed, compute, keep, running)


def empty_state(heads_here, query_count):
    return (
        jnp.full((heads_here, query_count), NEGATIVE, jnp.float32),
        jnp.zeros((heads_here, query_count), jnp.float32),
        jnp.zeros((heads_here, query_count, HEAD_DIM), jnp.float32),
    )


def finish(running):
    maximum_now, total_now, accum_now = running
    result = accum_now / total_now[:, :, None]
    result = jnp.transpose(result, (1, 0, 2))
    return result.reshape(result.shape[0], result.shape[1] * HEAD_DIM).astype(jnp.bfloat16)


def over_pieces(update, running, key_heads, value_heads, key_place, key_width):
    count_rows = key_heads.shape[0]
    number = count_rows // key_width
    heads_here = key_heads.shape[1]

    def stepper(carry_state, slices):
        return (update(carry_state, slices[0], slices[1], slices[2]), None)

    running, unused = lax.scan(
        stepper,
        running,
        (
            key_heads.reshape(number, key_width, heads_here, HEAD_DIM),
            value_heads.reshape(number, key_width, heads_here, HEAD_DIM),
            key_place.reshape(number, key_width),
        ),
    )
    return running


def body(
    query_rows,
    key_rows,
    value_rows,
    residual_in,
    out_weight,
    time_proj,
    levels,
    timestep_table,
    window_offset,
):
    span_rows = query_rows.shape[0]
    groups = lax.axis_size("tm")
    heads_here = query_rows.shape[1] // HEAD_DIM
    offset = window_offset[0]
    own_place = (lax.axis_index("tm") - offset) % groups
    key_width = 2 * span_rows
    query_heads = query_rows.reshape(span_rows, heads_here, HEAD_DIM)
    own_places = jnp.full((span_rows,), own_place, jnp.int32)

    def update(running, key_heads, value_heads, key_place):
        return guarded(
            running,
            query_heads,
            own_places,
            key_heads,
            value_heads,
            key_place,
            jnp.min(key_place) <= own_place,
        )

    initial = empty_state(heads_here, span_rows)
    pieces = (
        lax.all_gather(key_rows, "tm", axis=0, tiled=True),
        lax.all_gather(value_rows, "tm", axis=0, tiled=True),
    )
    count_rows = pieces[0].shape[0]
    key_heads = pieces[0].reshape(count_rows, heads_here, HEAD_DIM)
    value_heads = pieces[1].reshape(count_rows, heads_here, HEAD_DIM)
    folded = over_pieces(
        update,
        initial,
        key_heads,
        value_heads,
        (jnp.arange(count_rows, dtype=jnp.int32) // span_rows - offset) % groups,
        key_width,
    )
    attention = finish(folded)
    partial_sum = jnp.dot(attention, out_weight, preferred_element_type=jnp.float32)
    projected = lax.psum_scatter(
        partial_sum.astype(jnp.bfloat16), "head", scatter_dimension=1, tiled=True
    ).astype(jnp.float32)
    half_dim = time_proj.shape[0] // 2
    chosen_level = levels[0]
    stamp_value = jnp.sum(
        jnp.where(
            jnp.arange(timestep_table.shape[0], dtype=jnp.int32) == chosen_level, timestep_table, 0
        )
    ).astype(jnp.float32)
    frequency = jnp.exp(-math.log(10000.0) * jnp.arange(half_dim, dtype=jnp.float32) / half_dim)
    angles = stamp_value * frequency
    embedding = jnp.concatenate([jnp.cos(angles), jnp.sin(angles)])[None, :].astype(jnp.bfloat16)
    gate_row = jnp.dot(embedding, time_proj, preferred_element_type=jnp.float32)
    mixed_rows = (residual_in.astype(jnp.float32) + gate_row * projected).astype(jnp.bfloat16)
    return passed_along(mixed_rows, "tm", 1)


def solution(mesh):
    in_specs = (
        P("tm", "head"),
        P("tm", "head"),
        P("tm", "head"),
        P("tm", "head"),
        P("head", None),
        P(None, "head"),
        P("tm"),
        P(),
        P(),
    )
    out_specs = P("tm", "head")
    return jax.shard_map(body, mesh=mesh, in_specs=in_specs, out_specs=out_specs, check_vma=False)
```

profile of v0, /device:TPU:1, one launch (start us, length us, event | category | flops | bytes accessed | tf_op | source)
XLA Modules:
  0.0 423.7 jit_solution(10765980488572971824)
XLA Ops:
  10.1 112.3 %all-gather.3.cloned.1.call-done = bf16[8192,640]{1,0:T(8,128)(2,1)} async-done(((bf16[256,640]{1,0:T(8,128)(2,1)}), bf16[8192,640]{1,0:T(8,128)(2,1)}) %all-gather.3.cloned.1.call-update) | async-done | bytes 10485776 | tf_op jit(solution)/shard_map/all_gather | solution.py:118
  122.4 23.6 %reshape.88 = bf16[16,512,5,128]{3,2,1,0:T(8,128)(2,1)} reshape(bf16[8192,640]{1,0:T(8,128)(2,1)} %all-gather.3.cloned.1.call-done) | data formatting | bytes 20971520 | tf_op jit(solution)/shard_map/reshape;reshape | solution.py:77
  146.0 12.4 %copy.23 = bf16[16,512,5,128]{3,1,2,0:T(8,128)(2,1)} copy(bf16[16,512,5,128]{3,2,1,0:T(8,128)(2,1)} %reshape.88) | data formatting | bytes 20971520
  158.5 72.6 %all-gather.5.cloned.1.call-done = bf16[8192,640]{1,0:T(8,128)(2,1)} async-done(((bf16[256,640]{1,0:T(8,128)(2,1)}), bf16[8192,640]{1,0:T(8,128)(2,1)}) %all-gather.5.cloned.1.call-update) | async-done | bytes 10485776 | tf_op jit(solution)/shard_map/all_gather | solution.py:119
  231.1 23.6 %reshape.89 = bf16[16,512,5,128]{3,2,1,0:T(8,128)(2,1)} reshape(bf16[8192,640]{1,0:T(8,128)(2,1)} %all-gather.5.cloned.1.call-done) | data formatting | bytes 20971520 | tf_op jit(solution)/shard_map/reshape;reshape | solution.py:78
  254.7 12.5 %copy.25 = bf16[16,512,5,128]{3,1,2,0:T(8,128)(2,1)} copy(bf16[16,512,5,128]{3,2,1,0:T(8,128)(2,1)} %reshape.89) | data formatting | bytes 20971520
  267.3 54.8 %while.16 = (s32[]{:T(128)}, f32[5,256]{1,0:T(8,128)S(1)}, f32[5,256]{1,0:T(8,128)S(1)}, f32[5,256,128]{2,1,0:T(8,128)S(1)}, s32[16,512]{1,0:T(8,128)S(1)}, /*in...) while((s32[]{:T(128)}, f32[5,256]{1,0:T(8,128)S(1)}, ...), condition=%wide.region_7.8_spmd.clone.clone, body=%wide.region_1.7_spmd.clone.clone.sunk | while | flops 344395776 | bytes 10910975 | solution.py:73
  268.6 4.8 %conditional.4 = ((f32[5,256]{1,0:T(8,128)S(1)}, f32[5,256]{1,0:T(8,128)S(1)}, f32[5,256,128]{2,1,0:T(8,128)S(1)})) conditional(s32[]{:T(128)} %convert_element_type.68, (f32[5,256]{1,0:T(8,128)S(1)}, f32[5,256]{1,0:T(8,128)S(1)}, f32[5,256,128]{2,1,0:T(8,128)S(1)}) %tuple.50, (s32[1,512]{1,0:T(1,128)S(1)}, s32[]{:T(128)}, ...), branch_computations={%region_3.3_spmd, %region_4.6_spmd} | conditional | flops 344395264 | bytes 10906660 | solution.py:47
  271.0 2.4 fusion.8
  286.5 4.8 %conditional.4 = ((f32[5,256]{1,0:T(8,128)S(1)}, f32[5,256]{1,0:T(8,128)S(1)}, f32[5,256,128]{2,1,0:T(8,128)S(1)})) conditional(s32[]{:T(128)} %convert_element_type.68, (f32[5,256]{1,0:T(8,128)S(1)}, f32[5,256]{1,0:T(8,128)S(1)}, f32[5,256,128]{2,1,0:T(8,128)S(1)}) %tuple.50, (s32[1,512]{1,0:T(1,128)S(1)}, s32[]{:T(128)}, ...), branch_computations={%region_3.3_spmd, %region_4.6_spmd} | conditional | flops 344395264 | bytes 10906660 | solution.py:47
  289.0 2.4 fusion.8
  292.7 4.8 %conditional.4 = ((f32[5,256]{1,0:T(8,128)S(1)}, f32[5,256]{1,0:T(8,128)S(1)}, f32[5,256,128]{2,1,0:T(8,128)S(1)})) conditional(s32[]{:T(128)} %convert_element_type.68, (f32[5,256]{1,0:T(8,128)S(1)}, f32[5,256]{1,0:T(8,128)S(1)}, f32[5,256,128]{2,1,0:T(8,128)S(1)}) %tuple.50, (s32[1,512]{1,0:T(1,128)S(1)}, s32[]{:T(128)}, ...), branch_computations={%region_3.3_spmd, %region_4.6_spmd} | conditional | flops 344395264 | bytes 10906660 | solution.py:47
  298.8 4.8 %conditional.4 = ((f32[5,256]{1,0:T(8,128)S(1)}, f32[5,256]{1,0:T(8,128)S(1)}, f32[5,256,128]{2,1,0:T(8,128)S(1)})) conditional(s32[]{:T(128)} %convert_element_type.68, (f32[5,256]{1,0:T(8,128)S(1)}, f32[5,256]{1,0:T(8,128)S(1)}, f32[5,256,128]{2,1,0:T(8,128)S(1)}) %tuple.50, (s32[1,512]{1,0:T(1,128)S(1)}, s32[]{:T(128)}, ...), branch_computations={%region_3.3_spmd, %region_4.6_spmd} | conditional | flops 344395264 | bytes 10906660 | solution.py:47
  301.3 2.4 fusion.8
  305.0 4.8 %conditional.4 = ((f32[5,256]{1,0:T(8,128)S(1)}, f32[5,256]{1,0:T(8,128)S(1)}, f32[5,256,128]{2,1,0:T(8,128)S(1)})) conditional(s32[]{:T(128)} %convert_element_type.68, (f32[5,256]{1,0:T(8,128)S(1)}, f32[5,256]{1,0:T(8,128)S(1)}, f32[5,256,128]{2,1,0:T(8,128)S(1)}) %tuple.50, (s32[1,512]{1,0:T(1,128)S(1)}, s32[]{:T(128)}, ...), branch_computations={%region_3.3_spmd, %region_4.6_spmd} | conditional | flops 344395264 | bytes 10906660 | solution.py:47
  307.4 2.4 fusion.8
  311.1 4.8 %conditional.4 = ((f32[5,256]{1,0:T(8,128)S(1)}, f32[5,256]{1,0:T(8,128)S(1)}, f32[5,256,128]{2,1,0:T(8,128)S(1)})) conditional(s32[]{:T(128)} %convert_element_type.68, (f32[5,256]{1,0:T(8,128)S(1)}, f32[5,256]{1,0:T(8,128)S(1)}, f32[5,256,128]{2,1,0:T(8,128)S(1)}) %tuple.50, (s32[1,512]{1,0:T(1,128)S(1)}, s32[]{:T(128)}, ...), branch_computations={%region_3.3_spmd, %region_4.6_spmd} | conditional | flops 344395264 | bytes 10906660 | solution.py:47
  313.5 2.4 fusion.8
  317.2 4.8 %conditional.4 = ((f32[5,256]{1,0:T(8,128)S(1)}, f32[5,256]{1,0:T(8,128)S(1)}, f32[5,256,128]{2,1,0:T(8,128)S(1)})) conditional(s32[]{:T(128)} %convert_element_type.68, (f32[5,256]{1,0:T(8,128)S(1)}, f32[5,256]{1,0:T(8,128)S(1)}, f32[5,256,128]{2,1,0:T(8,128)S(1)}) %tuple.50, (s32[1,512]{1,0:T(1,128)S(1)}, s32[]{:T(128)}, ...), branch_computations={%region_3.3_spmd, %region_4.6_spmd} | conditional | flops 344395264 | bytes 10906660 | solution.py:47
  319.7 2.4 fusion.8
  322.4 5.1 %convolution_convert_fusion = bf16[256,5120]{1,0:T(8,128)(2,1)S(1)} fusion(bf16[256,640]{0,1:T(8,128)(2,1)S(1)} %bitcast.39, bf16[640,5120]{1,0:T(8,128)(2,1)} %param.17), kind=kOutput, calls=%fused_computation.22 | convolution fusion | flops 1679032320 | bytes 9502720 | tf_op jit(solution)/shard_map/dot_general | solution.py:133
  327.5 2.6 copy.32
  332.3 73.3 %reduce-scatter.4.cloned.1.call-done = bf16[640,256]{1,0:T(8,128)(2,1)} async-done(((bf16[5120,256]{1,0:T(8,128)(2,1)}), bf16[640,256]{1,0:T(8,128)(2,1)}) %reduce-scatter.4.cloned.1.call-update) | async-done | bytes 327696
  408.2 8.3 %collective-permute-done = bf16[256,640]{1,0:T(8,128)(2,1)S(1)} collective-permute-done((bf16[256,640]{1,0:T(8,128)(2,1)S(1)}, bf16[256,640]{1,0:T(8,128)(2,1)S(1)}, u32[]{:S(2)}, u32[]{:S(2)}) %collective-permute-start) | collective-permute-done | bytes 327712 | tf_op jit(solution)/shard_map/ppermute | solution.py:16
  (97 shorter events, 37.0 us)
Async XLA Ops:
  6.5 325.6 %copy-start = (bf16[256,640]{1,0:T(8,128)(2,1)S(1)}, bf16[256,640]{1,0:T(8,128)(2,1)}, u32[]{:S(2)}) copy-start(bf16[256,640]{1,0:T(8,128)(2,1)} %param.18) | copy-start | bytes 983044
  6.5 115.9 %all-gather.3.cloned.1.call-start = ((), (), s32[]{:S(2)}) async-start(), calls=%async_computation.1 | async-start | bytes 10813440 | tf_op jit(solution)/shard_map/all_gather | solution.py:118
  7.3 223.9 %all-gather.5.cloned.1.call-start = ((), (), s32[]{:S(2)}) async-start(), calls=%async_computation.2 | async-start | bytes 10813440 | tf_op jit(solution)/shard_map/all_gather | solution.py:119
  8.0 397.6 %reduce-scatter.4.cloned.1.call-start = ((), (), s32[]{:S(2)}) async-start(), calls=%async_computation.3 | async-start | bytes 2949120
  330.1 0.7 copy-start.2
  330.1 76.8 %copy-start.1 = (bf16[256,640]{1,0:T(8,128)(2,1)S(1)}, bf16[256,640]{1,0:T(8,128)(2,1)}, u32[]{:S(2)}) copy-start(bf16[256,640]{1,0:T(8,128)(2,1)} %param.16) | copy-start | bytes 983044
  406.9 9.6 %collective-permute-start = (bf16[256,640]{1,0:T(8,128)(2,1)S(1)}, bf16[256,640]{1,0:T(8,128)(2,1)S(1)}, u32[]{:S(2)}, u32[]{:S(2)}) collective-permute-start(bf16[256,640]{1,0:T(8,128)(2,1)S(1)} %add_convert_fusion), channel_id=1, source_target_pairs={{0,8},{8,16},{16,24},{24,32},{32,40},{40,48},{48,56},{56,64},{64,7... | collective-permute-start | bytes 983048 | tf_op jit(solution)/shard_map/ppermute | solution.py:16
Sparse Core Ops, SparseCore 0:
  9.9 112.4 all-gather.2
  125.0 106.0 all-gather.4
  330.2 75.3 reduce-scatter.3
where the time goes:
time: 429 us; the launch traced here: 424 us
  waiting for transfers between devices  268 us (62%)
  local copies, waits for them, and re-layouts  78.3 us (18%)
  matrix products  33.4 us (8%)
  other arithmetic  16.6 us (4%)
  between operations  15.2 us (4%)
  loops' own time  11 us (3%)
    all_gather x1, waiting for transfers between devices, body(): lax.all_gather(key_rows, 'tm', axis=0, tiled=True)  112 us
    unnamed x4, waiting for transfers between devices  74.7 us
    all_gather x1, waiting for transfers between devices, body(): lax.all_gather(value_rows, 'tm', axis=0, tiled=True)  72.6 us
    unnamed x13, local copies, waits for them, and re-layouts  30.7 us
    another operation x1, local copies, waits for them, and re-layouts, over_pieces(): key_heads.reshape(number, key_width, heads_here, HEAD_DIM)  23.6 us
    another operation x1, local copies, waits for them, and re-layouts, over_pieces(): value_heads.reshape(number, key_width, heads_here, HEAD_DIM)  23.6 us
    dot_general x7, matrix products, attend(): jnp.einsum('hqk,khd->hqd', weights.astype(jnp.bfloat16), value_heads, pre...  16.6 us
    dot_general x7, matrix products, attend(): jnp.einsum('qhd,khd->hqk', query_heads, key_heads, preferred_element_type...  11.5 us
  transfers between devices with their start and end apart: 4, of which 4 were waited for; matrix products, arithmetic and copies ran while one was open for 9% of the time, Pallas kernels for 0%

commit v1 on v0

v1 whole, which is shorter than its diff:
```python
import math

import jax
import jax.numpy as jnp
import numpy as np
from jax import lax
from jax.experimental import pallas as pl
from jax.experimental.pallas import tpu as pltpu
from jax.sharding import PartitionSpec as P

HEAD_DIM = 128
SPAN = 256
X, Z, Y, C = 4, 8, 4, 2
HERE = 5
SPANS = X * Z
NEGATIVE = -1e30
SCALE = math.log2(math.e) / math.sqrt(HEAD_DIM)
VMEM_LIMIT = 48 * 1024 * 1024

HOST = ((0, 1, 3, 4, 6), (0, 2, 4, 5, 7))
SHARED = tuple(z for z in HOST[0] if z in HOST[1])
SHIFTS = (0, 1, 7, 4, 2, 6, 3, 5)
AXES = ("tm", "head")


def device(x, z, y, c):
    return ((x % X) * Z + z % Z) * (Y * C) + (y % Y) * C + c


def head_at(c, z):
    return HOST[c].index(z % Z) if z % Z in HOST[c] else -1


def worker(c, z, r):
    if z % Z in SHARED:
        return (2 * c + r // 2, r % 2)
    return (r, c)


def work_of(x, z, c):
    if z in SHARED:
        return (x // 2, 2 * (x % 2) + c)
    return (c, x) if z in HOST[c] else None


ALL = [(x, z, y, c) for x in range(X) for z in range(Z) for y in range(Y) for c in range(C)]


def key_pairs(shift):
    return [
        (device(x, z, y, c), device(x, z + shift, y, c))
        for x, z, y, c in ALL
        if head_at(c, z + shift) >= 0
    ]


def query_pairs(shift):
    found = []
    for x, z, y, c in ALL:
        if head_at(c, z + shift) >= 0:
            to_x, to_c = worker(c, z + shift, (x + z) % X)
            found.append((device(x, z, y, c), device(to_x, z + shift, y, to_c)))
    return found


def result_pairs(shift):
    found = []
    for x, z, y, c in ALL:
        work = work_of(x, z, c)
        if work is not None:
            head_core, r = work
            from_z = (z - shift) % Z
            slot = (((r - from_z) % X) * Z + from_z + 1) % SPANS
            found.append((device(x, z, y, c), device(slot // Z, slot % Z, y, head_core)))
    return found


def across_pairs(m, half):
    found = []
    for x, z, y, c in ALL:
        to_x = (x + m) % X
        if z in SHARED:
            if to_x // 2 == c:
                found.append((device(x, z, y, c), device(to_x, z, y, half)))
        elif z in HOST[c]:
            found.append((device(x, z, y, c), device(to_x, z, y, c)))
    return found


def core_pairs(m, half):
    found = []
    for x, z, y, c in ALL:
        if z in SHARED and c == (x // 2 if m == 0 else half):
            found.append((device(x, z, y, c), device(x, z, y, 1 - c)))
    return found


ROUNDS = len(SHIFTS)
HALF = ROUNDS // 2
PACK, QSPAN, KSPAN, TAKE, FROM_OTHER, FROM_OTHER_0, ACTIVE, PLACE_Y, CORE = 0, 8, 16, 48, 56, 58, 59, 60, 61
WIDTH = 64


def table():
    rows = np.zeros((X * Z * Y * C, WIDTH), np.int32)
    for x, z, y, c in ALL:
        row = rows[device(x, z, y, c)]
        work = work_of(x, z, c)
        slot_before = (x * Z + z - 1) % SPANS
        for i, shift in enumerate(SHIFTS):
            row[PACK + i] = head_at(c, z + shift)
            row[TAKE + i] = head_at(c, slot_before % Z + shift)
            from_z = (z - shift) % Z
            if work is not None:
                row[QSPAN + i] = ((work[1] - from_z) % X) * Z + from_z
            for m in range(X):
                row[KSPAN + m * ROUNDS + i] = ((x - m) % X) * Z + from_z
        for half in range(2):
            row[FROM_OTHER + half] = int(z in SHARED and c != half)
        row[FROM_OTHER_0] = int(z in SHARED and c != x // 2)
        row[ACTIVE] = int(work is not None)
        row[PLACE_Y] = y
        row[CORE] = c
    return rows


def moved(block, pairs):
    return lax.ppermute(block, AXES, pairs)


def in_vmem():
    return pl.BlockSpec(memory_space=pltpu.VMEM)


def in_smem():
    return pl.BlockSpec(memory_space=pltpu.SMEM)


def anywhere():
    return pl.BlockSpec(memory_space=pl.ANY)


def shape(*dims, dtype=jnp.bfloat16):
    return jax.ShapeDtypeStruct(dims, dtype)


def pack_kernel(row_ref, query_ref, key_ref, value_ref, *outs):
    for i in range(ROUNDS):
        head = row_ref[PACK + i]

        @pl.when(head >= 0)
        def _():
            columns = pl.ds(pl.multiple_of(head * HEAD_DIM, HEAD_DIM), HEAD_DIM)
            outs[i][:, :HEAD_DIM] = key_ref[:, columns]
            outs[i][:, HEAD_DIM:] = value_ref[:, columns]
            outs[ROUNDS + i][...] = query_ref[:, columns]


def pack(row, query_rows, key_rows, value_rows):
    outs = pl.pallas_call(
        pack_kernel,
        out_shape=[shape(SPAN, 2 * HEAD_DIM)] * ROUNDS + [shape(SPAN, HEAD_DIM)] * ROUNDS,
        in_specs=[in_smem(), in_vmem(), in_vmem(), in_vmem()],
        out_specs=[in_vmem()] * (2 * ROUNDS),
        compiler_params=pltpu.CompilerParams(vmem_limit_bytes=VMEM_LIMIT),
        name="pack",
    )(row, query_rows, key_rows, value_rows)
    return outs[:ROUNDS], outs[ROUNDS:]


BLOCK = 512


def attend_kernel(row_ref, offset_ref, *refs):
    queries, refs = refs[:ROUNDS], refs[ROUNDS:]
    sources, refs = refs[: 4 * X], refs[4 * X :]
    results, (held, copied) = refs[:ROUNDS], refs[ROUNDS:]
    offset = offset_ref[0]

    def place_of(span):
        return lax.rem(span - offset + SPANS, SPANS)

    def rows_at(place):
        return pl.ds(pl.multiple_of(place * SPAN, SPAN), SPAN)

    @pl.when(row_ref[ACTIVE] == 1)
    def _():
        for m in range(X):
            for half in range(2):
                other = row_ref[FROM_OTHER_0 if m == 0 else FROM_OTHER + half]
                for taken in range(2):

                    @pl.when(other == taken)
                    def _():
                        source = sources[taken * 2 * X + m * 2 + half]
                        for i in range(HALF):
                            place = place_of(row_ref[KSPAN + m * ROUNDS + half * HALF + i])
                            pltpu.make_async_copy(
                                source.at[pl.ds(i * SPAN, SPAN)], held.at[rows_at(place)], copied
                            ).start()

        pltpu.make_async_copy(held, held, copied).wait()

        for i in range(ROUNDS):
            own = place_of(row_ref[QSPAN + i])
            query = queries[i][...]

            def step(at, carry, width):
                top, total, summed = carry
                key_rows = pl.ds(pl.multiple_of(at, SPAN), width)
                scores = lax.dot_general(
                    query,
                    held[key_rows, :HEAD_DIM],
                    (((1,), (1,)), ((), ())),
                    preferred_element_type=jnp.float32,
                )
                top_new = jnp.maximum(top, jnp.max(scores, axis=1, keepdims=True))
                weights = jnp.exp2((scores - top_new) * SCALE)
                factor = jnp.exp2((top - top_new) * SCALE)
                total = total * factor + jnp.sum(weights, axis=1, keepdims=True)
                summed = summed * factor + jnp.dot(
                    weights.astype(jnp.bfloat16),
                    held[key_rows, HEAD_DIM:],
                    preferred_element_type=jnp.float32,
                )
                return top_new, total, summed

            start = (
                jnp.full((SPAN, 1), NEGATIVE, jnp.float32),
                jnp.zeros((SPAN, 1), jnp.float32),
                jnp.zeros((SPAN, HEAD_DIM), jnp.float32),
            )
            visible = own + 1
            pairs = lax.div(visible, 2)
            carry = lax.fori_loop(0, pairs, lambda t, s: step(t * BLOCK, s, BLOCK), start)
            carry = lax.fori_loop(2 * pairs, visible, lambda t, s: step(t * SPAN, s, SPAN), carry)
            results[i][...] = (carry[2] / carry[1]).astype(jnp.bfloat16)


def attend(row, offset, queries, sources):
    return pl.pallas_call(
        attend_kernel,
        out_shape=[shape(SPAN, HEAD_DIM)] * ROUNDS,
        in_specs=[in_smem(), in_smem()] + [in_vmem()] * ROUNDS + [anywhere()] * len(sources),
        out_specs=[in_vmem()] * ROUNDS,
        scratch_shapes=[
            pltpu.VMEM((SPANS * SPAN, 2 * HEAD_DIM), jnp.bfloat16),
            pltpu.SemaphoreType.DMA,
        ],
        compiler_params=pltpu.CompilerParams(vmem_limit_bytes=VMEM_LIMIT),
        name="attend",
    )(row, offset, *queries, *sources)


def gather_kernel(row_ref, *refs):
    parts, out_ref = refs[:ROUNDS], refs[ROUNDS]
    for i in range(ROUNDS):
        head = row_ref[TAKE + i]

        @pl.when(head >= 0)
        def _():
            columns = pl.ds(pl.multiple_of(head * HEAD_DIM, HEAD_DIM), HEAD_DIM)
            out_ref[:, columns] = parts[i][...]


def gather_heads(row, parts):
    return pl.pallas_call(
        gather_kernel,
        out_shape=shape(SPAN, HERE * HEAD_DIM),
        in_specs=[in_smem()] + [in_vmem()] * ROUNDS,
        out_specs=in_vmem(),
        compiler_params=pltpu.CompilerParams(vmem_limit_bytes=VMEM_LIMIT),
        name="heads",
    )(row, *parts)


def project_kernel(row_ref, rows_ref, weight_ref, out_ref):
    out_ref[0] = jnp.dot(
        rows_ref[...], weight_ref[...], preferred_element_type=jnp.float32
    ).astype(jnp.bfloat16)


def project(row, rows, weight, other):
    wide = weight.shape[1] // (Y * C)

    def weight_at(m, row_ref):
        core = row_ref[CORE]
        core = 1 - core if other else core
        return (0, lax.rem(row_ref[PLACE_Y] + m, Y) * C + core)

    return pl.pallas_call(
        project_kernel,
        out_shape=shape(Y, SPAN, wide),
        grid_spec=pltpu.PrefetchScalarGridSpec(
            num_scalar_prefetch=1,
            grid=(Y,),
            in_specs=[
                pl.BlockSpec((SPAN, HERE * HEAD_DIM), lambda m, row_ref: (0, 0)),
                pl.BlockSpec((HERE * HEAD_DIM, wide), weight_at),
            ],
            out_specs=pl.BlockSpec((1, SPAN, wide), lambda m, row_ref: (m, 0, 0)),
        ),
        compiler_params=pltpu.CompilerParams(vmem_limit_bytes=VMEM_LIMIT),
        name="project",
    )(row, rows, weight)


def body(
    query_rows,
    key_rows,
    value_rows,
    residual_in,
    out_weight,
    time_proj,
    levels,
    timestep_table,
    window_offset,
):
    me = lax.axis_index("tm") * (Y * C) + lax.axis_index("head")
    row = lax.dynamic_slice(jnp.asarray(table()), (me, 0), (1, WIDTH))[0]
    packed, packed_queries = pack(row, query_rows, key_rows, value_rows)

    arrived = [
        packed[i] if shift == 0 else moved(packed[i], key_pairs(shift))
        for i, shift in enumerate(SHIFTS)
    ]
    queries = [moved(packed_queries[i], query_pairs(shift)) for i, shift in enumerate(SHIFTS)]

    own = [jnp.concatenate(arrived[half * HALF : (half + 1) * HALF]) for half in range(2)]
    direct, shared = {}, {}
    for half in range(2):
        for m in (2, 1, 3, 0):
            direct[m, half] = moved(own[half], across_pairs(m, half)) if m else own[half]
            shared[m, half] = moved(direct[m, half], core_pairs(m, half))
    order = [(m, half) for m in range(X) for half in range(2)]
    sources = [direct[key] for key in order] + [shared[key] for key in order]

    results = attend(row, window_offset, queries, sources)

    parts = [moved(results[i], result_pairs(shift)) for i, shift in enumerate(SHIFTS)]
    next_slot = [
        (device(x, z, y, c), device((x * Z + z + 1) % SPANS // Z, z + 1, y, c)) for x, z, y, c in ALL
    ]
    residual = moved(residual_in, next_slot)
    level = moved(levels, next_slot)[0]

    attention = gather_heads(row, parts)
    swap = [(device(x, z, y, c), device(x, z, y, 1 - c)) for x, z, y, c in ALL]
    from_core = moved(project(row, attention, out_weight, True), swap)
    kept = project(row, attention, out_weight, False)
    both = [kept[m].astype(jnp.float32) + from_core[m].astype(jnp.float32) for m in range(Y)]
    projected = both[0]
    for m in (2, 1, 3):
        pairs = [(device(x, z, y, c), device(x, z, y + m, c)) for x, z, y, c in ALL]
        projected = projected + moved(both[m].astype(jnp.bfloat16), pairs).astype(jnp.float32)

    half_dim = time_proj.shape[0] // 2
    stamp_value = jnp.sum(
        jnp.where(jnp.arange(timestep_table.shape[0], dtype=jnp.int32) == level, timestep_table, 0)
    ).astype(jnp.float32)
    frequency = jnp.exp(-math.log(10000.0) * jnp.arange(half_dim, dtype=jnp.float32) / half_dim)
    angles = stamp_value * frequency
    embedding = jnp.concatenate([jnp.cos(angles), jnp.sin(angles)])[None, :].astype(jnp.bfloat16)
    gate_row = jnp.dot(embedding, time_proj, preferred_element_type=jnp.float32)
    return (residual.astype(jnp.float32) + gate_row * projected).astype(jnp.bfloat16)


def solution(mesh):
    in_specs = (
        P("tm", "head"),
        P("tm", "head"),
        P("tm", "head"),
        P("tm", "head"),
        P("head", None),
        P(None, "head"),
        P("tm"),
        P(),
        P(),
    )
    out_specs = P("tm", "head")
    return jax.shard_map(body, mesh=mesh, in_specs=in_specs, out_specs=out_specs, check_vma=False)
```

time: 429 us -> 319 us (0.74)
  waiting for transfers between devices: 268 us -> 56.3 us
  starting transfers between devices: 1.3 us -> 204 us
  local copies, waits for them, and re-layouts: 78.3 us -> 4.56 us
  Pallas kernels: 0 us -> 47 us
  matrix products: 33.4 us -> 0.17 us
  between operations: 15.2 us -> 2.07 us
  other arithmetic: 16.6 us -> 3.51 us
  loops' own time: 11 us -> 0 us
    ppermute x1 -> x43, starting transfers between devices: 1.22 us -> 204 us  [moved(): return lax.ppermute(block, AXES, pairs)]
    all_gather x2 -> x0, waiting for transfers between devices: 185 us -> none  [the longest x1 112 us: body(): lax.all_gather(key_rows, 'tm', axis=0, tiled=True)]
    unnamed x4 -> x0, waiting for transfers between devices: 74.7 us -> none
    ppermute x1 -> x43, waiting for transfers between devices: 8.33 us -> 56.3 us  [moved(): return lax.ppermute(block, AXES, pairs)]
    another operation x2 -> x0, local copies, waits for them, and re-layouts: 47.2 us -> none  [the longest x1 23.6 us: over_pieces(): key_heads.reshape(number, key_width, heads_here, HEAD_DIM)]
    pallas_call x0 -> x5, Pallas kernels: none -> 47 us  [the longest x1 37 us: attend(): pl.pallas_call(attend_kernel, out_shape=[shape(SPAN, HEAD_DIM)] * ROUNDS,...]
    dot_general x15 -> x0, matrix products: 33.3 us -> none  [the longest x7 16.6 us: attend(): jnp.einsum('hqk,khd->hqd', weights.astype(jnp.bfloat16), value_heads, pre...]
    unnamed x13 -> x30, local copies, waits for them, and re-layouts: 30.7 us -> 3.79 us
  transfers between devices with their start and end apart: 4 -> 43, of which waited for: 4 -> 11; matrix products, arithmetic and copies ran while one was open for 9% -> 1% of each run, Pallas kernels for 0% -> 1%
where the time goes in v1:
time: 319 us; the launch traced here: 317 us
  starting transfers between devices  204 us (64%)
  waiting for transfers between devices  56.3 us (18%)
  Pallas kernels  47 us (15%)
  local copies, waits for them, and re-layouts  4.56 us (1%)
  other arithmetic  3.51 us (1%)
    ppermute x43, starting transfers between devices, moved(): return lax.ppermute(block, AXES, pairs)  204 us
    ppermute x43, waiting for transfers between devices, moved(): return lax.ppermute(block, AXES, pairs)  56.3 us
    pallas_call x1, Pallas kernels, attend(): pl.pallas_call(attend_kernel, out_shape=[shape(SPAN, HEAD_DIM)] * ROUNDS,...  37 us
    pallas_call x2, Pallas kernels, project(): pl.pallas_call(project_kernel, out_shape=shape(Y, SPAN, wide), grid_spec=...  8.66 us
  transfers between devices with their start and end apart: 43, of which 11 were waited for; matrix products, arithmetic and copies ran while one was open for 1% of the time, Pallas kernels for 1%

profile of v1, /device:TPU:1, one launch (start us, length us, event | category | flops | bytes accessed | tf_op | source)
XLA Modules:
  0.0 317.1 jit_solution(4175035995602048327)
XLA Ops:
  4.4 5.7 %collective-permute-start.13 = (bf16[256,256]{1,0:T(8,128)(2,1)S(1)}, bf16[256,256]{1,0:T(8,128)(2,1)S(1)}, u32[]{:S(2)}, u32[]{:S(2)}) collective-permute-start(bf16[256,256]{1,0:T(8,128)(2,1)S(1)} %get-tuple-element.41), channel_id=1, source_target_pairs={{1,17},{3,19},{5,21},{7,23},{8,24},{10,26},{12,28},{14,30},{16,32}... | collective-permute-start | bytes 393224 | tf_op jit(solution)/shard_map/ppermute | solution.py:128
  12.8 7.2 %collective-permute-start.16 = (bf16[256,256]{1,0:T(8,128)(2,1)S(1)}, bf16[256,256]{1,0:T(8,128)(2,1)S(1)}, u32[]{:S(2)}, u32[]{:S(2)}) collective-permute-start(bf16[256,256]{1,0:T(8,128)(2,1)S(1)} %get-tuple-element.44), channel_id=1, source_target_pairs={{1,41},{3,43},{5,45},{7,47},{8,48},{10,50},{12,52},{14,54},{17,57}... | collective-permute-start | bytes 393224 | tf_op jit(solution)/shard_map/ppermute | solution.py:128
  21.3 6.7 %collective-permute-start.11 = (bf16[256,256]{1,0:T(8,128)(2,1)S(1)}, bf16[256,256]{1,0:T(8,128)(2,1)S(1)}, u32[]{:S(2)}, u32[]{:S(2)}) collective-permute-start(bf16[256,256]{1,0:T(8,128)(2,1)S(1)} %get-tuple-element.39), channel_id=1, source_target_pairs={{1,57},{3,59},{5,61},{7,63},{8,0},{9,1},{10,2},{11,3},{12,4},{13,5... | collective-permute-start | bytes 393224 | tf_op jit(solution)/shard_map/ppermute | solution.py:128
  30.9 9.4 %collective-permute-start.2 = (bf16[256,128]{1,0:T(8,128)(2,1)S(1)}, bf16[256,128]{1,0:T(8,128)(2,1)S(1)}, u32[]{:S(2)}, u32[]{:S(2)}) collective-permute-start(bf16[256,128]{1,0:T(8,128)(2,1)S(1)} %get-tuple-element.29), channel_id=1, source_target_pairs={{0,0},{1,128},{2,2},{3,130},{4,4},{5,132},{6,6},{7,134},{8,72},{10... | collective-permute-start | bytes 196616 | tf_op jit(solution)/shard_map/ppermute | solution.py:128
  49.2 8.3 %collective-permute-done.3.refs_1_ = bf16[256,128]{1,0:T(8,128)(2,1)S(1)} collective-permute-done((bf16[256,128]{1,0:T(8,128)(2,1)S(1)}, bf16[256,128]{1,0:T(8,128)(2,1)S(1)}, u32[]{:S(2)}, u32[]{:S(2)}) %collective-permute-start.3) | collective-permute-done | bytes 65568 | tf_op jit(solution)/shard_map/ppermute | solution.py:128
  57.4 7.0 %collective-permute-start.4 = (bf16[256,128]{1,0:T(8,128)(2,1)S(1)}, bf16[256,128]{1,0:T(8,128)(2,1)S(1)}, u32[]{:S(2)}, u32[]{:S(2)}) collective-permute-start(bf16[256,128]{1,0:T(8,128)(2,1)S(1)} %get-tuple-element.31), channel_id=1, source_target_pairs={{1,57},{3,59},{5,61},{7,63},{8,1},{9,129},{10,3},{11,131},{12,5},{... | collective-permute-start | bytes 196616 | tf_op jit(solution)/shard_map/ppermute | solution.py:128
  68.3 10.3 %collective-permute-start.5 = (bf16[256,128]{1,0:T(8,128)(2,1)S(1)}, bf16[256,128]{1,0:T(8,128)(2,1)S(1)}, u32[]{:S(2)}, u32[]{:S(2)}) collective-permute-start(bf16[256,128]{1,0:T(8,128)(2,1)S(1)} %get-tuple-element.32), channel_id=1, source_target_pairs={{0,32},{1,160},{2,34},{3,162},{4,36},{5,164},{6,38},{7,166},{9,105... | collective-permute-start | bytes 196616 | tf_op jit(solution)/shard_map/ppermute | solution.py:128
  80.4 5.5 %collective-permute-start.6 = (bf16[256,128]{1,0:T(8,128)(2,1)S(1)}, bf16[256,128]{1,0:T(8,128)(2,1)S(1)}, u32[]{:S(2)}, u32[]{:S(2)}) collective-permute-start(bf16[256,128]{1,0:T(8,128)(2,1)S(1)} %get-tuple-element.33), channel_id=1, source_target_pairs={{1,17},{3,19},{5,21},{7,23},{8,88},{10,90},{12,92},{14,94},{16,96}... | collective-permute-start | bytes 196616 | tf_op jit(solution)/shard_map/ppermute | solution.py:128
  85.9 5.9 %collective-permute-done.6.refs_4_ = bf16[256,128]{1,0:T(8,128)(2,1)S(1)} collective-permute-done((bf16[256,128]{1,0:T(8,128)(2,1)S(1)}, bf16[256,128]{1,0:T(8,128)(2,1)S(1)}, u32[]{:S(2)}, u32[]{:S(2)}) %collective-permute-start.6) | collective-permute-done | bytes 65568 | tf_op jit(solution)/shard_map/ppermute | solution.py:128
  93.0 7.6 %collective-permute-done.7.refs_5_ = bf16[256,128]{1,0:T(8,128)(2,1)S(1)} collective-permute-done((bf16[256,128]{1,0:T(8,128)(2,1)S(1)}, bf16[256,128]{1,0:T(8,128)(2,1)S(1)}, u32[]{:S(2)}, u32[]{:S(2)}) %collective-permute-start.7) | collective-permute-done | bytes 65568 | tf_op jit(solution)/shard_map/ppermute | solution.py:128
  101.9 7.4 %collective-permute-done.8.refs_6_ = bf16[256,128]{1,0:T(8,128)(2,1)S(1)} collective-permute-done((bf16[256,128]{1,0:T(8,128)(2,1)S(1)}, bf16[256,128]{1,0:T(8,128)(2,1)S(1)}, u32[]{:S(2)}, u32[]{:S(2)}) %collective-permute-start.8) | collective-permute-done | bytes 65568 | tf_op jit(solution)/shard_map/ppermute | solution.py:128
  113.6 5.5 %collective-permute-done.9.refs_7_ = bf16[256,128]{1,0:T(8,128)(2,1)S(1)} collective-permute-done((bf16[256,128]{1,0:T(8,128)(2,1)S(1)}, bf16[256,128]{1,0:T(8,128)(2,1)S(1)}, u32[]{:S(2)}, u32[]{:S(2)}) %collective-permute-start.9) | collective-permute-done | bytes 65568 | tf_op jit(solution)/shard_map/ppermute | solution.py:128
  120.9 7.1 %collective-permute-start.21 = (bf16[1024,256]{1,0:T(8,128)(2,1)S(1)}, bf16[1024,256]{1,0:T(8,128)(2,1)S(1)}, u32[]{:S(2)}, u32[]{:S(2)}) collective-permute-start(bf16[1024,256]{1,0:T(8,128)(2,1)S(1)} %constant_dynamic-update-slice_fusion.refs_8_), channel_id=1, source_target_pairs={{1,192},{3,194},{5,196},{7,198},{8,200},{10,202},{12,204},{14,206}... | collective-permute-start | bytes 1572872 | tf_op jit(solution)/shard_map/ppermute | solution.py:128
  147.0 37.0 %attend.1 = (bf16[256,128]{1,0:T(8,128)(2,1)S(1)}, bf16[256,128]{1,0:T(8,128)(2,1)S(1)}, bf16[256,128]{1,0:T(8,128)(2,1)S(1)}, bf16[256,128]{1,0:T(8,128)(2,1)S(...) custom-call(s32[64]{0:T(128)S(1)} %dynamic-slice_bitcast_fusion.row_, ...), custom_call_target="tpu_custom_call" | custom-call | tf_op jit(solution)/shard_map/attend/pallas_call | solution.py:241
  193.3 12.0 %collective-permute-start.36 = (bf16[256,128]{1,0:T(8,128)(2,1)S(1)}, bf16[256,128]{1,0:T(8,128)(2,1)S(1)}, u32[]{:S(2)}, u32[]{:S(2)}) collective-permute-start(bf16[256,128]{1,0:T(8,128)(2,1)S(1)} %get-tuple-element.50), channel_id=1, source_target_pairs={{0,152},{1,216},{2,154},{3,218},{4,156},{5,220},{6,158},{7,222},{8... | collective-permute-start | bytes 196616 | tf_op jit(solution)/shard_map/ppermute | solution.py:128
  205.3 10.6 %collective-permute-start.37 = (bf16[256,128]{1,0:T(8,128)(2,1)S(1)}, bf16[256,128]{1,0:T(8,128)(2,1)S(1)}, u32[]{:S(2)}, u32[]{:S(2)}) collective-permute-start(bf16[256,128]{1,0:T(8,128)(2,1)S(1)} %get-tuple-element.51), channel_id=1, source_target_pairs={{0,240},{1,48},{2,242},{3,50},{4,244},{5,52},{6,246},{7,54},{8,184... | collective-permute-start | bytes 196616 | tf_op jit(solution)/shard_map/ppermute | solution.py:128
  215.9 6.3 %collective-permute-start.38 = (bf16[256,128]{1,0:T(8,128)(2,1)S(1)}, bf16[256,128]{1,0:T(8,128)(2,1)S(1)}, u32[]{:S(2)}, u32[]{:S(2)}) collective-permute-start(bf16[256,128]{1,0:T(8,128)(2,1)S(1)} %get-tuple-element.52), channel_id=1, source_target_pairs={{0,96},{1,160},{2,98},{3,162},{4,100},{5,164},{6,102},{7,166},{8,4... | collective-permute-start | bytes 196616 | tf_op jit(solution)/shard_map/ppermute | solution.py:128
  232.5 7.7 %collective-permute-start.39 = (bf16[4,256,640]{2,1,0:T(8,128)(2,1)S(1)}, bf16[4,256,640]{2,1,0:T(8,128)(2,1)S(1)}, u32[]{:S(2)}, u32[]{:S(2)}) collective-permute-start(bf16[4,256,640]{2,1,0:T(8,128)(2,1)S(1)} %project.3), channel_id=1, source_target_pairs={{0,1},{1,0},{2,3},{3,2},{4,5},{5,4},{6,7},{7,6},{8,9},{9,8},{10,11... | collective-permute-start | bytes 3932168 | tf_op jit(solution)/shard_map/ppermute | solution.py:128
  240.2 11.8 %collective-permute-start.1 = (s32[1]{0:T(128)}, s32[1]{0:T(128)}, u32[]{:S(2)}, u32[]{:S(2)}) collective-permute-start(s32[1]{0:T(128)} %param.16), channel_id=1, source_target_pairs={{0,8},{1,9},{2,10},{3,11},{4,12},{5,13},{6,14},{7,15},{8,16},{9,17... | collective-permute-start | bytes 20 | tf_op jit(solution)/shard_map/ppermute | solution.py:128
  252.1 11.8 %collective-permute-start = (bf16[256,640]{1,0:T(8,128)(2,1)}, bf16[256,640]{1,0:T(8,128)(2,1)}, u32[]{:S(2)}, u32[]{:S(2)}) collective-permute-start(bf16[256,640]{1,0:T(8,128)(2,1)} %param.13), channel_id=1, source_target_pairs={{0,8},{1,9},{2,10},{3,11},{4,12},{5,13},{6,14},{7,15},{8,16},{9,17... | collective-permute-start | bytes 983048 | tf_op jit(solution)/shard_map/ppermute | solution.py:128
  270.4 11.9 %collective-permute-start.40 = (bf16[256,640]{1,0:T(8,128)(2,1)S(1)}, bf16[256,640]{1,0:T(8,128)(2,1)S(1)}, u32[]{:S(2)}, u32[]{:S(2)}) collective-permute-start(bf16[256,640]{1,0:T(8,128)(2,1)S(1)} %get-tuple-element.53), channel_id=1, source_target_pairs={{0,4},{1,5},{2,6},{3,7},{4,0},{5,1},{6,2},{7,3},{8,12},{9,13},{10,... | collective-permute-start | bytes 983048 | tf_op jit(solution)/shard_map/ppermute | solution.py:128
  282.3 11.8 %collective-permute-start.41 = (bf16[256,640]{1,0:T(8,128)(2,1)S(1)}, bf16[256,640]{1,0:T(8,128)(2,1)S(1)}, u32[]{:S(2)}, u32[]{:S(2)}) collective-permute-start(bf16[256,640]{1,0:T(8,128)(2,1)S(1)} %get-tuple-element.55), channel_id=1, source_target_pairs={{0,2},{1,3},{2,4},{3,5},{4,6},{5,7},{6,0},{7,1},{8,10},{9,11},{10,... | collective-permute-start | bytes 983048 | tf_op jit(solution)/shard_map/ppermute | solution.py:128
  294.2 11.8 %collective-permute-start.42 = (bf16[256,640]{1,0:T(8,128)(2,1)S(1)}, bf16[256,640]{1,0:T(8,128)(2,1)S(1)}, u32[]{:S(2)}, u32[]{:S(2)}) collective-permute-start(bf16[256,640]{1,0:T(8,128)(2,1)S(1)} %get-tuple-element.54), channel_id=1, source_target_pairs={{0,6},{1,7},{2,0},{3,1},{4,2},{5,3},{6,4},{7,5},{8,14},{9,15},{10,... | collective-permute-start | bytes 983048 | tf_op jit(solution)/shard_map/ppermute | solution.py:128
  306.3 8.9 %collective-permute-done.42 = bf16[256,640]{1,0:T(8,128)(2,1)S(1)} collective-permute-done((bf16[256,640]{1,0:T(8,128)(2,1)S(1)}, bf16[256,640]{1,0:T(8,128)(2,1)S(1)}, u32[]{:S(2)}, u32[]{:S(2)}) %collective-permute-start.42) | collective-permute-done | bytes 327712 | tf_op jit(solution)/shard_map/ppermute | solution.py:128
  (107 shorter events, 79.7 us)
Async XLA Ops:
  10.2 17.9 %collective-permute-start.14 = (bf16[256,256]{1,0:T(8,128)(2,1)S(1)}, bf16[256,256]{1,0:T(8,128)(2,1)S(1)}, u32[]{:S(2)}, u32[]{:S(2)}) collective-permute-start(bf16[256,256]{1,0:T(8,128)(2,1)S(1)} %get-tuple-element.42), channel_id=1, source_target_pairs={{0,48},{2,50},{4,52},{6,54},{9,57},{11,59},{13,61},{15,63},{16,0},... | collective-permute-start | bytes 393224 | tf_op jit(solution)/shard_map/ppermute | solution.py:128
  11.5 19.4 %collective-permute-start.15 = (bf16[256,256]{1,0:T(8,128)(2,1)S(1)}, bf16[256,256]{1,0:T(8,128)(2,1)S(1)}, u32[]{:S(2)}, u32[]{:S(2)}) collective-permute-start(bf16[256,256]{1,0:T(8,128)(2,1)S(1)} %get-tuple-element.43), channel_id=1, source_target_pairs={{0,24},{2,26},{4,28},{6,30},{8,32},{9,33},{10,34},{11,35},{12,36},... | collective-permute-start | bytes 393224 | tf_op jit(solution)/shard_map/ppermute | solution.py:128
  12.8 27.6 %collective-permute-start.16 = (bf16[256,256]{1,0:T(8,128)(2,1)S(1)}, bf16[256,256]{1,0:T(8,128)(2,1)S(1)}, u32[]{:S(2)}, u32[]{:S(2)}) collective-permute-start(bf16[256,256]{1,0:T(8,128)(2,1)S(1)} %get-tuple-element.44), channel_id=1, source_target_pairs={{1,41},{3,43},{5,45},{7,47},{8,48},{10,50},{12,52},{14,54},{17,57}... | collective-permute-start | bytes 393224 | tf_op jit(solution)/shard_map/ppermute | solution.py:128
  20.0 21.7 %collective-permute-start.10 = (bf16[256,256]{1,0:T(8,128)(2,1)S(1)}, bf16[256,256]{1,0:T(8,128)(2,1)S(1)}, u32[]{:S(2)}, u32[]{:S(2)}) collective-permute-start(bf16[256,256]{1,0:T(8,128)(2,1)S(1)} %get-tuple-element.38), channel_id=1, source_target_pairs={{0,8},{2,10},{4,12},{6,14},{9,17},{11,19},{13,21},{15,23},{16,24},... | collective-permute-start | bytes 393224 | tf_op jit(solution)/shard_map/ppermute | solution.py:128
  21.3 23.8 %collective-permute-start.11 = (bf16[256,256]{1,0:T(8,128)(2,1)S(1)}, bf16[256,256]{1,0:T(8,128)(2,1)S(1)}, u32[]{:S(2)}, u32[]{:S(2)}) collective-permute-start(bf16[256,256]{1,0:T(8,128)(2,1)S(1)} %get-tuple-element.39), channel_id=1, source_target_pairs={{1,57},{3,59},{5,61},{7,63},{8,0},{9,1},{10,2},{11,3},{12,4},{13,5... | collective-permute-start | bytes 393224 | tf_op jit(solution)/shard_map/ppermute | solution.py:128
  28.0 19.1 %collective-permute-start.12 = (bf16[256,256]{1,0:T(8,128)(2,1)S(1)}, bf16[256,256]{1,0:T(8,128)(2,1)S(1)}, u32[]{:S(2)}, u32[]{:S(2)}) collective-permute-start(bf16[256,256]{1,0:T(8,128)(2,1)S(1)} %get-tuple-element.40), channel_id=1, source_target_pairs={{0,32},{1,33},{2,34},{3,35},{4,36},{5,37},{6,38},{7,39},{9,41},{11... | collective-permute-start | bytes 393224 | tf_op jit(solution)/shard_map/ppermute | solution.py:128
  30.9 17.0 %collective-permute-start.2 = (bf16[256,128]{1,0:T(8,128)(2,1)S(1)}, bf16[256,128]{1,0:T(8,128)(2,1)S(1)}, u32[]{:S(2)}, u32[]{:S(2)}) collective-permute-start(bf16[256,128]{1,0:T(8,128)(2,1)S(1)} %get-tuple-element.29), channel_id=1, source_target_pairs={{0,0},{1,128},{2,2},{3,130},{4,4},{5,132},{6,6},{7,134},{8,72},{10... | collective-permute-start | bytes 196616 | tf_op jit(solution)/shard_map/ppermute | solution.py:128
  40.4 80.6 %collective-permute-start.18 = (bf16[1024,256]{1,0:T(8,128)(2,1)S(1)}, bf16[1024,256]{1,0:T(8,128)(2,1)S(1)}, u32[]{:S(2)}, u32[]{:S(2)}) collective-permute-start(bf16[1024,256]{1,0:T(8,128)(2,1)S(1)} %constant_dynamic-update-slice_fusion.4.refs_9_), channel_id=1, source_target_pairs={{0,65},{2,67},{4,69},{6,71},{8,72},{10,74},{12,76},{14,78},{17,81}... | collective-permute-start | bytes 1572872 | tf_op jit(solution)/shard_map/ppermute | solution.py:128
  41.7 86.4 %collective-permute-start.20 = (bf16[1024,256]{1,0:T(8,128)(2,1)S(1)}, bf16[1024,256]{1,0:T(8,128)(2,1)S(1)}, u32[]{:S(2)}, u32[]{:S(2)}) collective-permute-start(bf16[1024,256]{1,0:T(8,128)(2,1)S(1)} %constant_dynamic-update-slice_fusion.4.refs_9_), channel_id=1, source_target_pairs={{1,129},{3,131},{5,133},{7,135},{8,136},{10,138},{12,140},{14,142}... | collective-permute-start | bytes 1572872 | tf_op jit(solution)/shard_map/ppermute | solution.py:128
  45.2 84.2 %collective-permute-start.22 = (bf16[1024,256]{1,0:T(8,128)(2,1)S(1)}, bf16[1024,256]{1,0:T(8,128)(2,1)S(1)}, u32[]{:S(2)}, u32[]{:S(2)}) collective-permute-start(bf16[1024,256]{1,0:T(8,128)(2,1)S(1)} %constant_dynamic-update-slice_fusion.4.refs_9_), channel_id=1, source_target_pairs={{1,193},{3,195},{5,197},{7,199},{8,200},{10,202},{12,204},{14,206}... | collective-permute-start | bytes 1572872 | tf_op jit(solution)/shard_map/ppermute | solution.py:128
  47.1 83.5 %collective-permute-start.17 = (bf16[1024,256]{1,0:T(8,128)(2,1)S(1)}, bf16[1024,256]{1,0:T(8,128)(2,1)S(1)}, u32[]{:S(2)}, u32[]{:S(2)}) collective-permute-start(bf16[1024,256]{1,0:T(8,128)(2,1)S(1)} %constant_dynamic-update-slice_fusion.refs_8_), channel_id=1, source_target_pairs={{0,64},{2,66},{4,68},{6,70},{8,72},{10,74},{12,76},{14,78},{17,81}... | collective-permute-start | bytes 1572872 | tf_op jit(solution)/shard_map/ppermute | solution.py:128
  120.9 17.3 %collective-permute-start.21 = (bf16[1024,256]{1,0:T(8,128)(2,1)S(1)}, bf16[1024,256]{1,0:T(8,128)(2,1)S(1)}, u32[]{:S(2)}, u32[]{:S(2)}) collective-permute-start(bf16[1024,256]{1,0:T(8,128)(2,1)S(1)} %constant_dynamic-update-slice_fusion.refs_8_), channel_id=1, source_target_pairs={{1,192},{3,194},{5,196},{7,198},{8,200},{10,202},{12,204},{14,206}... | collective-permute-start | bytes 1572872 | tf_op jit(solution)/shard_map/ppermute | solution.py:128
  187.2 18.1 %collective-permute-start.32 = (bf16[256,128]{1,0:T(8,128)(2,1)S(1)}, bf16[256,128]{1,0:T(8,128)(2,1)S(1)}, u32[]{:S(2)}, u32[]{:S(2)}) collective-permute-start(bf16[256,128]{1,0:T(8,128)(2,1)S(1)} %get-tuple-element.46), channel_id=1, source_target_pairs={{0,128},{1,192},{2,130},{3,194},{4,132},{5,196},{6,134},{7,198},{8... | collective-permute-start | bytes 196616 | tf_op jit(solution)/shard_map/ppermute | solution.py:128
  189.4 26.6 %collective-permute-start.33 = (bf16[256,128]{1,0:T(8,128)(2,1)S(1)}, bf16[256,128]{1,0:T(8,128)(2,1)S(1)}, u32[]{:S(2)}, u32[]{:S(2)}) collective-permute-start(bf16[256,128]{1,0:T(8,128)(2,1)S(1)} %get-tuple-element.47), channel_id=1, source_target_pairs={{0,208},{1,16},{2,210},{3,18},{4,212},{5,20},{6,214},{7,22},{8,152... | collective-permute-start | bytes 196616 | tf_op jit(solution)/shard_map/ppermute | solution.py:128
  190.7 31.6 %collective-permute-start.34 = (bf16[256,128]{1,0:T(8,128)(2,1)S(1)}, bf16[256,128]{1,0:T(8,128)(2,1)S(1)}, u32[]{:S(2)}, u32[]{:S(2)}) collective-permute-start(bf16[256,128]{1,0:T(8,128)(2,1)S(1)} %get-tuple-element.48), channel_id=1, source_target_pairs={{0,40},{1,104},{2,42},{3,106},{4,44},{5,108},{6,46},{7,110},{8,240... | collective-permute-start | bytes 196616 | tf_op jit(solution)/shard_map/ppermute | solution.py:128
  192.0 30.3 %collective-permute-start.35 = (bf16[256,128]{1,0:T(8,128)(2,1)S(1)}, bf16[256,128]{1,0:T(8,128)(2,1)S(1)}, u32[]{:S(2)}, u32[]{:S(2)}) collective-permute-start(bf16[256,128]{1,0:T(8,128)(2,1)S(1)} %get-tuple-element.49), channel_id=1, source_target_pairs={{0,184},{1,248},{2,186},{3,250},{4,188},{5,252},{6,190},{7,254},{8... | collective-permute-start | bytes 196616 | tf_op jit(solution)/shard_map/ppermute | solution.py:128
  193.3 29.0 %collective-permute-start.36 = (bf16[256,128]{1,0:T(8,128)(2,1)S(1)}, bf16[256,128]{1,0:T(8,128)(2,1)S(1)}, u32[]{:S(2)}, u32[]{:S(2)}) collective-permute-start(bf16[256,128]{1,0:T(8,128)(2,1)S(1)} %get-tuple-element.50), channel_id=1, source_target_pairs={{0,152},{1,216},{2,154},{3,218},{4,156},{5,220},{6,158},{7,222},{8... | collective-permute-start | bytes 196616 | tf_op jit(solution)/shard_map/ppermute | solution.py:128
  205.3 16.9 %collective-permute-start.37 = (bf16[256,128]{1,0:T(8,128)(2,1)S(1)}, bf16[256,128]{1,0:T(8,128)(2,1)S(1)}, u32[]{:S(2)}, u32[]{:S(2)}) collective-permute-start(bf16[256,128]{1,0:T(8,128)(2,1)S(1)} %get-tuple-element.51), channel_id=1, source_target_pairs={{0,240},{1,48},{2,242},{3,50},{4,244},{5,52},{6,246},{7,54},{8,184... | collective-permute-start | bytes 196616 | tf_op jit(solution)/shard_map/ppermute | solution.py:128
  232.5 37.6 %collective-permute-start.39 = (bf16[4,256,640]{2,1,0:T(8,128)(2,1)S(1)}, bf16[4,256,640]{2,1,0:T(8,128)(2,1)S(1)}, u32[]{:S(2)}, u32[]{:S(2)}) collective-permute-start(bf16[4,256,640]{2,1,0:T(8,128)(2,1)S(1)} %project.3), channel_id=1, source_target_pairs={{0,1},{1,0},{2,3},{3,2},{4,5},{5,4},{6,7},{7,6},{8,9},{9,8},{10,11... | collective-permute-start | bytes 3932168 | tf_op jit(solution)/shard_map/ppermute | solution.py:128
  240.2 23.7 %collective-permute-start.1 = (s32[1]{0:T(128)}, s32[1]{0:T(128)}, u32[]{:S(2)}, u32[]{:S(2)}) collective-permute-start(s32[1]{0:T(128)} %param.16), channel_id=1, source_target_pairs={{0,8},{1,9},{2,10},{3,11},{4,12},{5,13},{6,14},{7,15},{8,16},{9,17... | collective-permute-start | bytes 20 | tf_op jit(solution)/shard_map/ppermute | solution.py:128
  252.1 54.2 %collective-permute-start = (bf16[256,640]{1,0:T(8,128)(2,1)}, bf16[256,640]{1,0:T(8,128)(2,1)}, u32[]{:S(2)}, u32[]{:S(2)}) collective-permute-start(bf16[256,640]{1,0:T(8,128)(2,1)} %param.13), channel_id=1, source_target_pairs={{0,8},{1,9},{2,10},{3,11},{4,12},{5,13},{6,14},{7,15},{8,16},{9,17... | collective-permute-start | bytes 983048 | tf_op jit(solution)/shard_map/ppermute | solution.py:128
  270.4 35.9 %collective-permute-start.40 = (bf16[256,640]{1,0:T(8,128)(2,1)S(1)}, bf16[256,640]{1,0:T(8,128)(2,1)S(1)}, u32[]{:S(2)}, u32[]{:S(2)}) collective-permute-start(bf16[256,640]{1,0:T(8,128)(2,1)S(1)} %get-tuple-element.53), channel_id=1, source_target_pairs={{0,4},{1,5},{2,6},{3,7},{4,0},{5,1},{6,2},{7,3},{8,12},{9,13},{10,... | collective-permute-start | bytes 983048 | tf_op jit(solution)/shard_map/ppermute | solution.py:128
  282.3 24.0 %collective-permute-start.41 = (bf16[256,640]{1,0:T(8,128)(2,1)S(1)}, bf16[256,640]{1,0:T(8,128)(2,1)S(1)}, u32[]{:S(2)}, u32[]{:S(2)}) collective-permute-start(bf16[256,640]{1,0:T(8,128)(2,1)S(1)} %get-tuple-element.55), channel_id=1, source_target_pairs={{0,2},{1,3},{2,4},{3,5},{4,6},{5,7},{6,0},{7,1},{8,10},{9,11},{10,... | collective-permute-start | bytes 983048 | tf_op jit(solution)/shard_map/ppermute | solution.py:128
  294.2 21.0 %collective-permute-start.42 = (bf16[256,640]{1,0:T(8,128)(2,1)S(1)}, bf16[256,640]{1,0:T(8,128)(2,1)S(1)}, u32[]{:S(2)}, u32[]{:S(2)}) collective-permute-start(bf16[256,640]{1,0:T(8,128)(2,1)S(1)} %get-tuple-element.54), channel_id=1, source_target_pairs={{0,6},{1,7},{2,0},{3,1},{4,2},{5,3},{6,4},{7,5},{8,14},{9,15},{10,... | collective-permute-start | bytes 983048 | tf_op jit(solution)/shard_map/ppermute | solution.py:128
  (31 other events, 550.2 us)

commit v2 on v1

--- a/solution.py
+++ b/solution.py
@@ -19,7 +19,7 @@
 
 HOST = ((0, 1, 3, 4, 6), (0, 2, 4, 5, 7))
 SHARED = tuple(z for z in HOST[0] if z in HOST[1])
-SHIFTS = (0, 1, 7, 4, 2, 6, 3, 5)
+SHIFTS = (0, 4, 1, 5, 2, 6, 3, 7)
 AXES = ("tm", "head")
 
 
@@ -46,7 +46,7 @@
 ALL = [(x, z, y, c) for x in range(X) for z in range(Z) for y in range(Y) for c in range(C)]
 
 
-def key_pairs(shift):
+def plane_pairs(shift):
     return [
         (device(x, z, y, c), device(x, z + shift, y, c))
         for x, z, y, c in ALL
@@ -54,12 +54,12 @@
     ]
 
 
-def query_pairs(shift):
+def query_pairs(m):
     found = []
     for x, z, y, c in ALL:
-        if head_at(c, z + shift) >= 0:
-            to_x, to_c = worker(c, z + shift, (x + z) % X)
-            found.append((device(x, z, y, c), device(to_x, z + shift, y, to_c)))
+        if head_at(c, z) >= 0 and (m or z in SHARED):
+            to_x, to_c = worker(c, z, (x + m) % X)
+            found.append((device(x, z, y, c), device(to_x, z, y, to_c)))
     return found
 
 
@@ -70,7 +70,7 @@
         if work is not None:
             head_core, r = work
             from_z = (z - shift) % Z
-            slot = (((r - from_z) % X) * Z + from_z + 1) % SPANS
+            slot = (((r - shift) % X) * Z + from_z + 1) % SPANS
             found.append((device(x, z, y, c), device(slot // Z, slot % Z, y, head_core)))
     return found
 
@@ -87,17 +87,17 @@
     return found
 
 
-def core_pairs(m, half):
-    found = []
-    for x, z, y, c in ALL:
-        if z in SHARED and c == (x // 2 if m == 0 else half):
-            found.append((device(x, z, y, c), device(x, z, y, 1 - c)))
-    return found
+def core_pairs(own):
+    return [
+        (device(x, z, y, c), device(x, z, y, 1 - c))
+        for x, z, y, c in ALL
+        if z in SHARED and (not own or c == x // 2)
+    ]
 
 
 ROUNDS = len(SHIFTS)
 HALF = ROUNDS // 2
-PACK, QSPAN, KSPAN, TAKE, FROM_OTHER, FROM_OTHER_0, ACTIVE, PLACE_Y, CORE = 0, 8, 16, 48, 56, 58, 59, 60, 61
+PACK, QSPAN, KSPAN, TAKE, OTHER, OTHER_OWN, ACTIVE, PLACE_Y, CORE, SHARES = 0, 8, 16, 48, 56, 58, 59, 60, 61, 62
 WIDTH = 64
 
 
@@ -112,15 +112,16 @@
             row[TAKE + i] = head_at(c, slot_before % Z + shift)
             from_z = (z - shift) % Z
             if work is not None:
-                row[QSPAN + i] = ((work[1] - from_z) % X) * Z + from_z
+                row[QSPAN + i] = ((work[1] - shift) % X) * Z + from_z
             for m in range(X):
                 row[KSPAN + m * ROUNDS + i] = ((x - m) % X) * Z + from_z
         for half in range(2):
-            row[FROM_OTHER + half] = int(z in SHARED and c != half)
-        row[FROM_OTHER_0] = int(z in SHARED and c != x // 2)
+            row[OTHER + half] = int(z in SHARED and c != half)
+        row[OTHER_OWN] = int(z in SHARED and c != x // 2)
         row[ACTIVE] = int(work is not None)
         row[PLACE_Y] = y
         row[CORE] = c
+        row[SHARES] = int(z in SHARED)
     return rows
 
 
@@ -151,69 +152,120 @@
         @pl.when(head >= 0)
         def _():
             columns = pl.ds(pl.multiple_of(head * HEAD_DIM, HEAD_DIM), HEAD_DIM)
-            outs[i][:, :HEAD_DIM] = key_ref[:, columns]
-            outs[i][:, HEAD_DIM:] = value_ref[:, columns]
-            outs[ROUNDS + i][...] = query_ref[:, columns]
+            for part, ref in enumerate((key_ref, value_ref, query_ref)):
+                outs[i][:, part * HEAD_DIM : (part + 1) * HEAD_DIM] = ref[:, columns]
 
 
 def pack(row, query_rows, key_rows, value_rows):
-    outs = pl.pallas_call(
+    return pl.pallas_call(
         pack_kernel,
-        out_shape=[shape(SPAN, 2 * HEAD_DIM)] * ROUNDS + [shape(SPAN, HEAD_DIM)] * ROUNDS,
+        out_shape=[shape(SPAN, 3 * HEAD_DIM)] * ROUNDS,
         in_specs=[in_smem(), in_vmem(), in_vmem(), in_vmem()],
-        out_specs=[in_vmem()] * (2 * ROUNDS),
+        out_specs=[in_vmem()] * ROUNDS,
         compiler_params=pltpu.CompilerParams(vmem_limit_bytes=VMEM_LIMIT),
         name="pack",
     )(row, query_rows, key_rows, value_rows)
-    return outs[:ROUNDS], outs[ROUNDS:]
-
-
-BLOCK = 512
+
+
+STEP = 4
+LARGEST = 1e30
 
 
 def attend_kernel(row_ref, offset_ref, *refs):
-    queries, refs = refs[:ROUNDS], refs[ROUNDS:]
-    sources, refs = refs[: 4 * X], refs[4 * X :]
-    results, (held, copied) = refs[:ROUNDS], refs[ROUNDS:]
+    queries, refs = refs[: X + 1], refs[X + 1 :]
+    (own_0, own_1, own_other), refs = refs[:3], refs[3:]
+    direct, refs = refs[: 2 * (X - 1)], refs[2 * (X - 1) :]
+    other, refs = refs[: X - 1], refs[X - 1 :]
+    results, (held, rows, answer, copied) = refs[:ROUNDS], refs[ROUNDS:]
     offset = offset_ref[0]
 
     def place_of(span):
         return lax.rem(span - offset + SPANS, SPANS)
 
-    def rows_at(place):
-        return pl.ds(pl.multiple_of(place * SPAN, SPAN), SPAN)
+    def bring(source, first, m, half):
+        for i in range(HALF):
+            place = place_of(row_ref[KSPAN + m * ROUNDS + half * HALF + i])
+            at = pl.ds(pl.multiple_of(place * SPAN, SPAN), SPAN)
+            pltpu.make_async_copy(
+                source.at[pl.ds(first + i * SPAN, SPAN)], held.at[at], copied
+            ).start()
 
     @pl.when(row_ref[ACTIVE] == 1)
     def _():
-        for m in range(X):
-            for half in range(2):
-                other = row_ref[FROM_OTHER_0 if m == 0 else FROM_OTHER + half]
-                for taken in range(2):
-
-                    @pl.when(other == taken)
-                    def _():
-                        source = sources[taken * 2 * X + m * 2 + half]
-                        for i in range(HALF):
-                            place = place_of(row_ref[KSPAN + m * ROUNDS + half * HALF + i])
-                            pltpu.make_async_copy(
-                                source.at[pl.ds(i * SPAN, SPAN)], held.at[rows_at(place)], copied
-                            ).start()
+        for half, own in enumerate((own_0, own_1)):
+
+            @pl.when(row_ref[OTHER_OWN] == 0)
+            def _():
+                bring(own, 0, 0, half)
+
+            @pl.when(row_ref[OTHER_OWN] == 1)
+            def _():
+                bring(own_other, half * HALF * SPAN, 0, half)
+
+            for m in range(1, X):
+
+                @pl.when(row_ref[OTHER + half] == 0)
+                def _():
+                    bring(direct[(m - 1) * 2 + half], 0, m, half)
+
+                @pl.when(row_ref[OTHER + half] == 1)
+                def _():
+                    bring(other[m - 1], 0, m, half)
+
+        for m in range(1, X):
+            rows[m] = queries[m][...]
+
+        @pl.when(row_ref[SHARES] == 0)
+        def _():
+            rows[0] = queries[0][...]
+
+        @pl.when(row_ref[SHARES] == 1)
+        def _():
+            rows[0] = queries[X][...]
 
         pltpu.make_async_copy(held, held, copied).wait()
 
-        for i in range(ROUNDS):
-            own = place_of(row_ref[QSPAN + i])
-            query = queries[i][...]
-
-            def step(at, carry, width):
+        def scores_of(query, key_rows):
+            return lax.dot_general(
+                query,
+                held[key_rows, :HEAD_DIM],
+                (((1,), (1,)), ((), ())),
+                preferred_element_type=jnp.float32,
+            )
+
+        def chunk_rows(t):
+            return pl.ds(pl.multiple_of(t * STEP * SPAN, STEP * SPAN), STEP * SPAN)
+
+        def hidden(place, own):
+            return jnp.where(place <= own, 0.0, LARGEST)
+
+        def fixed_step(t, query, shift, owns):
+            scores = scores_of(query, chunk_rows(t))
+            weights = []
+            for u in range(STEP):
+                part = scores[:, u * SPAN : (u + 1) * SPAN]
+                moved_by = jnp.concatenate(
+                    [
+                        shift[n * SPAN : (n + 1) * SPAN] + hidden(t * STEP + u, own)
+                        for n, own in enumerate(owns)
+                    ]
+                )
+                weights.append(jnp.exp2(part * SCALE - moved_by))
+            total = sum(
+                w[:, g : g + HEAD_DIM] for w in weights for g in range(0, SPAN, HEAD_DIM)
+            )
+            summed = jnp.dot(
+                jnp.concatenate([w.astype(jnp.bfloat16) for w in weights], axis=1),
+                held[chunk_rows(t), HEAD_DIM:],
+                preferred_element_type=jnp.float32,
+            )
+            return total, summed
+
+        def running(query, own):
+            def step(t, carry):
                 top, total, summed = carry
-                key_rows = pl.ds(pl.multiple_of(at, SPAN), width)
-                scores = lax.dot_general(
-                    query,
-                    held[key_rows, :HEAD_DIM],
-                    (((1,), (1,)), ((), ())),
-                    preferred_element_type=jnp.float32,
-                )
+                key_rows = pl.ds(pl.multiple_of(t * SPAN, SPAN), SPAN)
+                scores = scores_of(query, key_rows)
                 top_new = jnp.maximum(top, jnp.max(scores, axis=1, keepdims=True))
                 weights = jnp.exp2((scores - top_new) * SCALE)
                 factor = jnp.exp2((top - top_new) * SCALE)
@@ -230,21 +282,64 @@
                 jnp.zeros((SPAN, 1), jnp.float32),
                 jnp.zeros((SPAN, HEAD_DIM), jnp.float32),
             )
-            visible = own + 1
-            pairs = lax.div(visible, 2)
-            carry = lax.fori_loop(0, pairs, lambda t, s: step(t * BLOCK, s, BLOCK), start)
-            carry = lax.fori_loop(2 * pairs, visible, lambda t, s: step(t * SPAN, s, SPAN), carry)
-            results[i][...] = (carry[2] / carry[1]).astype(jnp.bfloat16)
+            carry = lax.fori_loop(0, own + 1, step, start)
+            return carry[2] / carry[1]
+
+        def span_rows(n):
+            return pl.ds(pl.multiple_of(n * SPAN, SPAN), SPAN)
+
+        for m in range(X):
+            owns = [place_of(row_ref[QSPAN + 2 * m + n]) for n in range(2)]
+            query = rows[m]
+            shift = jnp.max(scores_of(query, pl.ds(0, SPAN)), axis=1, keepdims=True) * SCALE
+
+            def both(t, carry):
+                total, summed = fixed_step(t, query, shift, owns)
+                return carry[0] + total, carry[1] + summed
+
+            empty = jnp.zeros((2 * SPAN, HEAD_DIM), jnp.float32)
+            common = lax.div(jnp.minimum(owns[0], owns[1]), STEP) + 1
+            total, summed = lax.fori_loop(0, common, both, (empty, empty))
+            answer[0], answer[1] = total, summed
+
+            later = (owns[1] > owns[0]).astype(jnp.int32)
+            own = jnp.maximum(owns[0], owns[1])
+            late = span_rows(later)
+            late_query = rows[m, late, :]
+            late_shift = jnp.where(later == 1, shift[SPAN:], shift[:SPAN])
+
+            def one(t, carry):
+                total, summed = fixed_step(t, late_query, late_shift, [own])
+                return carry[0] + total, carry[1] + summed
+
+            total, summed = lax.fori_loop(
+                common, lax.div(own, STEP) + 1, one, (answer[0, late, :], answer[1, late, :])
+            )
+            answer[0, late, :], answer[1, late, :] = total, summed
+
+            total = jnp.sum(answer[0], axis=1, keepdims=True)
+            outcome = answer[1] / total
+            for n in range(2):
+                results[2 * m + n][...] = outcome[n * SPAN : (n + 1) * SPAN].astype(jnp.bfloat16)
+
+            @pl.when(jnp.logical_not(jnp.max(total) < 1e30))
+            def _():
+                for n in range(2):
+                    results[2 * m + n][...] = running(
+                        rows[m, n * SPAN : (n + 1) * SPAN, :], owns[n]
+                    ).astype(jnp.bfloat16)
 
 
 def attend(row, offset, queries, sources):
     return pl.pallas_call(
         attend_kernel,
         out_shape=[shape(SPAN, HEAD_DIM)] * ROUNDS,
-        in_specs=[in_smem(), in_smem()] + [in_vmem()] * ROUNDS + [anywhere()] * len(sources),
+        in_specs=[in_smem(), in_smem()] + [in_vmem()] * len(queries) + [anywhere()] * len(sources),
         out_specs=[in_vmem()] * ROUNDS,
         scratch_shapes=[
             pltpu.VMEM((SPANS * SPAN, 2 * HEAD_DIM), jnp.bfloat16),
+            pltpu.VMEM((X, 2 * SPAN, HEAD_DIM), jnp.bfloat16),
+            pltpu.VMEM((2, 2 * SPAN, HEAD_DIM), jnp.float32),
             pltpu.SemaphoreType.DMA,
         ],
         compiler_params=pltpu.CompilerParams(vmem_limit_bytes=VMEM_LIMIT),
@@ -318,22 +413,30 @@
 ):
     me = lax.axis_index("tm") * (Y * C) + lax.axis_index("head")
     row = lax.dynamic_slice(jnp.asarray(table()), (me, 0), (1, WIDTH))[0]
-    packed, packed_queries = pack(row, query_rows, key_rows, value_rows)
+    packed = pack(row, query_rows, key_rows, value_rows)
 
     arrived = [
-        packed[i] if shift == 0 else moved(packed[i], key_pairs(shift))
+        packed[i] if shift == 0 else moved(packed[i], plane_pairs(shift))
         for i, shift in enumerate(SHIFTS)
     ]
-    queries = [moved(packed_queries[i], query_pairs(shift)) for i, shift in enumerate(SHIFTS)]
-
-    own = [jnp.concatenate(arrived[half * HALF : (half + 1) * HALF]) for half in range(2)]
-    direct, shared = {}, {}
-    for half in range(2):
-        for m in (2, 1, 3, 0):
-            direct[m, half] = moved(own[half], across_pairs(m, half)) if m else own[half]
-            shared[m, half] = moved(direct[m, half], core_pairs(m, half))
-    order = [(m, half) for m in range(X) for half in range(2)]
-    sources = [direct[key] for key in order] + [shared[key] for key in order]
+
+    wide = 2 * HEAD_DIM
+    own = [
+        jnp.concatenate([a[:, :wide] for a in arrived[half * HALF : (half + 1) * HALF]])
+        for half in range(2)
+    ]
+    sent = [
+        jnp.concatenate([a[:, wide:] for a in arrived[2 * m : 2 * m + 2]]) for m in range(X)
+    ]
+    queries = [sent[0]] + [moved(sent[m], query_pairs(m)) for m in (1, 2, 3)]
+    queries.append(moved(sent[0], query_pairs(0)))
+    direct = [
+        [moved(own[half], across_pairs(m, half)) for half in range(2)] for m in range(1, X)
+    ]
+    own_other = moved(jnp.concatenate(own), core_pairs(True))
+    first = row[CORE] == 0
+    other = [moved(jnp.where(first, pair[0], pair[1]), core_pairs(False)) for pair in direct]
+    sources = own + [own_other] + [part for pair in direct for part in pair] + other
 
     results = attend(row, window_offset, queries, sources)
 

time: 319 us -> 272 us (0.85)
  starting transfers between devices: 204 us -> 104 us
  Pallas kernels: 47 us -> 95 us
    ppermute x43 -> x35, starting transfers between devices: 204 us -> 104 us  [moved(): return lax.ppermute(block, AXES, pairs)]
    pallas_call x1, Pallas kernels: 37 us -> 84.9 us  [attend(): pl.pallas_call(attend_kernel, out_shape=[shape(SPAN, HEAD_DIM)] * ROUNDS,...]
    ppermute x43 -> x35, waiting for transfers between devices: 56.3 us -> 57.4 us  [moved(): return lax.ppermute(block, AXES, pairs)]
  transfers between devices with their start and end apart: 43 -> 35, of which waited for: 11 -> 14; matrix products, arithmetic and copies ran while one was open for 1% -> 1% of each run, Pallas kernels for 1% -> 2%
where the time goes in v2:
time: 272 us; the launch traced here: 269 us
  starting transfers between devices  104 us (38%)
  Pallas kernels  95 us (35%)
  waiting for transfers between devices  57.4 us (21%)
  local copies, waits for them, and re-layouts  6.4 us (2%)
  other arithmetic  3.83 us (1%)
    ppermute x35, starting transfers between devices, moved(): return lax.ppermute(block, AXES, pairs)  104 us
    pallas_call x1, Pallas kernels, attend(): pl.pallas_call(attend_kernel, out_shape=[shape(SPAN, HEAD_DIM)] * ROUNDS,...  84.9 us
    ppermute x35, waiting for transfers between devices, moved(): return lax.ppermute(block, AXES, pairs)  57.4 us
    pallas_call x2, Pallas kernels, project(): pl.pallas_call(project_kernel, out_shape=shape(Y, SPAN, wide), grid_spec=...  8.66 us
  transfers between devices with their start and end apart: 35, of which 14 were waited for; matrix products, arithmetic and copies ran while one was open for 1% of the time, Pallas kernels for 2%

profile of v2, /device:TPU:1, one launch (start us, length us, event | category | flops | bytes accessed | tf_op | source)
XLA Modules:
  0.0 269.2 jit_solution(2063037476781974484)
XLA Ops:
  4.4 9.6 %collective-permute-start.2 = (bf16[256,384]{1,0:T(8,128)(2,1)S(1)}, bf16[256,384]{1,0:T(8,128)(2,1)S(1)}, u32[]{:S(2)}, u32[]{:S(2)}) collective-permute-start(bf16[256,384]{1,0:T(8,128)(2,1)S(1)} %get-tuple-element.22), channel_id=1, source_target_pairs={{0,32},{1,33},{2,34},{3,35},{4,36},{5,37},{6,38},{7,39},{9,41},{11... | collective-permute-start | bytes 589832 | tf_op jit(solution)/shard_map/ppermute | solution.py:129
  18.6 4.9 %collective-permute-start.6 = (bf16[256,384]{1,0:T(8,128)(2,1)S(1)}, bf16[256,384]{1,0:T(8,128)(2,1)S(1)}, u32[]{:S(2)}, u32[]{:S(2)}) collective-permute-start(bf16[256,384]{1,0:T(8,128)(2,1)S(1)} %get-tuple-element.25), channel_id=1, source_target_pairs={{1,17},{3,19},{5,21},{7,23},{8,24},{10,26},{12,28},{14,30},{16,32}... | collective-permute-start | bytes 589832 | tf_op jit(solution)/shard_map/ppermute | solution.py:129
  23.6 4.7 %collective-permute-start.10 = (bf16[256,384]{1,0:T(8,128)(2,1)S(1)}, bf16[256,384]{1,0:T(8,128)(2,1)S(1)}, u32[]{:S(2)}, u32[]{:S(2)}) collective-permute-start(bf16[256,384]{1,0:T(8,128)(2,1)S(1)} %get-tuple-element.28), channel_id=1, source_target_pairs={{1,57},{3,59},{5,61},{7,63},{8,0},{9,1},{10,2},{11,3},{12,4},{13,5... | collective-permute-start | bytes 589832 | tf_op jit(solution)/shard_map/ppermute | solution.py:129
  34.1 4.9 %collective-permute-done.9 = bf16[256,384]{1,0:T(8,128)(2,1)S(1)} collective-permute-done((bf16[256,384]{1,0:T(8,128)(2,1)S(1)}, bf16[256,384]{1,0:T(8,128)(2,1)S(1)}, u32[]{:S(2)}, u32[]{:S(2)}) %collective-permute-start.9) | collective-permute-done | bytes 196640 | tf_op jit(solution)/shard_map/ppermute | solution.py:129
  40.6 10.9 %collective-permute-start.16 = (bf16[1024,256]{1,0:T(8,128)(2,1)S(1)}, bf16[1024,256]{1,0:T(8,128)(2,1)S(1)}, u32[]{:S(2)}, u32[]{:S(2)}) collective-permute-start(bf16[1024,256]{1,0:T(8,128)(2,1)S(1)} %pad_maximum_fusion.refs_5_), channel_id=1, source_target_pairs={{1,128},{3,130},{5,132},{7,134},{8,136},{10,138},{12,140},{14,142}... | collective-permute-start | bytes 1572872 | tf_op jit(solution)/shard_map/ppermute | solution.py:129
  55.3 5.0 %collective-permute-start.18 = (bf16[1024,256]{1,0:T(8,128)(2,1)S(1)}, bf16[1024,256]{1,0:T(8,128)(2,1)S(1)}, u32[]{:S(2)}, u32[]{:S(2)}) collective-permute-start(bf16[1024,256]{1,0:T(8,128)(2,1)S(1)} %pad_maximum_fusion.refs_5_), channel_id=1, source_target_pairs={{1,192},{3,194},{5,196},{7,198},{8,200},{10,202},{12,204},{14,206}... | collective-permute-start | bytes 1572872 | tf_op jit(solution)/shard_map/ppermute | solution.py:129
  65.6 5.1 %collective-permute-done.17.refs_11_ = bf16[1024,256]{1,0:T(8,128)(2,1)S(1)} collective-permute-done((bf16[1024,256]{1,0:T(8,128)(2,1)S(1)}, bf16[1024,256]{1,0:T(8,128)(2,1)S(1)}, u32[]{:S(2)}, u32[]{:S(2)}) %collective-permute-start.17) | collective-permute-done | bytes 524320 | tf_op jit(solution)/shard_map/ppermute | solution.py:129
  75.1 3.5 %collective-permute-done.19.refs_13_ = bf16[1024,256]{1,0:T(8,128)(2,1)S(1)} collective-permute-done((bf16[1024,256]{1,0:T(8,128)(2,1)S(1)}, bf16[1024,256]{1,0:T(8,128)(2,1)S(1)}, u32[]{:S(2)}, u32[]{:S(2)}) %collective-permute-start.19) | collective-permute-done | bytes 524320 | tf_op jit(solution)/shard_map/ppermute | solution.py:129
  80.6 5.4 %collective-permute-start.8 = (bf16[512,128]{1,0:T(8,128)(2,1)S(1)}, bf16[512,128]{1,0:T(8,128)(2,1)S(1)}, u32[]{:S(2)}, u32[]{:S(2)}) collective-permute-start(bf16[512,128]{1,0:T(8,128)(2,1)S(1)} %pad_maximum_fusion.4), channel_id=1, source_target_pairs={{0,64},{1,192},{2,66},{3,194},{4,68},{5,196},{6,70},{7,198},{8,136... | collective-permute-start | bytes 393224 | tf_op jit(solution)/shard_map/ppermute | solution.py:129
  86.1 4.0 %collective-permute-done.8.refs_2_ = bf16[512,128]{1,0:T(8,128)(2,1)S(1)} collective-permute-done((bf16[512,128]{1,0:T(8,128)(2,1)S(1)}, bf16[512,128]{1,0:T(8,128)(2,1)S(1)}, u32[]{:S(2)}, u32[]{:S(2)}) %collective-permute-start.8) | collective-permute-done | bytes 131104 | tf_op jit(solution)/shard_map/ppermute | solution.py:129
  90.1 2.9 %collective-permute-start.11 = (bf16[512,128]{1,0:T(8,128)(2,1)S(1)}, bf16[512,128]{1,0:T(8,128)(2,1)S(1)}, u32[]{:S(2)}, u32[]{:S(2)}) collective-permute-start(bf16[512,128]{1,0:T(8,128)(2,1)S(1)} %pad_maximum_fusion.5), channel_id=1, source_target_pairs={{0,65},{1,193},{2,67},{3,195},{4,69},{5,197},{6,71},{7,199},{8,200... | collective-permute-start | bytes 393224 | tf_op jit(solution)/shard_map/ppermute | solution.py:129
  93.0 4.8 %collective-permute-done.11.refs_3_ = bf16[512,128]{1,0:T(8,128)(2,1)S(1)} collective-permute-done((bf16[512,128]{1,0:T(8,128)(2,1)S(1)}, bf16[512,128]{1,0:T(8,128)(2,1)S(1)}, u32[]{:S(2)}, u32[]{:S(2)}) %collective-permute-start.11) | collective-permute-done | bytes 131104 | tf_op jit(solution)/shard_map/ppermute | solution.py:129
  100.4 3.7 %collective-permute-done.12.refs_4_ = bf16[512,128]{1,0:T(8,128)(2,1)S(1)} collective-permute-done((bf16[512,128]{1,0:T(8,128)(2,1)S(1)}, bf16[512,128]{1,0:T(8,128)(2,1)S(1)}, u32[]{:S(2)}, u32[]{:S(2)}) %collective-permute-start.12) | collective-permute-done | bytes 131104 | tf_op jit(solution)/shard_map/ppermute | solution.py:129
  106.1 84.9 %attend.1 = (bf16[256,128]{1,0:T(8,128)(2,1)S(1)}, bf16[256,128]{1,0:T(8,128)(2,1)S(1)}, bf16[256,128]{1,0:T(8,128)(2,1)S(1)}, bf16[256,128]{1,0:T(8,128)(2,1)S(...) custom-call(s32[64]{0:T(128)S(1)} %get-tuple-element.57.row_ref, ...), custom_call_target="tpu_custom_call" | custom-call | tf_op jit(solution)/shard_map/attend/pallas_call | solution.py:334
  199.4 8.6 %collective-permute-start.28 = (bf16[256,128]{1,0:T(8,128)(2,1)S(1)}, bf16[256,128]{1,0:T(8,128)(2,1)S(1)}, u32[]{:S(2)}, u32[]{:S(2)}) collective-permute-start(bf16[256,128]{1,0:T(8,128)(2,1)S(1)} %get-tuple-element.34), channel_id=1, source_target_pairs={{0,152},{1,216},{2,154},{3,218},{4,156},{5,220},{6,158},{7,222},{8... | collective-permute-start | bytes 196616 | tf_op jit(solution)/shard_map/ppermute | solution.py:129
  208.0 10.6 %collective-permute-start.29 = (bf16[256,128]{1,0:T(8,128)(2,1)S(1)}, bf16[256,128]{1,0:T(8,128)(2,1)S(1)}, u32[]{:S(2)}, u32[]{:S(2)}) collective-permute-start(bf16[256,128]{1,0:T(8,128)(2,1)S(1)} %get-tuple-element.35), channel_id=1, source_target_pairs={{0,112},{1,176},{2,114},{3,178},{4,116},{5,180},{6,118},{7,182},{8... | collective-permute-start | bytes 196616 | tf_op jit(solution)/shard_map/ppermute | solution.py:129
  221.9 4.3 %project.3 = bf16[4,256,640]{2,1,0:T(8,128)(2,1)S(1)} custom-call(s32[64]{0:T(128)S(1)} %get-tuple-element.57.row_ref, bf16[256,640]{1,0:T(8,128)(2,1)S(1)} %heads.1.rows_ref, bf16[640,5120]{1,0:T(8,128)(2,1)} %weight_ref.3), custom_call_target="tpu_custom_call" | custom-call | tf_op jit(solution)/shard_map/project/pallas_call | solution.py:386
  226.2 3.0 %collective-permute-start.31 = (bf16[4,256,640]{2,1,0:T(8,128)(2,1)S(1)}, bf16[4,256,640]{2,1,0:T(8,128)(2,1)S(1)}, u32[]{:S(2)}, u32[]{:S(2)}) collective-permute-start(bf16[4,256,640]{2,1,0:T(8,128)(2,1)S(1)} %project.3), channel_id=1, source_target_pairs={{0,1},{1,0},{2,3},{3,2},{4,5},{5,4},{6,7},{7,6},{8,9},{9,8},{10,11... | collective-permute-start | bytes 3932168 | tf_op jit(solution)/shard_map/ppermute | solution.py:129
  229.3 12.9 %collective-permute-done.1 = s32[1]{0:T(128)} collective-permute-done((s32[1]{0:T(128)}, s32[1]{0:T(128)}, u32[]{:S(2)}, u32[]{:S(2)}) %collective-permute-start.1) | collective-permute-done | bytes 36 | tf_op jit(solution)/shard_map/ppermute | solution.py:129
  244.1 4.3 %project.2 = bf16[4,256,640]{2,1,0:T(8,128)(2,1)S(1)} custom-call(s32[64]{0:T(128)S(1)} %get-tuple-element.57.row_ref, bf16[256,640]{1,0:T(8,128)(2,1)S(1)} %heads.1.rows_ref, bf16[640,5120]{1,0:T(8,128)(2,1)} %weight_ref.3), custom_call_target="tpu_custom_call" | custom-call | tf_op jit(solution)/shard_map/project/pallas_call | solution.py:386
  248.7 3.3 %collective-permute-start.34 = (bf16[256,640]{1,0:T(8,128)(2,1)S(1)}, bf16[256,640]{1,0:T(8,128)(2,1)S(1)}, u32[]{:S(2)}, u32[]{:S(2)}) collective-permute-start(bf16[256,640]{1,0:T(8,128)(2,1)S(1)} %get-tuple-element.38), channel_id=1, source_target_pairs={{0,6},{1,7},{2,0},{3,1},{4,2},{5,3},{6,4},{7,5},{8,14},{9,15},{10,... | collective-permute-start | bytes 983048 | tf_op jit(solution)/shard_map/ppermute | solution.py:129
  253.9 5.0 %collective-permute-done.34 = bf16[256,640]{1,0:T(8,128)(2,1)S(1)} collective-permute-done((bf16[256,640]{1,0:T(8,128)(2,1)S(1)}, bf16[256,640]{1,0:T(8,128)(2,1)S(1)}, u32[]{:S(2)}, u32[]{:S(2)}) %collective-permute-start.34) | collective-permute-done | bytes 327712 | tf_op jit(solution)/shard_map/ppermute | solution.py:129
  259.0 3.3 %collective-permute-done.33 = bf16[256,640]{1,0:T(8,128)(2,1)S(1)} collective-permute-done((bf16[256,640]{1,0:T(8,128)(2,1)S(1)}, bf16[256,640]{1,0:T(8,128)(2,1)S(1)}, u32[]{:S(2)}, u32[]{:S(2)}) %collective-permute-start.33) | collective-permute-done | bytes 327712 | tf_op jit(solution)/shard_map/ppermute | solution.py:129
  262.2 5.0 %collective-permute-done.32 = bf16[256,640]{1,0:T(8,128)(2,1)S(1)} collective-permute-done((bf16[256,640]{1,0:T(8,128)(2,1)S(1)}, bf16[256,640]{1,0:T(8,128)(2,1)S(1)}, u32[]{:S(2)}, u32[]{:S(2)}) %collective-permute-start.32) | collective-permute-done | bytes 327712 | tf_op jit(solution)/shard_map/ppermute | solution.py:129
  (101 shorter events, 51.9 us)
Async XLA Ops:
  4.4 19.1 %collective-permute-start.2 = (bf16[256,384]{1,0:T(8,128)(2,1)S(1)}, bf16[256,384]{1,0:T(8,128)(2,1)S(1)}, u32[]{:S(2)}, u32[]{:S(2)}) collective-permute-start(bf16[256,384]{1,0:T(8,128)(2,1)S(1)} %get-tuple-element.22), channel_id=1, source_target_pairs={{0,32},{1,33},{2,34},{3,35},{4,36},{5,37},{6,38},{7,39},{9,41},{11... | collective-permute-start | bytes 589832 | tf_op jit(solution)/shard_map/ppermute | solution.py:129
  14.1 17.2 %collective-permute-start.4 = (bf16[256,384]{1,0:T(8,128)(2,1)S(1)}, bf16[256,384]{1,0:T(8,128)(2,1)S(1)}, u32[]{:S(2)}, u32[]{:S(2)}) collective-permute-start(bf16[256,384]{1,0:T(8,128)(2,1)S(1)} %get-tuple-element.24), channel_id=1, source_target_pairs={{1,41},{3,43},{5,45},{7,47},{8,48},{10,50},{12,52},{14,54},{17,57}... | collective-permute-start | bytes 589832 | tf_op jit(solution)/shard_map/ppermute | solution.py:129
  17.3 16.8 %collective-permute-start.7 = (bf16[256,384]{1,0:T(8,128)(2,1)S(1)}, bf16[256,384]{1,0:T(8,128)(2,1)S(1)}, u32[]{:S(2)}, u32[]{:S(2)}) collective-permute-start(bf16[256,384]{1,0:T(8,128)(2,1)S(1)} %get-tuple-element.26), channel_id=1, source_target_pairs={{0,48},{2,50},{4,52},{6,54},{9,57},{11,59},{13,61},{15,63},{16,0},... | collective-permute-start | bytes 589832 | tf_op jit(solution)/shard_map/ppermute | solution.py:129
  18.6 13.5 %collective-permute-start.6 = (bf16[256,384]{1,0:T(8,128)(2,1)S(1)}, bf16[256,384]{1,0:T(8,128)(2,1)S(1)}, u32[]{:S(2)}, u32[]{:S(2)}) collective-permute-start(bf16[256,384]{1,0:T(8,128)(2,1)S(1)} %get-tuple-element.25), channel_id=1, source_target_pairs={{1,17},{3,19},{5,21},{7,23},{8,24},{10,26},{12,28},{14,30},{16,32}... | collective-permute-start | bytes 589832 | tf_op jit(solution)/shard_map/ppermute | solution.py:129
  23.6 15.7 %collective-permute-start.10 = (bf16[256,384]{1,0:T(8,128)(2,1)S(1)}, bf16[256,384]{1,0:T(8,128)(2,1)S(1)}, u32[]{:S(2)}, u32[]{:S(2)}) collective-permute-start(bf16[256,384]{1,0:T(8,128)(2,1)S(1)} %get-tuple-element.28), channel_id=1, source_target_pairs={{1,57},{3,59},{5,61},{7,63},{8,0},{9,1},{10,2},{11,3},{12,4},{13,5... | collective-permute-start | bytes 589832 | tf_op jit(solution)/shard_map/ppermute | solution.py:129
  31.4 29.0 %collective-permute-start.14 = (bf16[1024,256]{1,0:T(8,128)(2,1)S(1)}, bf16[1024,256]{1,0:T(8,128)(2,1)S(1)}, u32[]{:S(2)}, u32[]{:S(2)}) collective-permute-start(bf16[1024,256]{1,0:T(8,128)(2,1)S(1)} %pad_maximum_fusion.refs_5_), channel_id=1, source_target_pairs={{0,64},{2,66},{4,68},{6,70},{8,72},{10,74},{12,76},{14,78},{17,81}... | collective-permute-start | bytes 1572872 | tf_op jit(solution)/shard_map/ppermute | solution.py:129
  39.3 23.0 %collective-permute-start.15 = (bf16[1024,256]{1,0:T(8,128)(2,1)S(1)}, bf16[1024,256]{1,0:T(8,128)(2,1)S(1)}, u32[]{:S(2)}, u32[]{:S(2)}) collective-permute-start(bf16[1024,256]{1,0:T(8,128)(2,1)S(1)} %pad_maximum_fusion.1.refs_6_), channel_id=1, source_target_pairs={{0,65},{2,67},{4,69},{6,71},{8,72},{10,74},{12,76},{14,78},{17,81}... | collective-permute-start | bytes 1572872 | tf_op jit(solution)/shard_map/ppermute | solution.py:129
  40.6 23.7 %collective-permute-start.16 = (bf16[1024,256]{1,0:T(8,128)(2,1)S(1)}, bf16[1024,256]{1,0:T(8,128)(2,1)S(1)}, u32[]{:S(2)}, u32[]{:S(2)}) collective-permute-start(bf16[1024,256]{1,0:T(8,128)(2,1)S(1)} %pad_maximum_fusion.refs_5_), channel_id=1, source_target_pairs={{1,128},{3,130},{5,132},{7,134},{8,136},{10,138},{12,140},{14,142}... | collective-permute-start | bytes 1572872 | tf_op jit(solution)/shard_map/ppermute | solution.py:129
  51.6 19.1 %collective-permute-start.17 = (bf16[1024,256]{1,0:T(8,128)(2,1)S(1)}, bf16[1024,256]{1,0:T(8,128)(2,1)S(1)}, u32[]{:S(2)}, u32[]{:S(2)}) collective-permute-start(bf16[1024,256]{1,0:T(8,128)(2,1)S(1)} %pad_maximum_fusion.1.refs_6_), channel_id=1, source_target_pairs={{1,129},{3,131},{5,133},{7,135},{8,136},{10,138},{12,140},{14,142}... | collective-permute-start | bytes 1572872 | tf_op jit(solution)/shard_map/ppermute | solution.py:129
  55.3 17.3 %collective-permute-start.18 = (bf16[1024,256]{1,0:T(8,128)(2,1)S(1)}, bf16[1024,256]{1,0:T(8,128)(2,1)S(1)}, u32[]{:S(2)}, u32[]{:S(2)}) collective-permute-start(bf16[1024,256]{1,0:T(8,128)(2,1)S(1)} %pad_maximum_fusion.refs_5_), channel_id=1, source_target_pairs={{1,192},{3,194},{5,196},{7,198},{8,200},{10,202},{12,204},{14,206}... | collective-permute-start | bytes 1572872 | tf_op jit(solution)/shard_map/ppermute | solution.py:129
  60.4 18.2 %collective-permute-start.19 = (bf16[1024,256]{1,0:T(8,128)(2,1)S(1)}, bf16[1024,256]{1,0:T(8,128)(2,1)S(1)}, u32[]{:S(2)}, u32[]{:S(2)}) collective-permute-start(bf16[1024,256]{1,0:T(8,128)(2,1)S(1)} %pad_maximum_fusion.1.refs_6_), channel_id=1, source_target_pairs={{1,193},{3,195},{5,197},{7,199},{8,200},{10,202},{12,204},{14,206}... | collective-permute-start | bytes 1572872 | tf_op jit(solution)/shard_map/ppermute | solution.py:129
  62.3 18.3 %collective-permute-start.5 = (bf16[512,128]{1,0:T(8,128)(2,1)S(1)}, bf16[512,128]{1,0:T(8,128)(2,1)S(1)}, u32[]{:S(2)}, u32[]{:S(2)}) collective-permute-start(bf16[512,128]{1,0:T(8,128)(2,1)S(1)} %pad_maximum_fusion.3), channel_id=1, source_target_pairs={{0,1},{1,129},{2,3},{3,131},{4,5},{5,133},{6,7},{7,135},{8,72},{10... | collective-permute-start | bytes 393224 | tf_op jit(solution)/shard_map/ppermute | solution.py:129
  64.3 39.8 %collective-permute-start.13 = (bf16[2048,256]{1,0:T(8,128)(2,1)S(1)}, bf16[2048,256]{1,0:T(8,128)(2,1)S(1)}, u32[]{:S(2)}, u32[]{:S(2)}) collective-permute-start(bf16[2048,256]{1,0:T(8,128)(2,1)S(1)} %get-tuple-element.40), channel_id=1, source_target_pairs={{0,1},{2,3},{4,5},{6,7},{32,33},{34,35},{36,37},{38,39},{64,65},{6... | collective-permute-start | bytes 3145736 | tf_op jit(solution)/shard_map/ppermute | solution.py:129
  70.7 33.5 %collective-permute-start.20 = (bf16[1024,256]{1,0:T(8,128)(2,1)S(1)}, bf16[1024,256]{1,0:T(8,128)(2,1)S(1)}, u32[]{:S(2)}, u32[]{:S(2)}) collective-permute-start(bf16[1024,256]{1,0:T(8,128)(2,1)S(1)} %broadcast_select_fusion.2), channel_id=1, source_target_pairs={{0,1},{1,0},{2,3},{3,2},{4,5},{5,4},{6,7},{7,6},{32,33},{33,32},{3... | collective-permute-start | bytes 1572872 | tf_op jit(solution)/shard_map/ppermute | solution.py:129
  72.7 31.5 %collective-permute-start.21 = (bf16[1024,256]{1,0:T(8,128)(2,1)S(1)}, bf16[1024,256]{1,0:T(8,128)(2,1)S(1)}, u32[]{:S(2)}, u32[]{:S(2)}) collective-permute-start(bf16[1024,256]{1,0:T(8,128)(2,1)S(1)} %broadcast_select_fusion.1), channel_id=1, source_target_pairs={{0,1},{1,0},{2,3},{3,2},{4,5},{5,4},{6,7},{7,6},{32,33},{33,32},{3... | collective-permute-start | bytes 1572872 | tf_op jit(solution)/shard_map/ppermute | solution.py:129
  78.6 25.5 %collective-permute-start.22 = (bf16[1024,256]{1,0:T(8,128)(2,1)S(1)}, bf16[1024,256]{1,0:T(8,128)(2,1)S(1)}, u32[]{:S(2)}, u32[]{:S(2)}) collective-permute-start(bf16[1024,256]{1,0:T(8,128)(2,1)S(1)} %broadcast_select_fusion), channel_id=1, source_target_pairs={{0,1},{1,0},{2,3},{3,2},{4,5},{5,4},{6,7},{7,6},{32,33},{33,32},{3... | collective-permute-start | bytes 1572872 | tf_op jit(solution)/shard_map/ppermute | solution.py:129
  192.9 15.1 %collective-permute-start.24 = (bf16[256,128]{1,0:T(8,128)(2,1)S(1)}, bf16[256,128]{1,0:T(8,128)(2,1)S(1)}, u32[]{:S(2)}, u32[]{:S(2)}) collective-permute-start(bf16[256,128]{1,0:T(8,128)(2,1)S(1)} %get-tuple-element.30), channel_id=1, source_target_pairs={{0,40},{1,104},{2,42},{3,106},{4,44},{5,108},{6,46},{7,110},{8,48}... | collective-permute-start | bytes 196616 | tf_op jit(solution)/shard_map/ppermute | solution.py:129
  194.2 24.4 %collective-permute-start.25 = (bf16[256,128]{1,0:T(8,128)(2,1)S(1)}, bf16[256,128]{1,0:T(8,128)(2,1)S(1)}, u32[]{:S(2)}, u32[]{:S(2)}) collective-permute-start(bf16[256,128]{1,0:T(8,128)(2,1)S(1)} %get-tuple-element.31), channel_id=1, source_target_pairs={{0,0},{1,64},{2,2},{3,66},{4,4},{5,68},{6,6},{7,70},{8,200},{10,20... | collective-permute-start | bytes 196616 | tf_op jit(solution)/shard_map/ppermute | solution.py:129
  196.2 23.8 %collective-permute-start.26 = (bf16[256,128]{1,0:T(8,128)(2,1)S(1)}, bf16[256,128]{1,0:T(8,128)(2,1)S(1)}, u32[]{:S(2)}, u32[]{:S(2)}) collective-permute-start(bf16[256,128]{1,0:T(8,128)(2,1)S(1)} %get-tuple-element.32), channel_id=1, source_target_pairs={{0,224},{1,32},{2,226},{3,34},{4,228},{5,36},{6,230},{7,38},{8,232... | collective-permute-start | bytes 196616 | tf_op jit(solution)/shard_map/ppermute | solution.py:129
  198.1 21.9 %collective-permute-start.27 = (bf16[256,128]{1,0:T(8,128)(2,1)S(1)}, bf16[256,128]{1,0:T(8,128)(2,1)S(1)}, u32[]{:S(2)}, u32[]{:S(2)}) collective-permute-start(bf16[256,128]{1,0:T(8,128)(2,1)S(1)} %get-tuple-element.33), channel_id=1, source_target_pairs={{0,184},{1,248},{2,186},{3,250},{4,188},{5,252},{6,190},{7,254},{8... | collective-permute-start | bytes 196616 | tf_op jit(solution)/shard_map/ppermute | solution.py:129
  199.4 20.6 %collective-permute-start.28 = (bf16[256,128]{1,0:T(8,128)(2,1)S(1)}, bf16[256,128]{1,0:T(8,128)(2,1)S(1)}, u32[]{:S(2)}, u32[]{:S(2)}) collective-permute-start(bf16[256,128]{1,0:T(8,128)(2,1)S(1)} %get-tuple-element.34), channel_id=1, source_target_pairs={{0,152},{1,216},{2,154},{3,218},{4,156},{5,220},{6,158},{7,222},{8... | collective-permute-start | bytes 196616 | tf_op jit(solution)/shard_map/ppermute | solution.py:129
  226.2 22.2 %collective-permute-start.31 = (bf16[4,256,640]{2,1,0:T(8,128)(2,1)S(1)}, bf16[4,256,640]{2,1,0:T(8,128)(2,1)S(1)}, u32[]{:S(2)}, u32[]{:S(2)}) collective-permute-start(bf16[4,256,640]{2,1,0:T(8,128)(2,1)S(1)} %project.3), channel_id=1, source_target_pairs={{0,1},{1,0},{2,3},{3,2},{4,5},{5,4},{6,7},{7,6},{8,9},{9,8},{10,11... | collective-permute-start | bytes 3932168 | tf_op jit(solution)/shard_map/ppermute | solution.py:129
  229.3 24.7 %collective-permute-start = (bf16[256,640]{1,0:T(8,128)(2,1)}, bf16[256,640]{1,0:T(8,128)(2,1)}, u32[]{:S(2)}, u32[]{:S(2)}) collective-permute-start(bf16[256,640]{1,0:T(8,128)(2,1)} %param.13), channel_id=1, source_target_pairs={{0,8},{1,9},{2,10},{3,11},{4,12},{5,13},{6,14},{7,15},{8,16},{9,17... | collective-permute-start | bytes 983048 | tf_op jit(solution)/shard_map/ppermute | solution.py:129
  252.0 15.2 %collective-permute-start.32 = (bf16[256,640]{1,0:T(8,128)(2,1)S(1)}, bf16[256,640]{1,0:T(8,128)(2,1)S(1)}, u32[]{:S(2)}, u32[]{:S(2)}) collective-permute-start(bf16[256,640]{1,0:T(8,128)(2,1)S(1)} %get-tuple-element.37), channel_id=1, source_target_pairs={{0,4},{1,5},{2,6},{3,7},{4,0},{5,1},{6,2},{7,3},{8,12},{9,13},{10,... | collective-permute-start | bytes 983048 | tf_op jit(solution)/shard_map/ppermute | solution.py:129
  (19 other events, 382.7 us)

commit v3 on v1

v3 whole, which is shorter than its diff:
```python
import math

import jax
import jax.numpy as jnp
import numpy as np
from jax import lax
from jax.experimental import pallas as pl
from jax.experimental.pallas import tpu as pltpu
from jax.sharding import PartitionSpec as P

HEAD_DIM = 128
SPAN = 256
X, Z, Y, C = 4, 8, 4, 2
HERE = 5
SPANS = X * Z
NEGATIVE = -1e30
SCALE = math.log2(math.e) / math.sqrt(HEAD_DIM)
VMEM_LIMIT = 48 * 1024 * 1024

HOST = ((0, 1, 3, 4, 6), (0, 2, 4, 5, 7))
AXES = ("tm", "head")
PIECE = SPAN // X
HALF = SPAN // 2


def device(x, z, y, c):
    return ((x % X) * Z + z % Z) * (Y * C) + (y % Y) * C + c


ALL = [(x, z, y, c) for x in range(X) for z in range(Z) for y in range(Y) for c in range(C)]
PLANES = [[x * Z + z for z in range(Z)] for x in range(X)]


def across_pairs(m):
    return [(device(x, z, y, c), device(x + m, z, y, c)) for x, z, y, c in ALL if z in HOST[c]]


HEAD, PLANE, ACTIVE, PLACE_X, PLACE_Y, CORE = 0, 8, 13, 14, 15, 16
WIDTH = 32


def table():
    rows = np.zeros((X * Z * Y * C, WIDTH), np.int32)
    for x, z, y, c in ALL:
        row = rows[device(x, z, y, c)]
        for to_z in range(Z):
            row[HEAD + to_z] = HOST[c].index(to_z) if to_z in HOST[c] else -1
        row[PLANE : PLANE + HERE] = HOST[c]
        row[ACTIVE] = int(z in HOST[c])
        row[PLACE_X] = x
        row[PLACE_Y] = y
        row[CORE] = c
    return rows


def moved(block, pairs):
    return lax.ppermute(block, AXES, pairs)


def in_vmem():
    return pl.BlockSpec(memory_space=pltpu.VMEM)


def in_smem():
    return pl.BlockSpec(memory_space=pltpu.SMEM)


def anywhere():
    return pl.BlockSpec(memory_space=pl.ANY)


def shape(*dims, dtype=jnp.bfloat16):
    return jax.ShapeDtypeStruct(dims, dtype)


def pack_kernel(row_ref, query_ref, key_ref, value_ref, first_ref, second_ref, pieces_ref):
    for z in range(Z):
        head = row_ref[HEAD + z]

        @pl.when(head >= 0)
        def _():
            columns = pl.ds(pl.multiple_of(head * HEAD_DIM, HEAD_DIM), HEAD_DIM)
            for half, out in enumerate((first_ref, second_ref)):
                rows = slice(half * HALF, (half + 1) * HALF)
                out[z, :, :HEAD_DIM] = key_ref[rows, columns]
                out[z, :, HEAD_DIM:] = value_ref[rows, columns]
            for x in range(X):
                pieces_ref[x * Z + z] = query_ref[x * PIECE : (x + 1) * PIECE, columns]


def pack(row, query_rows, key_rows, value_rows):
    return pl.pallas_call(
        pack_kernel,
        out_shape=[shape(Z, HALF, 2 * HEAD_DIM)] * 2 + [shape(SPANS, PIECE, HEAD_DIM)],
        in_specs=[in_smem(), in_vmem(), in_vmem(), in_vmem()],
        out_specs=[in_vmem()] * 3,
        compiler_params=pltpu.CompilerParams(vmem_limit_bytes=VMEM_LIMIT),
        name="pack",
    )(row, query_rows, key_rows, value_rows)


STEP = 4
TILE = 8
TILE_ROWS = TILE * PIECE
STEP_KEYS = STEP * SPAN
LARGEST = 1e30


def attend_kernel(row_ref, offset_ref, pieces_ref, *refs):
    sources, (out_ref, held, rows, copied, moved_rows) = refs[: 2 * X], refs[2 * X :]
    offset = offset_ref[0]

    def place_of(span):
        return lax.rem(span - offset + SPANS, SPANS)

    def scores_of(query, key_rows):
        return lax.dot_general(
            query, held[key_rows, :HEAD_DIM], (((1,), (1,)), ((), ())),
            preferred_element_type=jnp.float32,
        )

    def values_of(weights, key_rows):
        return jnp.dot(
            weights.astype(jnp.bfloat16), held[key_rows, HEAD_DIM:],
            preferred_element_type=jnp.float32,
        )

    def lanes(weights):
        parts = [weights[:, g : g + HEAD_DIM] for g in range(0, weights.shape[1], HEAD_DIM)]
        return sum(parts[1:], parts[0])

    def triangle(scores, shift):
        weights = []
        for g in range(STEP):
            at, seen = slice(g * PIECE, (g + 1) * PIECE), (g + 1) * SPAN
            own = jnp.exp2(scores[at, :seen] * SCALE - shift[at])
            if g + 1 < STEP:
                own = jnp.concatenate(
                    [own, jnp.zeros((PIECE, STEP_KEYS - seen), jnp.float32)], axis=1
                )
            weights.append(own)
        return jnp.concatenate(weights, axis=0)

    def running(query, first_place):
        place = first_place + lax.div(
            lax.broadcasted_iota(jnp.int32, (TILE_ROWS, 1), 0), jnp.int32(PIECE)
        )

        def step(t, carry):
            top, total, summed = carry
            key_rows = pl.ds(pl.multiple_of(t * SPAN, SPAN), SPAN)
            scores = jnp.where(place >= t, scores_of(query, key_rows), NEGATIVE)
            top_new = jnp.maximum(top, jnp.max(scores, axis=1, keepdims=True))
            weights = jnp.where(place >= t, jnp.exp2((scores - top_new) * SCALE), 0.0)
            factor = jnp.exp2((top - top_new) * SCALE)
            total = total * factor + jnp.sum(weights, axis=1, keepdims=True)
            return top_new, total, summed * factor + values_of(weights, key_rows)

        start = (
            jnp.full((TILE_ROWS, 1), NEGATIVE, jnp.float32),
            jnp.zeros((TILE_ROWS, 1), jnp.float32),
            jnp.zeros((TILE_ROWS, HEAD_DIM), jnp.float32),
        )
        carry = lax.fori_loop(0, first_place + TILE, step, start)
        return carry[2] / carry[1]

    @pl.when(row_ref[ACTIVE] == 1)
    def _():
        for m in range(X):
            from_x = lax.rem(row_ref[PLACE_X] - m + X, X)
            for z in range(Z):
                place = place_of(from_x * Z + z)
                for half in range(2):
                    at = pl.ds(pl.multiple_of(place * SPAN + half * HALF, HALF), HALF)
                    pltpu.make_async_copy(
                        sources[m * 2 + half].at[z], held.at[at], copied
                    ).start()
        for span in range(SPANS):
            at = pl.ds(pl.multiple_of(place_of(span) * PIECE, PIECE), PIECE)
            pltpu.make_async_copy(pieces_ref.at[span], rows.at[at], moved_rows).start()
        pltpu.make_async_copy(rows, rows, moved_rows).wait()
        pltpu.make_async_copy(held, held, copied).wait()

        for tile in range(SPANS // TILE):
            query = rows[tile * TILE_ROWS : (tile + 1) * TILE_ROWS, :]
            shift = jnp.max(scores_of(query, pl.ds(0, SPAN)), axis=1, keepdims=True) * SCALE

            def step(t, carry):
                key_rows = pl.ds(pl.multiple_of(t * STEP_KEYS, STEP_KEYS), STEP_KEYS)
                weights = jnp.exp2(scores_of(query, key_rows) * SCALE - shift)
                return carry[0] + lanes(weights), carry[1] + values_of(weights, key_rows)

            empty = jnp.zeros((TILE_ROWS, HEAD_DIM), jnp.float32)
            total, summed = lax.fori_loop(0, 2 * tile, step, (empty, empty))

            half = TILE_ROWS // 2
            key_rows = pl.ds(2 * tile * STEP_KEYS, STEP_KEYS)
            scores = scores_of(query, key_rows)
            weights = jnp.concatenate(
                [
                    triangle(scores[:half], shift[:half]),
                    jnp.exp2(scores[half:] * SCALE - shift[half:]),
                ],
                axis=0,
            )
            total, summed = total + lanes(weights), summed + values_of(weights, key_rows)
            key_rows = pl.ds((2 * tile + 1) * STEP_KEYS, STEP_KEYS)
            weights = triangle(scores_of(query[half:], key_rows), shift[half:])
            total = jnp.concatenate([total[:half], total[half:] + lanes(weights)], axis=0)
            summed = jnp.concatenate(
                [summed[:half], summed[half:] + values_of(weights, key_rows)], axis=0
            )
            total = jnp.sum(total, axis=1, keepdims=True)

            def put(answer):
                for n in range(TILE):
                    slot = lax.rem(offset + (tile * TILE + n + 1), SPANS)
                    out_ref[slot] = answer[n * PIECE : (n + 1) * PIECE].astype(jnp.bfloat16)

            put(summed / total)

            @pl.when(jnp.logical_not(jnp.max(total) < LARGEST))
            def _():
                put(running(query, tile * TILE))


def attend(row, offset, pieces, sources):
    return pl.pallas_call(
        attend_kernel,
        out_shape=shape(SPANS, PIECE, HEAD_DIM),
        in_specs=[in_smem(), in_smem(), in_vmem()] + [anywhere()] * len(sources),
        out_specs=in_vmem(),
        scratch_shapes=[
            pltpu.VMEM((SPANS * SPAN, 2 * HEAD_DIM), jnp.bfloat16),
            pltpu.VMEM((SPANS * PIECE, HEAD_DIM), jnp.bfloat16),
            pltpu.SemaphoreType.DMA,
            pltpu.SemaphoreType.DMA,
        ],
        compiler_params=pltpu.CompilerParams(vmem_limit_bytes=VMEM_LIMIT),
        name="attend",
    )(row, offset, pieces, *sources)


def gather_kernel(row_ref, parts_ref, out_ref):
    for head in range(HERE):
        for x in range(X):
            out_ref[x * PIECE : (x + 1) * PIECE, head * HEAD_DIM : (head + 1) * HEAD_DIM] = (
                parts_ref[x * Z + row_ref[PLANE + head]]
            )


def gather_heads(row, parts):
    return pl.pallas_call(
        gather_kernel,
        out_shape=shape(SPAN, HERE * HEAD_DIM),
        in_specs=[in_smem(), in_vmem()],
        out_specs=in_vmem(),
        compiler_params=pltpu.CompilerParams(vmem_limit_bytes=VMEM_LIMIT),
        name="heads",
    )(row, parts)


def project_kernel(row_ref, rows_ref, weight_ref, out_ref):
    out_ref[0] = jnp.dot(
        rows_ref[...], weight_ref[...], preferred_element_type=jnp.float32
    ).astype(jnp.bfloat16)


def project(row, rows, weight, other):
    wide = weight.shape[1] // (Y * C)

    def weight_at(m, row_ref):
        core = row_ref[CORE]
        core = 1 - core if other else core
        return (0, lax.rem(row_ref[PLACE_Y] + m, Y) * C + core)

    return pl.pallas_call(
        project_kernel,
        out_shape=shape(Y, SPAN, wide),
        grid_spec=pltpu.PrefetchScalarGridSpec(
            num_scalar_prefetch=1,
            grid=(Y,),
            in_specs=[
                pl.BlockSpec((SPAN, HERE * HEAD_DIM), lambda m, row_ref: (0, 0)),
                pl.BlockSpec((HERE * HEAD_DIM, wide), weight_at),
            ],
            out_specs=pl.BlockSpec((1, SPAN, wide), lambda m, row_ref: (m, 0, 0)),
        ),
        compiler_params=pltpu.CompilerParams(vmem_limit_bytes=VMEM_LIMIT),
        name="project",
    )(row, rows, weight)


def body(
    query_rows,
    key_rows,
    value_rows,
    residual_in,
    out_weight,
    time_proj,
    levels,
    timestep_table,
    window_offset,
):
    me = lax.axis_index("tm") * (Y * C) + lax.axis_index("head")
    row = lax.dynamic_slice(jnp.asarray(table()), (me, 0), (1, WIDTH))[0]
    first, second, pieces = pack(row, query_rows, key_rows, value_rows)

    arrived = [
        lax.all_to_all(part, "tm", 0, 0, axis_index_groups=PLANES, tiled=True)
        for part in (first, second)
    ]
    sources = []
    for m in range(X):
        sources += [moved(part, across_pairs(m)) if m else part for part in arrived]
    pieces = lax.all_to_all(pieces, "tm", 0, 0, tiled=True)
    answers = attend(row, window_offset, pieces, sources)
    answers = lax.all_to_all(answers, "tm", 0, 0, tiled=True)
    attention = gather_heads(row, answers)

    next_slot = [
        (device(x, z, y, c), device((x * Z + z + 1) % SPANS // Z, z + 1, y, c)) for x, z, y, c in ALL
    ]
    residual = moved(residual_in, next_slot)
    level = moved(levels, next_slot)[0]

    swap = [(device(x, z, y, c), device(x, z, y, 1 - c)) for x, z, y, c in ALL]
    from_core = moved(project(row, attention, out_weight, True), swap)
    kept = project(row, attention, out_weight, False)
    both = [kept[m].astype(jnp.float32) + from_core[m].astype(jnp.float32) for m in range(Y)]
    projected = both[0]
    for m in (2, 1, 3):
        pairs = [(device(x, z, y, c), device(x, z, y + m, c)) for x, z, y, c in ALL]
        projected = projected + moved(both[m].astype(jnp.bfloat16), pairs).astype(jnp.float32)

    half_dim = time_proj.shape[0] // 2
    stamp_value = jnp.sum(
        jnp.where(jnp.arange(timestep_table.shape[0], dtype=jnp.int32) == level, timestep_table, 0)
    ).astype(jnp.float32)
    frequency = jnp.exp(-math.log(10000.0) * jnp.arange(half_dim, dtype=jnp.float32) / half_dim)
    angles = stamp_value * frequency
    embedding = jnp.concatenate([jnp.cos(angles), jnp.sin(angles)])[None, :].astype(jnp.bfloat16)
    gate_row = jnp.dot(embedding, time_proj, preferred_element_type=jnp.float32)
    return (residual.astype(jnp.float32) + gate_row * projected).astype(jnp.bfloat16)


def solution(mesh):
    in_specs = (
        P("tm", "head"),
        P("tm", "head"),
        P("tm", "head"),
        P("tm", "head"),
        P("head", None),
        P(None, "head"),
        P("tm"),
        P(),
        P(),
    )
    out_specs = P("tm", "head")
    return jax.shard_map(body, mesh=mesh, in_specs=in_specs, out_specs=out_specs, check_vma=False)
```

time: 319 us -> 245 us (0.77)
  starting transfers between devices: 204 us -> 40 us
  blocking collectives: 0 us -> 43.9 us
  Pallas kernels: 47 us -> 77.5 us
  waiting for transfers between devices: 56.3 us -> 73.8 us
    ppermute x43 -> x12, starting transfers between devices: 204 us -> 30.7 us  [moved(): return lax.ppermute(block, AXES, pairs)]
    all_to_all x0 -> x2, blocking collectives: none -> 43.9 us  [the longest x1 24.8 us: body(): lax.all_to_all(part, 'tm', 0, 0, axis_index_groups=PLANES, tiled=True)]
    pallas_call x2, Pallas kernels: 37.7 us -> 68.2 us  [the longest x1 66.5 us: attend(): pl.pallas_call(attend_kernel, out_shape=shape(SPANS, PIECE, HEAD_DIM), in...]
    all_to_all x0 -> x2, waiting for transfers between devices: none -> 11.8 us  [the longest x1 11.8 us: body(): lax.all_to_all(part, 'tm', 0, 0, axis_index_groups=PLANES, tiled=True)]
    all_to_all x0 -> x2, starting transfers between devices: none -> 9.29 us  [the longest x1 5.8 us: body(): pieces = lax.all_to_all(pieces, 'tm', 0, 0, tiled=True)]
    ppermute x43 -> x12, waiting for transfers between devices: 56.3 us -> 62 us  [moved(): return lax.ppermute(block, AXES, pairs)]
  transfers between devices with their start and end apart: 43 -> 14, of which waited for: 11 -> 8; matrix products, arithmetic and copies ran while one was open for 1% -> 1% of each run, Pallas kernels for 1% -> 2%
where the time goes in v3:
time: 245 us; the launch traced here: 244 us
  Pallas kernels  77.5 us (32%)
  waiting for transfers between devices  73.8 us (30%)
  blocking collectives  43.9 us (18%)
  starting transfers between devices  40 us (16%)
  local copies, waits for them, and re-layouts  3.67 us (1%)
  other arithmetic  3.47 us (1%)
    pallas_call x1, Pallas kernels, attend(): pl.pallas_call(attend_kernel, out_shape=shape(SPANS, PIECE, HEAD_DIM), in...  66.5 us
    ppermute x12, waiting for transfers between devices, moved(): return lax.ppermute(block, AXES, pairs)  62 us
    ppermute x12, starting transfers between devices, moved(): return lax.ppermute(block, AXES, pairs)  30.7 us
    all_to_all x1, blocking collectives, body(): lax.all_to_all(part, 'tm', 0, 0, axis_index_groups=PLANES, tiled=True)  24.8 us
    all_to_all x1, blocking collectives, body(): answers = lax.all_to_all(answers, 'tm', 0, 0, tiled=True)  19.1 us
    all_to_all x1, waiting for transfers between devices, body(): lax.all_to_all(part, 'tm', 0, 0, axis_index_groups=PLANES, tiled=True)  11.8 us
    pallas_call x2, Pallas kernels, project(): pl.pallas_call(project_kernel, out_shape=shape(Y, SPAN, wide), grid_spec=...  8.66 us
    all_to_all x1, starting transfers between devices, body(): pieces = lax.all_to_all(pieces, 'tm', 0, 0, tiled=True)  5.8 us
  transfers between devices with their start and end apart: 14, of which 8 were waited for; matrix products, arithmetic and copies ran while one was open for 1% of the time, Pallas kernels for 2%

profile of v3, /device:TPU:1, one launch (start us, length us, event | category | flops | bytes accessed | tf_op | source)
XLA Modules:
  0.0 243.9 jit_solution(11768915271700760162)
XLA Ops:
  5.4 24.8 %all_to_all.20.refs_0_ = bf16[8,128,256]{2,1,0:T(8,128)(2,1)S(1)} all-to-all(bf16[8,128,256]{2,1,0:T(8,128)(2,1)S(1)} %get-tuple-element.9), channel_id=1, replica_groups={{0,8,16,24,32,40,48,56},{64,72,80,88,96,104,112,120},{128,136,144,152,1..., dimensions={0} | all-to-all | bytes 1048576 | tf_op jit(solution)/shard_map/all_to_all | solution.py:310
  30.2 3.5 %all-to-all-start.2 = ((bf16[8,128,256]{2,1,0:T(8,128)(2,1)}), bf16[8,128,256]{2,1,0:T(8,128)(2,1)S(1)}, u32[]{:S(2)}, u32[]{:S(2)}) async-start(bf16[8,128,256]{2,1,0:T(8,128)(2,1)} %get-tuple-element.10), calls=%async_computation.2 | async-start | bytes 1048576 | tf_op jit(solution)/shard_map/all_to_all | solution.py:310
  33.7 3.1 %collective-permute-start.2 = (bf16[8,128,256]{2,1,0:T(8,128)(2,1)S(1)}, bf16[8,128,256]{2,1,0:T(8,128)(2,1)S(1)}, u32[]{:S(2)}, u32[]{:S(2)}) collective-permute-start(bf16[8,128,256]{2,1,0:T(8,128)(2,1)S(1)} %all_to_all.20.refs_0_), channel_id=1, source_target_pairs={{0,64},{1,65},{2,66},{3,67},{4,68},{5,69},{6,70},{7,71},{8,72},{10... | collective-permute-start | bytes 1572872 | tf_op jit(solution)/shard_map/ppermute | solution.py:57
  36.8 11.8 %all-to-all-done.2.refs_1_ = bf16[8,128,256]{2,1,0:T(8,128)(2,1)S(1)} async-done(((bf16[8,128,256]{2,1,0:T(8,128)(2,1)}), bf16[8,128,256]{2,1,0:T(8,128)(2,1)S(1)}, u32[]{:S(2)}, u32[]{:S(2)}) %all-to-all-start.2) | async-done | bytes 524320 | tf_op jit(solution)/shard_map/all_to_all | solution.py:310
  48.6 5.8 %all-to-all-start = ((bf16[32,64,128]{2,1,0:T(8,128)(2,1)}), bf16[32,64,128]{2,1,0:T(8,128)(2,1)S(1)}, u32[]{:S(2)}, u32[]{:S(2)}) async-start(bf16[32,64,128]{2,1,0:T(8,128)(2,1)} %get-tuple-element.8), calls=%async_computation | async-start | bytes 1048576 | tf_op jit(solution)/shard_map/all_to_all | solution.py:316
  54.4 4.7 %collective-permute-start.4 = (bf16[8,128,256]{2,1,0:T(8,128)(2,1)S(1)}, bf16[8,128,256]{2,1,0:T(8,128)(2,1)S(1)}, u32[]{:S(2)}, u32[]{:S(2)}) collective-permute-start(bf16[8,128,256]{2,1,0:T(8,128)(2,1)S(1)} %all_to_all.20.refs_0_), channel_id=1, source_target_pairs={{0,128},{1,129},{2,130},{3,131},{4,132},{5,133},{6,134},{7,135},{8... | collective-permute-start | bytes 1572872 | tf_op jit(solution)/shard_map/ppermute | solution.py:57
  59.1 2.2 collective-permute-start.3
  61.3 3.7 %collective-permute-start.5 = (bf16[8,128,256]{2,1,0:T(8,128)(2,1)S(1)}, bf16[8,128,256]{2,1,0:T(8,128)(2,1)}, u32[]{:S(2)}, u32[]{:S(2)}) collective-permute-start(bf16[8,128,256]{2,1,0:T(8,128)(2,1)S(1)} %all-to-all-done.2.refs_1_), channel_id=1, source_target_pairs={{0,128},{1,129},{2,130},{3,131},{4,132},{5,133},{6,134},{7,135},{8... | collective-permute-start | bytes 1572872 | tf_op jit(solution)/shard_map/ppermute | solution.py:57
  65.0 2.6 %collective-permute-start.6 = (bf16[8,128,256]{2,1,0:T(8,128)(2,1)S(1)}, bf16[8,128,256]{2,1,0:T(8,128)(2,1)}, u32[]{:S(2)}, u32[]{:S(2)}) collective-permute-start(bf16[8,128,256]{2,1,0:T(8,128)(2,1)S(1)} %all_to_all.20.refs_0_), channel_id=1, source_target_pairs={{0,192},{1,193},{2,194},{3,195},{4,196},{5,197},{6,198},{7,199},{8... | collective-permute-start | bytes 1572872 | tf_op jit(solution)/shard_map/ppermute | solution.py:57
  67.6 2.8 %collective-permute-start.7 = (bf16[8,128,256]{2,1,0:T(8,128)(2,1)S(1)}, bf16[8,128,256]{2,1,0:T(8,128)(2,1)}, u32[]{:S(2)}, u32[]{:S(2)}) collective-permute-start(bf16[8,128,256]{2,1,0:T(8,128)(2,1)S(1)} %all-to-all-done.2.refs_1_), channel_id=1, source_target_pairs={{0,192},{1,193},{2,194},{3,195},{4,196},{5,197},{6,198},{7,199},{8... | collective-permute-start | bytes 1572872 | tf_op jit(solution)/shard_map/ppermute | solution.py:57
  71.0 18.4 %collective-permute-done.3.refs_3_ = bf16[8,128,256]{2,1,0:T(8,128)(2,1)S(1)} collective-permute-done((bf16[8,128,256]{2,1,0:T(8,128)(2,1)S(1)}, bf16[8,128,256]{2,1,0:T(8,128)(2,1)S(1)}, u32[]{:S(2)}, u32[]{:S(2)}) %collective-permute-start.3) | collective-permute-done | bytes 524320 | tf_op jit(solution)/shard_map/ppermute | solution.py:57
  89.5 8.9 %collective-permute-done.5.refs_5_ = bf16[8,128,256]{2,1,0:T(8,128)(2,1)} collective-permute-done((bf16[8,128,256]{2,1,0:T(8,128)(2,1)S(1)}, bf16[8,128,256]{2,1,0:T(8,128)(2,1)}, u32[]{:S(2)}, u32[]{:S(2)}) %collective-permute-start.5) | collective-permute-done | bytes 524320 | tf_op jit(solution)/shard_map/ppermute | solution.py:57
  98.4 10.3 %collective-permute-done.7.refs_7_ = bf16[8,128,256]{2,1,0:T(8,128)(2,1)} collective-permute-done((bf16[8,128,256]{2,1,0:T(8,128)(2,1)S(1)}, bf16[8,128,256]{2,1,0:T(8,128)(2,1)}, u32[]{:S(2)}, u32[]{:S(2)}) %collective-permute-start.7) | collective-permute-done | bytes 524320 | tf_op jit(solution)/shard_map/ppermute | solution.py:57
  108.7 66.5 %attend.1 = bf16[32,64,128]{2,1,0:T(8,128)(2,1)S(1)} custom-call(s32[32]{0:T(128)S(1)} %dynamic-slice_bitcast_fusion.row_ref, s32[1]{0:T(128)S(6)} %copy.11.offset_ref, bf16[32,64,128]{2,1,0:T(8,128)(2,1)S(1)} %all-to-all-done.pieces_ref, bf16[8,128,256]{2,1,0:T(8,128)(2,1)S(1)} %all_to_all.20.refs_0_, bf16[8,128,256]{2,1,0:T(8,128)(2,1)S(1)} %all-to-all-done.2.refs_1_, ...), custom_call_target="tpu_custom_call" | custom-call | tf_op jit(solution)/shard_map/attend/pallas_call | solution.py:228
  175.2 19.1 %all_to_all.21.parts_ref = bf16[32,64,128]{2,1,0:T(8,128)(2,1)S(1)} all-to-all(bf16[32,64,128]{2,1,0:T(8,128)(2,1)S(1)} %attend.1), channel_id=1, replica_groups=mesh['tm'=32,'head'=8] {'tm'}, dimensions={0} | all-to-all | bytes 1048576 | tf_op jit(solution)/shard_map/all_to_all | solution.py:318
  194.9 4.3 %project.3 = bf16[4,256,640]{2,1,0:T(8,128)(2,1)S(1)} custom-call(s32[32]{0:T(128)S(1)} %dynamic-slice_bitcast_fusion.row_ref, bf16[256,640]{1,0:T(8,128)(2,1)S(1)} %heads.1.rows_ref, bf16[640,5120]{1,0:T(8,128)(2,1)} %weight_ref.3), custom_call_target="tpu_custom_call" | custom-call | tf_op jit(solution)/shard_map/project/pallas_call | solution.py:277
  199.3 5.3 %collective-permute-start.8 = (bf16[4,256,640]{2,1,0:T(8,128)(2,1)S(1)}, bf16[4,256,640]{2,1,0:T(8,128)(2,1)S(1)}, u32[]{:S(2)}, u32[]{:S(2)}) collective-permute-start(bf16[4,256,640]{2,1,0:T(8,128)(2,1)S(1)} %project.3), channel_id=1, source_target_pairs={{0,1},{1,0},{2,3},{3,2},{4,5},{5,4},{6,7},{7,6},{8,9},{9,8},{10,11... | collective-permute-start | bytes 3932168 | tf_op jit(solution)/shard_map/ppermute | solution.py:57
  206.5 10.9 %collective-permute-done.1 = s32[1]{0:T(128)} collective-permute-done((s32[1]{0:T(128)}, s32[1]{0:T(128)}, u32[]{:S(2)}, u32[]{:S(2)}) %collective-permute-start.1) | collective-permute-done | bytes 36 | tf_op jit(solution)/shard_map/ppermute | solution.py:57
  219.3 4.3 %project.2 = bf16[4,256,640]{2,1,0:T(8,128)(2,1)S(1)} custom-call(s32[32]{0:T(128)S(1)} %dynamic-slice_bitcast_fusion.row_ref, bf16[256,640]{1,0:T(8,128)(2,1)S(1)} %heads.1.rows_ref, bf16[640,5120]{1,0:T(8,128)(2,1)} %weight_ref.3), custom_call_target="tpu_custom_call" | custom-call | tf_op jit(solution)/shard_map/project/pallas_call | solution.py:277
  223.9 2.8 %collective-permute-start.11 = (bf16[256,640]{1,0:T(8,128)(2,1)S(1)}, bf16[256,640]{1,0:T(8,128)(2,1)S(1)}, u32[]{:S(2)}, u32[]{:S(2)}) collective-permute-start(bf16[256,640]{1,0:T(8,128)(2,1)S(1)} %get-tuple-element.12), channel_id=1, source_target_pairs={{0,6},{1,7},{2,0},{3,1},{4,2},{5,3},{6,4},{7,5},{8,14},{9,15},{10,... | collective-permute-start | bytes 983048 | tf_op jit(solution)/shard_map/ppermute | solution.py:57
  228.7 5.2 %collective-permute-done.11 = bf16[256,640]{1,0:T(8,128)(2,1)S(1)} collective-permute-done((bf16[256,640]{1,0:T(8,128)(2,1)S(1)}, bf16[256,640]{1,0:T(8,128)(2,1)S(1)}, u32[]{:S(2)}, u32[]{:S(2)}) %collective-permute-start.11) | collective-permute-done | bytes 327712 | tf_op jit(solution)/shard_map/ppermute | solution.py:57
  233.9 3.1 %collective-permute-done.10 = bf16[256,640]{1,0:T(8,128)(2,1)S(1)} collective-permute-done((bf16[256,640]{1,0:T(8,128)(2,1)S(1)}, bf16[256,640]{1,0:T(8,128)(2,1)S(1)}, u32[]{:S(2)}, u32[]{:S(2)}) %collective-permute-start.10) | collective-permute-done | bytes 327712 | tf_op jit(solution)/shard_map/ppermute | solution.py:57
  237.0 5.0 %collective-permute-done.9 = bf16[256,640]{1,0:T(8,128)(2,1)S(1)} collective-permute-done((bf16[256,640]{1,0:T(8,128)(2,1)S(1)}, bf16[256,640]{1,0:T(8,128)(2,1)S(1)}, u32[]{:S(2)}, u32[]{:S(2)}) %collective-permute-start.9) | collective-permute-done | bytes 327712 | tf_op jit(solution)/shard_map/ppermute | solution.py:57
  242.0 2.0 fusion.4
  (29 shorter events, 11.3 us)
Async XLA Ops:
  0.0 228.5 %copy-start = (bf16[256,640]{1,0:T(8,128)(2,1)S(1)}, bf16[256,640]{1,0:T(8,128)(2,1)}, u32[]{:S(2)}) copy-start(bf16[256,640]{1,0:T(8,128)(2,1)} %param.15) | copy-start | bytes 983044
  0.7 1.0 copy-start.1
  1.7 1.0 copy-start.2
  2.7 1.0 copy-start.3
  30.2 18.4 %all-to-all-start.2 = ((bf16[8,128,256]{2,1,0:T(8,128)(2,1)}), bf16[8,128,256]{2,1,0:T(8,128)(2,1)S(1)}, u32[]{:S(2)}, u32[]{:S(2)}) async-start(bf16[8,128,256]{2,1,0:T(8,128)(2,1)} %get-tuple-element.10), calls=%async_computation.2 | async-start | bytes 1048576 | tf_op jit(solution)/shard_map/all_to_all | solution.py:310
  33.7 33.9 %collective-permute-start.2 = (bf16[8,128,256]{2,1,0:T(8,128)(2,1)S(1)}, bf16[8,128,256]{2,1,0:T(8,128)(2,1)S(1)}, u32[]{:S(2)}, u32[]{:S(2)}) collective-permute-start(bf16[8,128,256]{2,1,0:T(8,128)(2,1)S(1)} %all_to_all.20.refs_0_), channel_id=1, source_target_pairs={{0,64},{1,65},{2,66},{3,67},{4,68},{5,69},{6,70},{7,71},{8,72},{10... | collective-permute-start | bytes 1572872 | tf_op jit(solution)/shard_map/ppermute | solution.py:57
  48.6 22.4 %all-to-all-start = ((bf16[32,64,128]{2,1,0:T(8,128)(2,1)}), bf16[32,64,128]{2,1,0:T(8,128)(2,1)S(1)}, u32[]{:S(2)}, u32[]{:S(2)}) async-start(bf16[32,64,128]{2,1,0:T(8,128)(2,1)} %get-tuple-element.8), calls=%async_computation | async-start | bytes 1048576 | tf_op jit(solution)/shard_map/all_to_all | solution.py:316
  54.4 35.0 %collective-permute-start.4 = (bf16[8,128,256]{2,1,0:T(8,128)(2,1)S(1)}, bf16[8,128,256]{2,1,0:T(8,128)(2,1)S(1)}, u32[]{:S(2)}, u32[]{:S(2)}) collective-permute-start(bf16[8,128,256]{2,1,0:T(8,128)(2,1)S(1)} %all_to_all.20.refs_0_), channel_id=1, source_target_pairs={{0,128},{1,129},{2,130},{3,131},{4,132},{5,133},{6,134},{7,135},{8... | collective-permute-start | bytes 1572872 | tf_op jit(solution)/shard_map/ppermute | solution.py:57
  59.1 30.3 %collective-permute-start.3 = (bf16[8,128,256]{2,1,0:T(8,128)(2,1)S(1)}, bf16[8,128,256]{2,1,0:T(8,128)(2,1)S(1)}, u32[]{:S(2)}, u32[]{:S(2)}) collective-permute-start(bf16[8,128,256]{2,1,0:T(8,128)(2,1)S(1)} %all-to-all-done.2.refs_1_), channel_id=1, source_target_pairs={{0,64},{1,65},{2,66},{3,67},{4,68},{5,69},{6,70},{7,71},{8,72},{10... | collective-permute-start | bytes 1572872 | tf_op jit(solution)/shard_map/ppermute | solution.py:57
  61.3 37.0 %collective-permute-start.5 = (bf16[8,128,256]{2,1,0:T(8,128)(2,1)S(1)}, bf16[8,128,256]{2,1,0:T(8,128)(2,1)}, u32[]{:S(2)}, u32[]{:S(2)}) collective-permute-start(bf16[8,128,256]{2,1,0:T(8,128)(2,1)S(1)} %all-to-all-done.2.refs_1_), channel_id=1, source_target_pairs={{0,128},{1,129},{2,130},{3,131},{4,132},{5,133},{6,134},{7,135},{8... | collective-permute-start | bytes 1572872 | tf_op jit(solution)/shard_map/ppermute | solution.py:57
  65.0 33.4 %collective-permute-start.6 = (bf16[8,128,256]{2,1,0:T(8,128)(2,1)S(1)}, bf16[8,128,256]{2,1,0:T(8,128)(2,1)}, u32[]{:S(2)}, u32[]{:S(2)}) collective-permute-start(bf16[8,128,256]{2,1,0:T(8,128)(2,1)S(1)} %all_to_all.20.refs_0_), channel_id=1, source_target_pairs={{0,192},{1,193},{2,194},{3,195},{4,196},{5,197},{6,198},{7,199},{8... | collective-permute-start | bytes 1572872 | tf_op jit(solution)/shard_map/ppermute | solution.py:57
  67.6 41.1 %collective-permute-start.7 = (bf16[8,128,256]{2,1,0:T(8,128)(2,1)S(1)}, bf16[8,128,256]{2,1,0:T(8,128)(2,1)}, u32[]{:S(2)}, u32[]{:S(2)}) collective-permute-start(bf16[8,128,256]{2,1,0:T(8,128)(2,1)S(1)} %all-to-all-done.2.refs_1_), channel_id=1, source_target_pairs={{0,192},{1,193},{2,194},{3,195},{4,196},{5,197},{6,198},{7,199},{8... | collective-permute-start | bytes 1572872 | tf_op jit(solution)/shard_map/ppermute | solution.py:57
  194.9 22.5 %copy-start.4 = (s32[50]{0:T(128)S(1)}, s32[50]{0:T(128)}, u32[]{:S(2)}) copy-start(s32[50]{0:T(128)} %param.17) | copy-start | bytes 604
  199.3 24.4 %collective-permute-start.8 = (bf16[4,256,640]{2,1,0:T(8,128)(2,1)S(1)}, bf16[4,256,640]{2,1,0:T(8,128)(2,1)S(1)}, u32[]{:S(2)}, u32[]{:S(2)}) collective-permute-start(bf16[4,256,640]{2,1,0:T(8,128)(2,1)S(1)} %project.3), channel_id=1, source_target_pairs={{0,1},{1,0},{2,3},{3,2},{4,5},{5,4},{6,7},{7,6},{8,9},{9,8},{10,11... | collective-permute-start | bytes 3932168 | tf_op jit(solution)/shard_map/ppermute | solution.py:57
  204.6 24.1 %collective-permute-start = (bf16[256,640]{1,0:T(8,128)(2,1)}, bf16[256,640]{1,0:T(8,128)(2,1)}, u32[]{:S(2)}, u32[]{:S(2)}) collective-permute-start(bf16[256,640]{1,0:T(8,128)(2,1)} %param.13), channel_id=1, source_target_pairs={{0,8},{1,9},{2,10},{3,11},{4,12},{5,13},{6,14},{7,15},{8,16},{9,17... | collective-permute-start | bytes 983048 | tf_op jit(solution)/shard_map/ppermute | solution.py:57
  206.5 11.0 %collective-permute-start.1 = (s32[1]{0:T(128)}, s32[1]{0:T(128)}, u32[]{:S(2)}, u32[]{:S(2)}) collective-permute-start(s32[1]{0:T(128)} %param.16), channel_id=1, source_target_pairs={{0,8},{1,9},{2,10},{3,11},{4,12},{5,13},{6,14},{7,15},{8,16},{9,17... | collective-permute-start | bytes 20 | tf_op jit(solution)/shard_map/ppermute | solution.py:57
  223.9 10.0 %collective-permute-start.11 = (bf16[256,640]{1,0:T(8,128)(2,1)S(1)}, bf16[256,640]{1,0:T(8,128)(2,1)S(1)}, u32[]{:S(2)}, u32[]{:S(2)}) collective-permute-start(bf16[256,640]{1,0:T(8,128)(2,1)S(1)} %get-tuple-element.12), channel_id=1, source_target_pairs={{0,6},{1,7},{2,0},{3,1},{4,2},{5,3},{6,4},{7,5},{8,14},{9,15},{10,... | collective-permute-start | bytes 983048 | tf_op jit(solution)/shard_map/ppermute | solution.py:57
  226.7 10.2 %collective-permute-start.10 = (bf16[256,640]{1,0:T(8,128)(2,1)S(1)}, bf16[256,640]{1,0:T(8,128)(2,1)S(1)}, u32[]{:S(2)}, u32[]{:S(2)}) collective-permute-start(bf16[256,640]{1,0:T(8,128)(2,1)S(1)} %get-tuple-element.13), channel_id=1, source_target_pairs={{0,2},{1,3},{2,4},{3,5},{4,6},{5,7},{6,0},{7,1},{8,10},{9,11},{10,... | collective-permute-start | bytes 983048 | tf_op jit(solution)/shard_map/ppermute | solution.py:57
  226.7 15.2 %collective-permute-start.9 = (bf16[256,640]{1,0:T(8,128)(2,1)S(1)}, bf16[256,640]{1,0:T(8,128)(2,1)S(1)}, u32[]{:S(2)}, u32[]{:S(2)}) collective-permute-start(bf16[256,640]{1,0:T(8,128)(2,1)S(1)} %get-tuple-element.11), channel_id=1, source_target_pairs={{0,4},{1,5},{2,6},{3,7},{4,0},{5,1},{6,2},{7,3},{8,12},{9,13},{10,... | collective-permute-start | bytes 983048 | tf_op jit(solution)/shard_map/ppermute | solution.py:57

commit v4 on v3

v4 whole, which is shorter than its diff:
```python
import functools
import math

import jax
import jax.numpy as jnp
import numpy as np
from jax import lax
from jax.experimental import pallas as pl
from jax.experimental.pallas import tpu as pltpu
from jax.sharding import PartitionSpec as P

HEAD_DIM = 128
SPAN = 256
X, Z, Y, C = 4, 8, 4, 2
HERE = 5
SPANS = X * Z
NEGATIVE = -1e30
SCALE = math.log2(math.e) / math.sqrt(HEAD_DIM)
VMEM_LIMIT = 48 * 1024 * 1024

HOST = ((0, 1, 3, 4, 6), (0, 2, 4, 5, 7))
AXES = ("tm", "head")
PIECE = SPAN // X


def device(x, z, y, c):
    return ((x % X) * Z + z % Z) * (Y * C) + (y % Y) * C + c


ALL = [(x, z, y, c) for x in range(X) for z in range(Z) for y in range(Y) for c in range(C)]
PLANES = [[x * Z + z for z in range(Z)] for x in range(X)]


def across_pairs(m):
    return [(device(x, z, y, c), device(x + m, z, y, c)) for x, z, y, c in ALL if z in HOST[c]]


HEAD, PLANE, ACTIVE, PLACE_X, PLACE_Y, CORE = 0, 8, 13, 14, 15, 16
WIDTH = 32


def table():
    rows = np.zeros((X * Z * Y * C, WIDTH), np.int32)
    for x, z, y, c in ALL:
        row = rows[device(x, z, y, c)]
        for to_z in range(Z):
            row[HEAD + to_z] = HOST[c].index(to_z) if to_z in HOST[c] else -1
        row[PLANE : PLANE + HERE] = HOST[c]
        row[ACTIVE] = int(z in HOST[c])
        row[PLACE_X] = x
        row[PLACE_Y] = y
        row[CORE] = c
    return rows


def moved(block, pairs):
    return lax.ppermute(block, AXES, pairs)


def in_vmem():
    return pl.BlockSpec(memory_space=pltpu.VMEM)


def in_smem():
    return pl.BlockSpec(memory_space=pltpu.SMEM)


def anywhere():
    return pl.BlockSpec(memory_space=pl.ANY)


def shape(*dims, dtype=jnp.bfloat16):
    return jax.ShapeDtypeStruct(dims, dtype)


def pack_kernel(row_ref, query_ref, key_ref, value_ref, keys_ref, pieces_ref):
    for z in range(Z):
        head = row_ref[HEAD + z]

        @pl.when(head >= 0)
        def _():
            columns = pl.ds(pl.multiple_of(head * HEAD_DIM, HEAD_DIM), HEAD_DIM)
            keys_ref[z, :, :HEAD_DIM] = key_ref[:, columns]
            keys_ref[z, :, HEAD_DIM:] = value_ref[:, columns]
            for x in range(X):
                pieces_ref[x * Z + z] = query_ref[x * PIECE : (x + 1) * PIECE, columns]


def pack(row, query_rows, key_rows, value_rows):
    return pl.pallas_call(
        pack_kernel,
        out_shape=[shape(Z, SPAN, 2 * HEAD_DIM), shape(SPANS, PIECE, HEAD_DIM)],
        in_specs=[in_smem(), in_vmem(), in_vmem(), in_vmem()],
        out_specs=[in_vmem()] * 2,
        compiler_params=pltpu.CompilerParams(vmem_limit_bytes=VMEM_LIMIT),
        name="pack",
    )(row, query_rows, key_rows, value_rows)


STEP = Z // 2
STEP_KEYS = STEP * SPAN
STEPS = 2 * X
TILE = 8
TILES = SPANS // TILE
TILE_ROWS = TILE * PIECE
ROWS = SPANS * PIECE
SMALLEST, LARGEST = 1e-18, 1e30


def attend_kernel(places, ends, row_ref, offset_ref, pieces_ref, *refs):
    sources, refs = refs[: len(places)], refs[len(places) :]
    if ends:
        (total_in, summed_in, shift_ref), refs = refs[:3], refs[3:]
        later_steps, refs = refs[: STEPS - len(places)], refs[STEPS - len(places) :]
        refs = refs[len(refs) - 6 :]
        out_ref, held, rows, total_ref, summed_ref, copied = refs
    else:
        total_ref, summed_ref, shift_ref, held, rows, copied = refs
    offset = offset_ref[0]

    def place_of(span):
        return lax.rem(span - offset + SPANS, SPANS)

    def first_place(at):
        m, half = at
        return place_of(lax.rem(row_ref[PLACE_X] - m + X, X) * Z + half * STEP)

    def pick(values, i):
        found = values[0]
        for n, value in enumerate(values[1:], 1):
            found = jnp.where(i == n, value, found)
        return found

    def scores_of(query, keys):
        return lax.dot_general(
            query, keys, (((1,), (1,)), ((), ())), preferred_element_type=jnp.float32
        )

    def values_of(weights, values):
        return jnp.dot(
            weights.astype(jnp.bfloat16), values, preferred_element_type=jnp.float32
        )

    def lanes(weights):
        parts = [weights[:, g : g + HEAD_DIM] for g in range(0, weights.shape[1], HEAD_DIM)]
        return sum(parts[1:], parts[0])

    def tile_rows(tile):
        return pl.ds(pl.multiple_of(tile * TILE_ROWS, TILE_ROWS), TILE_ROWS)

    def row_places(tile):
        return tile * TILE + lax.div(
            lax.broadcasted_iota(jnp.int32, (TILE_ROWS, 1), 0), jnp.int32(PIECE)
        )

    def running(tile, firsts):
        query, own = rows[tile_rows(tile), :], row_places(tile)

        def step(t, carry):
            top, total, summed = carry
            key_rows = pl.ds(pl.multiple_of(lax.rem(t, STEP) * SPAN, SPAN), SPAN)
            at = lax.div(t, STEP)
            seen = own >= lax.rem(pick(firsts, at) + lax.rem(t, STEP), SPANS)
            scores = jnp.where(seen, scores_of(query, held[at, key_rows, :HEAD_DIM]), NEGATIVE)
            top_new = jnp.maximum(top, jnp.max(scores, axis=1, keepdims=True))
            weights = jnp.where(seen, jnp.exp2((scores - top_new) * SCALE), 0.0)
            factor = jnp.exp2((top - top_new) * SCALE)
            total = total * factor + jnp.sum(weights, axis=1, keepdims=True)
            summed = summed * factor + values_of(weights, held[at, key_rows, HEAD_DIM:])
            return top_new, total, summed

        start = (
            jnp.full((TILE_ROWS, 1), NEGATIVE, jnp.float32),
            jnp.zeros((TILE_ROWS, 1), jnp.float32),
            jnp.zeros((TILE_ROWS, HEAD_DIM), jnp.float32),
        )
        carry = lax.fori_loop(0, SPANS, step, start)
        return carry[2] / carry[1]

    @pl.when(row_ref[ACTIVE] == 1)
    def _():
        steps = len(places)
        for i, source in enumerate(sources):
            pltpu.make_async_copy(source, held.at[i], copied).start()
        for span in range(SPANS):
            at = pl.ds(pl.multiple_of(place_of(span) * PIECE, PIECE), PIECE)
            rows[at, :] = pieces_ref[span]
        firsts = [first_place(at) for at in places]
        if ends:
            total_ref[...] = total_in[...]
            summed_ref[...] = summed_in[...]
        else:
            total_ref[...] = jnp.zeros_like(total_ref)
            summed_ref[...] = jnp.zeros_like(summed_ref)
        brought = held.at[pl.ds(0, steps)]
        pltpu.make_async_copy(brought, brought, copied).wait()

        if not ends:
            for tile in range(TILES):
                at = slice(tile * TILE_ROWS, (tile + 1) * TILE_ROWS)
                top = jnp.max(
                    scores_of(rows[at, :], held[0, :HEAD_DIM, :HEAD_DIM]), axis=1, keepdims=True
                )
                shift_ref[at, :] = jnp.broadcast_to(top * SCALE, (TILE_ROWS, HEAD_DIM))

        def add(tile, i, masked, first):
            at = tile_rows(tile)
            scores = scores_of(rows[at, :], held[i, :, :HEAD_DIM])
            shift = shift_ref[at, :1]
            if masked:
                own = row_places(tile)
                weights = []
                for u in range(STEP):
                    hidden = own < lax.rem(first + u, SPANS)
                    part = scores[:, u * SPAN : (u + 1) * SPAN] * SCALE
                    weights.append(jnp.exp2(part - jnp.where(hidden, LARGEST, shift)))
                weights = jnp.concatenate(weights, axis=1)
            else:
                weights = jnp.exp2(scores * SCALE - shift)
            total_ref[at, :] += lanes(weights)
            summed_ref[at, :] += values_of(weights, held[i, :, HEAD_DIM:])

        def one(n, unused):
            tile, i = lax.div(n, steps), lax.rem(n, steps)
            first = pick(firsts, i)
            wraps = first > SPANS - STEP
            lowest = jnp.where(wraps, 0, first)
            highest = jnp.where(wraps, SPANS - 1, first + STEP - 1)
            whole = highest <= tile * TILE

            @pl.when(whole)
            def _():
                add(tile, i, False, first)

            @pl.when(jnp.logical_not(whole) & (lowest < (tile + 1) * TILE))
            def _():
                add(tile, i, True, first)

            return unused

        lax.fori_loop(0, TILES * steps, one, 0)

        if ends:

            def put(tile, answer):
                for n in range(TILE):
                    slot = lax.rem(offset + (tile * TILE + n + 1), SPANS)
                    out_ref[slot] = answer[n * PIECE : (n + 1) * PIECE].astype(jnp.bfloat16)

            total = jnp.sum(total_ref[...], axis=1, keepdims=True)
            for tile in range(TILES):
                at = slice(tile * TILE_ROWS, (tile + 1) * TILE_ROWS)
                put(tile, summed_ref[at, :] / total[at])

            safe = (jnp.max(total) < LARGEST) & (jnp.min(total) > SMALLEST)

            @pl.when(jnp.logical_not(safe))
            def _():
                for i, source in enumerate(later_steps):
                    pltpu.make_async_copy(source, held.at[steps + i], copied).start()
                brought = held.at[pl.ds(steps, STEPS - steps)]
                pltpu.make_async_copy(brought, brought, copied).wait()
                all_firsts = firsts + [first_place(at) for at in NEAR]
                for tile in range(TILES):
                    put(tile, running(tile, all_firsts))


NEAR = ((0, 0), (0, 1), (1, 0), (1, 1), (3, 0), (3, 1))
FAR = ((2, 0), (2, 1))


def attend_near(row, offset, pieces, near):
    held = shape(ROWS, HEAD_DIM, dtype=jnp.float32)
    return pl.pallas_call(
        functools.partial(attend_kernel, NEAR, False),
        out_shape=[held] * 3,
        in_specs=[in_smem(), in_smem(), in_vmem()] + [anywhere()] * len(near),
        out_specs=[in_vmem()] * 3,
        scratch_shapes=[
            pltpu.VMEM((len(near), STEP_KEYS, 2 * HEAD_DIM), jnp.bfloat16),
            pltpu.VMEM((ROWS, HEAD_DIM), jnp.bfloat16),
            pltpu.SemaphoreType.DMA,
        ],
        compiler_params=pltpu.CompilerParams(vmem_limit_bytes=VMEM_LIMIT),
        name="near",
    )(row, offset, pieces, *near)


def attend_far(row, offset, pieces, far, state, near, others):
    return pl.pallas_call(
        functools.partial(attend_kernel, FAR, True),
        out_shape=shape(SPANS, PIECE, HEAD_DIM),
        in_specs=[in_smem(), in_smem(), in_vmem()]
        + [anywhere()] * len(far)
        + [in_vmem()] * len(state)
        + [anywhere()] * (len(near) + len(others)),
        out_specs=in_vmem(),
        scratch_shapes=[
            pltpu.VMEM((STEPS, STEP_KEYS, 2 * HEAD_DIM), jnp.bfloat16),
            pltpu.VMEM((ROWS, HEAD_DIM), jnp.bfloat16),
            pltpu.VMEM((ROWS, HEAD_DIM), jnp.float32),
            pltpu.VMEM((ROWS, HEAD_DIM), jnp.float32),
            pltpu.SemaphoreType.DMA,
        ],
        compiler_params=pltpu.CompilerParams(vmem_limit_bytes=VMEM_LIMIT),
        name="far",
    )(row, offset, pieces, *far, *state, *near, *others)


def gather_kernel(row_ref, parts_ref, out_ref):
    for head in range(HERE):
        for x in range(X):
            out_ref[x * PIECE : (x + 1) * PIECE, head * HEAD_DIM : (head + 1) * HEAD_DIM] = (
                parts_ref[x * Z + row_ref[PLANE + head]]
            )


def gather_heads(row, parts):
    return pl.pallas_call(
        gather_kernel,
        out_shape=shape(SPAN, HERE * HEAD_DIM),
        in_specs=[in_smem(), in_vmem()],
        out_specs=in_vmem(),
        compiler_params=pltpu.CompilerParams(vmem_limit_bytes=VMEM_LIMIT),
        name="heads",
    )(row, parts)


def project_kernel(row_ref, rows_ref, weight_ref, out_ref):
    out_ref[0] = jnp.dot(
        rows_ref[...], weight_ref[...], preferred_element_type=jnp.float32
    ).astype(jnp.bfloat16)


def project(row, rows, weight, other):
    wide = weight.shape[1] // (Y * C)

    def weight_at(m, row_ref):
        core = row_ref[CORE]
        core = 1 - core if other else core
        return (0, lax.rem(row_ref[PLACE_Y] + m, Y) * C + core)

    return pl.pallas_call(
        project_kernel,
        out_shape=shape(Y, SPAN, wide),
        grid_spec=pltpu.PrefetchScalarGridSpec(
            num_scalar_prefetch=1,
            grid=(Y,),
            in_specs=[
                pl.BlockSpec((SPAN, HERE * HEAD_DIM), lambda m, row_ref: (0, 0)),
                pl.BlockSpec((HERE * HEAD_DIM, wide), weight_at),
            ],
            out_specs=pl.BlockSpec((1, SPAN, wide), lambda m, row_ref: (m, 0, 0)),
        ),
        compiler_params=pltpu.CompilerParams(vmem_limit_bytes=VMEM_LIMIT),
        name="project",
    )(row, rows, weight)


def body(
    query_rows,
    key_rows,
    value_rows,
    residual_in,
    out_weight,
    time_proj,
    levels,
    timestep_table,
    window_offset,
):
    me = lax.axis_index("tm") * (Y * C) + lax.axis_index("head")
    row = lax.dynamic_slice(jnp.asarray(table()), (me, 0), (1, WIDTH))[0]
    keys, pieces = pack(row, query_rows, key_rows, value_rows)

    keys = lax.all_to_all(keys, "tm", 0, 0, axis_index_groups=PLANES, tiled=True)
    pieces = lax.all_to_all(pieces, "tm", 0, 0, tiled=True)

    own = [keys[half * STEP : (half + 1) * STEP].reshape(STEP_KEYS, -1) for half in range(2)]
    back = [moved(part, across_pairs(1)) for part in own]
    ahead = [moved(part, across_pairs(-1)) for part in own]
    far = [moved(ahead[0], across_pairs(-1)), moved(back[1], across_pairs(1))]
    near = own + back + ahead

    next_slot = [
        (device(x, z, y, c), device((x * Z + z + 1) % SPANS // Z, z + 1, y, c)) for x, z, y, c in ALL
    ]
    residual = moved(residual_in, next_slot)
    level = moved(levels, next_slot)

    state = attend_near(row, window_offset, pieces, near)
    answers = attend_far(row, window_offset, pieces, far, state, near, [residual, level])
    answers = lax.all_to_all(answers, "tm", 0, 0, tiled=True)
    attention = gather_heads(row, answers)

    swap = [(device(x, z, y, c), device(x, z, y, 1 - c)) for x, z, y, c in ALL]
    from_core = moved(project(row, attention, out_weight, True), swap)
    kept = project(row, attention, out_weight, False)
    both = [kept[m].astype(jnp.float32) + from_core[m].astype(jnp.float32) for m in range(Y)]
    projected = both[0]
    for m in (2, 1, 3):
        pairs = [(device(x, z, y, c), device(x, z, y + m, c)) for x, z, y, c in ALL]
        projected = projected + moved(both[m].astype(jnp.bfloat16), pairs).astype(jnp.float32)

    half_dim = time_proj.shape[0] // 2
    stamp_value = jnp.sum(
        jnp.where(jnp.arange(timestep_table.shape[0], dtype=jnp.int32) == level[0], timestep_table, 0)
    ).astype(jnp.float32)
    frequency = jnp.exp(-math.log(10000.0) * jnp.arange(half_dim, dtype=jnp.float32) / half_dim)
    angles = stamp_value * frequency
    embedding = jnp.concatenate([jnp.cos(angles), jnp.sin(angles)])[None, :].astype(jnp.bfloat16)
    gate_row = jnp.dot(embedding, time_proj, preferred_element_type=jnp.float32)
    return (residual.astype(jnp.float32) + gate_row * projected).astype(jnp.bfloat16)


def solution(mesh):
    in_specs = (
        P("tm", "head"),
        P("tm", "head"),
        P("tm", "head"),
        P("tm", "head"),
        P("head", None),
        P(None, "head"),
        P("tm"),
        P(),
        P(),
    )
    out_specs = P("tm", "head")
    return jax.shard_map(body, mesh=mesh, in_specs=in_specs, out_specs=out_specs, check_vma=False)
```

time: 245 us -> 241 us (0.984)
  waiting for transfers between devices: 73.8 us -> 28.8 us
  Pallas kernels: 77.5 us -> 111 us
  blocking collectives: 43.9 us -> 53.6 us
  starting transfers between devices: 40 us -> 36.1 us
    pallas_call x2 -> x3, Pallas kernels: 68.2 us -> 101 us  [the longest x1 80.2 us: attend_far(): pl.pallas_call(functools.partial(attend_kernel, FAR, True), out_shape=sha...]
    ppermute x12, waiting for transfers between devices: 62 us -> 28.8 us  [moved(): return lax.ppermute(block, AXES, pairs)]
    all_to_all x1 -> x0, waiting for transfers between devices: 11.8 us -> none  [body(): lax.all_to_all(part, 'tm', 0, 0, axis_index_groups=PLANES, tiled=True)]
    all_to_all x1, blocking collectives: 24.8 us -> 36 us  [body(): lax.all_to_all(keys, 'tm', 0, 0, axis_index_groups=PLANES, tiled=True)]
    all_to_all x1 -> x0, starting transfers between devices: 3.49 us -> none  [body(): lax.all_to_all(part, 'tm', 0, 0, axis_index_groups=PLANES, tiled=True)]
  transfers between devices with their start and end apart: 14 -> 13, of which waited for: 8 -> 3; matrix products, arithmetic and copies ran while one was open for 1% -> 1% of each run, Pallas kernels for 2% -> 10%
where the time goes in v4:
time: 241 us; the launch traced here: 240 us
  Pallas kernels  111 us (46%)
  blocking collectives  53.6 us (22%)
  starting transfers between devices  36.1 us (15%)
  waiting for transfers between devices  28.8 us (12%)
  local copies, waits for them, and re-layouts  5.69 us (2%)
  other arithmetic  3.6 us (1%)
    pallas_call x1, Pallas kernels, attend_far(): pl.pallas_call(functools.partial(attend_kernel, FAR, True), out_shape=sha...  80.2 us
    all_to_all x1, blocking collectives, body(): lax.all_to_all(keys, 'tm', 0, 0, axis_index_groups=PLANES, tiled=True)  36 us
    ppermute x12, starting transfers between devices, moved(): return lax.ppermute(block, AXES, pairs)  30.7 us
    ppermute x12, waiting for transfers between devices, moved(): return lax.ppermute(block, AXES, pairs)  28.8 us
    pallas_call x1, Pallas kernels, attend_near(): pl.pallas_call(functools.partial(attend_kernel, NEAR, False), out_shape=[...  19.7 us
    all_to_all x1, blocking collectives, body(): answers = lax.all_to_all(answers, 'tm', 0, 0, tiled=True)  17.6 us
    pallas_call x2, Pallas kernels, project(): pl.pallas_call(project_kernel, out_shape=shape(Y, SPAN, wide), grid_spec=...  8.68 us
    all_to_all x1, starting transfers between devices, body(): pieces = lax.all_to_all(pieces, 'tm', 0, 0, tiled=True)  5.4 us
  transfers between devices with their start and end apart: 13, of which 3 were waited for; matrix products, arithmetic and copies ran while one was open for 1% of the time, Pallas kernels for 10%

profile of v4, /device:TPU:1, one launch (start us, length us, event | category | flops | bytes accessed | tf_op | source)
XLA Modules:
  0.0 240.2 jit_solution(4030111766565311814)
XLA Ops:
  3.7 1.6 pack.1
  5.2 36.0 %all_to_all.15 = bf16[8,256,256]{2,1,0:T(8,128)(2,1)S(1)} all-to-all(bf16[8,256,256]{2,1,0:T(8,128)(2,1)S(1)} %get-tuple-element.11), channel_id=1, replica_groups={{0,8,16,24,32,40,48,56},{64,72,80,88,96,104,112,120},{128,136,144,152,1..., dimensions={0} | all-to-all | bytes 2097152 | tf_op jit(solution)/shard_map/all_to_all | solution.py:375
  41.3 4.4 %collective-permute-start.2 = (bf16[1024,256]{1,0:T(8,128)(2,1)S(1)}, bf16[1024,256]{1,0:T(8,128)(2,1)S(1)}, u32[]{:S(2)}, u32[]{:S(2)}) collective-permute-start(bf16[1024,256]{1,0:T(8,128)(2,1)S(1)} %bitcast.29), channel_id=1, source_target_pairs={{0,192},{1,193},{2,194},{3,195},{4,196},{5,197},{6,198},{7,199},{8... | collective-permute-start | bytes 1572872 | tf_op jit(solution)/shard_map/ppermute | solution.py:57
  45.7 1.9 collective-permute-start.4
  47.6 5.4 %all-to-all-start = ((bf16[32,64,128]{2,1,0:T(8,128)(2,1)}), bf16[32,64,128]{2,1,0:T(8,128)(2,1)S(1)}, u32[]{:S(2)}, u32[]{:S(2)}) async-start(bf16[32,64,128]{2,1,0:T(8,128)(2,1)} %get-tuple-element.10), calls=%async_computation | async-start | bytes 1048576 | tf_op jit(solution)/shard_map/all_to_all | solution.py:376
  53.1 3.1 %collective-permute-start.6 = (bf16[1024,256]{1,0:T(8,128)(2,1)S(1)}, bf16[1024,256]{1,0:T(8,128)(2,1)S(1)}, u32[]{:S(2)}, u32[]{:S(2)}) collective-permute-start(bf16[1024,256]{1,0:T(8,128)(2,1)S(1)} %bitcast.30), channel_id=1, source_target_pairs={{0,64},{1,65},{2,66},{3,67},{4,68},{5,69},{6,70},{7,71},{8,72},{10... | collective-permute-start | bytes 1572872 | tf_op jit(solution)/shard_map/ppermute | solution.py:57
  56.2 3.4 %collective-permute-start.7 = (bf16[1024,256]{1,0:T(8,128)(2,1)S(1)}, bf16[1024,256]{1,0:T(8,128)(2,1)}, u32[]{:S(2)}, u32[]{:S(2)}) collective-permute-start(bf16[1024,256]{1,0:T(8,128)(2,1)S(1)} %bitcast.26), channel_id=1, source_target_pairs={{0,192},{1,193},{2,194},{3,195},{4,196},{5,197},{6,198},{7,199},{8... | collective-permute-start | bytes 1572872 | tf_op jit(solution)/shard_map/ppermute | solution.py:57
  59.6 3.2 %collective-permute-start.3 = (bf16[1024,256]{1,0:T(8,128)(2,1)S(1)}, bf16[1024,256]{1,0:T(8,128)(2,1)}, u32[]{:S(2)}, u32[]{:S(2)}) collective-permute-start(bf16[1024,256]{1,0:T(8,128)(2,1)S(1)} %collective-permute-done.2.refs_4_.refs_9_), channel_id=1, source_target_pairs={{0,192},{1,193},{2,194},{3,195},{4,196},{5,197},{6,198},{7,199},{8... | collective-permute-start | bytes 1572872 | tf_op jit(solution)/shard_map/ppermute | solution.py:57
  62.8 2.1 collective-permute-start.5
  65.6 14.6 %collective-permute-done.6.refs_2_.refs_7_ = bf16[1024,256]{1,0:T(8,128)(2,1)S(1)} collective-permute-done((bf16[1024,256]{1,0:T(8,128)(2,1)S(1)}, bf16[1024,256]{1,0:T(8,128)(2,1)S(1)}, u32[]{:S(2)}, u32[]{:S(2)}) %collective-permute-start.6) | collective-permute-done | bytes 524320 | tf_op jit(solution)/shard_map/ppermute | solution.py:57
  80.3 19.7 %near.1 = (f32[2048,128]{1,0:T(8,128)S(1)}, f32[2048,128]{1,0:T(8,128)S(1)}, f32[2048,128]{1,0:T(8,128)}) custom-call(s32[32]{0:T(128)S(1)} %dynamic-slice_bitcast_fusion.row_ref, s32[1]{0:T(128)S(6)} %copy.11.offset_ref, bf16[32,64,128]{2,1,0:T(8,128)(2,1)S(1)} %all-to-all-done.pieces_ref, bf16[1024,256]{1,0:T(8,128)(2,1)S(1)} %bitcast.31, ...), custom_call_target="tpu_custom_call" | custom-call | tf_op jit(solution)/shard_map/near/pallas_call | solution.py:274
  101.0 1.0 copy-done.2
  102.0 80.2 %far.1 = bf16[32,64,128]{2,1,0:T(8,128)(2,1)S(1)} custom-call(s32[32]{0:T(128)S(1)} %dynamic-slice_bitcast_fusion.row_ref, s32[1]{0:T(128)S(6)} %copy.11.offset_ref, bf16[32,64,128]{2,1,0:T(8,128)(2,1)S(1)} %all-to-all-done.pieces_ref, bf16[1024,256]{1,0:T(8,128)(2,1)} %collective-permute-done.3.refs_0_, bf16[1024,256]{1,0:T(8,128)(2,1)} %collective-permute-done.5.refs_1_, ...), custom_call_target="tpu_custom_call" | custom-call | tf_op jit(solution)/shard_map/far/pallas_call | solution.py:290
  182.1 17.6 %all_to_all.16.parts_ref = bf16[32,64,128]{2,1,0:T(8,128)(2,1)S(1)} all-to-all(bf16[32,64,128]{2,1,0:T(8,128)(2,1)S(1)} %far.1), channel_id=1, replica_groups=mesh['tm'=32,'head'=8] {'tm'}, dimensions={0} | all-to-all | bytes 1048576 | tf_op jit(solution)/shard_map/all_to_all | solution.py:392
  200.3 4.3 %project.3 = bf16[4,256,640]{2,1,0:T(8,128)(2,1)S(1)} custom-call(s32[32]{0:T(128)S(1)} %dynamic-slice_bitcast_fusion.row_ref, bf16[256,640]{1,0:T(8,128)(2,1)S(1)} %heads.1.rows_ref, bf16[640,5120]{1,0:T(8,128)(2,1)} %weight_ref.3), custom_call_target="tpu_custom_call" | custom-call | tf_op jit(solution)/shard_map/project/pallas_call | solution.py:343
  204.7 8.1 %collective-permute-start.8 = (bf16[4,256,640]{2,1,0:T(8,128)(2,1)S(1)}, bf16[4,256,640]{2,1,0:T(8,128)(2,1)S(1)}, u32[]{:S(2)}, u32[]{:S(2)}) collective-permute-start(bf16[4,256,640]{2,1,0:T(8,128)(2,1)S(1)} %project.3), channel_id=1, source_target_pairs={{0,1},{1,0},{2,3},{3,2},{4,5},{5,4},{6,7},{7,6},{8,9},{9,8},{10,11... | collective-permute-start | bytes 3932168 | tf_op jit(solution)/shard_map/ppermute | solution.py:57
  212.7 1.3 fusion.8
  214.7 4.3 %project.2 = bf16[4,256,640]{2,1,0:T(8,128)(2,1)S(1)} custom-call(s32[32]{0:T(128)S(1)} %dynamic-slice_bitcast_fusion.row_ref, bf16[256,640]{1,0:T(8,128)(2,1)S(1)} %heads.1.rows_ref, bf16[640,5120]{1,0:T(8,128)(2,1)} %weight_ref.3), custom_call_target="tpu_custom_call" | custom-call | tf_op jit(solution)/shard_map/project/pallas_call | solution.py:343
  219.3 1.4 collective-permute-start.10
  220.7 1.5 collective-permute-start.11
  222.2 1.6 collective-permute-start.9
  224.1 6.0 %collective-permute-done.10 = bf16[256,640]{1,0:T(8,128)(2,1)S(1)} collective-permute-done((bf16[256,640]{1,0:T(8,128)(2,1)S(1)}, bf16[256,640]{1,0:T(8,128)(2,1)S(1)}, u32[]{:S(2)}, u32[]{:S(2)}) %collective-permute-start.10) | collective-permute-done | bytes 327712 | tf_op jit(solution)/shard_map/ppermute | solution.py:57
  230.1 8.1 %collective-permute-done.9 = bf16[256,640]{1,0:T(8,128)(2,1)S(1)} collective-permute-done((bf16[256,640]{1,0:T(8,128)(2,1)S(1)}, bf16[256,640]{1,0:T(8,128)(2,1)S(1)}, u32[]{:S(2)}, u32[]{:S(2)}) %collective-permute-start.9) | collective-permute-done | bytes 327712 | tf_op jit(solution)/shard_map/ppermute | solution.py:57
  238.2 2.0 fusion.4
  (33 shorter events, 5.9 us)
Async XLA Ops:
  0.0 223.9 %copy-start = (bf16[256,640]{1,0:T(8,128)(2,1)S(1)}, bf16[256,640]{1,0:T(8,128)(2,1)}, u32[]{:S(2)}) copy-start(bf16[256,640]{1,0:T(8,128)(2,1)} %param.15) | copy-start | bytes 983044
  0.7 1.0 copy-start.3
  1.7 1.0 copy-start.4
  2.7 1.0 copy-start.5
  41.3 18.2 %collective-permute-start.2 = (bf16[1024,256]{1,0:T(8,128)(2,1)S(1)}, bf16[1024,256]{1,0:T(8,128)(2,1)S(1)}, u32[]{:S(2)}, u32[]{:S(2)}) collective-permute-start(bf16[1024,256]{1,0:T(8,128)(2,1)S(1)} %bitcast.29), channel_id=1, source_target_pairs={{0,192},{1,193},{2,194},{3,195},{4,196},{5,197},{6,198},{7,199},{8... | collective-permute-start | bytes 1572872 | tf_op jit(solution)/shard_map/ppermute | solution.py:57
  45.7 17.0 %collective-permute-start.4 = (bf16[1024,256]{1,0:T(8,128)(2,1)S(1)}, bf16[1024,256]{1,0:T(8,128)(2,1)S(1)}, u32[]{:S(2)}, u32[]{:S(2)}) collective-permute-start(bf16[1024,256]{1,0:T(8,128)(2,1)S(1)} %bitcast.25), channel_id=1, source_target_pairs={{0,64},{1,65},{2,66},{3,67},{4,68},{5,69},{6,70},{7,71},{8,72},{10... | collective-permute-start | bytes 1572872 | tf_op jit(solution)/shard_map/ppermute | solution.py:57
  47.6 32.6 %all-to-all-start = ((bf16[32,64,128]{2,1,0:T(8,128)(2,1)}), bf16[32,64,128]{2,1,0:T(8,128)(2,1)S(1)}, u32[]{:S(2)}, u32[]{:S(2)}) async-start(bf16[32,64,128]{2,1,0:T(8,128)(2,1)} %get-tuple-element.10), calls=%async_computation | async-start | bytes 1048576 | tf_op jit(solution)/shard_map/all_to_all | solution.py:376
  53.1 27.2 %collective-permute-start.6 = (bf16[1024,256]{1,0:T(8,128)(2,1)S(1)}, bf16[1024,256]{1,0:T(8,128)(2,1)S(1)}, u32[]{:S(2)}, u32[]{:S(2)}) collective-permute-start(bf16[1024,256]{1,0:T(8,128)(2,1)S(1)} %bitcast.30), channel_id=1, source_target_pairs={{0,64},{1,65},{2,66},{3,67},{4,68},{5,69},{6,70},{7,71},{8,72},{10... | collective-permute-start | bytes 1572872 | tf_op jit(solution)/shard_map/ppermute | solution.py:57
  56.2 24.1 %collective-permute-start.7 = (bf16[1024,256]{1,0:T(8,128)(2,1)S(1)}, bf16[1024,256]{1,0:T(8,128)(2,1)}, u32[]{:S(2)}, u32[]{:S(2)}) collective-permute-start(bf16[1024,256]{1,0:T(8,128)(2,1)S(1)} %bitcast.26), channel_id=1, source_target_pairs={{0,192},{1,193},{2,194},{3,195},{4,196},{5,197},{6,198},{7,199},{8... | collective-permute-start | bytes 1572872 | tf_op jit(solution)/shard_map/ppermute | solution.py:57
  59.6 42.4 %collective-permute-start.3 = (bf16[1024,256]{1,0:T(8,128)(2,1)S(1)}, bf16[1024,256]{1,0:T(8,128)(2,1)}, u32[]{:S(2)}, u32[]{:S(2)}) collective-permute-start(bf16[1024,256]{1,0:T(8,128)(2,1)S(1)} %collective-permute-done.2.refs_4_.refs_9_), channel_id=1, source_target_pairs={{0,192},{1,193},{2,194},{3,195},{4,196},{5,197},{6,198},{7,199},{8... | collective-permute-start | bytes 1572872 | tf_op jit(solution)/shard_map/ppermute | solution.py:57
  62.8 39.2 %collective-permute-start.5 = (bf16[1024,256]{1,0:T(8,128)(2,1)S(1)}, bf16[1024,256]{1,0:T(8,128)(2,1)}, u32[]{:S(2)}, u32[]{:S(2)}) collective-permute-start(bf16[1024,256]{1,0:T(8,128)(2,1)S(1)} %collective-permute-done.4.refs_3_.refs_8_), channel_id=1, source_target_pairs={{0,64},{1,65},{2,66},{3,67},{4,68},{5,69},{6,70},{7,71},{8,72},{10... | collective-permute-start | bytes 1572872 | tf_op jit(solution)/shard_map/ppermute | solution.py:57
  64.9 37.1 %collective-permute-start = (bf16[256,640]{1,0:T(8,128)(2,1)}, bf16[256,640]{1,0:T(8,128)(2,1)}, u32[]{:S(2)}, u32[]{:S(2)}) collective-permute-start(bf16[256,640]{1,0:T(8,128)(2,1)} %param.13), channel_id=1, source_target_pairs={{0,8},{1,9},{2,10},{3,11},{4,12},{5,13},{6,14},{7,15},{8,16},{9,17... | collective-permute-start | bytes 983048 | tf_op jit(solution)/shard_map/ppermute | solution.py:57
  80.3 21.7 %collective-permute-start.1 = (s32[1]{0:T(128)}, s32[1]{0:T(128)}, u32[]{:S(2)}, u32[]{:S(2)}) collective-permute-start(s32[1]{0:T(128)} %param.16), channel_id=1, source_target_pairs={{0,8},{1,9},{2,10},{3,11},{4,12},{5,13},{6,14},{7,15},{8,16},{9,17... | collective-permute-start | bytes 20 | tf_op jit(solution)/shard_map/ppermute | solution.py:57
  100.0 1.0 copy-start.1
  101.0 1.0 copy-start.2
  200.3 12.4 %copy-start.6 = (s32[50]{0:T(128)S(1)}, s32[50]{0:T(128)}, u32[]{:S(2)}) copy-start(s32[50]{0:T(128)} %param.17) | copy-start | bytes 604
  204.7 14.4 %collective-permute-start.8 = (bf16[4,256,640]{2,1,0:T(8,128)(2,1)S(1)}, bf16[4,256,640]{2,1,0:T(8,128)(2,1)S(1)}, u32[]{:S(2)}, u32[]{:S(2)}) collective-permute-start(bf16[4,256,640]{2,1,0:T(8,128)(2,1)S(1)} %project.3), channel_id=1, source_target_pairs={{0,1},{1,0},{2,3},{3,2},{4,5},{5,4},{6,7},{7,6},{8,9},{9,8},{10,11... | collective-permute-start | bytes 3932168 | tf_op jit(solution)/shard_map/ppermute | solution.py:57
  219.3 10.8 %collective-permute-start.10 = (bf16[256,640]{1,0:T(8,128)(2,1)S(1)}, bf16[256,640]{1,0:T(8,128)(2,1)S(1)}, u32[]{:S(2)}, u32[]{:S(2)}) collective-permute-start(bf16[256,640]{1,0:T(8,128)(2,1)S(1)} %get-tuple-element.17), channel_id=1, source_target_pairs={{0,2},{1,3},{2,4},{3,5},{4,6},{5,7},{6,0},{7,1},{8,10},{9,11},{10,... | collective-permute-start | bytes 983048 | tf_op jit(solution)/shard_map/ppermute | solution.py:57
  220.7 9.4 %collective-permute-start.11 = (bf16[256,640]{1,0:T(8,128)(2,1)S(1)}, bf16[256,640]{1,0:T(8,128)(2,1)S(1)}, u32[]{:S(2)}, u32[]{:S(2)}) collective-permute-start(bf16[256,640]{1,0:T(8,128)(2,1)S(1)} %get-tuple-element.16), channel_id=1, source_target_pairs={{0,6},{1,7},{2,0},{3,1},{4,2},{5,3},{6,4},{7,5},{8,14},{9,15},{10,... | collective-permute-start | bytes 983048 | tf_op jit(solution)/shard_map/ppermute | solution.py:57
  222.2 16.0 %collective-permute-start.9 = (bf16[256,640]{1,0:T(8,128)(2,1)S(1)}, bf16[256,640]{1,0:T(8,128)(2,1)S(1)}, u32[]{:S(2)}, u32[]{:S(2)}) collective-permute-start(bf16[256,640]{1,0:T(8,128)(2,1)S(1)} %get-tuple-element.15), channel_id=1, source_target_pairs={{0,4},{1,5},{2,6},{3,7},{4,0},{5,1},{6,2},{7,3},{8,12},{9,13},{10,... | collective-permute-start | bytes 983048 | tf_op jit(solution)/shard_map/ppermute | solution.py:57

commit v5 on v4

--- a/solution.py
+++ b/solution.py
@@ -19,6 +19,7 @@
 VMEM_LIMIT = 48 * 1024 * 1024
 
 HOST = ((0, 1, 3, 4, 6), (0, 2, 4, 5, 7))
+SHIFTS = (0, 4, 1, 7, 3, 5, 2, 6)
 AXES = ("tm", "head")
 PIECE = SPAN // X
 
@@ -28,15 +29,22 @@
 
 
 ALL = [(x, z, y, c) for x in range(X) for z in range(Z) for y in range(Y) for c in range(C)]
-PLANES = [[x * Z + z for z in range(Z)] for x in range(X)]
+
+
+def plane_pairs(shift):
+    return [
+        (device(x, z, y, c), device(x, z + shift, y, c))
+        for x, z, y, c in ALL
+        if (z + shift) % Z in HOST[c]
+    ]
 
 
 def across_pairs(m):
     return [(device(x, z, y, c), device(x + m, z, y, c)) for x, z, y, c in ALL if z in HOST[c]]
 
 
-HEAD, PLANE, ACTIVE, PLACE_X, PLACE_Y, CORE = 0, 8, 13, 14, 15, 16
-WIDTH = 32
+HEAD, PLANE, ACTIVE, PLACE_X, PLACE_Y, CORE, SEND, FROM = 0, 8, 13, 14, 15, 16, 17, 25
+WIDTH = 64
 
 
 def table():
@@ -50,6 +58,9 @@
         row[PLACE_X] = x
         row[PLACE_Y] = y
         row[CORE] = c
+        for i, shift in enumerate(SHIFTS):
+            row[SEND + i] = row[HEAD + (z + shift) % Z]
+            row[FROM + i] = (z - shift) % Z
     return rows
 
 
@@ -73,28 +84,37 @@
     return jax.ShapeDtypeStruct(dims, dtype)
 
 
-def pack_kernel(row_ref, query_ref, key_ref, value_ref, keys_ref, pieces_ref):
-    for z in range(Z):
-        head = row_ref[HEAD + z]
+def pack_kernel(row_ref, query_ref, key_ref, value_ref, *outs):
+    pieces_ref = outs[-1]
+    for i in range(Z):
+        head = row_ref[SEND + i]
 
         @pl.when(head >= 0)
         def _():
             columns = pl.ds(pl.multiple_of(head * HEAD_DIM, HEAD_DIM), HEAD_DIM)
-            keys_ref[z, :, :HEAD_DIM] = key_ref[:, columns]
-            keys_ref[z, :, HEAD_DIM:] = value_ref[:, columns]
+            outs[i][:, :HEAD_DIM] = key_ref[:, columns]
+            outs[i][:, HEAD_DIM:] = value_ref[:, columns]
+
+    for z in range(Z):
+        head = row_ref[HEAD + z]
+
+        @pl.when(head >= 0)
+        def _():
+            columns = pl.ds(pl.multiple_of(head * HEAD_DIM, HEAD_DIM), HEAD_DIM)
             for x in range(X):
                 pieces_ref[x * Z + z] = query_ref[x * PIECE : (x + 1) * PIECE, columns]
 
 
 def pack(row, query_rows, key_rows, value_rows):
-    return pl.pallas_call(
+    outs = pl.pallas_call(
         pack_kernel,
-        out_shape=[shape(Z, SPAN, 2 * HEAD_DIM), shape(SPANS, PIECE, HEAD_DIM)],
+        out_shape=[shape(SPAN, 2 * HEAD_DIM)] * Z + [shape(SPANS, PIECE, HEAD_DIM)],
         in_specs=[in_smem(), in_vmem(), in_vmem(), in_vmem()],
-        out_specs=[in_vmem()] * 2,
+        out_specs=[in_vmem()] * (Z + 1),
         compiler_params=pltpu.CompilerParams(vmem_limit_bytes=VMEM_LIMIT),
         name="pack",
     )(row, query_rows, key_rows, value_rows)
+    return outs[:Z], outs[Z]
 
 
 STEP = Z // 2
@@ -112,24 +132,20 @@
     if ends:
         (total_in, summed_in, shift_ref), refs = refs[:3], refs[3:]
         later_steps, refs = refs[: STEPS - len(places)], refs[STEPS - len(places) :]
-        refs = refs[len(refs) - 6 :]
-        out_ref, held, rows, total_ref, summed_ref, copied = refs
+        refs = refs[len(refs) - 7 :]
+        out_ref, held, rows, total_ref, summed_ref, keys_at, copied = refs
     else:
-        total_ref, summed_ref, shift_ref, held, rows, copied = refs
+        total_ref, summed_ref, shift_ref, held, rows, keys_at, copied = refs
     offset = offset_ref[0]
 
     def place_of(span):
         return lax.rem(span - offset + SPANS, SPANS)
 
-    def first_place(at):
-        m, half = at
-        return place_of(lax.rem(row_ref[PLACE_X] - m + X, X) * Z + half * STEP)
-
-    def pick(values, i):
-        found = values[0]
-        for n, value in enumerate(values[1:], 1):
-            found = jnp.where(i == n, value, found)
-        return found
+    def note_places(first, found):
+        for i, (m, half) in enumerate(found):
+            from_x = lax.rem(row_ref[PLACE_X] - m + X, X)
+            for u in range(STEP):
+                keys_at[first + i, u] = place_of(from_x * Z + row_ref[FROM + half * STEP + u])
 
     def scores_of(query, keys):
         return lax.dot_general(
@@ -153,14 +169,14 @@
             lax.broadcasted_iota(jnp.int32, (TILE_ROWS, 1), 0), jnp.int32(PIECE)
         )
 
-    def running(tile, firsts):
+    def running(tile):
         query, own = rows[tile_rows(tile), :], row_places(tile)
 
         def step(t, carry):
             top, total, summed = carry
             key_rows = pl.ds(pl.multiple_of(lax.rem(t, STEP) * SPAN, SPAN), SPAN)
             at = lax.div(t, STEP)
-            seen = own >= lax.rem(pick(firsts, at) + lax.rem(t, STEP), SPANS)
+            seen = own >= keys_at[at, lax.rem(t, STEP)]
             scores = jnp.where(seen, scores_of(query, held[at, key_rows, :HEAD_DIM]), NEGATIVE)
             top_new = jnp.maximum(top, jnp.max(scores, axis=1, keepdims=True))
             weights = jnp.where(seen, jnp.exp2((scores - top_new) * SCALE), 0.0)
@@ -185,7 +201,7 @@
         for span in range(SPANS):
             at = pl.ds(pl.multiple_of(place_of(span) * PIECE, PIECE), PIECE)
             rows[at, :] = pieces_ref[span]
-        firsts = [first_place(at) for at in places]
+        note_places(0, places)
         if ends:
             total_ref[...] = total_in[...]
             summed_ref[...] = summed_in[...]
@@ -203,7 +219,7 @@
                 )
                 shift_ref[at, :] = jnp.broadcast_to(top * SCALE, (TILE_ROWS, HEAD_DIM))
 
-        def add(tile, i, masked, first):
+        def add(tile, i, masked):
             at = tile_rows(tile)
             scores = scores_of(rows[at, :], held[i, :, :HEAD_DIM])
             shift = shift_ref[at, :1]
@@ -211,7 +227,7 @@
                 own = row_places(tile)
                 weights = []
                 for u in range(STEP):
-                    hidden = own < lax.rem(first + u, SPANS)
+                    hidden = own < keys_at[i, u]
                     part = scores[:, u * SPAN : (u + 1) * SPAN] * SCALE
                     weights.append(jnp.exp2(part - jnp.where(hidden, LARGEST, shift)))
                 weights = jnp.concatenate(weights, axis=1)
@@ -222,19 +238,18 @@
 
         def one(n, unused):
             tile, i = lax.div(n, steps), lax.rem(n, steps)
-            first = pick(firsts, i)
-            wraps = first > SPANS - STEP
-            lowest = jnp.where(wraps, 0, first)
-            highest = jnp.where(wraps, SPANS - 1, first + STEP - 1)
+            found = [keys_at[i, u] for u in range(STEP)]
+            lowest = functools.reduce(jnp.minimum, found)
+            highest = functools.reduce(jnp.maximum, found)
             whole = highest <= tile * TILE
 
             @pl.when(whole)
             def _():
-                add(tile, i, False, first)
+                add(tile, i, False)
 
             @pl.when(jnp.logical_not(whole) & (lowest < (tile + 1) * TILE))
             def _():
-                add(tile, i, True, first)
+                add(tile, i, True)
 
             return unused
 
@@ -260,9 +275,9 @@
                     pltpu.make_async_copy(source, held.at[steps + i], copied).start()
                 brought = held.at[pl.ds(steps, STEPS - steps)]
                 pltpu.make_async_copy(brought, brought, copied).wait()
-                all_firsts = firsts + [first_place(at) for at in NEAR]
+                note_places(steps, NEAR)
                 for tile in range(TILES):
-                    put(tile, running(tile, all_firsts))
+                    put(tile, running(tile))
 
 
 NEAR = ((0, 0), (0, 1), (1, 0), (1, 1), (3, 0), (3, 1))
@@ -279,6 +294,7 @@
         scratch_shapes=[
             pltpu.VMEM((len(near), STEP_KEYS, 2 * HEAD_DIM), jnp.bfloat16),
             pltpu.VMEM((ROWS, HEAD_DIM), jnp.bfloat16),
+            pltpu.SMEM((STEPS, STEP), jnp.int32),
             pltpu.SemaphoreType.DMA,
         ],
         compiler_params=pltpu.CompilerParams(vmem_limit_bytes=VMEM_LIMIT),
@@ -300,6 +316,7 @@
             pltpu.VMEM((ROWS, HEAD_DIM), jnp.bfloat16),
             pltpu.VMEM((ROWS, HEAD_DIM), jnp.float32),
             pltpu.VMEM((ROWS, HEAD_DIM), jnp.float32),
+            pltpu.SMEM((STEPS, STEP), jnp.int32),
             pltpu.SemaphoreType.DMA,
         ],
         compiler_params=pltpu.CompilerParams(vmem_limit_bytes=VMEM_LIMIT),
@@ -370,12 +387,14 @@
 ):
     me = lax.axis_index("tm") * (Y * C) + lax.axis_index("head")
     row = lax.dynamic_slice(jnp.asarray(table()), (me, 0), (1, WIDTH))[0]
-    keys, pieces = pack(row, query_rows, key_rows, value_rows)
-
-    keys = lax.all_to_all(keys, "tm", 0, 0, axis_index_groups=PLANES, tiled=True)
+    packed, pieces = pack(row, query_rows, key_rows, value_rows)
+
+    arrived = [
+        moved(part, plane_pairs(shift)) if shift else part for part, shift in zip(packed, SHIFTS)
+    ]
     pieces = lax.all_to_all(pieces, "tm", 0, 0, tiled=True)
 
-    own = [keys[half * STEP : (half + 1) * STEP].reshape(STEP_KEYS, -1) for half in range(2)]
+    own = [jnp.concatenate(arrived[half * STEP : (half + 1) * STEP]) for half in range(2)]
     back = [moved(part, across_pairs(1)) for part in own]
     ahead = [moved(part, across_pairs(-1)) for part in own]
     far = [moved(ahead[0], across_pairs(-1)), moved(back[1], across_pairs(1))]

time: 241 us -> 234 us (0.971)
  blocking collectives: 53.6 us -> 15 us
  starting transfers between devices: 36.1 us -> 71.2 us
  waiting for transfers between devices: 28.8 us -> 23.1 us
    all_to_all x1 -> x0, blocking collectives: 36 us -> none  [body(): lax.all_to_all(keys, 'tm', 0, 0, axis_index_groups=PLANES, tiled=True)]
    ppermute x12 -> x19, starting transfers between devices: 30.7 us -> 66.5 us  [moved(): return lax.ppermute(block, AXES, pairs)]
    ppermute x12 -> x19, waiting for transfers between devices: 28.8 us -> 23.1 us  [moved(): return lax.ppermute(block, AXES, pairs)]
    pallas_call x1, Pallas kernels: 80.2 us -> 83.4 us  [attend_far(): pl.pallas_call(functools.partial(attend_kernel, FAR, True), out_shape=sha...]
    all_to_all x1, blocking collectives: 17.6 us -> 15 us  [body(): answers = lax.all_to_all(answers, 'tm', 0, 0, tiled=True)]
    unnamed x14 -> x26, local copies, waits for them, and re-layouts: 4.88 us -> 6.78 us
  transfers between devices with their start and end apart: 13 -> 20, of which waited for: 3 -> 4; matrix products, arithmetic and copies ran while one was open for 1% -> 1% of each run, Pallas kernels for 10% -> 10%
where the time goes in v5:
time: 234 us
  Pallas kernels  112 us (48%)
  starting transfers between devices  71.2 us (30%)
  waiting for transfers between devices  23.1 us (10%)
  blocking collectives  15 us (6%)
  local copies, waits for them, and re-layouts  7.54 us (3%)
  other arithmetic  3.55 us (2%)
    pallas_call x1, Pallas kernels, attend_far(): pl.pallas_call(functools.partial(attend_kernel, FAR, True), out_shape=sha...  83.4 us
    ppermute x19, starting transfers between devices, moved(): return lax.ppermute(block, AXES, pairs)  66.5 us
    ppermute x19, waiting for transfers between devices, moved(): return lax.ppermute(block, AXES, pairs)  23.1 us
    pallas_call x1, Pallas kernels, attend_near(): pl.pallas_call(functools.partial(attend_kernel, NEAR, False), out_shape=[...  17.9 us
    all_to_all x1, blocking collectives, body(): answers = lax.all_to_all(answers, 'tm', 0, 0, tiled=True)  15 us
    pallas_call x2, Pallas kernels, project(): pl.pallas_call(project_kernel, out_shape=shape(Y, SPAN, wide), grid_spec=...  8.69 us
    unnamed x26, local copies, waits for them, and re-layouts  6.78 us
    all_to_all x1, starting transfers between devices, body(): pieces = lax.all_to_all(pieces, 'tm', 0, 0, tiled=True)  4.68 us
  transfers between devices with their start and end apart: 20, of which 4 were waited for; matrix products, arithmetic and copies ran while one was open for 1% of the time, Pallas kernels for 10%

profile of v5, /device:TPU:1, one launch (start us, length us, event | category | flops | bytes accessed | tf_op | source)
XLA Modules:
  0.0 234.4 jit_solution(13277217692669450931)
XLA Ops:
  3.7 1.6 pack.1
  6.6 9.8 %collective-permute-start.8 = (bf16[256,256]{1,0:T(8,128)(2,1)S(1)}, bf16[256,256]{1,0:T(8,128)(2,1)S(1)}, u32[]{:S(2)}, u32[]{:S(2)}) collective-permute-start(bf16[256,256]{1,0:T(8,128)(2,1)S(1)} %get-tuple-element.23), channel_id=1, source_target_pairs={{1,41},{3,43},{5,45},{7,47},{8,48},{10,50},{12,52},{14,54},{17,57}... | collective-permute-start | bytes 393224 | tf_op jit(solution)/shard_map/ppermute | solution.py:68
  16.4 3.1 %collective-permute-start.9 = (bf16[256,256]{1,0:T(8,128)(2,1)S(1)}, bf16[256,256]{1,0:T(8,128)(2,1)S(1)}, u32[]{:S(2)}, u32[]{:S(2)}) collective-permute-start(bf16[256,256]{1,0:T(8,128)(2,1)S(1)} %get-tuple-element.24), channel_id=1, source_target_pairs={{1,17},{3,19},{5,21},{7,23},{8,24},{10,26},{12,28},{14,30},{16,32}... | collective-permute-start | bytes 393224 | tf_op jit(solution)/shard_map/ppermute | solution.py:68
  20.8 6.4 %collective-permute-start.2 = (bf16[256,256]{1,0:T(8,128)(2,1)S(1)}, bf16[256,256]{1,0:T(8,128)(2,1)S(1)}, u32[]{:S(2)}, u32[]{:S(2)}) collective-permute-start(bf16[256,256]{1,0:T(8,128)(2,1)S(1)} %get-tuple-element.19), channel_id=1, source_target_pairs={{0,32},{1,33},{2,34},{3,35},{4,36},{5,37},{6,38},{7,39},{9,41},{11... | collective-permute-start | bytes 393224 | tf_op jit(solution)/shard_map/ppermute | solution.py:68
  28.6 5.2 %collective-permute-start.4 = (bf16[256,256]{1,0:T(8,128)(2,1)S(1)}, bf16[256,256]{1,0:T(8,128)(2,1)S(1)}, u32[]{:S(2)}, u32[]{:S(2)}) collective-permute-start(bf16[256,256]{1,0:T(8,128)(2,1)S(1)} %get-tuple-element.21), channel_id=1, source_target_pairs={{1,57},{3,59},{5,61},{7,63},{8,0},{9,1},{10,2},{11,3},{12,4},{13,5... | collective-permute-start | bytes 393224 | tf_op jit(solution)/shard_map/ppermute | solution.py:68
  33.9 3.1 %collective-permute-start.11 = (bf16[1024,256]{1,0:T(8,128)(2,1)S(1)}, bf16[1024,256]{1,0:T(8,128)(2,1)S(1)}, u32[]{:S(2)}, u32[]{:S(2)}) collective-permute-start(bf16[1024,256]{1,0:T(8,128)(2,1)S(1)} %constant_dynamic-update-slice_fusion.4.refs_1_.refs_6_), channel_id=1, source_target_pairs={{0,64},{1,65},{2,66},{3,67},{4,68},{5,69},{6,70},{7,71},{8,72},{10... | collective-permute-start | bytes 1572872 | tf_op jit(solution)/shard_map/ppermute | solution.py:68
  37.1 3.4 %collective-permute-start.5 = (bf16[1024,256]{1,0:T(8,128)(2,1)S(1)}, bf16[1024,256]{1,0:T(8,128)(2,1)S(1)}, u32[]{:S(2)}, u32[]{:S(2)}) collective-permute-start(bf16[1024,256]{1,0:T(8,128)(2,1)S(1)} %constant_dynamic-update-slice_fusion.refs_0_.refs_5_), channel_id=1, source_target_pairs={{0,192},{1,193},{2,194},{3,195},{4,196},{5,197},{6,198},{7,199},{8... | collective-permute-start | bytes 1572872 | tf_op jit(solution)/shard_map/ppermute | solution.py:68
  40.5 4.7 %all-to-all-start = ((bf16[32,64,128]{2,1,0:T(8,128)(2,1)}), bf16[32,64,128]{2,1,0:T(8,128)(2,1)S(1)}, u32[]{:S(2)}, u32[]{:S(2)}) async-start(bf16[32,64,128]{2,1,0:T(8,128)(2,1)} %get-tuple-element.17), calls=%async_computation | async-start | bytes 1048576 | tf_op jit(solution)/shard_map/all_to_all | solution.py:395
  45.1 4.4 %collective-permute-start.14 = (bf16[1024,256]{1,0:T(8,128)(2,1)S(1)}, bf16[1024,256]{1,0:T(8,128)(2,1)S(1)}, u32[]{:S(2)}, u32[]{:S(2)}) collective-permute-start(bf16[1024,256]{1,0:T(8,128)(2,1)S(1)} %constant_dynamic-update-slice_fusion.4.refs_1_.refs_6_), channel_id=1, source_target_pairs={{0,192},{1,193},{2,194},{3,195},{4,196},{5,197},{6,198},{7,199},{8... | collective-permute-start | bytes 1572872 | tf_op jit(solution)/shard_map/ppermute | solution.py:68
  49.5 1.9 collective-permute-start.13
  51.5 2.1 collective-permute-start.12
  53.6 4.4 %collective-permute-start.6 = (bf16[1024,256]{1,0:T(8,128)(2,1)S(1)}, bf16[1024,256]{1,0:T(8,128)(2,1)}, u32[]{:S(2)}, u32[]{:S(2)}) collective-permute-start(bf16[1024,256]{1,0:T(8,128)(2,1)S(1)} %collective-permute-done.5.refs_4_.refs_9_), channel_id=1, source_target_pairs={{0,192},{1,193},{2,194},{3,195},{4,196},{5,197},{6,198},{7,199},{8... | collective-permute-start | bytes 1572872 | tf_op jit(solution)/shard_map/ppermute | solution.py:68
  58.7 9.2 %collective-permute-done.14.refs_5_.refs_10_ = bf16[1024,256]{1,0:T(8,128)(2,1)S(1)} collective-permute-done((bf16[1024,256]{1,0:T(8,128)(2,1)S(1)}, bf16[1024,256]{1,0:T(8,128)(2,1)S(1)}, u32[]{:S(2)}, u32[]{:S(2)}) %collective-permute-start.14) | collective-permute-done | bytes 524320 | tf_op jit(solution)/shard_map/ppermute | solution.py:68
  71.3 17.9 %near.1 = (f32[2048,128]{1,0:T(8,128)S(1)}, f32[2048,128]{1,0:T(8,128)S(1)}, f32[2048,128]{1,0:T(8,128)}) custom-call(s32[64]{0:T(128)S(1)} %dynamic-slice_bitcast_fusion.row_ref, s32[1]{0:T(128)S(6)} %copy.17.offset_ref, bf16[32,64,128]{2,1,0:T(8,128)(2,1)S(1)} %all-to-all-done.pieces_ref, ...), custom_call_target="tpu_custom_call" | custom-call | tf_op jit(solution)/shard_map/near/pallas_call | solution.py:289
  91.3 83.4 %far.1 = bf16[32,64,128]{2,1,0:T(8,128)(2,1)S(1)} custom-call(s32[64]{0:T(128)S(1)} %dynamic-slice_bitcast_fusion.row_ref, s32[1]{0:T(128)S(6)} %copy.17.offset_ref, bf16[32,64,128]{2,1,0:T(8,128)(2,1)S(1)} %all-to-all-done.pieces_ref, bf16[1024,256]{1,0:T(8,128)(2,1)} %collective-permute-done.6.refs_0_, bf16[1024,256]{1,0:T(8,128)(2,1)} %collective-permute-done.12.refs_1_, ...), custom_call_target="tpu_custom_call" | custom-call | tf_op jit(solution)/shard_map/far/pallas_call | solution.py:306
  174.6 15.0 %all_to_all.10.parts_ref = bf16[32,64,128]{2,1,0:T(8,128)(2,1)S(1)} all-to-all(bf16[32,64,128]{2,1,0:T(8,128)(2,1)S(1)} %far.1), channel_id=1, replica_groups=mesh['tm'=32,'head'=8] {'tm'}, dimensions={0} | all-to-all | bytes 1048576 | tf_op jit(solution)/shard_map/all_to_all | solution.py:411
  190.2 4.3 %project.3 = bf16[4,256,640]{2,1,0:T(8,128)(2,1)S(1)} custom-call(s32[64]{0:T(128)S(1)} %dynamic-slice_bitcast_fusion.row_ref, bf16[256,640]{1,0:T(8,128)(2,1)S(1)} %heads.1.rows_ref, bf16[640,5120]{1,0:T(8,128)(2,1)} %weight_ref.3), custom_call_target="tpu_custom_call" | custom-call | tf_op jit(solution)/shard_map/project/pallas_call | solution.py:360
  194.6 13.0 %collective-permute-start.15 = (bf16[4,256,640]{2,1,0:T(8,128)(2,1)S(1)}, bf16[4,256,640]{2,1,0:T(8,128)(2,1)S(1)}, u32[]{:S(2)}, u32[]{:S(2)}) collective-permute-start(bf16[4,256,640]{2,1,0:T(8,128)(2,1)S(1)} %project.3), channel_id=1, source_target_pairs={{0,1},{1,0},{2,3},{3,2},{4,5},{5,4},{6,7},{7,6},{8,9},{9,8},{10,11... | collective-permute-start | bytes 3932168 | tf_op jit(solution)/shard_map/ppermute | solution.py:68
  209.5 4.3 %project.2 = bf16[4,256,640]{2,1,0:T(8,128)(2,1)S(1)} custom-call(s32[64]{0:T(128)S(1)} %dynamic-slice_bitcast_fusion.row_ref, bf16[256,640]{1,0:T(8,128)(2,1)S(1)} %heads.1.rows_ref, bf16[640,5120]{1,0:T(8,128)(2,1)} %weight_ref.3), custom_call_target="tpu_custom_call" | custom-call | tf_op jit(solution)/shard_map/project/pallas_call | solution.py:360
  214.1 3.0 %collective-permute-start.16 = (bf16[256,640]{1,0:T(8,128)(2,1)S(1)}, bf16[256,640]{1,0:T(8,128)(2,1)S(1)}, u32[]{:S(2)}, u32[]{:S(2)}) collective-permute-start(bf16[256,640]{1,0:T(8,128)(2,1)S(1)} %get-tuple-element.29), channel_id=1, source_target_pairs={{0,4},{1,5},{2,6},{3,7},{4,0},{5,1},{6,2},{7,3},{8,12},{9,13},{10,... | collective-permute-start | bytes 983048 | tf_op jit(solution)/shard_map/ppermute | solution.py:68
  217.5 2.3 collective-permute-start.18
  220.1 5.0 %collective-permute-done.16 = bf16[256,640]{1,0:T(8,128)(2,1)S(1)} collective-permute-done((bf16[256,640]{1,0:T(8,128)(2,1)S(1)}, bf16[256,640]{1,0:T(8,128)(2,1)S(1)}, u32[]{:S(2)}, u32[]{:S(2)}) %collective-permute-start.16) | collective-permute-done | bytes 327712 | tf_op jit(solution)/shard_map/ppermute | solution.py:68
  225.1 7.3 %collective-permute-done.17 = bf16[256,640]{1,0:T(8,128)(2,1)S(1)} collective-permute-done((bf16[256,640]{1,0:T(8,128)(2,1)S(1)}, bf16[256,640]{1,0:T(8,128)(2,1)S(1)}, u32[]{:S(2)}, u32[]{:S(2)}) %collective-permute-start.17) | collective-permute-done | bytes 327712 | tf_op jit(solution)/shard_map/ppermute | solution.py:68
  232.4 2.0 fusion.4
  (59 shorter events, 15.8 us)
Async XLA Ops:
  0.0 219.9 %copy-start = (bf16[256,640]{1,0:T(8,128)(2,1)S(1)}, bf16[256,640]{1,0:T(8,128)(2,1)}, u32[]{:S(2)}) copy-start(bf16[256,640]{1,0:T(8,128)(2,1)} %param.15) | copy-start | bytes 983044
  5.3 21.9 %collective-permute-start.7 = (bf16[256,256]{1,0:T(8,128)(2,1)S(1)}, bf16[256,256]{1,0:T(8,128)(2,1)S(1)}, u32[]{:S(2)}, u32[]{:S(2)}) collective-permute-start(bf16[256,256]{1,0:T(8,128)(2,1)S(1)} %get-tuple-element.22), channel_id=1, source_target_pairs={{0,24},{2,26},{4,28},{6,30},{8,32},{9,33},{10,34},{11,35},{12,36},... | collective-permute-start | bytes 393224 | tf_op jit(solution)/shard_map/ppermute | solution.py:68
  6.6 22.0 %collective-permute-start.8 = (bf16[256,256]{1,0:T(8,128)(2,1)S(1)}, bf16[256,256]{1,0:T(8,128)(2,1)S(1)}, u32[]{:S(2)}, u32[]{:S(2)}) collective-permute-start(bf16[256,256]{1,0:T(8,128)(2,1)S(1)} %get-tuple-element.23), channel_id=1, source_target_pairs={{1,41},{3,43},{5,45},{7,47},{8,48},{10,50},{12,52},{14,54},{17,57}... | collective-permute-start | bytes 393224 | tf_op jit(solution)/shard_map/ppermute | solution.py:68
  16.4 17.4 %collective-permute-start.9 = (bf16[256,256]{1,0:T(8,128)(2,1)S(1)}, bf16[256,256]{1,0:T(8,128)(2,1)S(1)}, u32[]{:S(2)}, u32[]{:S(2)}) collective-permute-start(bf16[256,256]{1,0:T(8,128)(2,1)S(1)} %get-tuple-element.24), channel_id=1, source_target_pairs={{1,17},{3,19},{5,21},{7,23},{8,24},{10,26},{12,28},{14,30},{16,32}... | collective-permute-start | bytes 393224 | tf_op jit(solution)/shard_map/ppermute | solution.py:68
  19.5 14.3 %collective-permute-start.10 = (bf16[256,256]{1,0:T(8,128)(2,1)S(1)}, bf16[256,256]{1,0:T(8,128)(2,1)S(1)}, u32[]{:S(2)}, u32[]{:S(2)}) collective-permute-start(bf16[256,256]{1,0:T(8,128)(2,1)S(1)} %get-tuple-element.25), channel_id=1, source_target_pairs={{0,48},{2,50},{4,52},{6,54},{9,57},{11,59},{13,61},{15,63},{16,0},... | collective-permute-start | bytes 393224 | tf_op jit(solution)/shard_map/ppermute | solution.py:68
  20.8 16.2 %collective-permute-start.2 = (bf16[256,256]{1,0:T(8,128)(2,1)S(1)}, bf16[256,256]{1,0:T(8,128)(2,1)S(1)}, u32[]{:S(2)}, u32[]{:S(2)}) collective-permute-start(bf16[256,256]{1,0:T(8,128)(2,1)S(1)} %get-tuple-element.19), channel_id=1, source_target_pairs={{0,32},{1,33},{2,34},{3,35},{4,36},{5,37},{6,38},{7,39},{9,41},{11... | collective-permute-start | bytes 393224 | tf_op jit(solution)/shard_map/ppermute | solution.py:68
  27.2 9.8 %collective-permute-start.3 = (bf16[256,256]{1,0:T(8,128)(2,1)S(1)}, bf16[256,256]{1,0:T(8,128)(2,1)S(1)}, u32[]{:S(2)}, u32[]{:S(2)}) collective-permute-start(bf16[256,256]{1,0:T(8,128)(2,1)S(1)} %get-tuple-element.20), channel_id=1, source_target_pairs={{0,8},{2,10},{4,12},{6,14},{9,17},{11,19},{13,21},{15,23},{16,24},... | collective-permute-start | bytes 393224 | tf_op jit(solution)/shard_map/ppermute | solution.py:68
  28.6 8.5 %collective-permute-start.4 = (bf16[256,256]{1,0:T(8,128)(2,1)S(1)}, bf16[256,256]{1,0:T(8,128)(2,1)S(1)}, u32[]{:S(2)}, u32[]{:S(2)}) collective-permute-start(bf16[256,256]{1,0:T(8,128)(2,1)S(1)} %get-tuple-element.21), channel_id=1, source_target_pairs={{1,57},{3,59},{5,61},{7,63},{8,0},{9,1},{10,2},{11,3},{12,4},{13,5... | collective-permute-start | bytes 393224 | tf_op jit(solution)/shard_map/ppermute | solution.py:68
  33.9 17.6 %collective-permute-start.11 = (bf16[1024,256]{1,0:T(8,128)(2,1)S(1)}, bf16[1024,256]{1,0:T(8,128)(2,1)S(1)}, u32[]{:S(2)}, u32[]{:S(2)}) collective-permute-start(bf16[1024,256]{1,0:T(8,128)(2,1)S(1)} %constant_dynamic-update-slice_fusion.4.refs_1_.refs_6_), channel_id=1, source_target_pairs={{0,64},{1,65},{2,66},{3,67},{4,68},{5,69},{6,70},{7,71},{8,72},{10... | collective-permute-start | bytes 1572872 | tf_op jit(solution)/shard_map/ppermute | solution.py:68
  37.1 16.5 %collective-permute-start.5 = (bf16[1024,256]{1,0:T(8,128)(2,1)S(1)}, bf16[1024,256]{1,0:T(8,128)(2,1)S(1)}, u32[]{:S(2)}, u32[]{:S(2)}) collective-permute-start(bf16[1024,256]{1,0:T(8,128)(2,1)S(1)} %constant_dynamic-update-slice_fusion.refs_0_.refs_5_), channel_id=1, source_target_pairs={{0,192},{1,193},{2,194},{3,195},{4,196},{5,197},{6,198},{7,199},{8... | collective-permute-start | bytes 1572872 | tf_op jit(solution)/shard_map/ppermute | solution.py:68
  40.5 29.8 %all-to-all-start = ((bf16[32,64,128]{2,1,0:T(8,128)(2,1)}), bf16[32,64,128]{2,1,0:T(8,128)(2,1)S(1)}, u32[]{:S(2)}, u32[]{:S(2)}) async-start(bf16[32,64,128]{2,1,0:T(8,128)(2,1)} %get-tuple-element.17), calls=%async_computation | async-start | bytes 1048576 | tf_op jit(solution)/shard_map/all_to_all | solution.py:395
  45.1 22.9 %collective-permute-start.14 = (bf16[1024,256]{1,0:T(8,128)(2,1)S(1)}, bf16[1024,256]{1,0:T(8,128)(2,1)S(1)}, u32[]{:S(2)}, u32[]{:S(2)}) collective-permute-start(bf16[1024,256]{1,0:T(8,128)(2,1)S(1)} %constant_dynamic-update-slice_fusion.4.refs_1_.refs_6_), channel_id=1, source_target_pairs={{0,192},{1,193},{2,194},{3,195},{4,196},{5,197},{6,198},{7,199},{8... | collective-permute-start | bytes 1572872 | tf_op jit(solution)/shard_map/ppermute | solution.py:68
  49.5 19.9 %collective-permute-start.13 = (bf16[1024,256]{1,0:T(8,128)(2,1)S(1)}, bf16[1024,256]{1,0:T(8,128)(2,1)S(1)}, u32[]{:S(2)}, u32[]{:S(2)}) collective-permute-start(bf16[1024,256]{1,0:T(8,128)(2,1)S(1)} %constant_dynamic-update-slice_fusion.refs_0_.refs_5_), channel_id=1, source_target_pairs={{0,64},{1,65},{2,66},{3,67},{4,68},{5,69},{6,70},{7,71},{8,72},{10... | collective-permute-start | bytes 1572872 | tf_op jit(solution)/shard_map/ppermute | solution.py:68
  51.5 39.7 %collective-permute-start.12 = (bf16[1024,256]{1,0:T(8,128)(2,1)S(1)}, bf16[1024,256]{1,0:T(8,128)(2,1)}, u32[]{:S(2)}, u32[]{:S(2)}) collective-permute-start(bf16[1024,256]{1,0:T(8,128)(2,1)S(1)} %collective-permute-done.11.refs_3_.refs_8_), channel_id=1, source_target_pairs={{0,64},{1,65},{2,66},{3,67},{4,68},{5,69},{6,70},{7,71},{8,72},{10... | collective-permute-start | bytes 1572872 | tf_op jit(solution)/shard_map/ppermute | solution.py:68
  53.6 37.6 %collective-permute-start.6 = (bf16[1024,256]{1,0:T(8,128)(2,1)S(1)}, bf16[1024,256]{1,0:T(8,128)(2,1)}, u32[]{:S(2)}, u32[]{:S(2)}) collective-permute-start(bf16[1024,256]{1,0:T(8,128)(2,1)S(1)} %collective-permute-done.5.refs_4_.refs_9_), channel_id=1, source_target_pairs={{0,192},{1,193},{2,194},{3,195},{4,196},{5,197},{6,198},{7,199},{8... | collective-permute-start | bytes 1572872 | tf_op jit(solution)/shard_map/ppermute | solution.py:68
  58.0 33.2 %collective-permute-start = (bf16[256,640]{1,0:T(8,128)(2,1)}, bf16[256,640]{1,0:T(8,128)(2,1)}, u32[]{:S(2)}, u32[]{:S(2)}) collective-permute-start(bf16[256,640]{1,0:T(8,128)(2,1)} %param.13), channel_id=1, source_target_pairs={{0,8},{1,9},{2,10},{3,11},{4,12},{5,13},{6,14},{7,15},{8,16},{9,17... | collective-permute-start | bytes 983048 | tf_op jit(solution)/shard_map/ppermute | solution.py:68
  68.0 23.2 %collective-permute-start.1 = (s32[1]{0:T(128)}, s32[1]{0:T(128)}, u32[]{:S(2)}, u32[]{:S(2)}) collective-permute-start(s32[1]{0:T(128)} %param.16), channel_id=1, source_target_pairs={{0,8},{1,9},{2,10},{3,11},{4,12},{5,13},{6,14},{7,15},{8,16},{9,17... | collective-permute-start | bytes 20 | tf_op jit(solution)/shard_map/ppermute | solution.py:68
  70.3 1.0 copy-start.2
  71.3 19.9 %copy-start.3 = (bf16[1024,256]{1,0:T(8,128)(2,1)S(1)}, bf16[1024,256]{1,0:T(8,128)(2,1)}, u32[]{:S(2)}) copy-start(bf16[1024,256]{1,0:T(8,128)(2,1)} %copy-done.1) | copy-start | bytes 1572868
  190.2 17.4 %copy-start.9 = (s32[50]{0:T(128)S(1)}, s32[50]{0:T(128)}, u32[]{:S(2)}) copy-start(s32[50]{0:T(128)} %param.17) | copy-start | bytes 604
  194.6 19.3 %collective-permute-start.15 = (bf16[4,256,640]{2,1,0:T(8,128)(2,1)S(1)}, bf16[4,256,640]{2,1,0:T(8,128)(2,1)S(1)}, u32[]{:S(2)}, u32[]{:S(2)}) collective-permute-start(bf16[4,256,640]{2,1,0:T(8,128)(2,1)S(1)} %project.3), channel_id=1, source_target_pairs={{0,1},{1,0},{2,3},{3,2},{4,5},{5,4},{6,7},{7,6},{8,9},{9,8},{10,11... | collective-permute-start | bytes 3932168 | tf_op jit(solution)/shard_map/ppermute | solution.py:68
  214.1 11.0 %collective-permute-start.16 = (bf16[256,640]{1,0:T(8,128)(2,1)S(1)}, bf16[256,640]{1,0:T(8,128)(2,1)S(1)}, u32[]{:S(2)}, u32[]{:S(2)}) collective-permute-start(bf16[256,640]{1,0:T(8,128)(2,1)S(1)} %get-tuple-element.29), channel_id=1, source_target_pairs={{0,4},{1,5},{2,6},{3,7},{4,0},{5,1},{6,2},{7,3},{8,12},{9,13},{10,... | collective-permute-start | bytes 983048 | tf_op jit(solution)/shard_map/ppermute | solution.py:68
  217.1 15.3 %collective-permute-start.17 = (bf16[256,640]{1,0:T(8,128)(2,1)S(1)}, bf16[256,640]{1,0:T(8,128)(2,1)S(1)}, u32[]{:S(2)}, u32[]{:S(2)}) collective-permute-start(bf16[256,640]{1,0:T(8,128)(2,1)S(1)} %get-tuple-element.31), channel_id=1, source_target_pairs={{0,2},{1,3},{2,4},{3,5},{4,6},{5,7},{6,0},{7,1},{8,10},{9,11},{10,... | collective-permute-start | bytes 983048 | tf_op jit(solution)/shard_map/ppermute | solution.py:68
  217.5 14.9 %collective-permute-start.18 = (bf16[256,640]{1,0:T(8,128)(2,1)S(1)}, bf16[256,640]{1,0:T(8,128)(2,1)S(1)}, u32[]{:S(2)}, u32[]{:S(2)}) collective-permute-start(bf16[256,640]{1,0:T(8,128)(2,1)S(1)} %get-tuple-element.30), channel_id=1, source_target_pairs={{0,6},{1,7},{2,0},{3,1},{4,2},{5,3},{6,4},{7,5},{8,14},{9,15},{10,... | collective-permute-start | bytes 983048 | tf_op jit(solution)/shard_map/ppermute | solution.py:68
  (6 other events, 5.7 us)

commit v6 on v5

--- a/solution.py
+++ b/solution.py
@@ -16,7 +16,7 @@
 SPANS = X * Z
 NEGATIVE = -1e30
 SCALE = math.log2(math.e) / math.sqrt(HEAD_DIM)
-VMEM_LIMIT = 48 * 1024 * 1024
+MIB = 1024 * 1024
 
 HOST = ((0, 1, 3, 4, 6), (0, 2, 4, 5, 7))
 SHIFTS = (0, 4, 1, 7, 3, 5, 2, 6)
@@ -84,17 +84,31 @@
     return jax.ShapeDtypeStruct(dims, dtype)
 
 
-def pack_kernel(row_ref, query_ref, key_ref, value_ref, *outs):
-    pieces_ref = outs[-1]
-    for i in range(Z):
+def pack_kernel(rounds, row_ref, key_ref, value_ref, *refs):
+    outs = refs[len(refs) - len(rounds) :]
+    for i, out in zip(rounds, outs):
         head = row_ref[SEND + i]
 
         @pl.when(head >= 0)
         def _():
             columns = pl.ds(pl.multiple_of(head * HEAD_DIM, HEAD_DIM), HEAD_DIM)
-            outs[i][:, :HEAD_DIM] = key_ref[:, columns]
-            outs[i][:, HEAD_DIM:] = value_ref[:, columns]
-
+            out[:, :HEAD_DIM] = key_ref[:, columns]
+            out[:, HEAD_DIM:] = value_ref[:, columns]
+
+
+def pack(row, key_rows, value_rows, rounds, after=()):
+    return pl.pallas_call(
+        functools.partial(pack_kernel, rounds),
+        out_shape=[shape(SPAN, 2 * HEAD_DIM)] * len(rounds),
+        in_specs=[in_smem(), in_vmem(), in_vmem()] + [anywhere()] * len(after),
+        out_specs=[in_vmem()] * len(rounds),
+        compiler_params=pltpu.CompilerParams(vmem_limit_bytes=8 * MIB),
+        name="pack",
+    )(row, key_rows, value_rows, *after)
+
+
+def pieces_kernel(row_ref, query_ref, residual_ref, unused_ref, pieces_ref, copy_ref):
+    copy_ref[...] = residual_ref[...]
     for z in range(Z):
         head = row_ref[HEAD + z]
 
@@ -105,16 +119,15 @@
                 pieces_ref[x * Z + z] = query_ref[x * PIECE : (x + 1) * PIECE, columns]
 
 
-def pack(row, query_rows, key_rows, value_rows):
-    outs = pl.pallas_call(
-        pack_kernel,
-        out_shape=[shape(SPAN, 2 * HEAD_DIM)] * Z + [shape(SPANS, PIECE, HEAD_DIM)],
-        in_specs=[in_smem(), in_vmem(), in_vmem(), in_vmem()],
-        out_specs=[in_vmem()] * (Z + 1),
-        compiler_params=pltpu.CompilerParams(vmem_limit_bytes=VMEM_LIMIT),
-        name="pack",
-    )(row, query_rows, key_rows, value_rows)
-    return outs[:Z], outs[Z]
+def cut_queries(row, query_rows, residual, after):
+    return pl.pallas_call(
+        pieces_kernel,
+        out_shape=[shape(SPANS, PIECE, HEAD_DIM), shape(*residual.shape)],
+        in_specs=[in_smem(), in_vmem(), in_vmem(), anywhere()],
+        out_specs=[in_vmem()] * 2,
+        compiler_params=pltpu.CompilerParams(vmem_limit_bytes=8 * MIB),
+        name="pieces",
+    )(row, query_rows, residual, after)
 
 
 STEP = Z // 2
@@ -297,7 +310,7 @@
             pltpu.SMEM((STEPS, STEP), jnp.int32),
             pltpu.SemaphoreType.DMA,
         ],
-        compiler_params=pltpu.CompilerParams(vmem_limit_bytes=VMEM_LIMIT),
+        compiler_params=pltpu.CompilerParams(vmem_limit_bytes=28 * MIB),
         name="near",
     )(row, offset, pieces, *near)
 
@@ -319,59 +332,72 @@
             pltpu.SMEM((STEPS, STEP), jnp.int32),
             pltpu.SemaphoreType.DMA,
         ],
-        compiler_params=pltpu.CompilerParams(vmem_limit_bytes=VMEM_LIMIT),
+        compiler_params=pltpu.CompilerParams(vmem_limit_bytes=28 * MIB),
         name="far",
     )(row, offset, pieces, *far, *state, *near, *others)
 
 
-def gather_kernel(row_ref, parts_ref, out_ref):
-    for head in range(HERE):
-        for x in range(X):
-            out_ref[x * PIECE : (x + 1) * PIECE, head * HEAD_DIM : (head + 1) * HEAD_DIM] = (
-                parts_ref[x * Z + row_ref[PLANE + head]]
+def project_kernel(other, row_ref, parts_ref, weight_ref, out_ref, *refs):
+    wide = out_ref.shape[2]
+    if other:
+        rows_ref, held, copied = refs
+    else:
+        held, copied = refs
+    core = 1 - row_ref[CORE] if other else row_ref[CORE]
+    copies = []
+    for m in range(Y):
+        block = lax.rem(row_ref[PLACE_Y] + m, Y) * C + core
+        columns = pl.ds(pl.multiple_of(block * wide, wide), wide)
+        for k in range(HERE):
+            at = pl.ds(k * HEAD_DIM, HEAD_DIM)
+            copies.append(
+                pltpu.make_async_copy(weight_ref.at[at, columns], held.at[m, at], copied.at[m, k])
             )
-
-
-def gather_heads(row, parts):
+            copies[-1].start()
+    if other:
+        for head in range(HERE):
+            for x in range(X):
+                rows_ref[x * PIECE : (x + 1) * PIECE, head * HEAD_DIM : (head + 1) * HEAD_DIM] = (
+                    parts_ref[x * Z + row_ref[PLANE + head]]
+                )
+        rows = rows_ref[...]
+    else:
+        rows = parts_ref[...]
+    for m in range(Y):
+        for copy in copies[m * HERE : (m + 1) * HERE]:
+            copy.wait()
+        out_ref[m] = jnp.dot(rows, held[m], preferred_element_type=jnp.float32).astype(jnp.bfloat16)
+
+
+def project(row, parts, weight, other):
+    wide = weight.shape[1] // (Y * C)
+    out = shape(Y, SPAN, wide)
+    rows = shape(SPAN, HERE * HEAD_DIM)
     return pl.pallas_call(
-        gather_kernel,
-        out_shape=shape(SPAN, HERE * HEAD_DIM),
-        in_specs=[in_smem(), in_vmem()],
-        out_specs=in_vmem(),
-        compiler_params=pltpu.CompilerParams(vmem_limit_bytes=VMEM_LIMIT),
-        name="heads",
-    )(row, parts)
-
-
-def project_kernel(row_ref, rows_ref, weight_ref, out_ref):
-    out_ref[0] = jnp.dot(
-        rows_ref[...], weight_ref[...], preferred_element_type=jnp.float32
-    ).astype(jnp.bfloat16)
-
-
-def project(row, rows, weight, other):
-    wide = weight.shape[1] // (Y * C)
-
-    def weight_at(m, row_ref):
-        core = row_ref[CORE]
-        core = 1 - core if other else core
-        return (0, lax.rem(row_ref[PLACE_Y] + m, Y) * C + core)
-
-    return pl.pallas_call(
-        project_kernel,
-        out_shape=shape(Y, SPAN, wide),
-        grid_spec=pltpu.PrefetchScalarGridSpec(
-            num_scalar_prefetch=1,
-            grid=(Y,),
-            in_specs=[
-                pl.BlockSpec((SPAN, HERE * HEAD_DIM), lambda m, row_ref: (0, 0)),
-                pl.BlockSpec((HERE * HEAD_DIM, wide), weight_at),
-            ],
-            out_specs=pl.BlockSpec((1, SPAN, wide), lambda m, row_ref: (m, 0, 0)),
-        ),
-        compiler_params=pltpu.CompilerParams(vmem_limit_bytes=VMEM_LIMIT),
+        functools.partial(project_kernel, other),
+        out_shape=[out, rows] if other else out,
+        in_specs=[in_smem(), in_vmem(), anywhere()],
+        out_specs=[in_vmem(), in_vmem()] if other else in_vmem(),
+        scratch_shapes=[
+            pltpu.VMEM((Y, HERE * HEAD_DIM, wide), jnp.bfloat16),
+            pltpu.SemaphoreType.DMA((Y, HERE)),
+        ],
+        compiler_params=pltpu.CompilerParams(vmem_limit_bytes=16 * MIB),
         name="project",
-    )(row, rows, weight)
+    )(row, parts, weight)
+
+
+def gate_of(level, time_proj, timestep_table):
+    half_dim = time_proj.shape[0] // 2
+    stamp_value = jnp.sum(
+        jnp.where(
+            jnp.arange(timestep_table.shape[0], dtype=jnp.int32) == level, timestep_table, 0
+        )
+    ).astype(jnp.float32)
+    frequency = jnp.exp(-math.log(10000.0) * jnp.arange(half_dim, dtype=jnp.float32) / half_dim)
+    angles = stamp_value * frequency
+    embedding = jnp.concatenate([jnp.cos(angles), jnp.sin(angles)])[None, :].astype(jnp.bfloat16)
+    return jnp.dot(embedding, time_proj, preferred_element_type=jnp.float32)
 
 
 def body(
@@ -387,14 +413,15 @@
 ):
     me = lax.axis_index("tm") * (Y * C) + lax.axis_index("head")
     row = lax.dynamic_slice(jnp.asarray(table()), (me, 0), (1, WIDTH))[0]
-    packed, pieces = pack(row, query_rows, key_rows, value_rows)
-
-    arrived = [
-        moved(part, plane_pairs(shift)) if shift else part for part, shift in zip(packed, SHIFTS)
-    ]
+    first, second = range(STEP), range(STEP, Z)
+    packed = pack(row, key_rows, value_rows, first)
+    early = [packed[0]] + [moved(packed[i], plane_pairs(SHIFTS[i])) for i in first[1:]]
+    packed = pack(row, key_rows, value_rows, second, early[1:])
+    late = [moved(part, plane_pairs(SHIFTS[i])) for part, i in zip(packed, second)]
+    pieces, residual = cut_queries(row, query_rows, residual_in, packed[0])
     pieces = lax.all_to_all(pieces, "tm", 0, 0, tiled=True)
 
-    own = [jnp.concatenate(arrived[half * STEP : (half + 1) * STEP]) for half in range(2)]
+    own = [jnp.concatenate(early), jnp.concatenate(late)]
     back = [moved(part, across_pairs(1)) for part in own]
     ahead = [moved(part, across_pairs(-1)) for part in own]
     far = [moved(ahead[0], across_pairs(-1)), moved(back[1], across_pairs(1))]
@@ -403,31 +430,22 @@
     next_slot = [
         (device(x, z, y, c), device((x * Z + z + 1) % SPANS // Z, z + 1, y, c)) for x, z, y, c in ALL
     ]
-    residual = moved(residual_in, next_slot)
-    level = moved(levels, next_slot)
+    residual = moved(residual, next_slot)
+    gate_row = gate_of(moved(levels, next_slot)[0], time_proj, timestep_table)
 
     state = attend_near(row, window_offset, pieces, near)
-    answers = attend_far(row, window_offset, pieces, far, state, near, [residual, level])
+    answers = attend_far(row, window_offset, pieces, far, state, near, [residual, gate_row])
     answers = lax.all_to_all(answers, "tm", 0, 0, tiled=True)
-    attention = gather_heads(row, answers)
 
     swap = [(device(x, z, y, c), device(x, z, y, 1 - c)) for x, z, y, c in ALL]
-    from_core = moved(project(row, attention, out_weight, True), swap)
+    leaving, attention = project(row, answers, out_weight, True)
+    from_core = moved(leaving, swap)
     kept = project(row, attention, out_weight, False)
     both = [kept[m].astype(jnp.float32) + from_core[m].astype(jnp.float32) for m in range(Y)]
     projected = both[0]
     for m in (2, 1, 3):
         pairs = [(device(x, z, y, c), device(x, z, y + m, c)) for x, z, y, c in ALL]
         projected = projected + moved(both[m].astype(jnp.bfloat16), pairs).astype(jnp.float32)
-
-    half_dim = time_proj.shape[0] // 2
-    stamp_value = jnp.sum(
-        jnp.where(jnp.arange(timestep_table.shape[0], dtype=jnp.int32) == level[0], timestep_table, 0)
-    ).astype(jnp.float32)
-    frequency = jnp.exp(-math.log(10000.0) * jnp.arange(half_dim, dtype=jnp.float32) / half_dim)
-    angles = stamp_value * frequency
-    embedding = jnp.concatenate([jnp.cos(angles), jnp.sin(angles)])[None, :].astype(jnp.bfloat16)
-    gate_row = jnp.dot(embedding, time_proj, preferred_element_type=jnp.float32)
     return (residual.astype(jnp.float32) + gate_row * projected).astype(jnp.bfloat16)
 
 

time: 234 us -> 236 us (level)
  waiting for transfers between devices: 23.1 us -> 32.1 us
  Pallas kernels: 112 us -> 107 us
  starting transfers between devices: 71.2 us -> 68.8 us
    ppermute x19, waiting for transfers between devices: 23.1 us -> 32.1 us  [moved(): return lax.ppermute(block, AXES, pairs)]
    ppermute x19, starting transfers between devices: 66.5 us -> 58.7 us  [moved(): return lax.ppermute(block, AXES, pairs)]
    all_to_all x1, starting transfers between devices: 4.68 us -> 10.1 us  [body(): pieces = lax.all_to_all(pieces, 'tm', 0, 0, tiled=True)]
    unnamed x26 -> x28, local copies, waits for them, and re-layouts: 6.78 us -> 4.71 us
    pallas_call x4 -> x5, Pallas kernels: 10.9 us -> 9.11 us  [the longest x2 6.39 us: project(): pl.pallas_call(functools.partial(project_kernel, other), out_shape=[out,...]
  transfers between devices with their start and end apart: 20 -> 20, of which waited for: 4 -> 6; matrix products, arithmetic and copies ran while one was open for 1% -> 1% of each run, Pallas kernels for 10% -> 9%
where the time goes in v6:
time: 236 us; the launch traced here: 235 us
  Pallas kernels  107 us (45%)
  starting transfers between devices  68.8 us (29%)
  waiting for transfers between devices  32.1 us (14%)
  blocking collectives  15.8 us (7%)
  local copies, waits for them, and re-layouts  5.47 us (2%)
  other arithmetic  3.65 us (2%)
    pallas_call x1, Pallas kernels, attend_far(): pl.pallas_call(functools.partial(attend_kernel, FAR, True), out_shape=sha...  81.7 us
    ppermute x19, starting transfers between devices, moved(): return lax.ppermute(block, AXES, pairs)  58.7 us
    ppermute x19, waiting for transfers between devices, moved(): return lax.ppermute(block, AXES, pairs)  32.1 us
    pallas_call x1, Pallas kernels, attend_near(): pl.pallas_call(functools.partial(attend_kernel, NEAR, False), out_shape=[...  16.4 us
    all_to_all x1, blocking collectives, body(): answers = lax.all_to_all(answers, 'tm', 0, 0, tiled=True)  15.8 us
    all_to_all x1, starting transfers between devices, body(): pieces = lax.all_to_all(pieces, 'tm', 0, 0, tiled=True)  10.1 us
    pallas_call x2, Pallas kernels, project(): pl.pallas_call(functools.partial(project_kernel, other), out_shape=[out,...  6.39 us
  transfers between devices with their start and end apart: 20, of which 6 were waited for; matrix products, arithmetic and copies ran while one was open for 1% of the time, Pallas kernels for 9%

profile of v6, /device:TPU:1, one launch (start us, length us, event | category | flops | bytes accessed | tf_op | source)
XLA Modules:
  0.0 234.9 jit_solution(759460712359267497)
XLA Ops:
  3.3 9.6 %collective-permute-start = (bf16[256,256]{1,0:T(8,128)(2,1)S(1)}, bf16[256,256]{1,0:T(8,128)(2,1)S(1)}, u32[]{:S(2)}, u32[]{:S(2)}) collective-permute-start(bf16[256,256]{1,0:T(8,128)(2,1)S(1)} %get-tuple-element.20), channel_id=1, source_target_pairs={{0,32},{1,33},{2,34},{3,35},{4,36},{5,37},{6,38},{7,39},{9,41},{11... | collective-permute-start | bytes 393224 | tf_op jit(solution)/shard_map/ppermute | solution.py:68
  14.3 5.2 %collective-permute-start.2 = (bf16[256,256]{1,0:T(8,128)(2,1)S(1)}, bf16[256,256]{1,0:T(8,128)(2,1)S(1)}, u32[]{:S(2)}, u32[]{:S(2)}) collective-permute-start(bf16[256,256]{1,0:T(8,128)(2,1)S(1)} %get-tuple-element.22), channel_id=1, source_target_pairs={{1,57},{3,59},{5,61},{7,63},{8,0},{9,1},{10,2},{11,3},{12,4},{13,5... | collective-permute-start | bytes 393224 | tf_op jit(solution)/shard_map/ppermute | solution.py:68
  19.9 1.5 collective-permute-done.2.refs_2_
  24.0 1.9 collective-permute-start.8
  25.9 7.1 %collective-permute-start.9 = (bf16[256,256]{1,0:T(8,128)(2,1)S(1)}, bf16[256,256]{1,0:T(8,128)(2,1)S(1)}, u32[]{:S(2)}, u32[]{:S(2)}) collective-permute-start(bf16[256,256]{1,0:T(8,128)(2,1)S(1)} %get-tuple-element.28), channel_id=1, source_target_pairs={{1,17},{3,19},{5,21},{7,23},{8,24},{10,26},{12,28},{14,30},{16,32}... | collective-permute-start | bytes 393224 | tf_op jit(solution)/shard_map/ppermute | solution.py:68
  35.7 4.4 %collective-permute-start.5 = (bf16[1024,256]{1,0:T(8,128)(2,1)S(1)}, bf16[1024,256]{1,0:T(8,128)(2,1)S(1)}, u32[]{:S(2)}, u32[]{:S(2)}) collective-permute-start(bf16[1024,256]{1,0:T(8,128)(2,1)S(1)} %constant_dynamic-update-slice_fusion.refs_0_.refs_5_), channel_id=1, source_target_pairs={{0,192},{1,193},{2,194},{3,195},{4,196},{5,197},{6,198},{7,199},{8... | collective-permute-start | bytes 1572872 | tf_op jit(solution)/shard_map/ppermute | solution.py:68
  40.1 3.1 %collective-permute-done.7 = bf16[256,256]{1,0:T(8,128)(2,1)S(1)} collective-permute-done((bf16[256,256]{1,0:T(8,128)(2,1)S(1)}, bf16[256,256]{1,0:T(8,128)(2,1)S(1)}, u32[]{:S(2)}, u32[]{:S(2)}) %collective-permute-start.7) | collective-permute-done | bytes 131104 | tf_op jit(solution)/shard_map/ppermute | solution.py:68
  43.3 3.1 %collective-permute-start.11 = (bf16[1024,256]{1,0:T(8,128)(2,1)S(1)}, bf16[1024,256]{1,0:T(8,128)(2,1)S(1)}, u32[]{:S(2)}, u32[]{:S(2)}) collective-permute-start(bf16[1024,256]{1,0:T(8,128)(2,1)S(1)} %constant_dynamic-update-slice_fusion.4.refs_1_.refs_6_), channel_id=1, source_target_pairs={{0,64},{1,65},{2,66},{3,67},{4,68},{5,69},{6,70},{7,71},{8,72},{10... | collective-permute-start | bytes 1572872 | tf_op jit(solution)/shard_map/ppermute | solution.py:68
  48.7 10.1 %all-to-all-start = ((bf16[32,64,128]{2,1,0:T(8,128)(2,1)}), bf16[32,64,128]{2,1,0:T(8,128)(2,1)S(1)}, u32[]{:S(2)}, u32[]{:S(2)}) async-start(bf16[32,64,128]{2,1,0:T(8,128)(2,1)} %get-tuple-element.25), calls=%async_computation | async-start | bytes 1048576 | tf_op jit(solution)/shard_map/all_to_all | solution.py:422
  60.7 3.1 %collective-permute-start.13 = (bf16[1024,256]{1,0:T(8,128)(2,1)S(1)}, bf16[1024,256]{1,0:T(8,128)(2,1)S(1)}, u32[]{:S(2)}, u32[]{:S(2)}) collective-permute-start(bf16[1024,256]{1,0:T(8,128)(2,1)S(1)} %constant_dynamic-update-slice_fusion.refs_0_.refs_5_), channel_id=1, source_target_pairs={{0,64},{1,65},{2,66},{3,67},{4,68},{5,69},{6,70},{7,71},{8,72},{10... | collective-permute-start | bytes 1572872 | tf_op jit(solution)/shard_map/ppermute | solution.py:68
  63.8 3.4 %collective-permute-start.14 = (bf16[1024,256]{1,0:T(8,128)(2,1)S(1)}, bf16[1024,256]{1,0:T(8,128)(2,1)}, u32[]{:S(2)}, u32[]{:S(2)}) collective-permute-start(bf16[1024,256]{1,0:T(8,128)(2,1)S(1)} %constant_dynamic-update-slice_fusion.4.refs_1_.refs_6_), channel_id=1, source_target_pairs={{0,192},{1,193},{2,194},{3,195},{4,196},{5,197},{6,198},{7,199},{8... | collective-permute-start | bytes 1572872 | tf_op jit(solution)/shard_map/ppermute | solution.py:68
  67.2 3.1 %collective-permute-start.6 = (bf16[1024,256]{1,0:T(8,128)(2,1)S(1)}, bf16[1024,256]{1,0:T(8,128)(2,1)}, u32[]{:S(2)}, u32[]{:S(2)}) collective-permute-start(bf16[1024,256]{1,0:T(8,128)(2,1)S(1)} %collective-permute-done.5.refs_4_.refs_9_), channel_id=1, source_target_pairs={{0,192},{1,193},{2,194},{3,195},{4,196},{5,197},{6,198},{7,199},{8... | collective-permute-start | bytes 1572872 | tf_op jit(solution)/shard_map/ppermute | solution.py:68
  70.4 2.1 collective-permute-start.12
  74.9 13.2 %collective-permute-done.13.refs_2_.refs_7_ = bf16[1024,256]{1,0:T(8,128)(2,1)S(1)} collective-permute-done((bf16[1024,256]{1,0:T(8,128)(2,1)S(1)}, bf16[1024,256]{1,0:T(8,128)(2,1)S(1)}, u32[]{:S(2)}, u32[]{:S(2)}) %collective-permute-start.13) | collective-permute-done | bytes 524320 | tf_op jit(solution)/shard_map/ppermute | solution.py:68
  88.1 16.4 %near.1 = (f32[2048,128]{1,0:T(8,128)S(1)}, f32[2048,128]{1,0:T(8,128)S(1)}, f32[2048,128]{1,0:T(8,128)S(1)}) custom-call(s32[64]{0:T(128)S(1)} %dynamic-slice_bitcast_fusion.row_ref, s32[1]{0:T(128)S(6)} %copy.17.offset_ref, bf16[32,64,128]{2,1,0:T(8,128)(2,1)S(1)} %all-to-all-done.pieces_ref, ...), custom_call_target="tpu_custom_call" | custom-call | tf_op jit(solution)/shard_map/near/pallas_call | solution.py:302
  104.6 81.7 %far.1 = bf16[32,64,128]{2,1,0:T(8,128)(2,1)S(1)} custom-call(s32[64]{0:T(128)S(1)} %dynamic-slice_bitcast_fusion.row_ref, s32[1]{0:T(128)S(6)} %copy.17.offset_ref, bf16[32,64,128]{2,1,0:T(8,128)(2,1)S(1)} %all-to-all-done.pieces_ref, bf16[1024,256]{1,0:T(8,128)(2,1)} %collective-permute-done.6.refs_0_, bf16[1024,256]{1,0:T(8,128)(2,1)} %collective-permute-done.12.refs_1_, ...), custom_call_target="tpu_custom_call" | custom-call | tf_op jit(solution)/shard_map/far/pallas_call | solution.py:319
  186.3 15.8 %all_to_all.10.parts_ref = bf16[32,64,128]{2,1,0:T(8,128)(2,1)S(1)} all-to-all(bf16[32,64,128]{2,1,0:T(8,128)(2,1)S(1)} %far.1), channel_id=1, replica_groups=mesh['tm'=32,'head'=8] {'tm'}, dimensions={0} | all-to-all | bytes 1048576 | tf_op jit(solution)/shard_map/all_to_all | solution.py:438
  202.1 3.2 %project.2 = (bf16[4,256,640]{2,1,0:T(8,128)(2,1)S(1)}, bf16[256,640]{1,0:T(8,128)(2,1)S(1)}) custom-call(s32[64]{0:T(128)S(1)} %dynamic-slice_bitcast_fusion.row_ref, bf16[32,64,128]{2,1,0:T(8,128)(2,1)S(1)} %all_to_all.10.parts_ref, bf16[640,5120]{1,0:T(8,128)(2,1)S(1)} %bitcast.24), custom_call_target="tpu_custom_call" | custom-call | tf_op jit(solution)/shard_map/project/pallas_call | solution.py:376
  205.3 5.3 %collective-permute-start.15 = (bf16[4,256,640]{2,1,0:T(8,128)(2,1)S(1)}, bf16[4,256,640]{2,1,0:T(8,128)(2,1)S(1)}, u32[]{:S(2)}, u32[]{:S(2)}) collective-permute-start(bf16[4,256,640]{2,1,0:T(8,128)(2,1)S(1)} %get-tuple-element.34), channel_id=1, source_target_pairs={{0,1},{1,0},{2,3},{3,2},{4,5},{5,4},{6,7},{7,6},{8,9},{9,8},{10,11... | collective-permute-start | bytes 3932168 | tf_op jit(solution)/shard_map/ppermute | solution.py:68
  210.6 3.2 %project.3 = bf16[4,256,640]{2,1,0:T(8,128)(2,1)S(1)} custom-call(s32[64]{0:T(128)S(1)} %dynamic-slice_bitcast_fusion.row_ref, bf16[256,640]{1,0:T(8,128)(2,1)S(1)} %get-tuple-element.33.parts_ref, bf16[640,5120]{1,0:T(8,128)(2,1)S(1)} %bitcast.24), custom_call_target="tpu_custom_call" | custom-call | tf_op jit(solution)/shard_map/project/pallas_call | solution.py:376
  214.0 3.6 %collective-permute-start.16 = (bf16[256,640]{1,0:T(8,128)(2,1)S(1)}, bf16[256,640]{1,0:T(8,128)(2,1)S(1)}, u32[]{:S(2)}, u32[]{:S(2)}) collective-permute-start(bf16[256,640]{1,0:T(8,128)(2,1)S(1)} %get-tuple-element.35), channel_id=1, source_target_pairs={{0,4},{1,5},{2,6},{3,7},{4,0},{5,1},{6,2},{7,3},{8,12},{9,13},{10,... | collective-permute-start | bytes 983048 | tf_op jit(solution)/shard_map/ppermute | solution.py:68
  219.1 6.6 %collective-permute-done.16 = bf16[256,640]{1,0:T(8,128)(2,1)S(1)} collective-permute-done((bf16[256,640]{1,0:T(8,128)(2,1)S(1)}, bf16[256,640]{1,0:T(8,128)(2,1)S(1)}, u32[]{:S(2)}, u32[]{:S(2)}) %collective-permute-start.16) | collective-permute-done | bytes 327712 | tf_op jit(solution)/shard_map/ppermute | solution.py:68
  225.7 7.2 %collective-permute-done.18 = bf16[256,640]{1,0:T(8,128)(2,1)S(1)} collective-permute-done((bf16[256,640]{1,0:T(8,128)(2,1)S(1)}, bf16[256,640]{1,0:T(8,128)(2,1)S(1)}, u32[]{:S(2)}, u32[]{:S(2)}) %collective-permute-start.18) | collective-permute-done | bytes 327712 | tf_op jit(solution)/shard_map/ppermute | solution.py:68
  232.9 2.0 fusion.4
  (63 shorter events, 17.2 us)
Async XLA Ops:
  0.0 74.7 %copy-start = (bf16[256,640]{1,0:T(8,128)(2,1)S(1)}, bf16[256,640]{1,0:T(8,128)(2,1)}, u32[]{:S(2)}) copy-start(bf16[256,640]{1,0:T(8,128)(2,1)} %param.15) | copy-start | bytes 983044
  3.3 16.2 %collective-permute-start = (bf16[256,256]{1,0:T(8,128)(2,1)S(1)}, bf16[256,256]{1,0:T(8,128)(2,1)S(1)}, u32[]{:S(2)}, u32[]{:S(2)}) collective-permute-start(bf16[256,256]{1,0:T(8,128)(2,1)S(1)} %get-tuple-element.20), channel_id=1, source_target_pairs={{0,32},{1,33},{2,34},{3,35},{4,36},{5,37},{6,38},{7,39},{9,41},{11... | collective-permute-start | bytes 393224 | tf_op jit(solution)/shard_map/ppermute | solution.py:68
  13.0 6.9 %collective-permute-start.1 = (bf16[256,256]{1,0:T(8,128)(2,1)S(1)}, bf16[256,256]{1,0:T(8,128)(2,1)S(1)}, u32[]{:S(2)}, u32[]{:S(2)}) collective-permute-start(bf16[256,256]{1,0:T(8,128)(2,1)S(1)} %get-tuple-element.21), channel_id=1, source_target_pairs={{0,8},{2,10},{4,12},{6,14},{9,17},{11,19},{13,21},{15,23},{16,24},... | collective-permute-start | bytes 393224 | tf_op jit(solution)/shard_map/ppermute | solution.py:68
  14.3 7.1 %collective-permute-start.2 = (bf16[256,256]{1,0:T(8,128)(2,1)S(1)}, bf16[256,256]{1,0:T(8,128)(2,1)S(1)}, u32[]{:S(2)}, u32[]{:S(2)}) collective-permute-start(bf16[256,256]{1,0:T(8,128)(2,1)S(1)} %get-tuple-element.22), channel_id=1, source_target_pairs={{1,57},{3,59},{5,61},{7,63},{8,0},{9,1},{10,2},{11,3},{12,4},{13,5... | collective-permute-start | bytes 393224 | tf_op jit(solution)/shard_map/ppermute | solution.py:68
  24.0 19.2 %collective-permute-start.8 = (bf16[256,256]{1,0:T(8,128)(2,1)S(1)}, bf16[256,256]{1,0:T(8,128)(2,1)S(1)}, u32[]{:S(2)}, u32[]{:S(2)}) collective-permute-start(bf16[256,256]{1,0:T(8,128)(2,1)S(1)} %get-tuple-element.27), channel_id=1, source_target_pairs={{1,41},{3,43},{5,45},{7,47},{8,48},{10,50},{12,52},{14,54},{17,57}... | collective-permute-start | bytes 393224 | tf_op jit(solution)/shard_map/ppermute | solution.py:68
  25.9 17.3 %collective-permute-start.9 = (bf16[256,256]{1,0:T(8,128)(2,1)S(1)}, bf16[256,256]{1,0:T(8,128)(2,1)S(1)}, u32[]{:S(2)}, u32[]{:S(2)}) collective-permute-start(bf16[256,256]{1,0:T(8,128)(2,1)S(1)} %get-tuple-element.28), channel_id=1, source_target_pairs={{1,17},{3,19},{5,21},{7,23},{8,24},{10,26},{12,28},{14,30},{16,32}... | collective-permute-start | bytes 393224 | tf_op jit(solution)/shard_map/ppermute | solution.py:68
  33.0 10.3 %collective-permute-start.10 = (bf16[256,256]{1,0:T(8,128)(2,1)S(1)}, bf16[256,256]{1,0:T(8,128)(2,1)S(1)}, u32[]{:S(2)}, u32[]{:S(2)}) collective-permute-start(bf16[256,256]{1,0:T(8,128)(2,1)S(1)} %get-tuple-element.29), channel_id=1, source_target_pairs={{0,48},{2,50},{4,52},{6,54},{9,57},{11,59},{13,61},{15,63},{16,0},... | collective-permute-start | bytes 393224 | tf_op jit(solution)/shard_map/ppermute | solution.py:68
  34.3 8.9 %collective-permute-start.7 = (bf16[256,256]{1,0:T(8,128)(2,1)S(1)}, bf16[256,256]{1,0:T(8,128)(2,1)S(1)}, u32[]{:S(2)}, u32[]{:S(2)}) collective-permute-start(bf16[256,256]{1,0:T(8,128)(2,1)S(1)} %get-tuple-element.23.unused_ref), channel_id=1, source_target_pairs={{0,24},{2,26},{4,28},{6,30},{8,32},{9,33},{10,34},{11,35},{12,36},... | collective-permute-start | bytes 393224 | tf_op jit(solution)/shard_map/ppermute | solution.py:68
  35.7 31.5 %collective-permute-start.5 = (bf16[1024,256]{1,0:T(8,128)(2,1)S(1)}, bf16[1024,256]{1,0:T(8,128)(2,1)S(1)}, u32[]{:S(2)}, u32[]{:S(2)}) collective-permute-start(bf16[1024,256]{1,0:T(8,128)(2,1)S(1)} %constant_dynamic-update-slice_fusion.refs_0_.refs_5_), channel_id=1, source_target_pairs={{0,192},{1,193},{2,194},{3,195},{4,196},{5,197},{6,198},{7,199},{8... | collective-permute-start | bytes 1572872 | tf_op jit(solution)/shard_map/ppermute | solution.py:68
  43.2 29.3 %copy-start.8 = (s32[50]{0:T(128)S(1)}, s32[50]{0:T(128)}, u32[]{:S(2)}) copy-start(s32[50]{0:T(128)} %param.17) | copy-start | bytes 604
  43.3 27.1 %collective-permute-start.11 = (bf16[1024,256]{1,0:T(8,128)(2,1)S(1)}, bf16[1024,256]{1,0:T(8,128)(2,1)S(1)}, u32[]{:S(2)}, u32[]{:S(2)}) collective-permute-start(bf16[1024,256]{1,0:T(8,128)(2,1)S(1)} %constant_dynamic-update-slice_fusion.4.refs_1_.refs_6_), channel_id=1, source_target_pairs={{0,64},{1,65},{2,66},{3,67},{4,68},{5,69},{6,70},{7,71},{8,72},{10... | collective-permute-start | bytes 1572872 | tf_op jit(solution)/shard_map/ppermute | solution.py:68
  48.7 39.5 %all-to-all-start = ((bf16[32,64,128]{2,1,0:T(8,128)(2,1)}), bf16[32,64,128]{2,1,0:T(8,128)(2,1)S(1)}, u32[]{:S(2)}, u32[]{:S(2)}) async-start(bf16[32,64,128]{2,1,0:T(8,128)(2,1)} %get-tuple-element.25), calls=%async_computation | async-start | bytes 1048576 | tf_op jit(solution)/shard_map/all_to_all | solution.py:422
  58.7 13.8 %collective-permute-start.4 = (s32[1]{0:T(128)}, s32[1]{0:T(128)}, u32[]{:S(2)}, u32[]{:S(2)}) collective-permute-start(s32[1]{0:T(128)} %param.16), channel_id=1, source_target_pairs={{0,8},{1,9},{2,10},{3,11},{4,12},{5,13},{6,14},{7,15},{8,16},{9,17... | collective-permute-start | bytes 20 | tf_op jit(solution)/shard_map/ppermute | solution.py:68
  60.7 27.4 %collective-permute-start.13 = (bf16[1024,256]{1,0:T(8,128)(2,1)S(1)}, bf16[1024,256]{1,0:T(8,128)(2,1)S(1)}, u32[]{:S(2)}, u32[]{:S(2)}) collective-permute-start(bf16[1024,256]{1,0:T(8,128)(2,1)S(1)} %constant_dynamic-update-slice_fusion.refs_0_.refs_5_), channel_id=1, source_target_pairs={{0,64},{1,65},{2,66},{3,67},{4,68},{5,69},{6,70},{7,71},{8,72},{10... | collective-permute-start | bytes 1572872 | tf_op jit(solution)/shard_map/ppermute | solution.py:68
  63.8 24.3 %collective-permute-start.14 = (bf16[1024,256]{1,0:T(8,128)(2,1)S(1)}, bf16[1024,256]{1,0:T(8,128)(2,1)}, u32[]{:S(2)}, u32[]{:S(2)}) collective-permute-start(bf16[1024,256]{1,0:T(8,128)(2,1)S(1)} %constant_dynamic-update-slice_fusion.4.refs_1_.refs_6_), channel_id=1, source_target_pairs={{0,192},{1,193},{2,194},{3,195},{4,196},{5,197},{6,198},{7,199},{8... | collective-permute-start | bytes 1572872 | tf_op jit(solution)/shard_map/ppermute | solution.py:68
  67.2 37.3 %collective-permute-start.6 = (bf16[1024,256]{1,0:T(8,128)(2,1)S(1)}, bf16[1024,256]{1,0:T(8,128)(2,1)}, u32[]{:S(2)}, u32[]{:S(2)}) collective-permute-start(bf16[1024,256]{1,0:T(8,128)(2,1)S(1)} %collective-permute-done.5.refs_4_.refs_9_), channel_id=1, source_target_pairs={{0,192},{1,193},{2,194},{3,195},{4,196},{5,197},{6,198},{7,199},{8... | collective-permute-start | bytes 1572872 | tf_op jit(solution)/shard_map/ppermute | solution.py:68
  70.4 34.2 %collective-permute-start.12 = (bf16[1024,256]{1,0:T(8,128)(2,1)S(1)}, bf16[1024,256]{1,0:T(8,128)(2,1)}, u32[]{:S(2)}, u32[]{:S(2)}) collective-permute-start(bf16[1024,256]{1,0:T(8,128)(2,1)S(1)} %collective-permute-done.11.refs_3_.refs_8_), channel_id=1, source_target_pairs={{0,64},{1,65},{2,66},{3,67},{4,68},{5,69},{6,70},{7,71},{8,72},{10... | collective-permute-start | bytes 1572872 | tf_op jit(solution)/shard_map/ppermute | solution.py:68
  74.6 29.9 %collective-permute-start.3 = (bf16[256,640]{1,0:T(8,128)(2,1)}, bf16[256,640]{1,0:T(8,128)(2,1)}, u32[]{:S(2)}, u32[]{:S(2)}) collective-permute-start(bf16[256,640]{1,0:T(8,128)(2,1)} %copy-done.7), channel_id=1, source_target_pairs={{0,8},{1,9},{2,10},{3,11},{4,12},{5,13},{6,14},{7,15},{8,16},{9,17... | collective-permute-start | bytes 983048 | tf_op jit(solution)/shard_map/ppermute | solution.py:68
  88.1 114.0 %slice-start = ((s8[6553600]{0:T(1024)(128)(4,1)}), s8[4194304]{0:T(1024)(128)(4,1)S(1)}, s32[]{:S(2)}) async-start(s8[6553600]{0:T(1024)(128)(4,1)} %bitcast.23), calls=%async_computation.2 | async-start | bytes 8388608
  104.5 97.6 %slice-start.1 = ((s8[6553600]{0:T(1024)(128)(4,1)}), s8[2359296]{0:T(1024)(128)(4,1)S(1)}, s32[]{:S(2)}) async-start(s8[6553600]{0:T(1024)(128)(4,1)} %bitcast.23), calls=%async_computation.3 | async-start | bytes 4718592
  205.3 8.4 %collective-permute-start.15 = (bf16[4,256,640]{2,1,0:T(8,128)(2,1)S(1)}, bf16[4,256,640]{2,1,0:T(8,128)(2,1)S(1)}, u32[]{:S(2)}, u32[]{:S(2)}) collective-permute-start(bf16[4,256,640]{2,1,0:T(8,128)(2,1)S(1)} %get-tuple-element.34), channel_id=1, source_target_pairs={{0,1},{1,0},{2,3},{3,2},{4,5},{5,4},{6,7},{7,6},{8,9},{9,8},{10,11... | collective-permute-start | bytes 3932168 | tf_op jit(solution)/shard_map/ppermute | solution.py:68
  214.0 11.7 %collective-permute-start.16 = (bf16[256,640]{1,0:T(8,128)(2,1)S(1)}, bf16[256,640]{1,0:T(8,128)(2,1)S(1)}, u32[]{:S(2)}, u32[]{:S(2)}) collective-permute-start(bf16[256,640]{1,0:T(8,128)(2,1)S(1)} %get-tuple-element.35), channel_id=1, source_target_pairs={{0,4},{1,5},{2,6},{3,7},{4,0},{5,1},{6,2},{7,3},{8,12},{9,13},{10,... | collective-permute-start | bytes 983048 | tf_op jit(solution)/shard_map/ppermute | solution.py:68
  217.6 15.3 %collective-permute-start.18 = (bf16[256,640]{1,0:T(8,128)(2,1)S(1)}, bf16[256,640]{1,0:T(8,128)(2,1)S(1)}, u32[]{:S(2)}, u32[]{:S(2)}) collective-permute-start(bf16[256,640]{1,0:T(8,128)(2,1)S(1)} %get-tuple-element.36), channel_id=1, source_target_pairs={{0,6},{1,7},{2,0},{3,1},{4,2},{5,3},{6,4},{7,5},{8,14},{9,15},{10,... | collective-permute-start | bytes 983048 | tf_op jit(solution)/shard_map/ppermute | solution.py:68
  218.4 14.6 %collective-permute-start.17 = (bf16[256,640]{1,0:T(8,128)(2,1)S(1)}, bf16[256,640]{1,0:T(8,128)(2,1)S(1)}, u32[]{:S(2)}, u32[]{:S(2)}) collective-permute-start(bf16[256,640]{1,0:T(8,128)(2,1)S(1)} %get-tuple-element.37), channel_id=1, source_target_pairs={{0,2},{1,3},{2,4},{3,5},{4,6},{5,7},{6,0},{7,1},{8,10},{9,11},{10,... | collective-permute-start | bytes 983048 | tf_op jit(solution)/shard_map/ppermute | solution.py:68
  (7 other events, 50.8 us)

commit v7 on v6

--- a/solution.py
+++ b/solution.py
@@ -84,27 +84,43 @@
     return jax.ShapeDtypeStruct(dims, dtype)
 
 
-def pack_kernel(rounds, row_ref, key_ref, value_ref, *refs):
-    outs = refs[len(refs) - len(rounds) :]
-    for i, out in zip(rounds, outs):
-        head = row_ref[SEND + i]
-
-        @pl.when(head >= 0)
+def pack_kernel(row_ref, key_ref, value_ref, *refs):
+    outs, copied = refs[:Z], refs[Z]
+
+    def copies(i):
+        columns = pl.ds(pl.multiple_of(row_ref[SEND + i] * HEAD_DIM, HEAD_DIM), HEAD_DIM)
+        return [
+            pltpu.make_async_copy(
+                ref.at[:, columns], outs[i].at[:, pl.ds(n * HEAD_DIM, HEAD_DIM)], copied.at[i, n]
+            )
+            for n, ref in enumerate((key_ref, value_ref))
+        ]
+
+    for i in range(Z):
+
+        @pl.when(row_ref[SEND + i] >= 0)
         def _():
-            columns = pl.ds(pl.multiple_of(head * HEAD_DIM, HEAD_DIM), HEAD_DIM)
-            out[:, :HEAD_DIM] = key_ref[:, columns]
-            out[:, HEAD_DIM:] = value_ref[:, columns]
-
-
-def pack(row, key_rows, value_rows, rounds, after=()):
+            for copy in copies(i):
+                copy.start()
+
+    for i in range(Z):
+
+        @pl.when(row_ref[SEND + i] >= 0)
+        def _():
+            for copy in copies(i):
+                copy.wait()
+
+
+def pack(row, key_rows, value_rows):
     return pl.pallas_call(
-        functools.partial(pack_kernel, rounds),
-        out_shape=[shape(SPAN, 2 * HEAD_DIM)] * len(rounds),
-        in_specs=[in_smem(), in_vmem(), in_vmem()] + [anywhere()] * len(after),
-        out_specs=[in_vmem()] * len(rounds),
+        pack_kernel,
+        out_shape=[shape(SPAN, 2 * HEAD_DIM)] * Z,
+        in_specs=[in_smem()] + [pl.BlockSpec(memory_space=pltpu.HBM)] * 2,
+        out_specs=[in_vmem()] * Z,
+        scratch_shapes=[pltpu.SemaphoreType.DMA((Z, 2))],
         compiler_params=pltpu.CompilerParams(vmem_limit_bytes=8 * MIB),
         name="pack",
-    )(row, key_rows, value_rows, *after)
+    )(row, key_rows, value_rows)
 
 
 def pieces_kernel(row_ref, query_ref, residual_ref, unused_ref, pieces_ref, copy_ref):
@@ -140,15 +156,18 @@
 SMALLEST, LARGEST = 1e-18, 1e30
 
 
-def attend_kernel(places, ends, row_ref, offset_ref, pieces_ref, *refs):
+def attend_kernel(places, begins, ends, row_ref, offset_ref, pieces_ref, *refs):
     sources, refs = refs[: len(places)], refs[len(places) :]
+    if not begins:
+        (total_in, summed_in, shift_ref), refs = refs[:3], refs[3:]
     if ends:
-        (total_in, summed_in, shift_ref), refs = refs[:3], refs[3:]
         later_steps, refs = refs[: STEPS - len(places)], refs[STEPS - len(places) :]
         refs = refs[len(refs) - 7 :]
         out_ref, held, rows, total_ref, summed_ref, keys_at, copied = refs
+    elif begins:
+        total_ref, summed_ref, shift_ref, held, rows, keys_at, copied = refs
     else:
-        total_ref, summed_ref, shift_ref, held, rows, keys_at, copied = refs
+        total_ref, summed_ref, held, rows, keys_at, copied = refs
     offset = offset_ref[0]
 
     def place_of(span):
@@ -215,16 +234,16 @@
             at = pl.ds(pl.multiple_of(place_of(span) * PIECE, PIECE), PIECE)
             rows[at, :] = pieces_ref[span]
         note_places(0, places)
-        if ends:
+        if begins:
+            total_ref[...] = jnp.zeros_like(total_ref)
+            summed_ref[...] = jnp.zeros_like(summed_ref)
+        else:
             total_ref[...] = total_in[...]
             summed_ref[...] = summed_in[...]
-        else:
-            total_ref[...] = jnp.zeros_like(total_ref)
-            summed_ref[...] = jnp.zeros_like(summed_ref)
         brought = held.at[pl.ds(0, steps)]
         pltpu.make_async_copy(brought, brought, copied).wait()
 
-        if not ends:
+        if begins:
             for tile in range(TILES):
                 at = slice(tile * TILE_ROWS, (tile + 1) * TILE_ROWS)
                 top = jnp.max(
@@ -288,36 +307,40 @@
                     pltpu.make_async_copy(source, held.at[steps + i], copied).start()
                 brought = held.at[pl.ds(steps, STEPS - steps)]
                 pltpu.make_async_copy(brought, brought, copied).wait()
-                note_places(steps, NEAR)
+                note_places(steps, BEHIND + AHEAD)
                 for tile in range(TILES):
                     put(tile, running(tile))
 
 
-NEAR = ((0, 0), (0, 1), (1, 0), (1, 1), (3, 0), (3, 1))
+BEHIND = ((0, 0), (0, 1), (1, 0), (1, 1))
+AHEAD = ((3, 0), (3, 1))
 FAR = ((2, 0), (2, 1))
 
 
-def attend_near(row, offset, pieces, near):
+def attend_part(places, row, offset, pieces, sources, state=()):
     held = shape(ROWS, HEAD_DIM, dtype=jnp.float32)
-    return pl.pallas_call(
-        functools.partial(attend_kernel, NEAR, False),
-        out_shape=[held] * 3,
-        in_specs=[in_smem(), in_smem(), in_vmem()] + [anywhere()] * len(near),
-        out_specs=[in_vmem()] * 3,
+    found = pl.pallas_call(
+        functools.partial(attend_kernel, places, not state, False),
+        out_shape=[held] * (2 if state else 3),
+        in_specs=[in_smem(), in_smem(), in_vmem()]
+        + [anywhere()] * len(sources)
+        + [in_vmem()] * len(state),
+        out_specs=[in_vmem()] * (2 if state else 3),
         scratch_shapes=[
-            pltpu.VMEM((len(near), STEP_KEYS, 2 * HEAD_DIM), jnp.bfloat16),
+            pltpu.VMEM((len(sources), STEP_KEYS, 2 * HEAD_DIM), jnp.bfloat16),
             pltpu.VMEM((ROWS, HEAD_DIM), jnp.bfloat16),
             pltpu.SMEM((STEPS, STEP), jnp.int32),
             pltpu.SemaphoreType.DMA,
         ],
         compiler_params=pltpu.CompilerParams(vmem_limit_bytes=28 * MIB),
-        name="near",
-    )(row, offset, pieces, *near)
+        name="part",
+    )(row, offset, pieces, *sources, *state)
+    return [*found, state[2]] if state else found
 
 
 def attend_far(row, offset, pieces, far, state, near, others):
     return pl.pallas_call(
-        functools.partial(attend_kernel, FAR, True),
+        functools.partial(attend_kernel, FAR, False, True),
         out_shape=shape(SPANS, PIECE, HEAD_DIM),
         in_specs=[in_smem(), in_smem(), in_vmem()]
         + [anywhere()] * len(far)
@@ -337,24 +360,12 @@
     )(row, offset, pieces, *far, *state, *near, *others)
 
 
-def project_kernel(other, row_ref, parts_ref, weight_ref, out_ref, *refs):
+def project_kernel(other, places, waits, row_ref, parts_ref, weight_ref, *refs):
+    refs = refs[waits:]
+    out_ref = refs[0]
     wide = out_ref.shape[2]
-    if other:
-        rows_ref, held, copied = refs
-    else:
-        held, copied = refs
-    core = 1 - row_ref[CORE] if other else row_ref[CORE]
-    copies = []
-    for m in range(Y):
-        block = lax.rem(row_ref[PLACE_Y] + m, Y) * C + core
-        columns = pl.ds(pl.multiple_of(block * wide, wide), wide)
-        for k in range(HERE):
-            at = pl.ds(k * HEAD_DIM, HEAD_DIM)
-            copies.append(
-                pltpu.make_async_copy(weight_ref.at[at, columns], held.at[m, at], copied.at[m, k])
-            )
-            copies[-1].start()
-    if other:
+    if len(refs) > 1:
+        rows_ref = refs[1]
         for head in range(HERE):
             for x in range(X):
                 rows_ref[x * PIECE : (x + 1) * PIECE, head * HEAD_DIM : (head + 1) * HEAD_DIM] = (
@@ -363,28 +374,28 @@
         rows = rows_ref[...]
     else:
         rows = parts_ref[...]
-    for m in range(Y):
-        for copy in copies[m * HERE : (m + 1) * HERE]:
-            copy.wait()
-        out_ref[m] = jnp.dot(rows, held[m], preferred_element_type=jnp.float32).astype(jnp.bfloat16)
-
-
-def project(row, parts, weight, other):
+    core = 1 - row_ref[CORE] if other else row_ref[CORE]
+    for n, m in enumerate(places):
+        block = lax.rem(row_ref[PLACE_Y] + m, Y) * C + core
+        columns = pl.ds(pl.multiple_of(block * wide, HEAD_DIM), wide)
+        out_ref[n] = jnp.dot(
+            rows, weight_ref[:, columns], preferred_element_type=jnp.float32
+        ).astype(jnp.bfloat16)
+
+
+def project(row, parts, weight, other, places, after=()):
     wide = weight.shape[1] // (Y * C)
-    out = shape(Y, SPAN, wide)
+    out = shape(len(places), SPAN, wide)
     rows = shape(SPAN, HERE * HEAD_DIM)
+    whole = parts.ndim == 3
     return pl.pallas_call(
-        functools.partial(project_kernel, other),
-        out_shape=[out, rows] if other else out,
-        in_specs=[in_smem(), in_vmem(), anywhere()],
-        out_specs=[in_vmem(), in_vmem()] if other else in_vmem(),
-        scratch_shapes=[
-            pltpu.VMEM((Y, HERE * HEAD_DIM, wide), jnp.bfloat16),
-            pltpu.SemaphoreType.DMA((Y, HERE)),
-        ],
+        functools.partial(project_kernel, other, places, len(after)),
+        out_shape=[out, rows] if whole else out,
+        in_specs=[in_smem(), in_vmem(), in_vmem()] + [anywhere()] * len(after),
+        out_specs=[in_vmem(), in_vmem()] if whole else in_vmem(),
         compiler_params=pltpu.CompilerParams(vmem_limit_bytes=16 * MIB),
         name="project",
-    )(row, parts, weight)
+    )(row, parts, weight, *after)
 
 
 def gate_of(level, time_proj, timestep_table):
@@ -413,19 +424,17 @@
 ):
     me = lax.axis_index("tm") * (Y * C) + lax.axis_index("head")
     row = lax.dynamic_slice(jnp.asarray(table()), (me, 0), (1, WIDTH))[0]
-    first, second = range(STEP), range(STEP, Z)
-    packed = pack(row, key_rows, value_rows, first)
-    early = [packed[0]] + [moved(packed[i], plane_pairs(SHIFTS[i])) for i in first[1:]]
-    packed = pack(row, key_rows, value_rows, second, early[1:])
-    late = [moved(part, plane_pairs(SHIFTS[i])) for part, i in zip(packed, second)]
+    packed = pack(row, key_rows, value_rows)
+    arrived = [
+        moved(part, plane_pairs(shift)) if shift else part for part, shift in zip(packed, SHIFTS)
+    ]
     pieces, residual = cut_queries(row, query_rows, residual_in, packed[0])
     pieces = lax.all_to_all(pieces, "tm", 0, 0, tiled=True)
 
-    own = [jnp.concatenate(early), jnp.concatenate(late)]
+    own = [jnp.concatenate(arrived[half * STEP : (half + 1) * STEP]) for half in range(2)]
     back = [moved(part, across_pairs(1)) for part in own]
     ahead = [moved(part, across_pairs(-1)) for part in own]
     far = [moved(ahead[0], across_pairs(-1)), moved(back[1], across_pairs(1))]
-    near = own + back + ahead
 
     next_slot = [
         (device(x, z, y, c), device((x * Z + z + 1) % SPANS // Z, z + 1, y, c)) for x, z, y, c in ALL
@@ -433,19 +442,35 @@
     residual = moved(residual, next_slot)
     gate_row = gate_of(moved(levels, next_slot)[0], time_proj, timestep_table)
 
-    state = attend_near(row, window_offset, pieces, near)
+    state = attend_part(BEHIND, row, window_offset, pieces, own + back)
+    state = attend_part(AHEAD, row, window_offset, pieces, ahead, state)
+    near = own + back + ahead
     answers = attend_far(row, window_offset, pieces, far, state, near, [residual, gate_row])
     answers = lax.all_to_all(answers, "tm", 0, 0, tiled=True)
 
     swap = [(device(x, z, y, c), device(x, z, y, 1 - c)) for x, z, y, c in ALL]
-    leaving, attention = project(row, answers, out_weight, True)
-    from_core = moved(leaving, swap)
-    kept = project(row, attention, out_weight, False)
-    both = [kept[m].astype(jnp.float32) + from_core[m].astype(jnp.float32) for m in range(Y)]
-    projected = both[0]
-    for m in (2, 1, 3):
-        pairs = [(device(x, z, y, c), device(x, z, y + m, c)) for x, z, y, c in ALL]
-        projected = projected + moved(both[m].astype(jnp.bfloat16), pairs).astype(jnp.float32)
+    along_y = {m: [(device(x, z, y, c), device(x, z, y + m, c)) for x, z, y, c in ALL] for m in (1, -1)}
+
+    def over_cores(leaving, places, after=()):
+        from_core = moved(leaving, swap)
+        kept = project(row, attention, out_weight, False, places, after)
+        return [
+            kept[n].astype(jnp.float32) + from_core[n].astype(jnp.float32)
+            for n in range(len(places))
+        ]
+
+    leaving, attention = project(row, answers, out_weight, True, (2,))
+    (opposite,) = over_cores(leaving, (2,))
+    opposite = opposite.astype(jnp.bfloat16)
+    half = SPAN // 2
+    forward = moved(opposite[:half], along_y[1])
+    backward = moved(opposite[half:], along_y[-1])
+    leaving = project(row, attention, out_weight, True, (1, 3, 0), [opposite])
+    following, preceding, projected = over_cores(leaving, (1, 3, 0), [forward, backward])
+    following = jnp.concatenate([following[:half] + forward.astype(jnp.float32), following[half:]])
+    preceding = jnp.concatenate([preceding[:half], preceding[half:] + backward.astype(jnp.float32)])
+    for share, m in ((following, 1), (preceding, -1)):
+        projected = projected + moved(share.astype(jnp.bfloat16), along_y[m]).astype(jnp.float32)
     return (residual.astype(jnp.float32) + gate_row * projected).astype(jnp.bfloat16)
 
 

time: 236 us -> 236 us (level)
    all_to_all x1, starting transfers between devices: 10.1 us -> 7.08 us  [body(): pieces = lax.all_to_all(pieces, 'tm', 0, 0, tiled=True)]
    ppermute x19 -> x21, waiting for transfers between devices: 32.1 us -> 33.2 us  [moved(): return lax.ppermute(block, AXES, pairs)]
    pallas_call x6 -> x8, Pallas kernels: 106 us -> 105 us  [the longest x1 82.6 us: attend_far(): pl.pallas_call(functools.partial(attend_kernel, FAR, False, True), out_sh...]
    ppermute x19 -> x21, starting transfers between devices: 58.7 us -> 59.5 us  [moved(): return lax.ppermute(block, AXES, pairs)]
  transfers between devices with their start and end apart: 20 -> 22, of which waited for: 6 -> 6; matrix products, arithmetic and copies ran while one was open for 1% -> 1% of each run, Pallas kernels for 9% -> 9%
where the time goes in v7:
time: 236 us; the launch traced here: 235 us
  Pallas kernels  106 us (45%)
  starting transfers between devices  66.6 us (28%)
  waiting for transfers between devices  33.2 us (14%)
  blocking collectives  17.5 us (7%)
  local copies, waits for them, and re-layouts  4.8 us (2%)
  other arithmetic  4.27 us (2%)
    pallas_call x1, Pallas kernels, attend_far(): pl.pallas_call(functools.partial(attend_kernel, FAR, False, True), out_sh...  82.6 us
    ppermute x21, starting transfers between devices, moved(): return lax.ppermute(block, AXES, pairs)  59.5 us
    ppermute x21, waiting for transfers between devices, moved(): return lax.ppermute(block, AXES, pairs)  33.2 us
    all_to_all x1, blocking collectives, body(): answers = lax.all_to_all(answers, 'tm', 0, 0, tiled=True)  17.5 us
    pallas_call x2, Pallas kernels, attend_part(): pl.pallas_call(functools.partial(attend_kernel, places, not state, False)...  16.1 us
    all_to_all x1, starting transfers between devices, body(): pieces = lax.all_to_all(pieces, 'tm', 0, 0, tiled=True)  7.08 us
    pallas_call x4, Pallas kernels, project(): pl.pallas_call(functools.partial(project_kernel, other, places, len(after...  5.27 us
  transfers between devices with their start and end apart: 22, of which 6 were waited for; matrix products, arithmetic and copies ran while one was open for 1% of the time, Pallas kernels for 9%

profile of v7, /device:TPU:1, one launch (start us, length us, event | category | flops | bytes accessed | tf_op | source)
XLA Modules:
  0.0 234.7 jit_solution(6586874405428583346)
XLA Ops:
  3.6 9.6 %collective-permute-start.2 = (bf16[256,256]{1,0:T(8,128)(2,1)S(1)}, bf16[256,256]{1,0:T(8,128)(2,1)S(1)}, u32[]{:S(2)}, u32[]{:S(2)}) collective-permute-start(bf16[256,256]{1,0:T(8,128)(2,1)S(1)} %get-tuple-element.25), channel_id=1, source_target_pairs={{0,32},{1,33},{2,34},{3,35},{4,36},{5,37},{6,38},{7,39},{9,41},{11... | collective-permute-start | bytes 393224 | tf_op jit(solution)/shard_map/ppermute | solution.py:68
  14.6 7.0 %collective-permute-start.8 = (bf16[256,256]{1,0:T(8,128)(2,1)S(1)}, bf16[256,256]{1,0:T(8,128)(2,1)S(1)}, u32[]{:S(2)}, u32[]{:S(2)}) collective-permute-start(bf16[256,256]{1,0:T(8,128)(2,1)S(1)} %get-tuple-element.29), channel_id=1, source_target_pairs={{1,41},{3,43},{5,45},{7,47},{8,48},{10,50},{12,52},{14,54},{17,57}... | collective-permute-start | bytes 393224 | tf_op jit(solution)/shard_map/ppermute | solution.py:68
  21.6 1.9 collective-permute-start.9
  24.8 5.2 %collective-permute-start.4 = (bf16[256,256]{1,0:T(8,128)(2,1)S(1)}, bf16[256,256]{1,0:T(8,128)(2,1)S(1)}, u32[]{:S(2)}, u32[]{:S(2)}) collective-permute-start(bf16[256,256]{1,0:T(8,128)(2,1)S(1)} %get-tuple-element.27), channel_id=1, source_target_pairs={{1,57},{3,59},{5,61},{7,63},{8,0},{9,1},{10,2},{11,3},{12,4},{13,5... | collective-permute-start | bytes 393224 | tf_op jit(solution)/shard_map/ppermute | solution.py:68
  32.8 4.2 %collective-permute-start.5 = (bf16[1024,256]{1,0:T(8,128)(2,1)S(1)}, bf16[1024,256]{1,0:T(8,128)(2,1)S(1)}, u32[]{:S(2)}, u32[]{:S(2)}) collective-permute-start(bf16[1024,256]{1,0:T(8,128)(2,1)S(1)} %constant_dynamic-update-slice_fusion.refs_0_.refs_5_), channel_id=1, source_target_pairs={{0,192},{1,193},{2,194},{3,195},{4,196},{5,197},{6,198},{7,199},{8... | collective-permute-start | bytes 1572872 | tf_op jit(solution)/shard_map/ppermute | solution.py:68
  37.0 4.0 %collective-permute-done.10 = bf16[256,256]{1,0:T(8,128)(2,1)S(1)} collective-permute-done((bf16[256,256]{1,0:T(8,128)(2,1)S(1)}, bf16[256,256]{1,0:T(8,128)(2,1)S(1)}, u32[]{:S(2)}, u32[]{:S(2)}) %collective-permute-start.10) | collective-permute-done | bytes 131104 | tf_op jit(solution)/shard_map/ppermute | solution.py:68
  41.0 3.0 %collective-permute-start.11 = (bf16[1024,256]{1,0:T(8,128)(2,1)S(1)}, bf16[1024,256]{1,0:T(8,128)(2,1)S(1)}, u32[]{:S(2)}, u32[]{:S(2)}) collective-permute-start(bf16[1024,256]{1,0:T(8,128)(2,1)S(1)} %constant_dynamic-update-slice_fusion.4.refs_1_.refs_6_), channel_id=1, source_target_pairs={{0,64},{1,65},{2,66},{3,67},{4,68},{5,69},{6,70},{7,71},{8,72},{10... | collective-permute-start | bytes 1572872 | tf_op jit(solution)/shard_map/ppermute | solution.py:68
  47.5 7.1 %all-to-all-start = ((bf16[32,64,128]{2,1,0:T(8,128)(2,1)}), bf16[32,64,128]{2,1,0:T(8,128)(2,1)S(1)}, u32[]{:S(2)}, u32[]{:S(2)}) async-start(bf16[32,64,128]{2,1,0:T(8,128)(2,1)} %get-tuple-element.24), calls=%async_computation | async-start | bytes 1048576 | tf_op jit(solution)/shard_map/all_to_all | solution.py:432
  57.8 3.1 %collective-permute-start.14 = (bf16[1024,256]{1,0:T(8,128)(2,1)S(1)}, bf16[1024,256]{1,0:T(8,128)(2,1)S(1)}, u32[]{:S(2)}, u32[]{:S(2)}) collective-permute-start(bf16[1024,256]{1,0:T(8,128)(2,1)S(1)} %constant_dynamic-update-slice_fusion.refs_0_.refs_5_), channel_id=1, source_target_pairs={{0,64},{1,65},{2,66},{3,67},{4,68},{5,69},{6,70},{7,71},{8,72},{10... | collective-permute-start | bytes 1572872 | tf_op jit(solution)/shard_map/ppermute | solution.py:68
  60.9 16.8 %collective-permute-done.1 = s32[1]{0:T(128)} collective-permute-done((s32[1]{0:T(128)}, s32[1]{0:T(128)}, u32[]{:S(2)}, u32[]{:S(2)}) %collective-permute-start.1) | collective-permute-done | bytes 36 | tf_op jit(solution)/shard_map/ppermute | solution.py:68
  77.6 2.4 %collective-permute-start.13 = (bf16[1024,256]{1,0:T(8,128)(2,1)S(1)}, bf16[1024,256]{1,0:T(8,128)(2,1)}, u32[]{:S(2)}, u32[]{:S(2)}) collective-permute-start(bf16[1024,256]{1,0:T(8,128)(2,1)S(1)} %constant_dynamic-update-slice_fusion.4.refs_1_.refs_6_), channel_id=1, source_target_pairs={{0,192},{1,193},{2,194},{3,195},{4,196},{5,197},{6,198},{7,199},{8... | collective-permute-start | bytes 1572872 | tf_op jit(solution)/shard_map/ppermute | solution.py:68
  80.1 2.2 collective-permute-start.6
  82.3 3.1 %collective-permute-start.12 = (bf16[1024,256]{1,0:T(8,128)(2,1)S(1)}, bf16[1024,256]{1,0:T(8,128)(2,1)}, u32[]{:S(2)}, u32[]{:S(2)}) collective-permute-start(bf16[1024,256]{1,0:T(8,128)(2,1)S(1)} %collective-permute-done.11.refs_3_.refs_8_), channel_id=1, source_target_pairs={{0,64},{1,65},{2,66},{3,67},{4,68},{5,69},{6,70},{7,71},{8,72},{10... | collective-permute-start | bytes 1572872 | tf_op jit(solution)/shard_map/ppermute | solution.py:68
  85.4 1.9 fusion.10
  88.2 11.5 %part.2 = (f32[2048,128]{1,0:T(8,128)S(1)}, f32[2048,128]{1,0:T(8,128)S(1)}, f32[2048,128]{1,0:T(8,128)S(1)}) custom-call(s32[64]{0:T(128)S(1)} %dynamic-slice_bitcast_fusion.row_ref, s32[1]{0:T(128)S(6)} %copy.17.offset_ref, bf16[32,64,128]{2,1,0:T(8,128)(2,1)S(1)} %all-to-all-done.pieces_ref, ...), custom_call_target="tpu_custom_call" | custom-call | tf_op jit(solution)/shard_map/part/pallas_call | solution.py:322
  99.7 4.6 %part.3 = (f32[2048,128]{1,0:T(8,128)S(1)}, f32[2048,128]{1,0:T(8,128)S(1)}) custom-call(s32[64]{0:T(128)S(1)} %dynamic-slice_bitcast_fusion.row_ref, s32[1]{0:T(128)S(6)} %copy.17.offset_ref, bf16[32,64,128]{2,1,0:T(8,128)(2,1)S(1)} %all-to-all-done.pieces_ref, bf16[1024,256]{1,0:T(8,128)(2,1)S(1)} %collective-permute-done.5.refs_0_.refs_9_, ...), custom_call_target="tpu_custom_call" | custom-call | tf_op jit(solution)/shard_map/part/pallas_call | solution.py:322
  104.4 82.6 %far.1 = bf16[32,64,128]{2,1,0:T(8,128)(2,1)S(1)} custom-call(s32[64]{0:T(128)S(1)} %dynamic-slice_bitcast_fusion.row_ref, s32[1]{0:T(128)S(6)} %copy.17.offset_ref, bf16[32,64,128]{2,1,0:T(8,128)(2,1)S(1)} %all-to-all-done.pieces_ref, bf16[1024,256]{1,0:T(8,128)(2,1)} %collective-permute-done.6.refs_0_, bf16[1024,256]{1,0:T(8,128)(2,1)} %collective-permute-done.12.refs_1_, ...), custom_call_target="tpu_custom_call" | custom-call | tf_op jit(solution)/shard_map/far/pallas_call | solution.py:342
  187.0 17.5 %all_to_all.10.parts_ref = bf16[32,64,128]{2,1,0:T(8,128)(2,1)S(1)} all-to-all(bf16[32,64,128]{2,1,0:T(8,128)(2,1)S(1)} %far.1), channel_id=1, replica_groups=mesh['tm'=32,'head'=8] {'tm'}, dimensions={0} | all-to-all | bytes 1048576 | tf_op jit(solution)/shard_map/all_to_all | solution.py:449
  205.6 5.2 %collective-permute-start.15 = (bf16[1,256,640]{2,1,0:T(8,128)(2,1)S(1)}, bf16[1,256,640]{2,1,0:T(8,128)(2,1)S(1)}, u32[]{:S(2)}, u32[]{:S(2)}) collective-permute-start(bf16[1,256,640]{2,1,0:T(8,128)(2,1)S(1)} %get-tuple-element.38), channel_id=1, source_target_pairs={{0,1},{1,0},{2,3},{3,2},{4,5},{5,4},{6,7},{7,6},{8,9},{9,8},{10,11... | collective-permute-start | bytes 983048 | tf_op jit(solution)/shard_map/ppermute | solution.py:68
  217.1 4.2 %collective-permute-done.16.refs_0_ = bf16[128,640]{1,0:T(8,128)(2,1)S(1)} collective-permute-done((bf16[128,640]{1,0:T(8,128)(2,1)S(1)}, bf16[128,640]{1,0:T(8,128)(2,1)S(1)}, u32[]{:S(2)}, u32[]{:S(2)}) %collective-permute-start.16) | collective-permute-done | bytes 163872 | tf_op jit(solution)/shard_map/ppermute | solution.py:68
  221.3 1.6 project.6
  224.3 1.8 collective-permute-start.20
  226.1 6.7 %collective-permute-done.19 = bf16[256,640]{1,0:T(8,128)(2,1)S(1)} collective-permute-done((bf16[256,640]{1,0:T(8,128)(2,1)S(1)}, bf16[256,640]{1,0:T(8,128)(2,1)S(1)}, u32[]{:S(2)}, u32[]{:S(2)}) %collective-permute-start.19) | collective-permute-done | bytes 327712 | tf_op jit(solution)/shard_map/ppermute | solution.py:68
  232.8 1.9 fusion.3
  (69 shorter events, 23.9 us)
Async XLA Ops:
  3.6 21.2 %collective-permute-start.2 = (bf16[256,256]{1,0:T(8,128)(2,1)S(1)}, bf16[256,256]{1,0:T(8,128)(2,1)S(1)}, u32[]{:S(2)}, u32[]{:S(2)}) collective-permute-start(bf16[256,256]{1,0:T(8,128)(2,1)S(1)} %get-tuple-element.25), channel_id=1, source_target_pairs={{0,32},{1,33},{2,34},{3,35},{4,36},{5,37},{6,38},{7,39},{9,41},{11... | collective-permute-start | bytes 393224 | tf_op jit(solution)/shard_map/ppermute | solution.py:68
  13.3 23.7 %collective-permute-start.7 = (bf16[256,256]{1,0:T(8,128)(2,1)S(1)}, bf16[256,256]{1,0:T(8,128)(2,1)S(1)}, u32[]{:S(2)}, u32[]{:S(2)}) collective-permute-start(bf16[256,256]{1,0:T(8,128)(2,1)S(1)} %get-tuple-element.28), channel_id=1, source_target_pairs={{0,24},{2,26},{4,28},{6,30},{8,32},{9,33},{10,34},{11,35},{12,36},... | collective-permute-start | bytes 393224 | tf_op jit(solution)/shard_map/ppermute | solution.py:68
  14.6 22.4 %collective-permute-start.8 = (bf16[256,256]{1,0:T(8,128)(2,1)S(1)}, bf16[256,256]{1,0:T(8,128)(2,1)S(1)}, u32[]{:S(2)}, u32[]{:S(2)}) collective-permute-start(bf16[256,256]{1,0:T(8,128)(2,1)S(1)} %get-tuple-element.29), channel_id=1, source_target_pairs={{1,41},{3,43},{5,45},{7,47},{8,48},{10,50},{12,52},{14,54},{17,57}... | collective-permute-start | bytes 393224 | tf_op jit(solution)/shard_map/ppermute | solution.py:68
  21.6 15.4 %collective-permute-start.9 = (bf16[256,256]{1,0:T(8,128)(2,1)S(1)}, bf16[256,256]{1,0:T(8,128)(2,1)S(1)}, u32[]{:S(2)}, u32[]{:S(2)}) collective-permute-start(bf16[256,256]{1,0:T(8,128)(2,1)S(1)} %get-tuple-element.30), channel_id=1, source_target_pairs={{1,17},{3,19},{5,21},{7,23},{8,24},{10,26},{12,28},{14,30},{16,32}... | collective-permute-start | bytes 393224 | tf_op jit(solution)/shard_map/ppermute | solution.py:68
  23.5 7.9 %collective-permute-start.3 = (bf16[256,256]{1,0:T(8,128)(2,1)S(1)}, bf16[256,256]{1,0:T(8,128)(2,1)S(1)}, u32[]{:S(2)}, u32[]{:S(2)}) collective-permute-start(bf16[256,256]{1,0:T(8,128)(2,1)S(1)} %get-tuple-element.26), channel_id=1, source_target_pairs={{0,8},{2,10},{4,12},{6,14},{9,17},{11,19},{13,21},{15,23},{16,24},... | collective-permute-start | bytes 393224 | tf_op jit(solution)/shard_map/ppermute | solution.py:68
  24.8 7.9 %collective-permute-start.4 = (bf16[256,256]{1,0:T(8,128)(2,1)S(1)}, bf16[256,256]{1,0:T(8,128)(2,1)S(1)}, u32[]{:S(2)}, u32[]{:S(2)}) collective-permute-start(bf16[256,256]{1,0:T(8,128)(2,1)S(1)} %get-tuple-element.27), channel_id=1, source_target_pairs={{1,57},{3,59},{5,61},{7,63},{8,0},{9,1},{10,2},{11,3},{12,4},{13,5... | collective-permute-start | bytes 393224 | tf_op jit(solution)/shard_map/ppermute | solution.py:68
  31.4 9.6 %collective-permute-start.10 = (bf16[256,256]{1,0:T(8,128)(2,1)S(1)}, bf16[256,256]{1,0:T(8,128)(2,1)S(1)}, u32[]{:S(2)}, u32[]{:S(2)}) collective-permute-start(bf16[256,256]{1,0:T(8,128)(2,1)S(1)} %get-tuple-element.31), channel_id=1, source_target_pairs={{0,48},{2,50},{4,52},{6,54},{9,57},{11,59},{13,61},{15,63},{16,0},... | collective-permute-start | bytes 393224 | tf_op jit(solution)/shard_map/ppermute | solution.py:68
  32.8 47.3 %collective-permute-start.5 = (bf16[1024,256]{1,0:T(8,128)(2,1)S(1)}, bf16[1024,256]{1,0:T(8,128)(2,1)S(1)}, u32[]{:S(2)}, u32[]{:S(2)}) collective-permute-start(bf16[1024,256]{1,0:T(8,128)(2,1)S(1)} %constant_dynamic-update-slice_fusion.refs_0_.refs_5_), channel_id=1, source_target_pairs={{0,192},{1,193},{2,194},{3,195},{4,196},{5,197},{6,198},{7,199},{8... | collective-permute-start | bytes 1572872 | tf_op jit(solution)/shard_map/ppermute | solution.py:68
  41.0 41.2 %collective-permute-start.11 = (bf16[1024,256]{1,0:T(8,128)(2,1)S(1)}, bf16[1024,256]{1,0:T(8,128)(2,1)S(1)}, u32[]{:S(2)}, u32[]{:S(2)}) collective-permute-start(bf16[1024,256]{1,0:T(8,128)(2,1)S(1)} %constant_dynamic-update-slice_fusion.4.refs_1_.refs_6_), channel_id=1, source_target_pairs={{0,64},{1,65},{2,66},{3,67},{4,68},{5,69},{6,70},{7,71},{8,72},{10... | collective-permute-start | bytes 1572872 | tf_op jit(solution)/shard_map/ppermute | solution.py:68
  47.5 40.7 %all-to-all-start = ((bf16[32,64,128]{2,1,0:T(8,128)(2,1)}), bf16[32,64,128]{2,1,0:T(8,128)(2,1)S(1)}, u32[]{:S(2)}, u32[]{:S(2)}) async-start(bf16[32,64,128]{2,1,0:T(8,128)(2,1)} %get-tuple-element.24), calls=%async_computation | async-start | bytes 1048576 | tf_op jit(solution)/shard_map/all_to_all | solution.py:432
  54.6 49.7 %collective-permute-start = (bf16[256,640]{1,0:T(8,128)(2,1)}, bf16[256,640]{1,0:T(8,128)(2,1)}, u32[]{:S(2)}, u32[]{:S(2)}) collective-permute-start(bf16[256,640]{1,0:T(8,128)(2,1)} %get-tuple-element.23), channel_id=1, source_target_pairs={{0,8},{1,9},{2,10},{3,11},{4,12},{5,13},{6,14},{7,15},{8,16},{9,17... | collective-permute-start | bytes 983048 | tf_op jit(solution)/shard_map/ppermute | solution.py:68
  55.9 21.7 %collective-permute-start.1 = (s32[1]{0:T(128)}, s32[1]{0:T(128)}, u32[]{:S(2)}, u32[]{:S(2)}) collective-permute-start(s32[1]{0:T(128)} %param.16), channel_id=1, source_target_pairs={{0,8},{1,9},{2,10},{3,11},{4,12},{5,13},{6,14},{7,15},{8,16},{9,17... | collective-permute-start | bytes 20 | tf_op jit(solution)/shard_map/ppermute | solution.py:68
  57.8 30.4 %collective-permute-start.14 = (bf16[1024,256]{1,0:T(8,128)(2,1)S(1)}, bf16[1024,256]{1,0:T(8,128)(2,1)S(1)}, u32[]{:S(2)}, u32[]{:S(2)}) collective-permute-start(bf16[1024,256]{1,0:T(8,128)(2,1)S(1)} %constant_dynamic-update-slice_fusion.refs_0_.refs_5_), channel_id=1, source_target_pairs={{0,64},{1,65},{2,66},{3,67},{4,68},{5,69},{6,70},{7,71},{8,72},{10... | collective-permute-start | bytes 1572872 | tf_op jit(solution)/shard_map/ppermute | solution.py:68
  77.6 22.1 %collective-permute-start.13 = (bf16[1024,256]{1,0:T(8,128)(2,1)S(1)}, bf16[1024,256]{1,0:T(8,128)(2,1)}, u32[]{:S(2)}, u32[]{:S(2)}) collective-permute-start(bf16[1024,256]{1,0:T(8,128)(2,1)S(1)} %constant_dynamic-update-slice_fusion.4.refs_1_.refs_6_), channel_id=1, source_target_pairs={{0,192},{1,193},{2,194},{3,195},{4,196},{5,197},{6,198},{7,199},{8... | collective-permute-start | bytes 1572872 | tf_op jit(solution)/shard_map/ppermute | solution.py:68
  80.1 24.3 %collective-permute-start.6 = (bf16[1024,256]{1,0:T(8,128)(2,1)S(1)}, bf16[1024,256]{1,0:T(8,128)(2,1)}, u32[]{:S(2)}, u32[]{:S(2)}) collective-permute-start(bf16[1024,256]{1,0:T(8,128)(2,1)S(1)} %collective-permute-done.5.refs_0_.refs_9_), channel_id=1, source_target_pairs={{0,192},{1,193},{2,194},{3,195},{4,196},{5,197},{6,198},{7,199},{8... | collective-permute-start | bytes 1572872 | tf_op jit(solution)/shard_map/ppermute | solution.py:68
  82.3 22.1 %collective-permute-start.12 = (bf16[1024,256]{1,0:T(8,128)(2,1)S(1)}, bf16[1024,256]{1,0:T(8,128)(2,1)}, u32[]{:S(2)}, u32[]{:S(2)}) collective-permute-start(bf16[1024,256]{1,0:T(8,128)(2,1)S(1)} %collective-permute-done.11.refs_3_.refs_8_), channel_id=1, source_target_pairs={{0,64},{1,65},{2,66},{3,67},{4,68},{5,69},{6,70},{7,71},{8,72},{10... | collective-permute-start | bytes 1572872 | tf_op jit(solution)/shard_map/ppermute | solution.py:68
  99.7 104.8 %slice-start = ((s8[6553600]{0:T(1024)(128)(4,1)}), s8[4194304]{0:T(1024)(128)(4,1)S(1)}, s32[]{:S(2)}) async-start(s8[6553600]{0:T(1024)(128)(4,1)} %bitcast.36), calls=%async_computation.2 | async-start | bytes 8388608
  104.4 100.1 %slice-start.1 = ((s8[6553600]{0:T(1024)(128)(4,1)}), s8[2359296]{0:T(1024)(128)(4,1)S(1)}, s32[]{:S(2)}) async-start(s8[6553600]{0:T(1024)(128)(4,1)} %bitcast.36), calls=%async_computation.3 | async-start | bytes 4718592
  205.6 6.5 %collective-permute-start.15 = (bf16[1,256,640]{2,1,0:T(8,128)(2,1)S(1)}, bf16[1,256,640]{2,1,0:T(8,128)(2,1)S(1)}, u32[]{:S(2)}, u32[]{:S(2)}) collective-permute-start(bf16[1,256,640]{2,1,0:T(8,128)(2,1)S(1)} %get-tuple-element.38), channel_id=1, source_target_pairs={{0,1},{1,0},{2,3},{3,2},{4,5},{5,4},{6,7},{7,6},{8,9},{9,8},{10,11... | collective-permute-start | bytes 983048 | tf_op jit(solution)/shard_map/ppermute | solution.py:68
  213.7 9.2 %collective-permute-start.18 = (bf16[3,256,640]{2,1,0:T(8,128)(2,1)S(1)}, bf16[3,256,640]{2,1,0:T(8,128)(2,1)S(1)}, u32[]{:S(2)}, u32[]{:S(2)}) collective-permute-start(bf16[3,256,640]{2,1,0:T(8,128)(2,1)S(1)} %project.7), channel_id=1, source_target_pairs={{0,1},{1,0},{2,3},{3,2},{4,5},{5,4},{6,7},{7,6},{8,9},{9,8},{10,11... | collective-permute-start | bytes 2949128 | tf_op jit(solution)/shard_map/ppermute | solution.py:68
  214.2 7.1 %collective-permute-start.16 = (bf16[128,640]{1,0:T(8,128)(2,1)S(1)}, bf16[128,640]{1,0:T(8,128)(2,1)S(1)}, u32[]{:S(2)}, u32[]{:S(2)}) collective-permute-start(bf16[128,640]{1,0:T(8,128)(2,1)S(1)} %get-tuple-element.42), channel_id=1, source_target_pairs={{0,2},{1,3},{2,4},{3,5},{4,6},{5,7},{6,0},{7,1},{8,10},{9,11},{10,... | collective-permute-start | bytes 491528 | tf_op jit(solution)/shard_map/ppermute | solution.py:68
  215.6 5.7 %collective-permute-start.17 = (bf16[128,640]{1,0:T(8,128)(2,1)S(1)}, bf16[128,640]{1,0:T(8,128)(2,1)S(1)}, u32[]{:S(2)}, u32[]{:S(2)}) collective-permute-start(bf16[128,640]{1,0:T(8,128)(2,1)S(1)} %get-tuple-element.41), channel_id=1, source_target_pairs={{0,6},{1,7},{2,0},{3,1},{4,2},{5,3},{6,4},{7,5},{8,14},{9,15},{10,... | collective-permute-start | bytes 491528 | tf_op jit(solution)/shard_map/ppermute | solution.py:68
  223.2 9.6 %collective-permute-start.19 = (bf16[256,640]{1,0:T(8,128)(2,1)S(1)}, bf16[256,640]{1,0:T(8,128)(2,1)S(1)}, u32[]{:S(2)}, u32[]{:S(2)}) collective-permute-start(bf16[256,640]{1,0:T(8,128)(2,1)S(1)} %pad_maximum_fusion), channel_id=1, source_target_pairs={{0,2},{1,3},{2,4},{3,5},{4,6},{5,7},{6,0},{7,1},{8,10},{9,11},{10,... | collective-permute-start | bytes 983048 | tf_op jit(solution)/shard_map/ppermute | solution.py:68
  224.3 8.5 %collective-permute-start.20 = (bf16[256,640]{1,0:T(8,128)(2,1)S(1)}, bf16[256,640]{1,0:T(8,128)(2,1)S(1)}, u32[]{:S(2)}, u32[]{:S(2)}) collective-permute-start(bf16[256,640]{1,0:T(8,128)(2,1)S(1)} %pad_maximum_fusion.1), channel_id=1, source_target_pairs={{0,6},{1,7},{2,0},{3,1},{4,2},{5,3},{6,4},{7,5},{8,14},{9,15},{10,... | collective-permute-start | bytes 983048 | tf_op jit(solution)/shard_map/ppermute | solution.py:68
  (5 other events, 91.9 us)

commit v8 on v7

--- a/solution.py
+++ b/solution.py
@@ -123,8 +123,7 @@
     )(row, key_rows, value_rows)
 
 
-def pieces_kernel(row_ref, query_ref, residual_ref, unused_ref, pieces_ref, copy_ref):
-    copy_ref[...] = residual_ref[...]
+def pieces_kernel(row_ref, query_ref, unused_ref, pieces_ref):
     for z in range(Z):
         head = row_ref[HEAD + z]
 
@@ -135,15 +134,15 @@
                 pieces_ref[x * Z + z] = query_ref[x * PIECE : (x + 1) * PIECE, columns]
 
 
-def cut_queries(row, query_rows, residual, after):
+def cut_queries(row, query_rows, after):
     return pl.pallas_call(
         pieces_kernel,
-        out_shape=[shape(SPANS, PIECE, HEAD_DIM), shape(*residual.shape)],
-        in_specs=[in_smem(), in_vmem(), in_vmem(), anywhere()],
-        out_specs=[in_vmem()] * 2,
+        out_shape=shape(SPANS, PIECE, HEAD_DIM),
+        in_specs=[in_smem(), in_vmem(), anywhere()],
+        out_specs=in_vmem(),
         compiler_params=pltpu.CompilerParams(vmem_limit_bytes=8 * MIB),
         name="pieces",
-    )(row, query_rows, residual, after)
+    )(row, query_rows, after)
 
 
 STEP = Z // 2
@@ -165,7 +164,10 @@
         refs = refs[len(refs) - 7 :]
         out_ref, held, rows, total_ref, summed_ref, keys_at, copied = refs
     elif begins:
-        total_ref, summed_ref, shift_ref, held, rows, keys_at, copied = refs
+        passed, refs = refs[0], refs[1:]
+        total_ref, summed_ref, shift_ref, passed_on, held, rows, keys_at, copied, passing = refs
+        pass_on = pltpu.make_async_copy(passed, passed_on, passing)
+        pass_on.start()
     else:
         total_ref, summed_ref, held, rows, keys_at, copied = refs
     offset = offset_ref[0]
@@ -311,31 +313,39 @@
                 for tile in range(TILES):
                     put(tile, running(tile))
 
+    if begins:
+        pass_on.wait()
+
 
 BEHIND = ((0, 0), (0, 1), (1, 0), (1, 1))
 AHEAD = ((3, 0), (3, 1))
 FAR = ((2, 0), (2, 1))
 
 
-def attend_part(places, row, offset, pieces, sources, state=()):
+def attend_part(places, row, offset, pieces, sources, state=(), passed=None):
     held = shape(ROWS, HEAD_DIM, dtype=jnp.float32)
+    begins = not state
+    out_specs, outs = [in_vmem()] * 2, [held] * 2
+    if begins:
+        out_specs, outs = out_specs + [in_vmem(), anywhere()], outs + [held, shape(*passed.shape)]
     found = pl.pallas_call(
-        functools.partial(attend_kernel, places, not state, False),
-        out_shape=[held] * (2 if state else 3),
+        functools.partial(attend_kernel, places, begins, False),
+        out_shape=outs,
         in_specs=[in_smem(), in_smem(), in_vmem()]
         + [anywhere()] * len(sources)
-        + [in_vmem()] * len(state),
-        out_specs=[in_vmem()] * (2 if state else 3),
+        + ([anywhere()] if begins else [in_vmem()] * len(state)),
+        out_specs=out_specs,
         scratch_shapes=[
             pltpu.VMEM((len(sources), STEP_KEYS, 2 * HEAD_DIM), jnp.bfloat16),
             pltpu.VMEM((ROWS, HEAD_DIM), jnp.bfloat16),
             pltpu.SMEM((STEPS, STEP), jnp.int32),
             pltpu.SemaphoreType.DMA,
-        ],
+        ]
+        + [pltpu.SemaphoreType.DMA] * begins,
         compiler_params=pltpu.CompilerParams(vmem_limit_bytes=28 * MIB),
         name="part",
-    )(row, offset, pieces, *sources, *state)
-    return [*found, state[2]] if state else found
+    )(row, offset, pieces, *sources, *((passed,) if begins else state))
+    return found if begins else [*found, state[2]]
 
 
 def attend_far(row, offset, pieces, far, state, near, others):
@@ -398,8 +408,7 @@
     )(row, parts, weight, *after)
 
 
-def gate_of(level, time_proj, timestep_table):
-    half_dim = time_proj.shape[0] // 2
+def embedding_of(level, timestep_table, half_dim):
     stamp_value = jnp.sum(
         jnp.where(
             jnp.arange(timestep_table.shape[0], dtype=jnp.int32) == level, timestep_table, 0
@@ -407,8 +416,7 @@
     ).astype(jnp.float32)
     frequency = jnp.exp(-math.log(10000.0) * jnp.arange(half_dim, dtype=jnp.float32) / half_dim)
     angles = stamp_value * frequency
-    embedding = jnp.concatenate([jnp.cos(angles), jnp.sin(angles)])[None, :].astype(jnp.bfloat16)
-    return jnp.dot(embedding, time_proj, preferred_element_type=jnp.float32)
+    return jnp.concatenate([jnp.cos(angles), jnp.sin(angles)])[None, :].astype(jnp.bfloat16)
 
 
 def body(
@@ -428,24 +436,29 @@
     arrived = [
         moved(part, plane_pairs(shift)) if shift else part for part, shift in zip(packed, SHIFTS)
     ]
-    pieces, residual = cut_queries(row, query_rows, residual_in, packed[0])
-    pieces = lax.all_to_all(pieces, "tm", 0, 0, tiled=True)
 
     own = [jnp.concatenate(arrived[half * STEP : (half + 1) * STEP]) for half in range(2)]
     back = [moved(part, across_pairs(1)) for part in own]
     ahead = [moved(part, across_pairs(-1)) for part in own]
+    pieces = cut_queries(row, query_rows, own[1])
+    pieces = lax.all_to_all(pieces, "tm", 0, 0, tiled=True)
     far = [moved(ahead[0], across_pairs(-1)), moved(back[1], across_pairs(1))]
 
+    freq_dim = time_proj.shape[0]
+    embedding = embedding_of(levels[0], timestep_table, freq_dim // 2)
+    below = jnp.pad(embedding, ((0, 15), (0, residual_in.shape[1] - freq_dim)))
+    passed = jnp.concatenate([residual_in, below])
     next_slot = [
         (device(x, z, y, c), device((x * Z + z + 1) % SPANS // Z, z + 1, y, c)) for x, z, y, c in ALL
     ]
-    residual = moved(residual, next_slot)
-    gate_row = gate_of(moved(levels, next_slot)[0], time_proj, timestep_table)
-
-    state = attend_part(BEHIND, row, window_offset, pieces, own + back)
+    *state, passed = attend_part(BEHIND, row, window_offset, pieces, own + back, passed=passed)
+    passed = moved(passed, next_slot)
+    residual, embedding = passed[:SPAN], passed[SPAN : SPAN + 1, :freq_dim]
+    gate_row = jnp.dot(embedding, time_proj, preferred_element_type=jnp.float32)
+
     state = attend_part(AHEAD, row, window_offset, pieces, ahead, state)
     near = own + back + ahead
-    answers = attend_far(row, window_offset, pieces, far, state, near, [residual, gate_row])
+    answers = attend_far(row, window_offset, pieces, far, state, near, [passed])
     answers = lax.all_to_all(answers, "tm", 0, 0, tiled=True)
 
     swap = [(device(x, z, y, c), device(x, z, y, 1 - c)) for x, z, y, c in ALL]

time: 236 us -> 224 us (0.949)
  waiting for transfers between devices: 33.2 us -> 17.5 us
  starting transfers between devices: 66.6 us -> 72.4 us
    ppermute x21 -> x20, waiting for transfers between devices: 33.2 us -> 17.5 us  [moved(): return lax.ppermute(block, AXES, pairs)]
    ppermute x21 -> x20, starting transfers between devices: 59.5 us -> 68.2 us  [moved(): return lax.ppermute(block, AXES, pairs)]
    all_to_all x1, starting transfers between devices: 7.08 us -> 4.12 us  [body(): pieces = lax.all_to_all(pieces, 'tm', 0, 0, tiled=True)]
  transfers between devices with their start and end apart: 22 -> 21, of which waited for: 6 -> 4; matrix products, arithmetic and copies ran while one was open for 1% -> 2% of each run, Pallas kernels for 9% -> 9%
where the time goes in v8:
time: 224 us; the launch traced here: 225 us
  Pallas kernels  106 us (47%)
  starting transfers between devices  72.4 us (32%)
  waiting for transfers between devices  17.5 us (8%)
  blocking collectives  16.9 us (8%)
  local copies, waits for them, and re-layouts  4.8 us (2%)
  other arithmetic  4.46 us (2%)
  between operations  2.38 us (1%)
    pallas_call x1, Pallas kernels, attend_far(): pl.pallas_call(functools.partial(attend_kernel, FAR, False, True), out_sh...  82.5 us
    ppermute x20, starting transfers between devices, moved(): return lax.ppermute(block, AXES, pairs)  68.2 us
    ppermute x20, waiting for transfers between devices, moved(): return lax.ppermute(block, AXES, pairs)  17.5 us
    all_to_all x1, blocking collectives, body(): answers = lax.all_to_all(answers, 'tm', 0, 0, tiled=True)  16.9 us
    pallas_call x2, Pallas kernels, attend_part(): pl.pallas_call(functools.partial(attend_kernel, places, begins, False), o...  15.9 us
    pallas_call x4, Pallas kernels, project(): pl.pallas_call(functools.partial(project_kernel, other, places, len(after...  5.26 us
  transfers between devices with their start and end apart: 21, of which 4 were waited for; matrix products, arithmetic and copies ran while one was open for 2% of the time, Pallas kernels for 9%

profile of v8, /device:TPU:1, one launch (start us, length us, event | category | flops | bytes accessed | tf_op | source)
XLA Modules:
  0.0 224.6 jit_solution(2321046156835020102)
XLA Ops:
  4.9 9.8 %collective-permute-start.1 = (bf16[256,256]{1,0:T(8,128)(2,1)S(1)}, bf16[256,256]{1,0:T(8,128)(2,1)S(1)}, u32[]{:S(2)}, u32[]{:S(2)}) collective-permute-start(bf16[256,256]{1,0:T(8,128)(2,1)S(1)} %get-tuple-element.22), channel_id=1, source_target_pairs={{1,41},{3,43},{5,45},{7,47},{8,48},{10,50},{12,52},{14,54},{17,57}... | collective-permute-start | bytes 393224 | tf_op jit(solution)/shard_map/ppermute | solution.py:68
  14.8 3.1 %collective-permute-start.2 = (bf16[256,256]{1,0:T(8,128)(2,1)S(1)}, bf16[256,256]{1,0:T(8,128)(2,1)S(1)}, u32[]{:S(2)}, u32[]{:S(2)}) collective-permute-start(bf16[256,256]{1,0:T(8,128)(2,1)S(1)} %get-tuple-element.23), channel_id=1, source_target_pairs={{1,17},{3,19},{5,21},{7,23},{8,24},{10,26},{12,28},{14,30},{16,32}... | collective-permute-start | bytes 393224 | tf_op jit(solution)/shard_map/ppermute | solution.py:68
  19.2 6.4 %collective-permute-start.4 = (bf16[256,256]{1,0:T(8,128)(2,1)S(1)}, bf16[256,256]{1,0:T(8,128)(2,1)S(1)}, u32[]{:S(2)}, u32[]{:S(2)}) collective-permute-start(bf16[256,256]{1,0:T(8,128)(2,1)S(1)} %get-tuple-element.26), channel_id=1, source_target_pairs={{0,32},{1,33},{2,34},{3,35},{4,36},{5,37},{6,38},{7,39},{9,41},{11... | collective-permute-start | bytes 393224 | tf_op jit(solution)/shard_map/ppermute | solution.py:68
  26.9 5.2 %collective-permute-start.6 = (bf16[256,256]{1,0:T(8,128)(2,1)S(1)}, bf16[256,256]{1,0:T(8,128)(2,1)S(1)}, u32[]{:S(2)}, u32[]{:S(2)}) collective-permute-start(bf16[256,256]{1,0:T(8,128)(2,1)S(1)} %get-tuple-element.28), channel_id=1, source_target_pairs={{1,57},{3,59},{5,61},{7,63},{8,0},{9,1},{10,2},{11,3},{12,4},{13,5... | collective-permute-start | bytes 393224 | tf_op jit(solution)/shard_map/ppermute | solution.py:68
  32.2 3.1 %collective-permute-start.8 = (bf16[1024,256]{1,0:T(8,128)(2,1)S(1)}, bf16[1024,256]{1,0:T(8,128)(2,1)S(1)}, u32[]{:S(2)}, u32[]{:S(2)}) collective-permute-start(bf16[1024,256]{1,0:T(8,128)(2,1)S(1)} %constant_dynamic-update-slice_fusion.unused_ref.refs_1_.refs_6_), channel_id=1, source_target_pairs={{0,64},{1,65},{2,66},{3,67},{4,68},{5,69},{6,70},{7,71},{8,72},{10... | collective-permute-start | bytes 1572872 | tf_op jit(solution)/shard_map/ppermute | solution.py:68
  37.8 4.1 %all-to-all-start = ((bf16[32,64,128]{2,1,0:T(8,128)(2,1)}), bf16[32,64,128]{2,1,0:T(8,128)(2,1)S(1)}, u32[]{:S(2)}, u32[]{:S(2)}) async-start(bf16[32,64,128]{2,1,0:T(8,128)(2,1)} %pieces.1), calls=%async_computation | async-start | bytes 1048576 | tf_op jit(solution)/shard_map/all_to_all | solution.py:444
  42.0 4.4 %collective-permute-start.10 = (bf16[1024,256]{1,0:T(8,128)(2,1)S(1)}, bf16[1024,256]{1,0:T(8,128)(2,1)S(1)}, u32[]{:S(2)}, u32[]{:S(2)}) collective-permute-start(bf16[1024,256]{1,0:T(8,128)(2,1)S(1)} %constant_dynamic-update-slice_fusion.4.refs_0_.refs_5_), channel_id=1, source_target_pairs={{0,192},{1,193},{2,194},{3,195},{4,196},{5,197},{6,198},{7,199},{8... | collective-permute-start | bytes 1572872 | tf_op jit(solution)/shard_map/ppermute | solution.py:68
  46.4 1.9 collective-permute-start.7
  51.0 4.6 %collective-permute-start.13 = (bf16[1024,256]{1,0:T(8,128)(2,1)S(1)}, bf16[1024,256]{1,0:T(8,128)(2,1)S(1)}, u32[]{:S(2)}, u32[]{:S(2)}) collective-permute-start(bf16[1024,256]{1,0:T(8,128)(2,1)S(1)} %constant_dynamic-update-slice_fusion.unused_ref.refs_1_.refs_6_), channel_id=1, source_target_pairs={{0,192},{1,193},{2,194},{3,195},{4,196},{5,197},{6,198},{7,199},{8... | collective-permute-start | bytes 1572872 | tf_op jit(solution)/shard_map/ppermute | solution.py:68
  55.6 1.9 collective-permute-start.12
  57.5 4.7 %collective-permute-start.11 = (bf16[1024,256]{1,0:T(8,128)(2,1)S(1)}, bf16[1024,256]{1,0:T(8,128)(2,1)}, u32[]{:S(2)}, u32[]{:S(2)}) collective-permute-start(bf16[1024,256]{1,0:T(8,128)(2,1)S(1)} %collective-permute-done.10.refs_0_.refs_9_), channel_id=1, source_target_pairs={{0,192},{1,193},{2,194},{3,195},{4,196},{5,197},{6,198},{7,199},{8... | collective-permute-start | bytes 1572872 | tf_op jit(solution)/shard_map/ppermute | solution.py:68
  62.9 1.7 pad_maximum_fusion.refs_4_
  65.7 12.4 %part.2 = (f32[2048,128]{1,0:T(8,128)S(1)}, f32[2048,128]{1,0:T(8,128)S(1)}, f32[2048,128]{1,0:T(8,128)S(1)}, bf16[272,640]{1,0:T(8,128)(2,1)S(1)}) custom-call(s32[64]{0:T(128)S(1)} %dynamic-slice_bitcast_fusion.row_ref, s32[1]{0:T(128)S(6)} %copy.18.offset_ref, bf16[32,64,128]{2,1,0:T(8,128)(2,1)S(1)} %all-to-all-done.pieces_ref, ...), custom_call_target="tpu_custom_call" | custom-call | tf_op jit(solution)/shard_map/part/pallas_call | solution.py:331
  78.1 3.5 %part.3 = (f32[2048,128]{1,0:T(8,128)S(1)}, f32[2048,128]{1,0:T(8,128)S(1)}) custom-call(s32[64]{0:T(128)S(1)} %dynamic-slice_bitcast_fusion.row_ref, s32[1]{0:T(128)S(6)} %copy.18.offset_ref, bf16[32,64,128]{2,1,0:T(8,128)(2,1)S(1)} %all-to-all-done.pieces_ref, bf16[1024,256]{1,0:T(8,128)(2,1)S(1)} %collective-permute-done.10.refs_0_.refs_9_, ...), custom_call_target="tpu_custom_call" | custom-call | tf_op jit(solution)/shard_map/part/pallas_call | solution.py:331
  81.7 6.5 %collective-permute-done.9.refs_11_ = bf16[272,640]{1,0:T(8,128)(2,1)S(1)} collective-permute-done((bf16[272,640]{1,0:T(8,128)(2,1)S(1)}, bf16[272,640]{1,0:T(8,128)(2,1)S(1)}, u32[]{:S(2)}, u32[]{:S(2)}) %collective-permute-start.9) | collective-permute-done | bytes 348192 | tf_op jit(solution)/shard_map/ppermute | solution.py:68
  88.2 82.5 %far.1 = bf16[32,64,128]{2,1,0:T(8,128)(2,1)S(1)} custom-call(s32[64]{0:T(128)S(1)} %dynamic-slice_bitcast_fusion.row_ref, s32[1]{0:T(128)S(6)} %copy.18.offset_ref, bf16[32,64,128]{2,1,0:T(8,128)(2,1)S(1)} %all-to-all-done.pieces_ref, bf16[1024,256]{1,0:T(8,128)(2,1)} %collective-permute-done.11.refs_0_, bf16[1024,256]{1,0:T(8,128)(2,1)} %collective-permute-done.12.refs_1_, ...), custom_call_target="tpu_custom_call" | custom-call | tf_op jit(solution)/shard_map/far/pallas_call | solution.py:352
  170.7 16.9 %all_to_all.10.parts_ref = bf16[32,64,128]{2,1,0:T(8,128)(2,1)S(1)} all-to-all(bf16[32,64,128]{2,1,0:T(8,128)(2,1)S(1)} %far.1), channel_id=1, replica_groups=mesh['tm'=32,'head'=8] {'tm'}, dimensions={0} | all-to-all | bytes 1048576 | tf_op jit(solution)/shard_map/all_to_all | solution.py:462
  188.7 12.9 %collective-permute-start.14 = (bf16[1,256,640]{2,1,0:T(8,128)(2,1)S(1)}, bf16[1,256,640]{2,1,0:T(8,128)(2,1)S(1)}, u32[]{:S(2)}, u32[]{:S(2)}) collective-permute-start(bf16[1,256,640]{2,1,0:T(8,128)(2,1)S(1)} %get-tuple-element.36), channel_id=1, source_target_pairs={{0,1},{1,0},{2,3},{3,2},{4,5},{5,4},{6,7},{7,6},{8,9},{9,8},{10,11... | collective-permute-start | bytes 983048 | tf_op jit(solution)/shard_map/ppermute | solution.py:68
  202.9 1.6 project.7
  206.4 1.5 collective-permute-start.16
  207.9 4.2 %collective-permute-done.15.refs_0_ = bf16[128,640]{1,0:T(8,128)(2,1)S(1)} collective-permute-done((bf16[128,640]{1,0:T(8,128)(2,1)S(1)}, bf16[128,640]{1,0:T(8,128)(2,1)S(1)}, u32[]{:S(2)}, u32[]{:S(2)}) %collective-permute-start.15) | collective-permute-done | bytes 163872 | tf_op jit(solution)/shard_map/ppermute | solution.py:68
  212.1 1.6 project.6
  215.1 1.8 collective-permute-start.19
  217.1 6.5 %collective-permute-done.18 = bf16[256,640]{1,0:T(8,128)(2,1)S(1)} collective-permute-done((bf16[256,640]{1,0:T(8,128)(2,1)S(1)}, bf16[256,640]{1,0:T(8,128)(2,1)S(1)}, u32[]{:S(2)}, u32[]{:S(2)}) %collective-permute-start.18) | collective-permute-done | bytes 327712 | tf_op jit(solution)/shard_map/ppermute | solution.py:68
  (67 shorter events, 19.2 us)
Async XLA Ops:
  0.0 216.9 %copy-start = (bf16[256,640]{1,0:T(8,128)(2,1)S(1)}, bf16[256,640]{1,0:T(8,128)(2,1)}, u32[]{:S(2)}) copy-start(bf16[256,640]{1,0:T(8,128)(2,1)} %param.15) | copy-start | bytes 983044
  3.6 21.9 %collective-permute-start = (bf16[256,256]{1,0:T(8,128)(2,1)S(1)}, bf16[256,256]{1,0:T(8,128)(2,1)S(1)}, u32[]{:S(2)}, u32[]{:S(2)}) collective-permute-start(bf16[256,256]{1,0:T(8,128)(2,1)S(1)} %get-tuple-element.21), channel_id=1, source_target_pairs={{0,24},{2,26},{4,28},{6,30},{8,32},{9,33},{10,34},{11,35},{12,36},... | collective-permute-start | bytes 393224 | tf_op jit(solution)/shard_map/ppermute | solution.py:68
  4.9 22.0 %collective-permute-start.1 = (bf16[256,256]{1,0:T(8,128)(2,1)S(1)}, bf16[256,256]{1,0:T(8,128)(2,1)S(1)}, u32[]{:S(2)}, u32[]{:S(2)}) collective-permute-start(bf16[256,256]{1,0:T(8,128)(2,1)S(1)} %get-tuple-element.22), channel_id=1, source_target_pairs={{1,41},{3,43},{5,45},{7,47},{8,48},{10,50},{12,52},{14,54},{17,57}... | collective-permute-start | bytes 393224 | tf_op jit(solution)/shard_map/ppermute | solution.py:68
  14.8 17.4 %collective-permute-start.2 = (bf16[256,256]{1,0:T(8,128)(2,1)S(1)}, bf16[256,256]{1,0:T(8,128)(2,1)S(1)}, u32[]{:S(2)}, u32[]{:S(2)}) collective-permute-start(bf16[256,256]{1,0:T(8,128)(2,1)S(1)} %get-tuple-element.23), channel_id=1, source_target_pairs={{1,17},{3,19},{5,21},{7,23},{8,24},{10,26},{12,28},{14,30},{16,32}... | collective-permute-start | bytes 393224 | tf_op jit(solution)/shard_map/ppermute | solution.py:68
  17.9 14.3 %collective-permute-start.3 = (bf16[256,256]{1,0:T(8,128)(2,1)S(1)}, bf16[256,256]{1,0:T(8,128)(2,1)S(1)}, u32[]{:S(2)}, u32[]{:S(2)}) collective-permute-start(bf16[256,256]{1,0:T(8,128)(2,1)S(1)} %get-tuple-element.24), channel_id=1, source_target_pairs={{0,48},{2,50},{4,52},{6,54},{9,57},{11,59},{13,61},{15,63},{16,0},... | collective-permute-start | bytes 393224 | tf_op jit(solution)/shard_map/ppermute | solution.py:68
  19.2 22.7 %collective-permute-start.4 = (bf16[256,256]{1,0:T(8,128)(2,1)S(1)}, bf16[256,256]{1,0:T(8,128)(2,1)S(1)}, u32[]{:S(2)}, u32[]{:S(2)}) collective-permute-start(bf16[256,256]{1,0:T(8,128)(2,1)S(1)} %get-tuple-element.26), channel_id=1, source_target_pairs={{0,32},{1,33},{2,34},{3,35},{4,36},{5,37},{6,38},{7,39},{9,41},{11... | collective-permute-start | bytes 393224 | tf_op jit(solution)/shard_map/ppermute | solution.py:68
  25.6 16.3 %collective-permute-start.5 = (bf16[256,256]{1,0:T(8,128)(2,1)S(1)}, bf16[256,256]{1,0:T(8,128)(2,1)S(1)}, u32[]{:S(2)}, u32[]{:S(2)}) collective-permute-start(bf16[256,256]{1,0:T(8,128)(2,1)S(1)} %get-tuple-element.27), channel_id=1, source_target_pairs={{0,8},{2,10},{4,12},{6,14},{9,17},{11,19},{13,21},{15,23},{16,24},... | collective-permute-start | bytes 393224 | tf_op jit(solution)/shard_map/ppermute | solution.py:68
  26.9 15.0 %collective-permute-start.6 = (bf16[256,256]{1,0:T(8,128)(2,1)S(1)}, bf16[256,256]{1,0:T(8,128)(2,1)S(1)}, u32[]{:S(2)}, u32[]{:S(2)}) collective-permute-start(bf16[256,256]{1,0:T(8,128)(2,1)S(1)} %get-tuple-element.28), channel_id=1, source_target_pairs={{1,57},{3,59},{5,61},{7,63},{8,0},{9,1},{10,2},{11,3},{12,4},{13,5... | collective-permute-start | bytes 393224 | tf_op jit(solution)/shard_map/ppermute | solution.py:68
  32.2 23.4 %collective-permute-start.8 = (bf16[1024,256]{1,0:T(8,128)(2,1)S(1)}, bf16[1024,256]{1,0:T(8,128)(2,1)S(1)}, u32[]{:S(2)}, u32[]{:S(2)}) collective-permute-start(bf16[1024,256]{1,0:T(8,128)(2,1)S(1)} %constant_dynamic-update-slice_fusion.unused_ref.refs_1_.refs_6_), channel_id=1, source_target_pairs={{0,64},{1,65},{2,66},{3,67},{4,68},{5,69},{6,70},{7,71},{8,72},{10... | collective-permute-start | bytes 1572872 | tf_op jit(solution)/shard_map/ppermute | solution.py:68
  37.8 26.9 %all-to-all-start = ((bf16[32,64,128]{2,1,0:T(8,128)(2,1)}), bf16[32,64,128]{2,1,0:T(8,128)(2,1)S(1)}, u32[]{:S(2)}, u32[]{:S(2)}) async-start(bf16[32,64,128]{2,1,0:T(8,128)(2,1)} %pieces.1), calls=%async_computation | async-start | bytes 1048576 | tf_op jit(solution)/shard_map/all_to_all | solution.py:444
  42.0 15.6 %collective-permute-start.10 = (bf16[1024,256]{1,0:T(8,128)(2,1)S(1)}, bf16[1024,256]{1,0:T(8,128)(2,1)S(1)}, u32[]{:S(2)}, u32[]{:S(2)}) collective-permute-start(bf16[1024,256]{1,0:T(8,128)(2,1)S(1)} %constant_dynamic-update-slice_fusion.4.refs_0_.refs_5_), channel_id=1, source_target_pairs={{0,192},{1,193},{2,194},{3,195},{4,196},{5,197},{6,198},{7,199},{8... | collective-permute-start | bytes 1572872 | tf_op jit(solution)/shard_map/ppermute | solution.py:68
  46.4 18.3 %collective-permute-start.7 = (bf16[1024,256]{1,0:T(8,128)(2,1)S(1)}, bf16[1024,256]{1,0:T(8,128)(2,1)}, u32[]{:S(2)}, u32[]{:S(2)}) collective-permute-start(bf16[1024,256]{1,0:T(8,128)(2,1)S(1)} %constant_dynamic-update-slice_fusion.4.refs_0_.refs_5_), channel_id=1, source_target_pairs={{0,64},{1,65},{2,66},{3,67},{4,68},{5,69},{6,70},{7,71},{8,72},{10... | collective-permute-start | bytes 1572872 | tf_op jit(solution)/shard_map/ppermute | solution.py:68
  51.0 27.1 %collective-permute-start.13 = (bf16[1024,256]{1,0:T(8,128)(2,1)S(1)}, bf16[1024,256]{1,0:T(8,128)(2,1)S(1)}, u32[]{:S(2)}, u32[]{:S(2)}) collective-permute-start(bf16[1024,256]{1,0:T(8,128)(2,1)S(1)} %constant_dynamic-update-slice_fusion.unused_ref.refs_1_.refs_6_), channel_id=1, source_target_pairs={{0,192},{1,193},{2,194},{3,195},{4,196},{5,197},{6,198},{7,199},{8... | collective-permute-start | bytes 1572872 | tf_op jit(solution)/shard_map/ppermute | solution.py:68
  55.6 26.1 %collective-permute-start.12 = (bf16[1024,256]{1,0:T(8,128)(2,1)S(1)}, bf16[1024,256]{1,0:T(8,128)(2,1)}, u32[]{:S(2)}, u32[]{:S(2)}) collective-permute-start(bf16[1024,256]{1,0:T(8,128)(2,1)S(1)} %collective-permute-done.8.refs_3_.refs_8_), channel_id=1, source_target_pairs={{0,64},{1,65},{2,66},{3,67},{4,68},{5,69},{6,70},{7,71},{8,72},{10... | collective-permute-start | bytes 1572872 | tf_op jit(solution)/shard_map/ppermute | solution.py:68
  57.5 24.1 %collective-permute-start.11 = (bf16[1024,256]{1,0:T(8,128)(2,1)S(1)}, bf16[1024,256]{1,0:T(8,128)(2,1)}, u32[]{:S(2)}, u32[]{:S(2)}) collective-permute-start(bf16[1024,256]{1,0:T(8,128)(2,1)S(1)} %collective-permute-done.10.refs_0_.refs_9_), channel_id=1, source_target_pairs={{0,192},{1,193},{2,194},{3,195},{4,196},{5,197},{6,198},{7,199},{8... | collective-permute-start | bytes 1572872 | tf_op jit(solution)/shard_map/ppermute | solution.py:68
  78.0 10.1 %collective-permute-start.9 = (bf16[272,640]{1,0:T(8,128)(2,1)S(1)}, bf16[272,640]{1,0:T(8,128)(2,1)S(1)}, u32[]{:S(2)}, u32[]{:S(2)}) collective-permute-start(bf16[272,640]{1,0:T(8,128)(2,1)S(1)} %get-tuple-element.29), channel_id=1, source_target_pairs={{0,8},{1,9},{2,10},{3,11},{4,12},{5,13},{6,14},{7,15},{8,16},{9,17... | collective-permute-start | bytes 1044488 | tf_op jit(solution)/shard_map/ppermute | solution.py:68
  78.1 109.5 %slice-start = ((s8[6553600]{0:T(1024)(128)(4,1)}), s8[4194304]{0:T(1024)(128)(4,1)S(1)}, s32[]{:S(2)}) async-start(s8[6553600]{0:T(1024)(128)(4,1)} %bitcast.43), calls=%async_computation.2 | async-start | bytes 8388608
  88.2 99.4 %slice-start.1 = ((s8[6553600]{0:T(1024)(128)(4,1)}), s8[2359296]{0:T(1024)(128)(4,1)S(1)}, s32[]{:S(2)}) async-start(s8[6553600]{0:T(1024)(128)(4,1)} %bitcast.43), calls=%async_computation.3 | async-start | bytes 4718592
  188.7 14.2 %collective-permute-start.14 = (bf16[1,256,640]{2,1,0:T(8,128)(2,1)S(1)}, bf16[1,256,640]{2,1,0:T(8,128)(2,1)S(1)}, u32[]{:S(2)}, u32[]{:S(2)}) collective-permute-start(bf16[1,256,640]{2,1,0:T(8,128)(2,1)S(1)} %get-tuple-element.36), channel_id=1, source_target_pairs={{0,1},{1,0},{2,3},{3,2},{4,5},{5,4},{6,7},{7,6},{8,9},{9,8},{10,11... | collective-permute-start | bytes 983048 | tf_op jit(solution)/shard_map/ppermute | solution.py:68
  204.5 9.2 %collective-permute-start.17 = (bf16[3,256,640]{2,1,0:T(8,128)(2,1)S(1)}, bf16[3,256,640]{2,1,0:T(8,128)(2,1)S(1)}, u32[]{:S(2)}, u32[]{:S(2)}) collective-permute-start(bf16[3,256,640]{2,1,0:T(8,128)(2,1)S(1)} %project.7), channel_id=1, source_target_pairs={{0,1},{1,0},{2,3},{3,2},{4,5},{5,4},{6,7},{7,6},{8,9},{9,8},{10,11... | collective-permute-start | bytes 2949128 | tf_op jit(solution)/shard_map/ppermute | solution.py:68
  205.0 7.1 %collective-permute-start.15 = (bf16[128,640]{1,0:T(8,128)(2,1)S(1)}, bf16[128,640]{1,0:T(8,128)(2,1)S(1)}, u32[]{:S(2)}, u32[]{:S(2)}) collective-permute-start(bf16[128,640]{1,0:T(8,128)(2,1)S(1)} %get-tuple-element.40), channel_id=1, source_target_pairs={{0,2},{1,3},{2,4},{3,5},{4,6},{5,7},{6,0},{7,1},{8,10},{9,11},{10,... | collective-permute-start | bytes 491528 | tf_op jit(solution)/shard_map/ppermute | solution.py:68
  206.4 5.7 %collective-permute-start.16 = (bf16[128,640]{1,0:T(8,128)(2,1)S(1)}, bf16[128,640]{1,0:T(8,128)(2,1)S(1)}, u32[]{:S(2)}, u32[]{:S(2)}) collective-permute-start(bf16[128,640]{1,0:T(8,128)(2,1)S(1)} %get-tuple-element.39), channel_id=1, source_target_pairs={{0,6},{1,7},{2,0},{3,1},{4,2},{5,3},{6,4},{7,5},{8,14},{9,15},{10,... | collective-permute-start | bytes 491528 | tf_op jit(solution)/shard_map/ppermute | solution.py:68
  214.0 9.6 %collective-permute-start.18 = (bf16[256,640]{1,0:T(8,128)(2,1)S(1)}, bf16[256,640]{1,0:T(8,128)(2,1)S(1)}, u32[]{:S(2)}, u32[]{:S(2)}) collective-permute-start(bf16[256,640]{1,0:T(8,128)(2,1)S(1)} %pad_maximum_fusion.1), channel_id=1, source_target_pairs={{0,2},{1,3},{2,4},{3,5},{4,6},{5,7},{6,0},{7,1},{8,10},{9,11},{10,... | collective-permute-start | bytes 983048 | tf_op jit(solution)/shard_map/ppermute | solution.py:68
  215.1 8.5 %collective-permute-start.19 = (bf16[256,640]{1,0:T(8,128)(2,1)S(1)}, bf16[256,640]{1,0:T(8,128)(2,1)S(1)}, u32[]{:S(2)}, u32[]{:S(2)}) collective-permute-start(bf16[256,640]{1,0:T(8,128)(2,1)S(1)} %pad_maximum_fusion.2), channel_id=1, source_target_pairs={{0,6},{1,7},{2,0},{3,1},{4,2},{5,3},{6,4},{7,5},{8,14},{9,15},{10,... | collective-permute-start | bytes 983048 | tf_op jit(solution)/shard_map/ppermute | solution.py:68
  (4 other events, 3.9 us)

commit v9 on v8

--- a/solution.py
+++ b/solution.py
@@ -84,11 +84,20 @@
     return jax.ShapeDtypeStruct(dims, dtype)
 
 
-def pack_kernel(row_ref, key_ref, value_ref, *refs):
+def pack_kernel(key_ref, value_ref, *refs):
     outs, copied = refs[:Z], refs[Z]
+    z = lax.rem(lax.axis_index("tm"), Z)
+    core = lax.rem(lax.axis_index("head"), C)
+
+    hosted = [sum((HOST[c].index(to_z) + 8) << (4 * to_z) for to_z in HOST[c]) for c in range(C)]
+    hosted = [have - (1 << 32) if have >= 1 << 31 else have for have in hosted]
+    hosted = jnp.where(core == 0, jnp.int32(hosted[0]), jnp.int32(hosted[1]))
+    heads = [
+        lax.shift_right_logical(hosted, 4 * lax.rem(z + shift, Z)) & 15 for shift in SHIFTS
+    ]
 
     def copies(i):
-        columns = pl.ds(pl.multiple_of(row_ref[SEND + i] * HEAD_DIM, HEAD_DIM), HEAD_DIM)
+        columns = pl.ds(pl.multiple_of((heads[i] & 7) * HEAD_DIM, HEAD_DIM), HEAD_DIM)
         return [
             pltpu.make_async_copy(
                 ref.at[:, columns], outs[i].at[:, pl.ds(n * HEAD_DIM, HEAD_DIM)], copied.at[i, n]
@@ -98,29 +107,29 @@
 
     for i in range(Z):
 
-        @pl.when(row_ref[SEND + i] >= 0)
+        @pl.when(heads[i] >= 8)
         def _():
             for copy in copies(i):
                 copy.start()
 
     for i in range(Z):
 
-        @pl.when(row_ref[SEND + i] >= 0)
+        @pl.when(heads[i] >= 8)
         def _():
             for copy in copies(i):
                 copy.wait()
 
 
-def pack(row, key_rows, value_rows):
+def pack(key_rows, value_rows):
     return pl.pallas_call(
         pack_kernel,
         out_shape=[shape(SPAN, 2 * HEAD_DIM)] * Z,
-        in_specs=[in_smem()] + [pl.BlockSpec(memory_space=pltpu.HBM)] * 2,
+        in_specs=[anywhere()] * 2,
         out_specs=[in_vmem()] * Z,
         scratch_shapes=[pltpu.SemaphoreType.DMA((Z, 2))],
         compiler_params=pltpu.CompilerParams(vmem_limit_bytes=8 * MIB),
         name="pack",
-    )(row, key_rows, value_rows)
+    )(key_rows, value_rows)
 
 
 def pieces_kernel(row_ref, query_ref, unused_ref, pieces_ref):
@@ -153,6 +162,8 @@
 TILE_ROWS = TILE * PIECE
 ROWS = SPANS * PIECE
 SMALLEST, LARGEST = 1e-18, 1e30
+HALF_FREQ = 128
+BELOW = 16
 
 
 def attend_kernel(places, begins, ends, row_ref, offset_ref, pieces_ref, *refs):
@@ -164,10 +175,21 @@
         refs = refs[len(refs) - 7 :]
         out_ref, held, rows, total_ref, summed_ref, keys_at, copied = refs
     elif begins:
-        passed, refs = refs[0], refs[1:]
-        total_ref, summed_ref, shift_ref, passed_on, held, rows, keys_at, copied, passing = refs
-        pass_on = pltpu.make_async_copy(passed, passed_on, passing)
-        pass_on.start()
+        (residual_ref, level_ref, table_ref), refs = refs[:3], refs[3:]
+        total_ref, summed_ref, shift_ref, passed_on, held, rows, keys_at, copied = refs[:8]
+        below, passing = refs[8:]
+        pass_on = [
+            pltpu.make_async_copy(residual_ref, passed_on.at[pl.ds(0, SPAN)], passing.at[0]),
+            pltpu.make_async_copy(below, passed_on.at[pl.ds(SPAN, BELOW)], passing.at[1]),
+        ]
+        pass_on[0].start()
+        steps_of = lax.broadcasted_iota(jnp.int32, (BELOW, HEAD_DIM), 1).astype(jnp.float32)
+        stamp = table_ref[level_ref[0]].astype(jnp.float32)
+        angles = stamp * jnp.exp(-math.log(10000.0) * steps_of / HALF_FREQ)
+        below[:, :HALF_FREQ] = jnp.cos(angles).astype(jnp.bfloat16)
+        below[:, HALF_FREQ : 2 * HALF_FREQ] = jnp.sin(angles).astype(jnp.bfloat16)
+        below[:, 2 * HALF_FREQ :] = jnp.zeros_like(below[:, 2 * HALF_FREQ :])
+        pass_on[1].start()
     else:
         total_ref, summed_ref, held, rows, keys_at, copied = refs
     offset = offset_ref[0]
@@ -231,7 +253,7 @@
     def _():
         steps = len(places)
         for i, source in enumerate(sources):
-            pltpu.make_async_copy(source, held.at[i], copied).start()
+            pltpu.make_async_copy(source, held.at[i], copied.at[i]).start()
         for span in range(SPANS):
             at = pl.ds(pl.multiple_of(place_of(span) * PIECE, PIECE), PIECE)
             rows[at, :] = pieces_ref[span]
@@ -242,10 +264,12 @@
         else:
             total_ref[...] = total_in[...]
             summed_ref[...] = summed_in[...]
-        brought = held.at[pl.ds(0, steps)]
-        pltpu.make_async_copy(brought, brought, copied).wait()
+
+        def wait_for(i):
+            pltpu.make_async_copy(held.at[i], held.at[i], copied.at[i]).wait()
 
         if begins:
+            wait_for(0)
             for tile in range(TILES):
                 at = slice(tile * TILE_ROWS, (tile + 1) * TILE_ROWS)
                 top = jnp.max(
@@ -271,7 +295,12 @@
             summed_ref[at, :] += values_of(weights, held[i, :, HEAD_DIM:])
 
         def one(n, unused):
-            tile, i = lax.div(n, steps), lax.rem(n, steps)
+            i, tile = lax.div(n, TILES), lax.rem(n, TILES)
+
+            @pl.when((tile == 0) & (i >= int(begins)))
+            def _():
+                wait_for(i)
+
             found = [keys_at[i, u] for u in range(STEP)]
             lowest = functools.reduce(jnp.minimum, found)
             highest = functools.reduce(jnp.maximum, found)
@@ -305,16 +334,17 @@
 
             @pl.when(jnp.logical_not(safe))
             def _():
-                for i, source in enumerate(later_steps):
-                    pltpu.make_async_copy(source, held.at[steps + i], copied).start()
-                brought = held.at[pl.ds(steps, STEPS - steps)]
-                pltpu.make_async_copy(brought, brought, copied).wait()
+                for i, source in enumerate(later_steps, steps):
+                    pltpu.make_async_copy(source, held.at[i], copied.at[i]).start()
+                for i in range(steps, STEPS):
+                    wait_for(i)
                 note_places(steps, BEHIND + AHEAD)
                 for tile in range(TILES):
                     put(tile, running(tile))
 
     if begins:
-        pass_on.wait()
+        for copy in pass_on:
+            copy.wait()
 
 
 BEHIND = ((0, 0), (0, 1), (1, 0), (1, 1))
@@ -322,40 +352,43 @@
 FAR = ((2, 0), (2, 1))
 
 
-def attend_part(places, row, offset, pieces, sources, state=(), passed=None):
+def attend_part(places, row, offset, pieces, sources, state=(), residual=None, level=None, table=None):
     held = shape(ROWS, HEAD_DIM, dtype=jnp.float32)
     begins = not state
     out_specs, outs = [in_vmem()] * 2, [held] * 2
+    scratch = [
+        pltpu.VMEM((len(sources), STEP_KEYS, 2 * HEAD_DIM), jnp.bfloat16),
+        pltpu.VMEM((ROWS, HEAD_DIM), jnp.bfloat16),
+        pltpu.SMEM((STEPS, STEP), jnp.int32),
+        pltpu.SemaphoreType.DMA((STEPS,)),
+    ]
     if begins:
-        out_specs, outs = out_specs + [in_vmem(), anywhere()], outs + [held, shape(*passed.shape)]
+        wide = residual.shape[1]
+        out_specs = out_specs + [in_vmem(), anywhere()]
+        outs = outs + [held, shape(SPAN + BELOW, wide)]
+        scratch += [pltpu.VMEM((BELOW, wide), jnp.bfloat16), pltpu.SemaphoreType.DMA((2,))]
     found = pl.pallas_call(
         functools.partial(attend_kernel, places, begins, False),
         out_shape=outs,
         in_specs=[in_smem(), in_smem(), in_vmem()]
         + [anywhere()] * len(sources)
-        + ([anywhere()] if begins else [in_vmem()] * len(state)),
+        + ([anywhere(), in_smem(), in_smem()] if begins else [in_vmem()] * len(state)),
         out_specs=out_specs,
-        scratch_shapes=[
-            pltpu.VMEM((len(sources), STEP_KEYS, 2 * HEAD_DIM), jnp.bfloat16),
-            pltpu.VMEM((ROWS, HEAD_DIM), jnp.bfloat16),
-            pltpu.SMEM((STEPS, STEP), jnp.int32),
-            pltpu.SemaphoreType.DMA,
-        ]
-        + [pltpu.SemaphoreType.DMA] * begins,
+        scratch_shapes=scratch,
         compiler_params=pltpu.CompilerParams(vmem_limit_bytes=28 * MIB),
         name="part",
-    )(row, offset, pieces, *sources, *((passed,) if begins else state))
+    )(row, offset, pieces, *sources, *((residual, level, table) if begins else state))
     return found if begins else [*found, state[2]]
 
 
-def attend_far(row, offset, pieces, far, state, near, others):
+def attend_far(row, offset, pieces, far, state, near):
     return pl.pallas_call(
         functools.partial(attend_kernel, FAR, False, True),
         out_shape=shape(SPANS, PIECE, HEAD_DIM),
         in_specs=[in_smem(), in_smem(), in_vmem()]
         + [anywhere()] * len(far)
         + [in_vmem()] * len(state)
-        + [anywhere()] * (len(near) + len(others)),
+        + [anywhere()] * len(near),
         out_specs=in_vmem(),
         scratch_shapes=[
             pltpu.VMEM((STEPS, STEP_KEYS, 2 * HEAD_DIM), jnp.bfloat16),
@@ -363,27 +396,15 @@
             pltpu.VMEM((ROWS, HEAD_DIM), jnp.float32),
             pltpu.VMEM((ROWS, HEAD_DIM), jnp.float32),
             pltpu.SMEM((STEPS, STEP), jnp.int32),
-            pltpu.SemaphoreType.DMA,
+            pltpu.SemaphoreType.DMA((STEPS,)),
         ],
         compiler_params=pltpu.CompilerParams(vmem_limit_bytes=28 * MIB),
         name="far",
-    )(row, offset, pieces, *far, *state, *near, *others)
-
-
-def project_kernel(other, places, waits, row_ref, parts_ref, weight_ref, *refs):
-    refs = refs[waits:]
-    out_ref = refs[0]
+    )(row, offset, pieces, *far, *state, *near)
+
+
+def share_of(row_ref, rows, weight_ref, out_ref, other, places):
     wide = out_ref.shape[2]
-    if len(refs) > 1:
-        rows_ref = refs[1]
-        for head in range(HERE):
-            for x in range(X):
-                rows_ref[x * PIECE : (x + 1) * PIECE, head * HEAD_DIM : (head + 1) * HEAD_DIM] = (
-                    parts_ref[x * Z + row_ref[PLANE + head]]
-                )
-        rows = rows_ref[...]
-    else:
-        rows = parts_ref[...]
     core = 1 - row_ref[CORE] if other else row_ref[CORE]
     for n, m in enumerate(places):
         block = lax.rem(row_ref[PLACE_Y] + m, Y) * C + core
@@ -393,30 +414,44 @@
         ).astype(jnp.bfloat16)
 
 
-def project(row, parts, weight, other, places, after=()):
+def first_kernel(row_ref, parts_ref, weight_ref, passed_ref, out_ref, rows_ref, passed_on, passing):
+    pass_on = pltpu.make_async_copy(passed_ref, passed_on, passing)
+    pass_on.start()
+    for head in range(HERE):
+        for x in range(X):
+            rows_ref[x * PIECE : (x + 1) * PIECE, head * HEAD_DIM : (head + 1) * HEAD_DIM] = (
+                parts_ref[x * Z + row_ref[PLANE + head]]
+            )
+    share_of(row_ref, rows_ref[...], weight_ref, out_ref, True, (2,))
+    pass_on.wait()
+
+
+def project_first(row, parts, weight, passed):
     wide = weight.shape[1] // (Y * C)
-    out = shape(len(places), SPAN, wide)
-    rows = shape(SPAN, HERE * HEAD_DIM)
-    whole = parts.ndim == 3
+    return pl.pallas_call(
+        first_kernel,
+        out_shape=[shape(1, SPAN, wide), shape(SPAN, HERE * HEAD_DIM), shape(*passed.shape)],
+        in_specs=[in_smem(), in_vmem(), in_vmem(), in_vmem()],
+        out_specs=[in_vmem()] * 3,
+        scratch_shapes=[pltpu.SemaphoreType.DMA],
+        compiler_params=pltpu.CompilerParams(vmem_limit_bytes=16 * MIB),
+        name="first",
+    )(row, parts, weight, passed)
+
+
+def project_kernel(other, places, waits, row_ref, rows_ref, weight_ref, *refs):
+    share_of(row_ref, rows_ref[...], weight_ref, refs[waits], other, places)
+
+
+def project(row, rows, weight, other, places, after=()):
     return pl.pallas_call(
         functools.partial(project_kernel, other, places, len(after)),
-        out_shape=[out, rows] if whole else out,
+        out_shape=shape(len(places), SPAN, weight.shape[1] // (Y * C)),
         in_specs=[in_smem(), in_vmem(), in_vmem()] + [anywhere()] * len(after),
-        out_specs=[in_vmem(), in_vmem()] if whole else in_vmem(),
+        out_specs=in_vmem(),
         compiler_params=pltpu.CompilerParams(vmem_limit_bytes=16 * MIB),
         name="project",
-    )(row, parts, weight, *after)
-
-
-def embedding_of(level, timestep_table, half_dim):
-    stamp_value = jnp.sum(
-        jnp.where(
-            jnp.arange(timestep_table.shape[0], dtype=jnp.int32) == level, timestep_table, 0
-        )
-    ).astype(jnp.float32)
-    frequency = jnp.exp(-math.log(10000.0) * jnp.arange(half_dim, dtype=jnp.float32) / half_dim)
-    angles = stamp_value * frequency
-    return jnp.concatenate([jnp.cos(angles), jnp.sin(angles)])[None, :].astype(jnp.bfloat16)
+    )(row, rows, weight, *after)
 
 
 def body(
@@ -432,7 +467,7 @@
 ):
     me = lax.axis_index("tm") * (Y * C) + lax.axis_index("head")
     row = lax.dynamic_slice(jnp.asarray(table()), (me, 0), (1, WIDTH))[0]
-    packed = pack(row, key_rows, value_rows)
+    packed = pack(key_rows, value_rows)
     arrived = [
         moved(part, plane_pairs(shift)) if shift else part for part, shift in zip(packed, SHIFTS)
     ]
@@ -444,21 +479,12 @@
     pieces = lax.all_to_all(pieces, "tm", 0, 0, tiled=True)
     far = [moved(ahead[0], across_pairs(-1)), moved(back[1], across_pairs(1))]
 
-    freq_dim = time_proj.shape[0]
-    embedding = embedding_of(levels[0], timestep_table, freq_dim // 2)
-    below = jnp.pad(embedding, ((0, 15), (0, residual_in.shape[1] - freq_dim)))
-    passed = jnp.concatenate([residual_in, below])
-    next_slot = [
-        (device(x, z, y, c), device((x * Z + z + 1) % SPANS // Z, z + 1, y, c)) for x, z, y, c in ALL
-    ]
-    *state, passed = attend_part(BEHIND, row, window_offset, pieces, own + back, passed=passed)
-    passed = moved(passed, next_slot)
-    residual, embedding = passed[:SPAN], passed[SPAN : SPAN + 1, :freq_dim]
-    gate_row = jnp.dot(embedding, time_proj, preferred_element_type=jnp.float32)
-
+    *state, passed = attend_part(
+        BEHIND, row, window_offset, pieces, own + back, (), residual_in, levels, timestep_table
+    )
     state = attend_part(AHEAD, row, window_offset, pieces, ahead, state)
     near = own + back + ahead
-    answers = attend_far(row, window_offset, pieces, far, state, near, [passed])
+    answers = attend_far(row, window_offset, pieces, far, state, near)
     answers = lax.all_to_all(answers, "tm", 0, 0, tiled=True)
 
     swap = [(device(x, z, y, c), device(x, z, y, 1 - c)) for x, z, y, c in ALL]
@@ -472,7 +498,14 @@
             for n in range(len(places))
         ]
 
-    leaving, attention = project(row, answers, out_weight, True, (2,))
+    leaving, attention, passed = project_first(row, answers, out_weight, passed)
+    next_slot = [
+        (device(x, z, y, c), device((x * Z + z + 1) % SPANS // Z, z + 1, y, c)) for x, z, y, c in ALL
+    ]
+    passed = moved(passed, next_slot)
+    residual, embedding = passed[:SPAN], passed[SPAN : SPAN + 1, : time_proj.shape[0]]
+    gate_row = jnp.dot(embedding, time_proj, preferred_element_type=jnp.float32)
+
     (opposite,) = over_cores(leaving, (2,))
     opposite = opposite.astype(jnp.bfloat16)
     half = SPAN // 2

time: 224 us -> 217 us (0.969)
  waiting for transfers between devices: 17.5 us -> 13 us
  other arithmetic: 4.46 us -> 1.3 us
    ppermute x20, waiting for transfers between devices: 17.5 us -> 13 us  [moved(): return lax.ppermute(block, AXES, pairs)]
    pallas_call x4 -> x3, Pallas kernels: 5.26 us -> 4.23 us  [project(): pl.pallas_call(functools.partial(project_kernel, other, places, len(after...]
    unnamed x20 -> x22, local copies, waits for them, and re-layouts: 3.97 us -> 4.68 us
  transfers between devices with their start and end apart: 21 -> 21, of which waited for: 4 -> 5; matrix products, arithmetic and copies ran while one was open for 2% -> 1% of each run, Pallas kernels for 9% -> 10%
where the time goes in v9:
time: 217 us; the launch traced here: 216 us
  Pallas kernels  107 us (49%)
  starting transfers between devices  70.8 us (33%)
  blocking collectives  16.6 us (8%)
  waiting for transfers between devices  13 us (6%)
  local copies, waits for them, and re-layouts  5.47 us (3%)
    pallas_call x1, Pallas kernels, attend_far(): pl.pallas_call(functools.partial(attend_kernel, FAR, False, True), out_sh...  82.3 us
    ppermute x20, starting transfers between devices, moved(): return lax.ppermute(block, AXES, pairs)  66.1 us
    pallas_call x2, Pallas kernels, attend_part(): pl.pallas_call(functools.partial(attend_kernel, places, begins, False), o...  17.8 us
    all_to_all x1, blocking collectives, body(): answers = lax.all_to_all(answers, 'tm', 0, 0, tiled=True)  16.6 us
    ppermute x20, waiting for transfers between devices, moved(): return lax.ppermute(block, AXES, pairs)  13 us
    unnamed x22, local copies, waits for them, and re-layouts  4.68 us
    all_to_all x1, starting transfers between devices, body(): pieces = lax.all_to_all(pieces, 'tm', 0, 0, tiled=True)  4.67 us
  transfers between devices with their start and end apart: 21, of which 5 were waited for; matrix products, arithmetic and copies ran while one was open for 1% of the time, Pallas kernels for 10%

profile of v9, /device:TPU:1, one launch (start us, length us, event | category | flops | bytes accessed | tf_op | source)
XLA Modules:
  0.0 216.4 jit_solution(2955576070361150082)
XLA Ops:
  3.6 9.8 %collective-permute-start.1 = (bf16[256,256]{1,0:T(8,128)(2,1)S(1)}, bf16[256,256]{1,0:T(8,128)(2,1)S(1)}, u32[]{:S(2)}, u32[]{:S(2)}) collective-permute-start(bf16[256,256]{1,0:T(8,128)(2,1)S(1)} %get-tuple-element.23), channel_id=1, source_target_pairs={{1,41},{3,43},{5,45},{7,47},{8,48},{10,50},{12,52},{14,54},{17,57}... | collective-permute-start | bytes 393224 | tf_op jit(solution)/shard_map/ppermute | solution.py:68
  13.5 3.1 %collective-permute-start.2 = (bf16[256,256]{1,0:T(8,128)(2,1)S(1)}, bf16[256,256]{1,0:T(8,128)(2,1)S(1)}, u32[]{:S(2)}, u32[]{:S(2)}) collective-permute-start(bf16[256,256]{1,0:T(8,128)(2,1)S(1)} %get-tuple-element.24), channel_id=1, source_target_pairs={{1,17},{3,19},{5,21},{7,23},{8,24},{10,26},{12,28},{14,30},{16,32}... | collective-permute-start | bytes 393224 | tf_op jit(solution)/shard_map/ppermute | solution.py:68
  17.9 6.4 %collective-permute-start.4 = (bf16[256,256]{1,0:T(8,128)(2,1)S(1)}, bf16[256,256]{1,0:T(8,128)(2,1)S(1)}, u32[]{:S(2)}, u32[]{:S(2)}) collective-permute-start(bf16[256,256]{1,0:T(8,128)(2,1)S(1)} %get-tuple-element.27), channel_id=1, source_target_pairs={{0,32},{1,33},{2,34},{3,35},{4,36},{5,37},{6,38},{7,39},{9,41},{11... | collective-permute-start | bytes 393224 | tf_op jit(solution)/shard_map/ppermute | solution.py:68
  25.6 5.2 %collective-permute-start.6 = (bf16[256,256]{1,0:T(8,128)(2,1)S(1)}, bf16[256,256]{1,0:T(8,128)(2,1)S(1)}, u32[]{:S(2)}, u32[]{:S(2)}) collective-permute-start(bf16[256,256]{1,0:T(8,128)(2,1)S(1)} %get-tuple-element.29), channel_id=1, source_target_pairs={{1,57},{3,59},{5,61},{7,63},{8,0},{9,1},{10,2},{11,3},{12,4},{13,5... | collective-permute-start | bytes 393224 | tf_op jit(solution)/shard_map/ppermute | solution.py:68
  30.9 3.1 %collective-permute-start.9 = (bf16[1024,256]{1,0:T(8,128)(2,1)S(1)}, bf16[1024,256]{1,0:T(8,128)(2,1)S(1)}, u32[]{:S(2)}, u32[]{:S(2)}) collective-permute-start(bf16[1024,256]{1,0:T(8,128)(2,1)S(1)} %constant_dynamic-update-slice_fusion.unused_ref.refs_1_.refs_6_), channel_id=1, source_target_pairs={{0,64},{1,65},{2,66},{3,67},{4,68},{5,69},{6,70},{7,71},{8,72},{10... | collective-permute-start | bytes 1572872 | tf_op jit(solution)/shard_map/ppermute | solution.py:68
  34.1 3.4 %collective-permute-start.7 = (bf16[1024,256]{1,0:T(8,128)(2,1)S(1)}, bf16[1024,256]{1,0:T(8,128)(2,1)S(1)}, u32[]{:S(2)}, u32[]{:S(2)}) collective-permute-start(bf16[1024,256]{1,0:T(8,128)(2,1)S(1)} %constant_dynamic-update-slice_fusion.4.refs_0_.refs_5_), channel_id=1, source_target_pairs={{0,192},{1,193},{2,194},{3,195},{4,196},{5,197},{6,198},{7,199},{8... | collective-permute-start | bytes 1572872 | tf_op jit(solution)/shard_map/ppermute | solution.py:68
  40.6 4.7 %all-to-all-start = ((bf16[32,64,128]{2,1,0:T(8,128)(2,1)}), bf16[32,64,128]{2,1,0:T(8,128)(2,1)S(1)}, u32[]{:S(2)}, u32[]{:S(2)}) async-start(bf16[32,64,128]{2,1,0:T(8,128)(2,1)} %pieces.1), calls=%async_computation | async-start | bytes 1048576 | tf_op jit(solution)/shard_map/all_to_all | solution.py:479
  45.3 3.1 %collective-permute-start.12 = (bf16[1024,256]{1,0:T(8,128)(2,1)S(1)}, bf16[1024,256]{1,0:T(8,128)(2,1)S(1)}, u32[]{:S(2)}, u32[]{:S(2)}) collective-permute-start(bf16[1024,256]{1,0:T(8,128)(2,1)S(1)} %constant_dynamic-update-slice_fusion.4.refs_0_.refs_5_), channel_id=1, source_target_pairs={{0,64},{1,65},{2,66},{3,67},{4,68},{5,69},{6,70},{7,71},{8,72},{10... | collective-permute-start | bytes 1572872 | tf_op jit(solution)/shard_map/ppermute | solution.py:68
  48.4 3.4 %collective-permute-start.11 = (bf16[1024,256]{1,0:T(8,128)(2,1)S(1)}, bf16[1024,256]{1,0:T(8,128)(2,1)}, u32[]{:S(2)}, u32[]{:S(2)}) collective-permute-start(bf16[1024,256]{1,0:T(8,128)(2,1)S(1)} %constant_dynamic-update-slice_fusion.unused_ref.refs_1_.refs_6_), channel_id=1, source_target_pairs={{0,192},{1,193},{2,194},{3,195},{4,196},{5,197},{6,198},{7,199},{8... | collective-permute-start | bytes 1572872 | tf_op jit(solution)/shard_map/ppermute | solution.py:68
  51.8 1.9 collective-permute-start.10
  53.8 4.6 %collective-permute-start.8 = (bf16[1024,256]{1,0:T(8,128)(2,1)S(1)}, bf16[1024,256]{1,0:T(8,128)(2,1)}, u32[]{:S(2)}, u32[]{:S(2)}) collective-permute-start(bf16[1024,256]{1,0:T(8,128)(2,1)S(1)} %collective-permute-done.7.refs_0_.refs_9_), channel_id=1, source_target_pairs={{0,192},{1,193},{2,194},{3,195},{4,196},{5,197},{6,198},{7,199},{8... | collective-permute-start | bytes 1572872 | tf_op jit(solution)/shard_map/ppermute | solution.py:68
  59.6 4.5 %collective-permute-done.12.refs_2_.refs_7_ = bf16[1024,256]{1,0:T(8,128)(2,1)S(1)} collective-permute-done((bf16[1024,256]{1,0:T(8,128)(2,1)S(1)}, bf16[1024,256]{1,0:T(8,128)(2,1)S(1)}, u32[]{:S(2)}, u32[]{:S(2)}) %collective-permute-start.12) | collective-permute-done | bytes 524320 | tf_op jit(solution)/shard_map/ppermute | solution.py:68
  65.7 13.5 %part.2 = (f32[2048,128]{1,0:T(8,128)S(1)}, f32[2048,128]{1,0:T(8,128)S(1)}, f32[2048,128]{1,0:T(8,128)S(1)}, bf16[272,640]{1,0:T(8,128)(2,1)S(1)}) custom-call(s32[64]{0:T(128)S(1)} %dynamic-slice_bitcast_fusion.row_ref, s32[1]{0:T(128)S(6)} %copy.18.offset_ref, bf16[32,64,128]{2,1,0:T(8,128)(2,1)S(1)} %all-to-all-done.pieces_ref, ...), custom_call_target="tpu_custom_call" | custom-call | tf_op jit(solution)/shard_map/part/pallas_call | solution.py:370
  79.2 4.4 %part.3 = (f32[2048,128]{1,0:T(8,128)S(1)}, f32[2048,128]{1,0:T(8,128)S(1)}) custom-call(s32[64]{0:T(128)S(1)} %dynamic-slice_bitcast_fusion.row_ref, s32[1]{0:T(128)S(6)} %copy.18.offset_ref, bf16[32,64,128]{2,1,0:T(8,128)(2,1)S(1)} %all-to-all-done.pieces_ref, bf16[1024,256]{1,0:T(8,128)(2,1)S(1)} %collective-permute-done.7.refs_0_.refs_9_, ...), custom_call_target="tpu_custom_call" | custom-call | tf_op jit(solution)/shard_map/part/pallas_call | solution.py:370
  83.6 82.3 %far.1 = bf16[32,64,128]{2,1,0:T(8,128)(2,1)S(1)} custom-call(s32[64]{0:T(128)S(1)} %dynamic-slice_bitcast_fusion.row_ref, s32[1]{0:T(128)S(6)} %copy.18.offset_ref, bf16[32,64,128]{2,1,0:T(8,128)(2,1)S(1)} %all-to-all-done.pieces_ref, bf16[1024,256]{1,0:T(8,128)(2,1)} %collective-permute-done.8.refs_0_, bf16[1024,256]{1,0:T(8,128)(2,1)} %collective-permute-done.10.refs_1_, ...), custom_call_target="tpu_custom_call" | custom-call | tf_op jit(solution)/shard_map/far/pallas_call | solution.py:385
  165.9 16.6 %all_to_all.10.parts_ref = bf16[32,64,128]{2,1,0:T(8,128)(2,1)S(1)} all-to-all(bf16[32,64,128]{2,1,0:T(8,128)(2,1)S(1)} %far.1), channel_id=1, replica_groups=mesh['tm'=32,'head'=8] {'tm'}, dimensions={0} | all-to-all | bytes 1048576 | tf_op jit(solution)/shard_map/all_to_all | solution.py:488
  183.7 9.7 %collective-permute-start.14 = (bf16[1,256,640]{2,1,0:T(8,128)(2,1)S(1)}, bf16[1,256,640]{2,1,0:T(8,128)(2,1)S(1)}, u32[]{:S(2)}, u32[]{:S(2)}) collective-permute-start(bf16[1,256,640]{2,1,0:T(8,128)(2,1)S(1)} %get-tuple-element.38), channel_id=1, source_target_pairs={{0,1},{1,0},{2,3},{3,2},{4,5},{5,4},{6,7},{7,6},{8,9},{9,8},{10,11... | collective-permute-start | bytes 983048 | tf_op jit(solution)/shard_map/ppermute | solution.py:68
  194.7 1.6 project.5
  199.7 2.4 %collective-permute-start.13 = (bf16[272,640]{1,0:T(8,128)(2,1)S(1)}, bf16[272,640]{1,0:T(8,128)(2,1)S(1)}, u32[]{:S(2)}, u32[]{:S(2)}) collective-permute-start(bf16[272,640]{1,0:T(8,128)(2,1)S(1)} %get-tuple-element.36), channel_id=1, source_target_pairs={{0,8},{1,9},{2,10},{3,11},{4,12},{5,13},{6,14},{7,15},{8,16},{9,17... | collective-permute-start | bytes 1044488 | tf_op jit(solution)/shard_map/ppermute | solution.py:68
  202.1 1.8 collective-permute-done.15.refs_0_
  203.9 1.6 project.4
  206.9 1.8 collective-permute-start.19
  208.7 3.5 %collective-permute-done.13 = bf16[272,640]{1,0:T(8,128)(2,1)S(1)} collective-permute-done((bf16[272,640]{1,0:T(8,128)(2,1)S(1)}, bf16[272,640]{1,0:T(8,128)(2,1)S(1)}, u32[]{:S(2)}, u32[]{:S(2)}) %collective-permute-start.13) | collective-permute-done | bytes 348192 | tf_op jit(solution)/shard_map/ppermute | solution.py:68
  212.3 3.1 %collective-permute-done.18 = bf16[256,640]{1,0:T(8,128)(2,1)S(1)} collective-permute-done((bf16[256,640]{1,0:T(8,128)(2,1)S(1)}, bf16[256,640]{1,0:T(8,128)(2,1)S(1)}, u32[]{:S(2)}, u32[]{:S(2)}) %collective-permute-start.18) | collective-permute-done | bytes 327712 | tf_op jit(solution)/shard_map/ppermute | solution.py:68
  (65 shorter events, 19.4 us)
Async XLA Ops:
  0.0 212.2 %copy-start = (bf16[256,640]{1,0:T(8,128)(2,1)S(1)}, bf16[256,640]{1,0:T(8,128)(2,1)}, u32[]{:S(2)}) copy-start(bf16[256,640]{1,0:T(8,128)(2,1)} %param.15) | copy-start | bytes 983044
  2.3 22.0 %collective-permute-start = (bf16[256,256]{1,0:T(8,128)(2,1)S(1)}, bf16[256,256]{1,0:T(8,128)(2,1)S(1)}, u32[]{:S(2)}, u32[]{:S(2)}) collective-permute-start(bf16[256,256]{1,0:T(8,128)(2,1)S(1)} %get-tuple-element.22), channel_id=1, source_target_pairs={{0,24},{2,26},{4,28},{6,30},{8,32},{9,33},{10,34},{11,35},{12,36},... | collective-permute-start | bytes 393224 | tf_op jit(solution)/shard_map/ppermute | solution.py:68
  3.6 22.0 %collective-permute-start.1 = (bf16[256,256]{1,0:T(8,128)(2,1)S(1)}, bf16[256,256]{1,0:T(8,128)(2,1)S(1)}, u32[]{:S(2)}, u32[]{:S(2)}) collective-permute-start(bf16[256,256]{1,0:T(8,128)(2,1)S(1)} %get-tuple-element.23), channel_id=1, source_target_pairs={{1,41},{3,43},{5,45},{7,47},{8,48},{10,50},{12,52},{14,54},{17,57}... | collective-permute-start | bytes 393224 | tf_op jit(solution)/shard_map/ppermute | solution.py:68
  13.5 17.4 %collective-permute-start.2 = (bf16[256,256]{1,0:T(8,128)(2,1)S(1)}, bf16[256,256]{1,0:T(8,128)(2,1)S(1)}, u32[]{:S(2)}, u32[]{:S(2)}) collective-permute-start(bf16[256,256]{1,0:T(8,128)(2,1)S(1)} %get-tuple-element.24), channel_id=1, source_target_pairs={{1,17},{3,19},{5,21},{7,23},{8,24},{10,26},{12,28},{14,30},{16,32}... | collective-permute-start | bytes 393224 | tf_op jit(solution)/shard_map/ppermute | solution.py:68
  16.6 14.3 %collective-permute-start.3 = (bf16[256,256]{1,0:T(8,128)(2,1)S(1)}, bf16[256,256]{1,0:T(8,128)(2,1)S(1)}, u32[]{:S(2)}, u32[]{:S(2)}) collective-permute-start(bf16[256,256]{1,0:T(8,128)(2,1)S(1)} %get-tuple-element.25), channel_id=1, source_target_pairs={{0,48},{2,50},{4,52},{6,54},{9,57},{11,59},{13,61},{15,63},{16,0},... | collective-permute-start | bytes 393224 | tf_op jit(solution)/shard_map/ppermute | solution.py:68
  17.9 16.2 %collective-permute-start.4 = (bf16[256,256]{1,0:T(8,128)(2,1)S(1)}, bf16[256,256]{1,0:T(8,128)(2,1)S(1)}, u32[]{:S(2)}, u32[]{:S(2)}) collective-permute-start(bf16[256,256]{1,0:T(8,128)(2,1)S(1)} %get-tuple-element.27), channel_id=1, source_target_pairs={{0,32},{1,33},{2,34},{3,35},{4,36},{5,37},{6,38},{7,39},{9,41},{11... | collective-permute-start | bytes 393224 | tf_op jit(solution)/shard_map/ppermute | solution.py:68
  24.3 9.8 %collective-permute-start.5 = (bf16[256,256]{1,0:T(8,128)(2,1)S(1)}, bf16[256,256]{1,0:T(8,128)(2,1)S(1)}, u32[]{:S(2)}, u32[]{:S(2)}) collective-permute-start(bf16[256,256]{1,0:T(8,128)(2,1)S(1)} %get-tuple-element.28), channel_id=1, source_target_pairs={{0,8},{2,10},{4,12},{6,14},{9,17},{11,19},{13,21},{15,23},{16,24},... | collective-permute-start | bytes 393224 | tf_op jit(solution)/shard_map/ppermute | solution.py:68
  25.6 8.5 %collective-permute-start.6 = (bf16[256,256]{1,0:T(8,128)(2,1)S(1)}, bf16[256,256]{1,0:T(8,128)(2,1)S(1)}, u32[]{:S(2)}, u32[]{:S(2)}) collective-permute-start(bf16[256,256]{1,0:T(8,128)(2,1)S(1)} %get-tuple-element.29), channel_id=1, source_target_pairs={{1,57},{3,59},{5,61},{7,63},{8,0},{9,1},{10,2},{11,3},{12,4},{13,5... | collective-permute-start | bytes 393224 | tf_op jit(solution)/shard_map/ppermute | solution.py:68
  30.9 20.9 %collective-permute-start.9 = (bf16[1024,256]{1,0:T(8,128)(2,1)S(1)}, bf16[1024,256]{1,0:T(8,128)(2,1)S(1)}, u32[]{:S(2)}, u32[]{:S(2)}) collective-permute-start(bf16[1024,256]{1,0:T(8,128)(2,1)S(1)} %constant_dynamic-update-slice_fusion.unused_ref.refs_1_.refs_6_), channel_id=1, source_target_pairs={{0,64},{1,65},{2,66},{3,67},{4,68},{5,69},{6,70},{7,71},{8,72},{10... | collective-permute-start | bytes 1572872 | tf_op jit(solution)/shard_map/ppermute | solution.py:68
  34.1 19.6 %collective-permute-start.7 = (bf16[1024,256]{1,0:T(8,128)(2,1)S(1)}, bf16[1024,256]{1,0:T(8,128)(2,1)S(1)}, u32[]{:S(2)}, u32[]{:S(2)}) collective-permute-start(bf16[1024,256]{1,0:T(8,128)(2,1)S(1)} %constant_dynamic-update-slice_fusion.4.refs_0_.refs_5_), channel_id=1, source_target_pairs={{0,192},{1,193},{2,194},{3,195},{4,196},{5,197},{6,198},{7,199},{8... | collective-permute-start | bytes 1572872 | tf_op jit(solution)/shard_map/ppermute | solution.py:68
  40.6 23.5 %all-to-all-start = ((bf16[32,64,128]{2,1,0:T(8,128)(2,1)}), bf16[32,64,128]{2,1,0:T(8,128)(2,1)S(1)}, u32[]{:S(2)}, u32[]{:S(2)}) async-start(bf16[32,64,128]{2,1,0:T(8,128)(2,1)} %pieces.1), calls=%async_computation | async-start | bytes 1048576 | tf_op jit(solution)/shard_map/all_to_all | solution.py:479
  45.3 18.8 %collective-permute-start.12 = (bf16[1024,256]{1,0:T(8,128)(2,1)S(1)}, bf16[1024,256]{1,0:T(8,128)(2,1)S(1)}, u32[]{:S(2)}, u32[]{:S(2)}) collective-permute-start(bf16[1024,256]{1,0:T(8,128)(2,1)S(1)} %constant_dynamic-update-slice_fusion.4.refs_0_.refs_5_), channel_id=1, source_target_pairs={{0,64},{1,65},{2,66},{3,67},{4,68},{5,69},{6,70},{7,71},{8,72},{10... | collective-permute-start | bytes 1572872 | tf_op jit(solution)/shard_map/ppermute | solution.py:68
  48.4 30.7 %collective-permute-start.11 = (bf16[1024,256]{1,0:T(8,128)(2,1)S(1)}, bf16[1024,256]{1,0:T(8,128)(2,1)}, u32[]{:S(2)}, u32[]{:S(2)}) collective-permute-start(bf16[1024,256]{1,0:T(8,128)(2,1)S(1)} %constant_dynamic-update-slice_fusion.unused_ref.refs_1_.refs_6_), channel_id=1, source_target_pairs={{0,192},{1,193},{2,194},{3,195},{4,196},{5,197},{6,198},{7,199},{8... | collective-permute-start | bytes 1572872 | tf_op jit(solution)/shard_map/ppermute | solution.py:68
  51.8 31.7 %collective-permute-start.10 = (bf16[1024,256]{1,0:T(8,128)(2,1)S(1)}, bf16[1024,256]{1,0:T(8,128)(2,1)}, u32[]{:S(2)}, u32[]{:S(2)}) collective-permute-start(bf16[1024,256]{1,0:T(8,128)(2,1)S(1)} %collective-permute-done.9.refs_3_.refs_8_), channel_id=1, source_target_pairs={{0,64},{1,65},{2,66},{3,67},{4,68},{5,69},{6,70},{7,71},{8,72},{10... | collective-permute-start | bytes 1572872 | tf_op jit(solution)/shard_map/ppermute | solution.py:68
  53.8 29.8 %collective-permute-start.8 = (bf16[1024,256]{1,0:T(8,128)(2,1)S(1)}, bf16[1024,256]{1,0:T(8,128)(2,1)}, u32[]{:S(2)}, u32[]{:S(2)}) collective-permute-start(bf16[1024,256]{1,0:T(8,128)(2,1)S(1)} %collective-permute-done.7.refs_0_.refs_9_), channel_id=1, source_target_pairs={{0,192},{1,193},{2,194},{3,195},{4,196},{5,197},{6,198},{7,199},{8... | collective-permute-start | bytes 1572872 | tf_op jit(solution)/shard_map/ppermute | solution.py:68
  79.2 103.3 %slice-start = ((s8[6553600]{0:T(1024)(128)(4,1)}), s8[4194304]{0:T(1024)(128)(4,1)S(1)}, s32[]{:S(2)}) async-start(s8[6553600]{0:T(1024)(128)(4,1)} %bitcast.37), calls=%async_computation.2 | async-start | bytes 8388608
  83.6 98.9 %slice-start.1 = ((s8[6553600]{0:T(1024)(128)(4,1)}), s8[2359296]{0:T(1024)(128)(4,1)S(1)}, s32[]{:S(2)}) async-start(s8[6553600]{0:T(1024)(128)(4,1)} %bitcast.37), calls=%async_computation.3 | async-start | bytes 4718592
  183.7 10.9 %collective-permute-start.14 = (bf16[1,256,640]{2,1,0:T(8,128)(2,1)S(1)}, bf16[1,256,640]{2,1,0:T(8,128)(2,1)S(1)}, u32[]{:S(2)}, u32[]{:S(2)}) collective-permute-start(bf16[1,256,640]{2,1,0:T(8,128)(2,1)S(1)} %get-tuple-element.38), channel_id=1, source_target_pairs={{0,1},{1,0},{2,3},{3,2},{4,5},{5,4},{6,7},{7,6},{8,9},{9,8},{10,11... | collective-permute-start | bytes 983048 | tf_op jit(solution)/shard_map/ppermute | solution.py:68
  196.3 9.2 %collective-permute-start.17 = (bf16[3,256,640]{2,1,0:T(8,128)(2,1)S(1)}, bf16[3,256,640]{2,1,0:T(8,128)(2,1)S(1)}, u32[]{:S(2)}, u32[]{:S(2)}) collective-permute-start(bf16[3,256,640]{2,1,0:T(8,128)(2,1)S(1)} %project.5), channel_id=1, source_target_pairs={{0,1},{1,0},{2,3},{3,2},{4,5},{5,4},{6,7},{7,6},{8,9},{9,8},{10,11... | collective-permute-start | bytes 2949128 | tf_op jit(solution)/shard_map/ppermute | solution.py:68
  196.8 7.1 %collective-permute-start.15 = (bf16[128,640]{1,0:T(8,128)(2,1)S(1)}, bf16[128,640]{1,0:T(8,128)(2,1)S(1)}, u32[]{:S(2)}, u32[]{:S(2)}) collective-permute-start(bf16[128,640]{1,0:T(8,128)(2,1)S(1)} %get-tuple-element.42), channel_id=1, source_target_pairs={{0,2},{1,3},{2,4},{3,5},{4,6},{5,7},{6,0},{7,1},{8,10},{9,11},{10,... | collective-permute-start | bytes 491528 | tf_op jit(solution)/shard_map/ppermute | solution.py:68
  198.2 5.7 %collective-permute-start.16 = (bf16[128,640]{1,0:T(8,128)(2,1)S(1)}, bf16[128,640]{1,0:T(8,128)(2,1)S(1)}, u32[]{:S(2)}, u32[]{:S(2)}) collective-permute-start(bf16[128,640]{1,0:T(8,128)(2,1)S(1)} %get-tuple-element.41), channel_id=1, source_target_pairs={{0,6},{1,7},{2,0},{3,1},{4,2},{5,3},{6,4},{7,5},{8,14},{9,15},{10,... | collective-permute-start | bytes 491528 | tf_op jit(solution)/shard_map/ppermute | solution.py:68
  199.7 12.5 %collective-permute-start.13 = (bf16[272,640]{1,0:T(8,128)(2,1)S(1)}, bf16[272,640]{1,0:T(8,128)(2,1)S(1)}, u32[]{:S(2)}, u32[]{:S(2)}) collective-permute-start(bf16[272,640]{1,0:T(8,128)(2,1)S(1)} %get-tuple-element.36), channel_id=1, source_target_pairs={{0,8},{1,9},{2,10},{3,11},{4,12},{5,13},{6,14},{7,15},{8,16},{9,17... | collective-permute-start | bytes 1044488 | tf_op jit(solution)/shard_map/ppermute | solution.py:68
  205.8 9.6 %collective-permute-start.18 = (bf16[256,640]{1,0:T(8,128)(2,1)S(1)}, bf16[256,640]{1,0:T(8,128)(2,1)S(1)}, u32[]{:S(2)}, u32[]{:S(2)}) collective-permute-start(bf16[256,640]{1,0:T(8,128)(2,1)S(1)} %pad_maximum_fusion), channel_id=1, source_target_pairs={{0,2},{1,3},{2,4},{3,5},{4,6},{5,7},{6,0},{7,1},{8,10},{9,11},{10,... | collective-permute-start | bytes 983048 | tf_op jit(solution)/shard_map/ppermute | solution.py:68
  206.9 8.5 %collective-permute-start.19 = (bf16[256,640]{1,0:T(8,128)(2,1)S(1)}, bf16[256,640]{1,0:T(8,128)(2,1)S(1)}, u32[]{:S(2)}, u32[]{:S(2)}) collective-permute-start(bf16[256,640]{1,0:T(8,128)(2,1)S(1)} %pad_maximum_fusion.1), channel_id=1, source_target_pairs={{0,6},{1,7},{2,0},{3,1},{4,2},{5,3},{6,4},{7,5},{8,14},{9,15},{10,... | collective-permute-start | bytes 983048 | tf_op jit(solution)/shard_map/ppermute | solution.py:68
  (5 other events, 4.6 us)

commit v10 on v9

--- a/solution.py
+++ b/solution.py
@@ -338,7 +338,7 @@
                     pltpu.make_async_copy(source, held.at[i], copied.at[i]).start()
                 for i in range(steps, STEPS):
                     wait_for(i)
-                note_places(steps, BEHIND + AHEAD)
+                note_places(steps, OWN + BEHIND + AHEAD)
                 for tile in range(TILES):
                     put(tile, running(tile))
 
@@ -347,7 +347,8 @@
             copy.wait()
 
 
-BEHIND = ((0, 0), (0, 1), (1, 0), (1, 1))
+OWN = ((0, 0), (0, 1))
+BEHIND = ((1, 0), (1, 1))
 AHEAD = ((3, 0), (3, 1))
 FAR = ((2, 0), (2, 1))
 
@@ -480,8 +481,9 @@
     far = [moved(ahead[0], across_pairs(-1)), moved(back[1], across_pairs(1))]
 
     *state, passed = attend_part(
-        BEHIND, row, window_offset, pieces, own + back, (), residual_in, levels, timestep_table
+        OWN, row, window_offset, pieces, own, (), residual_in, levels, timestep_table
     )
+    state = attend_part(BEHIND, row, window_offset, pieces, back, state)
     state = attend_part(AHEAD, row, window_offset, pieces, ahead, state)
     near = own + back + ahead
     answers = attend_far(row, window_offset, pieces, far, state, near)

time: 217 us -> 214 us (0.986)
  waiting for transfers between devices: 13 us -> 8.38 us
    ppermute x20, waiting for transfers between devices: 13 us -> 8.37 us  [moved(): return lax.ppermute(block, AXES, pairs)]
    pallas_call x2 -> x3, Pallas kernels: 17.8 us -> 18.5 us  [attend_part(): pl.pallas_call(functools.partial(attend_kernel, places, begins, False), o...]
  transfers between devices with their start and end apart: 21 -> 21, of which waited for: 5 -> 4; matrix products, arithmetic and copies ran while one was open for 1% -> 1% of each run, Pallas kernels for 10% -> 11%
where the time goes in v10:
time: 214 us; the launch traced here: 213 us
  Pallas kernels  108 us (50%)
  starting transfers between devices  70 us (33%)
  blocking collectives  17.9 us (8%)
  waiting for transfers between devices  8.38 us (4%)
  local copies, waits for them, and re-layouts  5.46 us (3%)
    pallas_call x1, Pallas kernels, attend_far(): pl.pallas_call(functools.partial(attend_kernel, FAR, False, True), out_sh...  82.5 us
    ppermute x20, starting transfers between devices, moved(): return lax.ppermute(block, AXES, pairs)  65.4 us
    pallas_call x3, Pallas kernels, attend_part(): pl.pallas_call(functools.partial(attend_kernel, places, begins, False), o...  18.5 us
    all_to_all x1, blocking collectives, body(): answers = lax.all_to_all(answers, 'tm', 0, 0, tiled=True)  17.9 us
    ppermute x20, waiting for transfers between devices, moved(): return lax.ppermute(block, AXES, pairs)  8.37 us
    all_to_all x1, starting transfers between devices, body(): pieces = lax.all_to_all(pieces, 'tm', 0, 0, tiled=True)  4.67 us
    unnamed x22, local copies, waits for them, and re-layouts  4.67 us
  transfers between devices with their start and end apart: 21, of which 4 were waited for; matrix products, arithmetic and copies ran while one was open for 1% of the time, Pallas kernels for 11%

profile of v10, /device:TPU:1, one launch (start us, length us, event | category | flops | bytes accessed | tf_op | source)
XLA Modules:
  0.0 213.2 jit_solution(17799828906536748998)
XLA Ops:
  3.6 9.8 %collective-permute-start.1 = (bf16[256,256]{1,0:T(8,128)(2,1)S(1)}, bf16[256,256]{1,0:T(8,128)(2,1)S(1)}, u32[]{:S(2)}, u32[]{:S(2)}) collective-permute-start(bf16[256,256]{1,0:T(8,128)(2,1)S(1)} %get-tuple-element.25), channel_id=1, source_target_pairs={{1,41},{3,43},{5,45},{7,47},{8,48},{10,50},{12,52},{14,54},{17,57}... | collective-permute-start | bytes 393224 | tf_op jit(solution)/shard_map/ppermute | solution.py:68
  13.5 3.1 %collective-permute-start.2 = (bf16[256,256]{1,0:T(8,128)(2,1)S(1)}, bf16[256,256]{1,0:T(8,128)(2,1)S(1)}, u32[]{:S(2)}, u32[]{:S(2)}) collective-permute-start(bf16[256,256]{1,0:T(8,128)(2,1)S(1)} %get-tuple-element.26), channel_id=1, source_target_pairs={{1,17},{3,19},{5,21},{7,23},{8,24},{10,26},{12,28},{14,30},{16,32}... | collective-permute-start | bytes 393224 | tf_op jit(solution)/shard_map/ppermute | solution.py:68
  17.9 6.4 %collective-permute-start.4 = (bf16[256,256]{1,0:T(8,128)(2,1)S(1)}, bf16[256,256]{1,0:T(8,128)(2,1)S(1)}, u32[]{:S(2)}, u32[]{:S(2)}) collective-permute-start(bf16[256,256]{1,0:T(8,128)(2,1)S(1)} %get-tuple-element.29), channel_id=1, source_target_pairs={{0,32},{1,33},{2,34},{3,35},{4,36},{5,37},{6,38},{7,39},{9,41},{11... | collective-permute-start | bytes 393224 | tf_op jit(solution)/shard_map/ppermute | solution.py:68
  25.6 5.2 %collective-permute-start.6 = (bf16[256,256]{1,0:T(8,128)(2,1)S(1)}, bf16[256,256]{1,0:T(8,128)(2,1)S(1)}, u32[]{:S(2)}, u32[]{:S(2)}) collective-permute-start(bf16[256,256]{1,0:T(8,128)(2,1)S(1)} %get-tuple-element.31), channel_id=1, source_target_pairs={{1,57},{3,59},{5,61},{7,63},{8,0},{9,1},{10,2},{11,3},{12,4},{13,5... | collective-permute-start | bytes 393224 | tf_op jit(solution)/shard_map/ppermute | solution.py:68
  30.9 3.1 %collective-permute-start.9 = (bf16[1024,256]{1,0:T(8,128)(2,1)S(1)}, bf16[1024,256]{1,0:T(8,128)(2,1)S(1)}, u32[]{:S(2)}, u32[]{:S(2)}) collective-permute-start(bf16[1024,256]{1,0:T(8,128)(2,1)S(1)} %constant_dynamic-update-slice_fusion.unused_ref.refs_1_.refs_6_), channel_id=1, source_target_pairs={{0,64},{1,65},{2,66},{3,67},{4,68},{5,69},{6,70},{7,71},{8,72},{10... | collective-permute-start | bytes 1572872 | tf_op jit(solution)/shard_map/ppermute | solution.py:68
  34.1 3.4 %collective-permute-start.7 = (bf16[1024,256]{1,0:T(8,128)(2,1)S(1)}, bf16[1024,256]{1,0:T(8,128)(2,1)S(1)}, u32[]{:S(2)}, u32[]{:S(2)}) collective-permute-start(bf16[1024,256]{1,0:T(8,128)(2,1)S(1)} %constant_dynamic-update-slice_fusion.4.refs_0_.refs_5_), channel_id=1, source_target_pairs={{0,192},{1,193},{2,194},{3,195},{4,196},{5,197},{6,198},{7,199},{8... | collective-permute-start | bytes 1572872 | tf_op jit(solution)/shard_map/ppermute | solution.py:68
  40.6 4.7 %all-to-all-start = ((bf16[32,64,128]{2,1,0:T(8,128)(2,1)}), bf16[32,64,128]{2,1,0:T(8,128)(2,1)S(1)}, u32[]{:S(2)}, u32[]{:S(2)}) async-start(bf16[32,64,128]{2,1,0:T(8,128)(2,1)} %pieces.1), calls=%async_computation | async-start | bytes 1048576 | tf_op jit(solution)/shard_map/all_to_all | solution.py:480
  45.3 3.1 %collective-permute-start.12 = (bf16[1024,256]{1,0:T(8,128)(2,1)S(1)}, bf16[1024,256]{1,0:T(8,128)(2,1)S(1)}, u32[]{:S(2)}, u32[]{:S(2)}) collective-permute-start(bf16[1024,256]{1,0:T(8,128)(2,1)S(1)} %constant_dynamic-update-slice_fusion.4.refs_0_.refs_5_), channel_id=1, source_target_pairs={{0,64},{1,65},{2,66},{3,67},{4,68},{5,69},{6,70},{7,71},{8,72},{10... | collective-permute-start | bytes 1572872 | tf_op jit(solution)/shard_map/ppermute | solution.py:68
  48.4 3.4 %collective-permute-start.11 = (bf16[1024,256]{1,0:T(8,128)(2,1)S(1)}, bf16[1024,256]{1,0:T(8,128)(2,1)}, u32[]{:S(2)}, u32[]{:S(2)}) collective-permute-start(bf16[1024,256]{1,0:T(8,128)(2,1)S(1)} %constant_dynamic-update-slice_fusion.unused_ref.refs_1_.refs_6_), channel_id=1, source_target_pairs={{0,192},{1,193},{2,194},{3,195},{4,196},{5,197},{6,198},{7,199},{8... | collective-permute-start | bytes 1572872 | tf_op jit(solution)/shard_map/ppermute | solution.py:68
  51.8 1.9 collective-permute-start.10
  53.8 4.6 %collective-permute-start.8 = (bf16[1024,256]{1,0:T(8,128)(2,1)S(1)}, bf16[1024,256]{1,0:T(8,128)(2,1)}, u32[]{:S(2)}, u32[]{:S(2)}) collective-permute-start(bf16[1024,256]{1,0:T(8,128)(2,1)S(1)} %collective-permute-done.7.refs_0_.refs_9_), channel_id=1, source_target_pairs={{0,192},{1,193},{2,194},{3,195},{4,196},{5,197},{6,198},{7,199},{8... | collective-permute-start | bytes 1572872 | tf_op jit(solution)/shard_map/ppermute | solution.py:68
  61.3 6.7 %part.3 = (f32[2048,128]{1,0:T(8,128)S(1)}, f32[2048,128]{1,0:T(8,128)S(1)}, f32[2048,128]{1,0:T(8,128)S(1)}, bf16[272,640]{1,0:T(8,128)(2,1)S(1)}) custom-call(s32[64]{0:T(128)S(1)} %dynamic-slice_bitcast_fusion.row_ref, s32[1]{0:T(128)S(6)} %copy.18.offset_ref, bf16[32,64,128]{2,1,0:T(8,128)(2,1)S(1)} %all-to-all-done.pieces_ref, ...), custom_call_target="tpu_custom_call" | custom-call | tf_op jit(solution)/shard_map/part/pallas_call | solution.py:371
  68.0 7.5 %part.4 = (f32[2048,128]{1,0:T(8,128)S(1)}, f32[2048,128]{1,0:T(8,128)S(1)}) custom-call(s32[64]{0:T(128)S(1)} %dynamic-slice_bitcast_fusion.row_ref, s32[1]{0:T(128)S(6)} %copy.18.offset_ref, bf16[32,64,128]{2,1,0:T(8,128)(2,1)S(1)} %all-to-all-done.pieces_ref, bf16[1024,256]{1,0:T(8,128)(2,1)S(1)} %collective-permute-done.12.refs_0_.refs_7_, ...), custom_call_target="tpu_custom_call" | custom-call | tf_op jit(solution)/shard_map/part/pallas_call | solution.py:371
  75.5 4.4 %part.5 = (f32[2048,128]{1,0:T(8,128)S(1)}, f32[2048,128]{1,0:T(8,128)S(1)}) custom-call(s32[64]{0:T(128)S(1)} %dynamic-slice_bitcast_fusion.row_ref, s32[1]{0:T(128)S(6)} %copy.18.offset_ref, bf16[32,64,128]{2,1,0:T(8,128)(2,1)S(1)} %all-to-all-done.pieces_ref, bf16[1024,256]{1,0:T(8,128)(2,1)S(1)} %collective-permute-done.7.refs_0_.refs_9_, ...), custom_call_target="tpu_custom_call" | custom-call | tf_op jit(solution)/shard_map/part/pallas_call | solution.py:371
  79.9 82.5 %far.1 = bf16[32,64,128]{2,1,0:T(8,128)(2,1)S(1)} custom-call(s32[64]{0:T(128)S(1)} %dynamic-slice_bitcast_fusion.row_ref, s32[1]{0:T(128)S(6)} %copy.18.offset_ref, bf16[32,64,128]{2,1,0:T(8,128)(2,1)S(1)} %all-to-all-done.pieces_ref, bf16[1024,256]{1,0:T(8,128)(2,1)} %collective-permute-done.8.refs_0_, bf16[1024,256]{1,0:T(8,128)(2,1)} %collective-permute-done.10.refs_1_, ...), custom_call_target="tpu_custom_call" | custom-call | tf_op jit(solution)/shard_map/far/pallas_call | solution.py:386
  162.4 17.9 %all_to_all.10.parts_ref = bf16[32,64,128]{2,1,0:T(8,128)(2,1)S(1)} all-to-all(bf16[32,64,128]{2,1,0:T(8,128)(2,1)S(1)} %far.1), channel_id=1, replica_groups=mesh['tm'=32,'head'=8] {'tm'}, dimensions={0} | all-to-all | bytes 1048576 | tf_op jit(solution)/shard_map/all_to_all | solution.py:490
  181.5 8.7 %collective-permute-start.14 = (bf16[1,256,640]{2,1,0:T(8,128)(2,1)S(1)}, bf16[1,256,640]{2,1,0:T(8,128)(2,1)S(1)}, u32[]{:S(2)}, u32[]{:S(2)}) collective-permute-start(bf16[1,256,640]{2,1,0:T(8,128)(2,1)S(1)} %get-tuple-element.42), channel_id=1, source_target_pairs={{0,1},{1,0},{2,3},{3,2},{4,5},{5,4},{6,7},{7,6},{8,9},{9,8},{10,11... | collective-permute-start | bytes 983048 | tf_op jit(solution)/shard_map/ppermute | solution.py:68
  191.6 1.6 project.5
  196.6 2.6 %collective-permute-start.13 = (bf16[272,640]{1,0:T(8,128)(2,1)S(1)}, bf16[272,640]{1,0:T(8,128)(2,1)S(1)}, u32[]{:S(2)}, u32[]{:S(2)}) collective-permute-start(bf16[272,640]{1,0:T(8,128)(2,1)S(1)} %get-tuple-element.40), channel_id=1, source_target_pairs={{0,8},{1,9},{2,10},{3,11},{4,12},{5,13},{6,14},{7,15},{8,16},{9,17... | collective-permute-start | bytes 1044488 | tf_op jit(solution)/shard_map/ppermute | solution.py:68
  199.1 1.6 collective-permute-done.15.refs_0_
  200.7 1.6 project.4
  203.7 1.8 collective-permute-start.19
  205.6 3.4 %collective-permute-done.13 = bf16[272,640]{1,0:T(8,128)(2,1)S(1)} collective-permute-done((bf16[272,640]{1,0:T(8,128)(2,1)S(1)}, bf16[272,640]{1,0:T(8,128)(2,1)S(1)}, u32[]{:S(2)}, u32[]{:S(2)}) %collective-permute-start.13) | collective-permute-done | bytes 348192 | tf_op jit(solution)/shard_map/ppermute | solution.py:68
  209.2 3.1 %collective-permute-done.18 = bf16[256,640]{1,0:T(8,128)(2,1)S(1)} collective-permute-done((bf16[256,640]{1,0:T(8,128)(2,1)S(1)}, bf16[256,640]{1,0:T(8,128)(2,1)S(1)}, u32[]{:S(2)}, u32[]{:S(2)}) %collective-permute-start.18) | collective-permute-done | bytes 327712 | tf_op jit(solution)/shard_map/ppermute | solution.py:68
  (66 shorter events, 19.4 us)
Async XLA Ops:
  0.0 209.0 %copy-start = (bf16[256,640]{1,0:T(8,128)(2,1)S(1)}, bf16[256,640]{1,0:T(8,128)(2,1)}, u32[]{:S(2)}) copy-start(bf16[256,640]{1,0:T(8,128)(2,1)} %param.15) | copy-start | bytes 983044
  2.3 22.0 %collective-permute-start = (bf16[256,256]{1,0:T(8,128)(2,1)S(1)}, bf16[256,256]{1,0:T(8,128)(2,1)S(1)}, u32[]{:S(2)}, u32[]{:S(2)}) collective-permute-start(bf16[256,256]{1,0:T(8,128)(2,1)S(1)} %get-tuple-element.24), channel_id=1, source_target_pairs={{0,24},{2,26},{4,28},{6,30},{8,32},{9,33},{10,34},{11,35},{12,36},... | collective-permute-start | bytes 393224 | tf_op jit(solution)/shard_map/ppermute | solution.py:68
  3.6 22.0 %collective-permute-start.1 = (bf16[256,256]{1,0:T(8,128)(2,1)S(1)}, bf16[256,256]{1,0:T(8,128)(2,1)S(1)}, u32[]{:S(2)}, u32[]{:S(2)}) collective-permute-start(bf16[256,256]{1,0:T(8,128)(2,1)S(1)} %get-tuple-element.25), channel_id=1, source_target_pairs={{1,41},{3,43},{5,45},{7,47},{8,48},{10,50},{12,52},{14,54},{17,57}... | collective-permute-start | bytes 393224 | tf_op jit(solution)/shard_map/ppermute | solution.py:68
  13.5 17.4 %collective-permute-start.2 = (bf16[256,256]{1,0:T(8,128)(2,1)S(1)}, bf16[256,256]{1,0:T(8,128)(2,1)S(1)}, u32[]{:S(2)}, u32[]{:S(2)}) collective-permute-start(bf16[256,256]{1,0:T(8,128)(2,1)S(1)} %get-tuple-element.26), channel_id=1, source_target_pairs={{1,17},{3,19},{5,21},{7,23},{8,24},{10,26},{12,28},{14,30},{16,32}... | collective-permute-start | bytes 393224 | tf_op jit(solution)/shard_map/ppermute | solution.py:68
  16.6 14.3 %collective-permute-start.3 = (bf16[256,256]{1,0:T(8,128)(2,1)S(1)}, bf16[256,256]{1,0:T(8,128)(2,1)S(1)}, u32[]{:S(2)}, u32[]{:S(2)}) collective-permute-start(bf16[256,256]{1,0:T(8,128)(2,1)S(1)} %get-tuple-element.27), channel_id=1, source_target_pairs={{0,48},{2,50},{4,52},{6,54},{9,57},{11,59},{13,61},{15,63},{16,0},... | collective-permute-start | bytes 393224 | tf_op jit(solution)/shard_map/ppermute | solution.py:68
  17.9 16.2 %collective-permute-start.4 = (bf16[256,256]{1,0:T(8,128)(2,1)S(1)}, bf16[256,256]{1,0:T(8,128)(2,1)S(1)}, u32[]{:S(2)}, u32[]{:S(2)}) collective-permute-start(bf16[256,256]{1,0:T(8,128)(2,1)S(1)} %get-tuple-element.29), channel_id=1, source_target_pairs={{0,32},{1,33},{2,34},{3,35},{4,36},{5,37},{6,38},{7,39},{9,41},{11... | collective-permute-start | bytes 393224 | tf_op jit(solution)/shard_map/ppermute | solution.py:68
  24.3 9.8 %collective-permute-start.5 = (bf16[256,256]{1,0:T(8,128)(2,1)S(1)}, bf16[256,256]{1,0:T(8,128)(2,1)S(1)}, u32[]{:S(2)}, u32[]{:S(2)}) collective-permute-start(bf16[256,256]{1,0:T(8,128)(2,1)S(1)} %get-tuple-element.30), channel_id=1, source_target_pairs={{0,8},{2,10},{4,12},{6,14},{9,17},{11,19},{13,21},{15,23},{16,24},... | collective-permute-start | bytes 393224 | tf_op jit(solution)/shard_map/ppermute | solution.py:68
  25.6 8.5 %collective-permute-start.6 = (bf16[256,256]{1,0:T(8,128)(2,1)S(1)}, bf16[256,256]{1,0:T(8,128)(2,1)S(1)}, u32[]{:S(2)}, u32[]{:S(2)}) collective-permute-start(bf16[256,256]{1,0:T(8,128)(2,1)S(1)} %get-tuple-element.31), channel_id=1, source_target_pairs={{1,57},{3,59},{5,61},{7,63},{8,0},{9,1},{10,2},{11,3},{12,4},{13,5... | collective-permute-start | bytes 393224 | tf_op jit(solution)/shard_map/ppermute | solution.py:68
  30.9 20.9 %collective-permute-start.9 = (bf16[1024,256]{1,0:T(8,128)(2,1)S(1)}, bf16[1024,256]{1,0:T(8,128)(2,1)S(1)}, u32[]{:S(2)}, u32[]{:S(2)}) collective-permute-start(bf16[1024,256]{1,0:T(8,128)(2,1)S(1)} %constant_dynamic-update-slice_fusion.unused_ref.refs_1_.refs_6_), channel_id=1, source_target_pairs={{0,64},{1,65},{2,66},{3,67},{4,68},{5,69},{6,70},{7,71},{8,72},{10... | collective-permute-start | bytes 1572872 | tf_op jit(solution)/shard_map/ppermute | solution.py:68
  34.1 19.6 %collective-permute-start.7 = (bf16[1024,256]{1,0:T(8,128)(2,1)S(1)}, bf16[1024,256]{1,0:T(8,128)(2,1)S(1)}, u32[]{:S(2)}, u32[]{:S(2)}) collective-permute-start(bf16[1024,256]{1,0:T(8,128)(2,1)S(1)} %constant_dynamic-update-slice_fusion.4.refs_0_.refs_5_), channel_id=1, source_target_pairs={{0,192},{1,193},{2,194},{3,195},{4,196},{5,197},{6,198},{7,199},{8... | collective-permute-start | bytes 1572872 | tf_op jit(solution)/shard_map/ppermute | solution.py:68
  40.6 19.0 %all-to-all-start = ((bf16[32,64,128]{2,1,0:T(8,128)(2,1)}), bf16[32,64,128]{2,1,0:T(8,128)(2,1)S(1)}, u32[]{:S(2)}, u32[]{:S(2)}) async-start(bf16[32,64,128]{2,1,0:T(8,128)(2,1)} %pieces.1), calls=%async_computation | async-start | bytes 1048576 | tf_op jit(solution)/shard_map/all_to_all | solution.py:480
  45.3 22.7 %collective-permute-start.12 = (bf16[1024,256]{1,0:T(8,128)(2,1)S(1)}, bf16[1024,256]{1,0:T(8,128)(2,1)S(1)}, u32[]{:S(2)}, u32[]{:S(2)}) collective-permute-start(bf16[1024,256]{1,0:T(8,128)(2,1)S(1)} %constant_dynamic-update-slice_fusion.4.refs_0_.refs_5_), channel_id=1, source_target_pairs={{0,64},{1,65},{2,66},{3,67},{4,68},{5,69},{6,70},{7,71},{8,72},{10... | collective-permute-start | bytes 1572872 | tf_op jit(solution)/shard_map/ppermute | solution.py:68
  48.4 27.0 %collective-permute-start.11 = (bf16[1024,256]{1,0:T(8,128)(2,1)S(1)}, bf16[1024,256]{1,0:T(8,128)(2,1)}, u32[]{:S(2)}, u32[]{:S(2)}) collective-permute-start(bf16[1024,256]{1,0:T(8,128)(2,1)S(1)} %constant_dynamic-update-slice_fusion.unused_ref.refs_1_.refs_6_), channel_id=1, source_target_pairs={{0,192},{1,193},{2,194},{3,195},{4,196},{5,197},{6,198},{7,199},{8... | collective-permute-start | bytes 1572872 | tf_op jit(solution)/shard_map/ppermute | solution.py:68
  51.8 28.0 %collective-permute-start.10 = (bf16[1024,256]{1,0:T(8,128)(2,1)S(1)}, bf16[1024,256]{1,0:T(8,128)(2,1)}, u32[]{:S(2)}, u32[]{:S(2)}) collective-permute-start(bf16[1024,256]{1,0:T(8,128)(2,1)S(1)} %collective-permute-done.9.refs_1_.refs_8_), channel_id=1, source_target_pairs={{0,64},{1,65},{2,66},{3,67},{4,68},{5,69},{6,70},{7,71},{8,72},{10... | collective-permute-start | bytes 1572872 | tf_op jit(solution)/shard_map/ppermute | solution.py:68
  53.8 26.1 %collective-permute-start.8 = (bf16[1024,256]{1,0:T(8,128)(2,1)S(1)}, bf16[1024,256]{1,0:T(8,128)(2,1)}, u32[]{:S(2)}, u32[]{:S(2)}) collective-permute-start(bf16[1024,256]{1,0:T(8,128)(2,1)S(1)} %collective-permute-done.7.refs_0_.refs_9_), channel_id=1, source_target_pairs={{0,192},{1,193},{2,194},{3,195},{4,196},{5,197},{6,198},{7,199},{8... | collective-permute-start | bytes 1572872 | tf_op jit(solution)/shard_map/ppermute | solution.py:68
  75.5 104.8 %slice-start = ((s8[6553600]{0:T(1024)(128)(4,1)}), s8[4194304]{0:T(1024)(128)(4,1)S(1)}, s32[]{:S(2)}) async-start(s8[6553600]{0:T(1024)(128)(4,1)} %bitcast.37), calls=%async_computation.2 | async-start | bytes 8388608
  79.9 100.4 %slice-start.1 = ((s8[6553600]{0:T(1024)(128)(4,1)}), s8[2359296]{0:T(1024)(128)(4,1)S(1)}, s32[]{:S(2)}) async-start(s8[6553600]{0:T(1024)(128)(4,1)} %bitcast.37), calls=%async_computation.3 | async-start | bytes 4718592
  181.5 10.0 %collective-permute-start.14 = (bf16[1,256,640]{2,1,0:T(8,128)(2,1)S(1)}, bf16[1,256,640]{2,1,0:T(8,128)(2,1)S(1)}, u32[]{:S(2)}, u32[]{:S(2)}) collective-permute-start(bf16[1,256,640]{2,1,0:T(8,128)(2,1)S(1)} %get-tuple-element.42), channel_id=1, source_target_pairs={{0,1},{1,0},{2,3},{3,2},{4,5},{5,4},{6,7},{7,6},{8,9},{9,8},{10,11... | collective-permute-start | bytes 983048 | tf_op jit(solution)/shard_map/ppermute | solution.py:68
  193.2 9.2 %collective-permute-start.17 = (bf16[3,256,640]{2,1,0:T(8,128)(2,1)S(1)}, bf16[3,256,640]{2,1,0:T(8,128)(2,1)S(1)}, u32[]{:S(2)}, u32[]{:S(2)}) collective-permute-start(bf16[3,256,640]{2,1,0:T(8,128)(2,1)S(1)} %project.5), channel_id=1, source_target_pairs={{0,1},{1,0},{2,3},{3,2},{4,5},{5,4},{6,7},{7,6},{8,9},{9,8},{10,11... | collective-permute-start | bytes 2949128 | tf_op jit(solution)/shard_map/ppermute | solution.py:68
  193.7 7.1 %collective-permute-start.15 = (bf16[128,640]{1,0:T(8,128)(2,1)S(1)}, bf16[128,640]{1,0:T(8,128)(2,1)S(1)}, u32[]{:S(2)}, u32[]{:S(2)}) collective-permute-start(bf16[128,640]{1,0:T(8,128)(2,1)S(1)} %get-tuple-element.46), channel_id=1, source_target_pairs={{0,2},{1,3},{2,4},{3,5},{4,6},{5,7},{6,0},{7,1},{8,10},{9,11},{10,... | collective-permute-start | bytes 491528 | tf_op jit(solution)/shard_map/ppermute | solution.py:68
  195.0 5.7 %collective-permute-start.16 = (bf16[128,640]{1,0:T(8,128)(2,1)S(1)}, bf16[128,640]{1,0:T(8,128)(2,1)S(1)}, u32[]{:S(2)}, u32[]{:S(2)}) collective-permute-start(bf16[128,640]{1,0:T(8,128)(2,1)S(1)} %get-tuple-element.45), channel_id=1, source_target_pairs={{0,6},{1,7},{2,0},{3,1},{4,2},{5,3},{6,4},{7,5},{8,14},{9,15},{10,... | collective-permute-start | bytes 491528 | tf_op jit(solution)/shard_map/ppermute | solution.py:68
  196.6 12.5 %collective-permute-start.13 = (bf16[272,640]{1,0:T(8,128)(2,1)S(1)}, bf16[272,640]{1,0:T(8,128)(2,1)S(1)}, u32[]{:S(2)}, u32[]{:S(2)}) collective-permute-start(bf16[272,640]{1,0:T(8,128)(2,1)S(1)} %get-tuple-element.40), channel_id=1, source_target_pairs={{0,8},{1,9},{2,10},{3,11},{4,12},{5,13},{6,14},{7,15},{8,16},{9,17... | collective-permute-start | bytes 1044488 | tf_op jit(solution)/shard_map/ppermute | solution.py:68
  202.6 9.6 %collective-permute-start.18 = (bf16[256,640]{1,0:T(8,128)(2,1)S(1)}, bf16[256,640]{1,0:T(8,128)(2,1)S(1)}, u32[]{:S(2)}, u32[]{:S(2)}) collective-permute-start(bf16[256,640]{1,0:T(8,128)(2,1)S(1)} %pad_maximum_fusion), channel_id=1, source_target_pairs={{0,2},{1,3},{2,4},{3,5},{4,6},{5,7},{6,0},{7,1},{8,10},{9,11},{10,... | collective-permute-start | bytes 983048 | tf_op jit(solution)/shard_map/ppermute | solution.py:68
  203.7 8.5 %collective-permute-start.19 = (bf16[256,640]{1,0:T(8,128)(2,1)S(1)}, bf16[256,640]{1,0:T(8,128)(2,1)S(1)}, u32[]{:S(2)}, u32[]{:S(2)}) collective-permute-start(bf16[256,640]{1,0:T(8,128)(2,1)S(1)} %pad_maximum_fusion.1), channel_id=1, source_target_pairs={{0,6},{1,7},{2,0},{3,1},{4,2},{5,3},{6,4},{7,5},{8,14},{9,15},{10,... | collective-permute-start | bytes 983048 | tf_op jit(solution)/shard_map/ppermute | solution.py:68
  (5 other events, 4.6 us)

commit v11 on v10

--- a/solution.py
+++ b/solution.py
@@ -476,7 +476,7 @@
     own = [jnp.concatenate(arrived[half * STEP : (half + 1) * STEP]) for half in range(2)]
     back = [moved(part, across_pairs(1)) for part in own]
     ahead = [moved(part, across_pairs(-1)) for part in own]
-    pieces = cut_queries(row, query_rows, own[1])
+    pieces = cut_queries(row, query_rows, arrived[6])
     pieces = lax.all_to_all(pieces, "tm", 0, 0, tiled=True)
     far = [moved(ahead[0], across_pairs(-1)), moved(back[1], across_pairs(1))]
 

time: 214 us -> 214 us (level); the launches traced: 213 us -> 211 us
    pallas_call x1, Pallas kernels: 82.5 us -> 78.4 us  [attend_far(): pl.pallas_call(functools.partial(attend_kernel, FAR, False, True), out_sh...]
where the time goes in v11:
time: 214 us; the launch traced here: 211 us
  Pallas kernels  106 us (50%)
  starting transfers between devices  70 us (33%)
  blocking collectives  18 us (8%)
  waiting for transfers between devices  8.41 us (4%)
  local copies, waits for them, and re-layouts  5.46 us (3%)
    pallas_call x1, Pallas kernels, attend_far(): pl.pallas_call(functools.partial(attend_kernel, FAR, False, True), out_sh...  78.4 us
    ppermute x20, starting transfers between devices, moved(): return lax.ppermute(block, AXES, pairs)  65.4 us
    pallas_call x3, Pallas kernels, attend_part(): pl.pallas_call(functools.partial(attend_kernel, places, begins, False), o...  20 us
    all_to_all x1, blocking collectives, body(): answers = lax.all_to_all(answers, 'tm', 0, 0, tiled=True)  18 us
    ppermute x20, waiting for transfers between devices, moved(): return lax.ppermute(block, AXES, pairs)  8.41 us
    all_to_all x1, starting transfers between devices, body(): pieces = lax.all_to_all(pieces, 'tm', 0, 0, tiled=True)  4.67 us
    unnamed x22, local copies, waits for them, and re-layouts  4.67 us
  transfers between devices with their start and end apart: 21, of which 4 were waited for; matrix products, arithmetic and copies ran while one was open for 1% of the time, Pallas kernels for 11%

profile of v11, /device:TPU:1, one launch (start us, length us, event | category | flops | bytes accessed | tf_op | source)
XLA Modules:
  0.0 210.8 jit_solution(10266843537511586933)
XLA Ops:
  3.6 9.8 %collective-permute-start.7 = (bf16[256,256]{1,0:T(8,128)(2,1)S(1)}, bf16[256,256]{1,0:T(8,128)(2,1)S(1)}, u32[]{:S(2)}, u32[]{:S(2)}) collective-permute-start(bf16[256,256]{1,0:T(8,128)(2,1)S(1)} %get-tuple-element.30), channel_id=1, source_target_pairs={{1,41},{3,43},{5,45},{7,47},{8,48},{10,50},{12,52},{14,54},{17,57}... | collective-permute-start | bytes 393224 | tf_op jit(solution)/shard_map/ppermute | solution.py:68
  13.5 3.1 %collective-permute-start = (bf16[256,256]{1,0:T(8,128)(2,1)S(1)}, bf16[256,256]{1,0:T(8,128)(2,1)S(1)}, u32[]{:S(2)}, u32[]{:S(2)}) collective-permute-start(bf16[256,256]{1,0:T(8,128)(2,1)S(1)} %get-tuple-element.24), channel_id=1, source_target_pairs={{1,17},{3,19},{5,21},{7,23},{8,24},{10,26},{12,28},{14,30},{16,32}... | collective-permute-start | bytes 393224 | tf_op jit(solution)/shard_map/ppermute | solution.py:68
  17.9 6.4 %collective-permute-start.1 = (bf16[256,256]{1,0:T(8,128)(2,1)S(1)}, bf16[256,256]{1,0:T(8,128)(2,1)S(1)}, u32[]{:S(2)}, u32[]{:S(2)}) collective-permute-start(bf16[256,256]{1,0:T(8,128)(2,1)S(1)} %get-tuple-element.26), channel_id=1, source_target_pairs={{0,32},{1,33},{2,34},{3,35},{4,36},{5,37},{6,38},{7,39},{9,41},{11... | collective-permute-start | bytes 393224 | tf_op jit(solution)/shard_map/ppermute | solution.py:68
  25.6 5.2 %collective-permute-start.3 = (bf16[256,256]{1,0:T(8,128)(2,1)S(1)}, bf16[256,256]{1,0:T(8,128)(2,1)S(1)}, u32[]{:S(2)}, u32[]{:S(2)}) collective-permute-start(bf16[256,256]{1,0:T(8,128)(2,1)S(1)} %get-tuple-element.28), channel_id=1, source_target_pairs={{1,57},{3,59},{5,61},{7,63},{8,0},{9,1},{10,2},{11,3},{12,4},{13,5... | collective-permute-start | bytes 393224 | tf_op jit(solution)/shard_map/ppermute | solution.py:68
  30.9 3.1 %collective-permute-start.9 = (bf16[1024,256]{1,0:T(8,128)(2,1)S(1)}, bf16[1024,256]{1,0:T(8,128)(2,1)S(1)}, u32[]{:S(2)}, u32[]{:S(2)}) collective-permute-start(bf16[1024,256]{1,0:T(8,128)(2,1)S(1)} %constant_dynamic-update-slice_fusion.4.refs_1_.refs_6_), channel_id=1, source_target_pairs={{0,64},{1,65},{2,66},{3,67},{4,68},{5,69},{6,70},{7,71},{8,72},{10... | collective-permute-start | bytes 1572872 | tf_op jit(solution)/shard_map/ppermute | solution.py:68
  34.1 3.4 %collective-permute-start.4 = (bf16[1024,256]{1,0:T(8,128)(2,1)S(1)}, bf16[1024,256]{1,0:T(8,128)(2,1)S(1)}, u32[]{:S(2)}, u32[]{:S(2)}) collective-permute-start(bf16[1024,256]{1,0:T(8,128)(2,1)S(1)} %constant_dynamic-update-slice_fusion.refs_0_.refs_5_), channel_id=1, source_target_pairs={{0,192},{1,193},{2,194},{3,195},{4,196},{5,197},{6,198},{7,199},{8... | collective-permute-start | bytes 1572872 | tf_op jit(solution)/shard_map/ppermute | solution.py:68
  40.6 4.7 %all-to-all-start = ((bf16[32,64,128]{2,1,0:T(8,128)(2,1)}), bf16[32,64,128]{2,1,0:T(8,128)(2,1)S(1)}, u32[]{:S(2)}, u32[]{:S(2)}) async-start(bf16[32,64,128]{2,1,0:T(8,128)(2,1)} %pieces.1), calls=%async_computation | async-start | bytes 1048576 | tf_op jit(solution)/shard_map/all_to_all | solution.py:480
  45.3 3.1 %collective-permute-start.12 = (bf16[1024,256]{1,0:T(8,128)(2,1)S(1)}, bf16[1024,256]{1,0:T(8,128)(2,1)S(1)}, u32[]{:S(2)}, u32[]{:S(2)}) collective-permute-start(bf16[1024,256]{1,0:T(8,128)(2,1)S(1)} %constant_dynamic-update-slice_fusion.refs_0_.refs_5_), channel_id=1, source_target_pairs={{0,64},{1,65},{2,66},{3,67},{4,68},{5,69},{6,70},{7,71},{8,72},{10... | collective-permute-start | bytes 1572872 | tf_op jit(solution)/shard_map/ppermute | solution.py:68
  48.4 3.4 %collective-permute-start.11 = (bf16[1024,256]{1,0:T(8,128)(2,1)S(1)}, bf16[1024,256]{1,0:T(8,128)(2,1)}, u32[]{:S(2)}, u32[]{:S(2)}) collective-permute-start(bf16[1024,256]{1,0:T(8,128)(2,1)S(1)} %constant_dynamic-update-slice_fusion.4.refs_1_.refs_6_), channel_id=1, source_target_pairs={{0,192},{1,193},{2,194},{3,195},{4,196},{5,197},{6,198},{7,199},{8... | collective-permute-start | bytes 1572872 | tf_op jit(solution)/shard_map/ppermute | solution.py:68
  51.8 1.9 collective-permute-start.10
  53.8 4.6 %collective-permute-start.5 = (bf16[1024,256]{1,0:T(8,128)(2,1)S(1)}, bf16[1024,256]{1,0:T(8,128)(2,1)}, u32[]{:S(2)}, u32[]{:S(2)}) collective-permute-start(bf16[1024,256]{1,0:T(8,128)(2,1)S(1)} %collective-permute-done.4.refs_0_.refs_9_), channel_id=1, source_target_pairs={{0,192},{1,193},{2,194},{3,195},{4,196},{5,197},{6,198},{7,199},{8... | collective-permute-start | bytes 1572872 | tf_op jit(solution)/shard_map/ppermute | solution.py:68
  61.3 7.4 %part.3 = (f32[2048,128]{1,0:T(8,128)S(1)}, f32[2048,128]{1,0:T(8,128)S(1)}, f32[2048,128]{1,0:T(8,128)S(1)}, bf16[272,640]{1,0:T(8,128)(2,1)S(1)}) custom-call(s32[64]{0:T(128)S(1)} %dynamic-slice_bitcast_fusion.row_ref, s32[1]{0:T(128)S(6)} %copy.18.offset_ref, bf16[32,64,128]{2,1,0:T(8,128)(2,1)S(1)} %all-to-all-done.pieces_ref, ...), custom_call_target="tpu_custom_call" | custom-call | tf_op jit(solution)/shard_map/part/pallas_call | solution.py:371
  68.7 7.5 %part.4 = (f32[2048,128]{1,0:T(8,128)S(1)}, f32[2048,128]{1,0:T(8,128)S(1)}) custom-call(s32[64]{0:T(128)S(1)} %dynamic-slice_bitcast_fusion.row_ref, s32[1]{0:T(128)S(6)} %copy.18.offset_ref, bf16[32,64,128]{2,1,0:T(8,128)(2,1)S(1)} %all-to-all-done.pieces_ref, bf16[1024,256]{1,0:T(8,128)(2,1)S(1)} %collective-permute-done.12.refs_0_.refs_7_, ...), custom_call_target="tpu_custom_call" | custom-call | tf_op jit(solution)/shard_map/part/pallas_call | solution.py:371
  76.3 5.1 %part.5 = (f32[2048,128]{1,0:T(8,128)S(1)}, f32[2048,128]{1,0:T(8,128)S(1)}) custom-call(s32[64]{0:T(128)S(1)} %dynamic-slice_bitcast_fusion.row_ref, s32[1]{0:T(128)S(6)} %copy.18.offset_ref, bf16[32,64,128]{2,1,0:T(8,128)(2,1)S(1)} %all-to-all-done.pieces_ref, bf16[1024,256]{1,0:T(8,128)(2,1)S(1)} %collective-permute-done.4.refs_0_.refs_9_, ...), custom_call_target="tpu_custom_call" | custom-call | tf_op jit(solution)/shard_map/part/pallas_call | solution.py:371
  81.4 78.4 %far.1 = bf16[32,64,128]{2,1,0:T(8,128)(2,1)S(1)} custom-call(s32[64]{0:T(128)S(1)} %dynamic-slice_bitcast_fusion.row_ref, s32[1]{0:T(128)S(6)} %copy.18.offset_ref, bf16[32,64,128]{2,1,0:T(8,128)(2,1)S(1)} %all-to-all-done.pieces_ref, bf16[1024,256]{1,0:T(8,128)(2,1)} %collective-permute-done.5.refs_0_, bf16[1024,256]{1,0:T(8,128)(2,1)} %collective-permute-done.10.refs_1_, ...), custom_call_target="tpu_custom_call" | custom-call | tf_op jit(solution)/shard_map/far/pallas_call | solution.py:386
  159.8 18.0 %all_to_all.10.parts_ref = bf16[32,64,128]{2,1,0:T(8,128)(2,1)S(1)} all-to-all(bf16[32,64,128]{2,1,0:T(8,128)(2,1)S(1)} %far.1), channel_id=1, replica_groups=mesh['tm'=32,'head'=8] {'tm'}, dimensions={0} | all-to-all | bytes 1048576 | tf_op jit(solution)/shard_map/all_to_all | solution.py:490
  179.0 8.7 %collective-permute-start.14 = (bf16[1,256,640]{2,1,0:T(8,128)(2,1)S(1)}, bf16[1,256,640]{2,1,0:T(8,128)(2,1)S(1)}, u32[]{:S(2)}, u32[]{:S(2)}) collective-permute-start(bf16[1,256,640]{2,1,0:T(8,128)(2,1)S(1)} %get-tuple-element.42), channel_id=1, source_target_pairs={{0,1},{1,0},{2,3},{3,2},{4,5},{5,4},{6,7},{7,6},{8,9},{9,8},{10,11... | collective-permute-start | bytes 983048 | tf_op jit(solution)/shard_map/ppermute | solution.py:68
  189.1 1.6 project.5
  194.1 2.6 %collective-permute-start.13 = (bf16[272,640]{1,0:T(8,128)(2,1)S(1)}, bf16[272,640]{1,0:T(8,128)(2,1)S(1)}, u32[]{:S(2)}, u32[]{:S(2)}) collective-permute-start(bf16[272,640]{1,0:T(8,128)(2,1)S(1)} %get-tuple-element.40), channel_id=1, source_target_pairs={{0,8},{1,9},{2,10},{3,11},{4,12},{5,13},{6,14},{7,15},{8,16},{9,17... | collective-permute-start | bytes 1044488 | tf_op jit(solution)/shard_map/ppermute | solution.py:68
  196.7 1.6 collective-permute-done.15.refs_0_
  198.3 1.6 project.4
  201.3 1.8 collective-permute-start.19
  203.1 3.5 %collective-permute-done.13 = bf16[272,640]{1,0:T(8,128)(2,1)S(1)} collective-permute-done((bf16[272,640]{1,0:T(8,128)(2,1)S(1)}, bf16[272,640]{1,0:T(8,128)(2,1)S(1)}, u32[]{:S(2)}, u32[]{:S(2)}) %collective-permute-start.13) | collective-permute-done | bytes 348192 | tf_op jit(solution)/shard_map/ppermute | solution.py:68
  206.8 3.1 %collective-permute-done.18 = bf16[256,640]{1,0:T(8,128)(2,1)S(1)} collective-permute-done((bf16[256,640]{1,0:T(8,128)(2,1)S(1)}, bf16[256,640]{1,0:T(8,128)(2,1)S(1)}, u32[]{:S(2)}, u32[]{:S(2)}) %collective-permute-start.18) | collective-permute-done | bytes 327712 | tf_op jit(solution)/shard_map/ppermute | solution.py:68
  (66 shorter events, 19.4 us)
Async XLA Ops:
  0.0 206.6 %copy-start = (bf16[256,640]{1,0:T(8,128)(2,1)S(1)}, bf16[256,640]{1,0:T(8,128)(2,1)}, u32[]{:S(2)}) copy-start(bf16[256,640]{1,0:T(8,128)(2,1)} %param.15) | copy-start | bytes 983044
  2.3 22.0 %collective-permute-start.6 = (bf16[256,256]{1,0:T(8,128)(2,1)S(1)}, bf16[256,256]{1,0:T(8,128)(2,1)S(1)}, u32[]{:S(2)}, u32[]{:S(2)}) collective-permute-start(bf16[256,256]{1,0:T(8,128)(2,1)S(1)} %get-tuple-element.29), channel_id=1, source_target_pairs={{0,24},{2,26},{4,28},{6,30},{8,32},{9,33},{10,34},{11,35},{12,36},... | collective-permute-start | bytes 393224 | tf_op jit(solution)/shard_map/ppermute | solution.py:68
  3.6 22.0 %collective-permute-start.7 = (bf16[256,256]{1,0:T(8,128)(2,1)S(1)}, bf16[256,256]{1,0:T(8,128)(2,1)S(1)}, u32[]{:S(2)}, u32[]{:S(2)}) collective-permute-start(bf16[256,256]{1,0:T(8,128)(2,1)S(1)} %get-tuple-element.30), channel_id=1, source_target_pairs={{1,41},{3,43},{5,45},{7,47},{8,48},{10,50},{12,52},{14,54},{17,57}... | collective-permute-start | bytes 393224 | tf_op jit(solution)/shard_map/ppermute | solution.py:68
  13.5 17.4 %collective-permute-start = (bf16[256,256]{1,0:T(8,128)(2,1)S(1)}, bf16[256,256]{1,0:T(8,128)(2,1)S(1)}, u32[]{:S(2)}, u32[]{:S(2)}) collective-permute-start(bf16[256,256]{1,0:T(8,128)(2,1)S(1)} %get-tuple-element.24), channel_id=1, source_target_pairs={{1,17},{3,19},{5,21},{7,23},{8,24},{10,26},{12,28},{14,30},{16,32}... | collective-permute-start | bytes 393224 | tf_op jit(solution)/shard_map/ppermute | solution.py:68
  16.6 14.3 %collective-permute-start.8 = (bf16[256,256]{1,0:T(8,128)(2,1)S(1)}, bf16[256,256]{1,0:T(8,128)(2,1)S(1)}, u32[]{:S(2)}, u32[]{:S(2)}) collective-permute-start(bf16[256,256]{1,0:T(8,128)(2,1)S(1)} %get-tuple-element.31), channel_id=1, source_target_pairs={{0,48},{2,50},{4,52},{6,54},{9,57},{11,59},{13,61},{15,63},{16,0},... | collective-permute-start | bytes 393224 | tf_op jit(solution)/shard_map/ppermute | solution.py:68
  17.9 16.2 %collective-permute-start.1 = (bf16[256,256]{1,0:T(8,128)(2,1)S(1)}, bf16[256,256]{1,0:T(8,128)(2,1)S(1)}, u32[]{:S(2)}, u32[]{:S(2)}) collective-permute-start(bf16[256,256]{1,0:T(8,128)(2,1)S(1)} %get-tuple-element.26), channel_id=1, source_target_pairs={{0,32},{1,33},{2,34},{3,35},{4,36},{5,37},{6,38},{7,39},{9,41},{11... | collective-permute-start | bytes 393224 | tf_op jit(solution)/shard_map/ppermute | solution.py:68
  24.3 9.8 %collective-permute-start.2 = (bf16[256,256]{1,0:T(8,128)(2,1)S(1)}, bf16[256,256]{1,0:T(8,128)(2,1)S(1)}, u32[]{:S(2)}, u32[]{:S(2)}) collective-permute-start(bf16[256,256]{1,0:T(8,128)(2,1)S(1)} %get-tuple-element.27), channel_id=1, source_target_pairs={{0,8},{2,10},{4,12},{6,14},{9,17},{11,19},{13,21},{15,23},{16,24},... | collective-permute-start | bytes 393224 | tf_op jit(solution)/shard_map/ppermute | solution.py:68
  25.6 8.5 %collective-permute-start.3 = (bf16[256,256]{1,0:T(8,128)(2,1)S(1)}, bf16[256,256]{1,0:T(8,128)(2,1)S(1)}, u32[]{:S(2)}, u32[]{:S(2)}) collective-permute-start(bf16[256,256]{1,0:T(8,128)(2,1)S(1)} %get-tuple-element.28), channel_id=1, source_target_pairs={{1,57},{3,59},{5,61},{7,63},{8,0},{9,1},{10,2},{11,3},{12,4},{13,5... | collective-permute-start | bytes 393224 | tf_op jit(solution)/shard_map/ppermute | solution.py:68
  30.9 20.9 %collective-permute-start.9 = (bf16[1024,256]{1,0:T(8,128)(2,1)S(1)}, bf16[1024,256]{1,0:T(8,128)(2,1)S(1)}, u32[]{:S(2)}, u32[]{:S(2)}) collective-permute-start(bf16[1024,256]{1,0:T(8,128)(2,1)S(1)} %constant_dynamic-update-slice_fusion.4.refs_1_.refs_6_), channel_id=1, source_target_pairs={{0,64},{1,65},{2,66},{3,67},{4,68},{5,69},{6,70},{7,71},{8,72},{10... | collective-permute-start | bytes 1572872 | tf_op jit(solution)/shard_map/ppermute | solution.py:68
  34.1 19.6 %collective-permute-start.4 = (bf16[1024,256]{1,0:T(8,128)(2,1)S(1)}, bf16[1024,256]{1,0:T(8,128)(2,1)S(1)}, u32[]{:S(2)}, u32[]{:S(2)}) collective-permute-start(bf16[1024,256]{1,0:T(8,128)(2,1)S(1)} %constant_dynamic-update-slice_fusion.refs_0_.refs_5_), channel_id=1, source_target_pairs={{0,192},{1,193},{2,194},{3,195},{4,196},{5,197},{6,198},{7,199},{8... | collective-permute-start | bytes 1572872 | tf_op jit(solution)/shard_map/ppermute | solution.py:68
  40.6 19.0 %all-to-all-start = ((bf16[32,64,128]{2,1,0:T(8,128)(2,1)}), bf16[32,64,128]{2,1,0:T(8,128)(2,1)S(1)}, u32[]{:S(2)}, u32[]{:S(2)}) async-start(bf16[32,64,128]{2,1,0:T(8,128)(2,1)} %pieces.1), calls=%async_computation | async-start | bytes 1048576 | tf_op jit(solution)/shard_map/all_to_all | solution.py:480
  45.3 23.4 %collective-permute-start.12 = (bf16[1024,256]{1,0:T(8,128)(2,1)S(1)}, bf16[1024,256]{1,0:T(8,128)(2,1)S(1)}, u32[]{:S(2)}, u32[]{:S(2)}) collective-permute-start(bf16[1024,256]{1,0:T(8,128)(2,1)S(1)} %constant_dynamic-update-slice_fusion.refs_0_.refs_5_), channel_id=1, source_target_pairs={{0,64},{1,65},{2,66},{3,67},{4,68},{5,69},{6,70},{7,71},{8,72},{10... | collective-permute-start | bytes 1572872 | tf_op jit(solution)/shard_map/ppermute | solution.py:68
  48.4 27.8 %collective-permute-start.11 = (bf16[1024,256]{1,0:T(8,128)(2,1)S(1)}, bf16[1024,256]{1,0:T(8,128)(2,1)}, u32[]{:S(2)}, u32[]{:S(2)}) collective-permute-start(bf16[1024,256]{1,0:T(8,128)(2,1)S(1)} %constant_dynamic-update-slice_fusion.4.refs_1_.refs_6_), channel_id=1, source_target_pairs={{0,192},{1,193},{2,194},{3,195},{4,196},{5,197},{6,198},{7,199},{8... | collective-permute-start | bytes 1572872 | tf_op jit(solution)/shard_map/ppermute | solution.py:68
  51.8 29.5 %collective-permute-start.10 = (bf16[1024,256]{1,0:T(8,128)(2,1)S(1)}, bf16[1024,256]{1,0:T(8,128)(2,1)}, u32[]{:S(2)}, u32[]{:S(2)}) collective-permute-start(bf16[1024,256]{1,0:T(8,128)(2,1)S(1)} %collective-permute-done.9.refs_1_.refs_8_), channel_id=1, source_target_pairs={{0,64},{1,65},{2,66},{3,67},{4,68},{5,69},{6,70},{7,71},{8,72},{10... | collective-permute-start | bytes 1572872 | tf_op jit(solution)/shard_map/ppermute | solution.py:68
  53.8 27.6 %collective-permute-start.5 = (bf16[1024,256]{1,0:T(8,128)(2,1)S(1)}, bf16[1024,256]{1,0:T(8,128)(2,1)}, u32[]{:S(2)}, u32[]{:S(2)}) collective-permute-start(bf16[1024,256]{1,0:T(8,128)(2,1)S(1)} %collective-permute-done.4.refs_0_.refs_9_), channel_id=1, source_target_pairs={{0,192},{1,193},{2,194},{3,195},{4,196},{5,197},{6,198},{7,199},{8... | collective-permute-start | bytes 1572872 | tf_op jit(solution)/shard_map/ppermute | solution.py:68
  76.3 101.6 %slice-start = ((s8[6553600]{0:T(1024)(128)(4,1)}), s8[4194304]{0:T(1024)(128)(4,1)S(1)}, s32[]{:S(2)}) async-start(s8[6553600]{0:T(1024)(128)(4,1)} %bitcast.37), calls=%async_computation.2 | async-start | bytes 8388608
  81.4 96.5 %slice-start.1 = ((s8[6553600]{0:T(1024)(128)(4,1)}), s8[2359296]{0:T(1024)(128)(4,1)S(1)}, s32[]{:S(2)}) async-start(s8[6553600]{0:T(1024)(128)(4,1)} %bitcast.37), calls=%async_computation.3 | async-start | bytes 4718592
  179.0 10.0 %collective-permute-start.14 = (bf16[1,256,640]{2,1,0:T(8,128)(2,1)S(1)}, bf16[1,256,640]{2,1,0:T(8,128)(2,1)S(1)}, u32[]{:S(2)}, u32[]{:S(2)}) collective-permute-start(bf16[1,256,640]{2,1,0:T(8,128)(2,1)S(1)} %get-tuple-element.42), channel_id=1, source_target_pairs={{0,1},{1,0},{2,3},{3,2},{4,5},{5,4},{6,7},{7,6},{8,9},{9,8},{10,11... | collective-permute-start | bytes 983048 | tf_op jit(solution)/shard_map/ppermute | solution.py:68
  190.7 9.2 %collective-permute-start.17 = (bf16[3,256,640]{2,1,0:T(8,128)(2,1)S(1)}, bf16[3,256,640]{2,1,0:T(8,128)(2,1)S(1)}, u32[]{:S(2)}, u32[]{:S(2)}) collective-permute-start(bf16[3,256,640]{2,1,0:T(8,128)(2,1)S(1)} %project.5), channel_id=1, source_target_pairs={{0,1},{1,0},{2,3},{3,2},{4,5},{5,4},{6,7},{7,6},{8,9},{9,8},{10,11... | collective-permute-start | bytes 2949128 | tf_op jit(solution)/shard_map/ppermute | solution.py:68
  191.2 7.1 %collective-permute-start.15 = (bf16[128,640]{1,0:T(8,128)(2,1)S(1)}, bf16[128,640]{1,0:T(8,128)(2,1)S(1)}, u32[]{:S(2)}, u32[]{:S(2)}) collective-permute-start(bf16[128,640]{1,0:T(8,128)(2,1)S(1)} %get-tuple-element.46), channel_id=1, source_target_pairs={{0,2},{1,3},{2,4},{3,5},{4,6},{5,7},{6,0},{7,1},{8,10},{9,11},{10,... | collective-permute-start | bytes 491528 | tf_op jit(solution)/shard_map/ppermute | solution.py:68
  192.6 5.7 %collective-permute-start.16 = (bf16[128,640]{1,0:T(8,128)(2,1)S(1)}, bf16[128,640]{1,0:T(8,128)(2,1)S(1)}, u32[]{:S(2)}, u32[]{:S(2)}) collective-permute-start(bf16[128,640]{1,0:T(8,128)(2,1)S(1)} %get-tuple-element.45), channel_id=1, source_target_pairs={{0,6},{1,7},{2,0},{3,1},{4,2},{5,3},{6,4},{7,5},{8,14},{9,15},{10,... | collective-permute-start | bytes 491528 | tf_op jit(solution)/shard_map/ppermute | solution.py:68
  194.1 12.5 %collective-permute-start.13 = (bf16[272,640]{1,0:T(8,128)(2,1)S(1)}, bf16[272,640]{1,0:T(8,128)(2,1)S(1)}, u32[]{:S(2)}, u32[]{:S(2)}) collective-permute-start(bf16[272,640]{1,0:T(8,128)(2,1)S(1)} %get-tuple-element.40), channel_id=1, source_target_pairs={{0,8},{1,9},{2,10},{3,11},{4,12},{5,13},{6,14},{7,15},{8,16},{9,17... | collective-permute-start | bytes 1044488 | tf_op jit(solution)/shard_map/ppermute | solution.py:68
  200.2 9.6 %collective-permute-start.18 = (bf16[256,640]{1,0:T(8,128)(2,1)S(1)}, bf16[256,640]{1,0:T(8,128)(2,1)S(1)}, u32[]{:S(2)}, u32[]{:S(2)}) collective-permute-start(bf16[256,640]{1,0:T(8,128)(2,1)S(1)} %pad_maximum_fusion), channel_id=1, source_target_pairs={{0,2},{1,3},{2,4},{3,5},{4,6},{5,7},{6,0},{7,1},{8,10},{9,11},{10,... | collective-permute-start | bytes 983048 | tf_op jit(solution)/shard_map/ppermute | solution.py:68
  201.3 8.5 %collective-permute-start.19 = (bf16[256,640]{1,0:T(8,128)(2,1)S(1)}, bf16[256,640]{1,0:T(8,128)(2,1)S(1)}, u32[]{:S(2)}, u32[]{:S(2)}) collective-permute-start(bf16[256,640]{1,0:T(8,128)(2,1)S(1)} %pad_maximum_fusion.1), channel_id=1, source_target_pairs={{0,6},{1,7},{2,0},{3,1},{4,2},{5,3},{6,4},{7,5},{8,14},{9,15},{10,... | collective-permute-start | bytes 983048 | tf_op jit(solution)/shard_map/ppermute | solution.py:68
  (5 other events, 4.6 us)
